TPU v7x, 32 devices: a whole 2x2x4 slice. The times are simulated.
32 devices in a mesh: dev: 32 (over z, y, x, core).
Axes of the slice: x: 2, y: 2, z: 4, core: 2. Of those that a mesh axis runs over, the one named last changes fastest.
Arguments:
- inputs: bfloat16 [8192, 1536], P('dev'), may hold values from -6 to 6
- positions: int32 [8192], P('dev'), may hold values from 0 to 2047, as said below
- norm_first: bfloat16 [1536], P('dev'), may hold values from 0.25 to 1.75
- query_weight: bfloat16 [1536, 1536], P('dev'), may hold values from -0.15625 to 0.15625
- key_weight: bfloat16 [1536, 768], P('dev'), may hold values from -0.15625 to 0.15625
- value_weight: bfloat16 [1536, 768], P('dev'), may hold values from -0.15625 to 0.15625
- out_weight: bfloat16 [1536, 1536], P('dev'), may hold values from -2.5 to 2.5
- norm_second: bfloat16 [1536], P('dev'), may hold values from 0.25 to 1.75
- gate_weight: bfloat16 [1536, 4096], P('dev'), may hold values from -0.15625 to 0.15625
- up_weight: bfloat16 [1536, 4096], P('dev'), may hold values from -0.15625 to 0.15625
- down_weight: bfloat16 [4096, 1536], P('dev'), may hold values from -0.09375 to 0.09375
- cotangent: bfloat16 [8192, 1536], P('dev'), may hold values from -6 to 6
Outputs:
- outputs: bfloat16 [8192, 1536], P('dev')
- input_grad: float32 [8192, 1536], P('dev')
- first_grad: float32 [1536], P('dev')
- query_grad: float32 [1536, 1536], P('dev')
- key_grad: float32 [1536, 768], P('dev')
- value_grad: float32 [1536, 768], P('dev')
- out_grad: float32 [1536, 1536], P('dev')
- second_grad: float32 [1536], P('dev')
- gate_grad: float32 [1536, 4096], P('dev')
- up_grad: float32 [1536, 4096], P('dev')
- down_grad: float32 [4096, 1536], P('dev')
Inputs may be any that keep to these rules, and one draw needn't show every extreme that they name: positions count 0, 1, 2, ... along each sequence and start at 0 at the first token; every sequence but the last has 1024 to 2048 tokens, one has exactly 2048.
All inputs are finite; a program needn't handle non-finite values.
Results may differ from a plain program's by a relative error of at most 0.02.
Values may be sent and summed in bfloat16 or wider, within the bound.
No kernel may reach another device: no remote copies, remote signals or barrier semaphores. Data moves between devices by JAX's collectives and lax.ppermute only.
A program may use at most 448 MiB of HBM per device.

v0:
```python
import math

import jax
import jax.numpy as jnp
from jax import lax
from jax.sharding import PartitionSpec as P

HEADS = 16
KV_HEADS = 8
HEAD_DIM = 96


eps_norm = 1e-05
rope_base = 100000.0
masked_score = -1e30


def shifted_2(value, axis, steps):
    count = lax.axis_size(axis)
    leading, last = (max(0, -steps), min(count, count - steps))
    return lax.ppermute(value, axis, [(source, source + steps) for source in range(leading, last)])


def rms_scale(values, gain):
    return values * lax.rsqrt(jnp.mean(values * values, axis=-1, keepdims=True) + eps_norm) * gain


def rope_tables(positions):
    half_dim = HEAD_DIM // 2
    frequency = rope_base ** (-(jnp.arange(half_dim, dtype=jnp.float32) * 2.0 / HEAD_DIM))
    angles = positions.astype(jnp.float32)[:, None] * frequency[None, :]
    angles = jnp.concatenate([angles, angles], axis=1)
    return (jnp.cos(angles), jnp.sin(angles))


def rotate(values, cosine, sine_table):
    half_dim = values.shape[-1] // 2
    turned = jnp.concatenate([-values[..., half_dim:], values[..., :half_dim]], axis=-1)
    return values * cosine[:, None, :] + turned * sine_table[:, None, :]


def unrotate(gradient, cosine, sine_table):
    half_dim = gradient.shape[-1] // 2
    scaled = gradient * sine_table[:, None, :]
    turned = jnp.concatenate([scaled[..., half_dim:], -scaled[..., :half_dim]], axis=-1)
    return gradient * cosine[:, None, :] + turned


def multiply(operand, weights):
    return jnp.dot(operand, weights, preferred_element_type=jnp.float32)


def inner_rows(operand, weights):
    return lax.dot_general(
        operand, weights, (((0,), (0,)), ((), ())), preferred_element_type=jnp.float32
    )


def outer_cols(operand, weights):
    return lax.dot_general(
        operand, weights, (((1,), (1,)), ((), ())), preferred_element_type=jnp.float32
    )


def split_piece(kv_piece):
    tokens_dev = kv_piece.shape[0]
    kv_width = kv_piece.shape[1] // 2
    key_piece = kv_piece[:, :kv_width].reshape(tokens_dev, KV_HEADS, HEAD_DIM)
    value_piece = kv_piece[:, kv_width:].reshape(tokens_dev, KV_HEADS, HEAD_DIM)
    return (key_piece, value_piece)


def piece_scores(query_groups, key_piece, offset, positions):
    tokens_dev = query_groups.shape[0]
    score_scale = 1.0 / math.sqrt(HEAD_DIM)
    scores = (
        jnp.einsum("qkgd,tkd->kgqt", query_groups, key_piece, preferred_element_type=jnp.float32)
        * score_scale
    )
    row_index = jnp.arange(tokens_dev, dtype=jnp.int32)
    distance = offset * tokens_dev + row_index[:, None] - row_index[None, :]
    visible = (distance >= 0) & (distance <= positions[:, None])
    return jnp.where(visible, scores, masked_score)


def online_pass(query_groups, pieces, positions):
    query_shape = query_groups.shape
    stat_shape = (query_shape[1], query_shape[2], query_shape[0])
    initial = (
        jnp.full(stat_shape, masked_score, jnp.float32),
        jnp.zeros(stat_shape, jnp.float32),
        jnp.zeros(query_shape, jnp.float32),
    )

    def online_advance(running, packed):
        running_max, running_sum, summed = running
        offset, kv_piece = packed
        key_piece, value_piece = split_piece(kv_piece)
        scores = piece_scores(query_groups, key_piece, offset, positions)
        new_max = jnp.maximum(running_max, jnp.max(scores, axis=-1))
        factor = jnp.exp(running_max - new_max)
        weights = jnp.exp(scores - new_max[..., None])
        running_sum = running_sum * factor + jnp.sum(weights, axis=-1)
        summed = summed * jnp.transpose(factor, (2, 0, 1))[..., None] + jnp.einsum(
            "kgqt,tkd->qkgd",
            weights.astype(jnp.bfloat16),
            value_piece,
            preferred_element_type=jnp.float32,
        )
        return ((new_max, running_sum, summed), None)

    offsets = jnp.arange(pieces.shape[0], dtype=jnp.int32)
    (running_max, running_sum, summed), unused = lax.scan(
        online_advance, initial, (offsets, pieces)
    )
    attended_f = summed / jnp.transpose(running_sum, (2, 0, 1))[..., None]
    return (running_max + jnp.log(running_sum), attended_f)


def gradient_pass(query_groups, grad_groups, pieces, positions, normalizer, delta):
    tokens_dev = query_groups.shape[0]
    score_scale = 1.0 / math.sqrt(HEAD_DIM)

    def gradient_advance(summed, packed):
        offset, kv_piece = packed
        key_piece, value_piece = split_piece(kv_piece)
        scores = piece_scores(query_groups, key_piece, offset, positions)
        softmax_f = jnp.exp(scores - normalizer[..., None])
        slopes = jnp.einsum(
            "qkgd,tkd->kgqt", grad_groups, value_piece, preferred_element_type=jnp.float32
        )
        grad_scores = (softmax_f * (slopes - delta[..., None])).astype(jnp.bfloat16)
        summed = summed + jnp.einsum(
            "kgqt,tkd->qkgd", grad_scores, key_piece, preferred_element_type=jnp.float32
        )
        key_part = (
            jnp.einsum(
                "kgqt,qkgd->tkd", grad_scores, query_groups, preferred_element_type=jnp.float32
            )
            * score_scale
        )
        value_part = jnp.einsum(
            "kgqt,qkgd->tkd",
            softmax_f.astype(jnp.bfloat16),
            grad_groups,
            preferred_element_type=jnp.float32,
        )
        piece_grads = jnp.concatenate(
            [key_part.reshape(tokens_dev, -1), value_part.reshape(tokens_dev, -1)], axis=1
        )
        return (summed, piece_grads)

    offsets = jnp.arange(pieces.shape[0], dtype=jnp.int32)
    summed, piece_grads = lax.scan(
        gradient_advance, jnp.zeros(query_groups.shape, jnp.float32), (offsets, pieces)
    )
    return (summed * score_scale, piece_grads)


def per_device(
    inputs,
    positions,
    norm_first,
    query_weight,
    key_weight,
    value_weight,
    out_weight,
    norm_second,
    gate_weight,
    up_weight,
    down_weight,
    cotangent,
):
    tokens_dev = inputs.shape[0]
    kv_width = key_weight.shape[1]
    group_size = HEADS // KV_HEADS
    longest = tokens_dev * lax.axis_size("dev") // 4
    steps_back = (longest - 2) // tokens_dev + 1
    cosine, sine_table = rope_tables(positions)
    features = inputs.astype(jnp.float32)
    attention_weights = (
        lax.all_gather(norm_first, "dev", axis=0, tiled=True),
        lax.all_gather(query_weight, "dev", axis=0, tiled=True),
        lax.all_gather(key_weight, "dev", axis=0, tiled=True),
        lax.all_gather(value_weight, "dev", axis=0, tiled=True),
        lax.all_gather(out_weight, "dev", axis=0, tiled=True),
    )
    gain_full, query_full, key_full, value_full, out_full = attention_weights
    normed_f = rms_scale(features, gain_full.astype(jnp.float32))
    normed_b = normed_f.astype(jnp.bfloat16)
    query_lin = multiply(normed_b, query_full).reshape(tokens_dev, HEADS, HEAD_DIM)
    key_lin = multiply(normed_b, key_full).reshape(tokens_dev, KV_HEADS, HEAD_DIM)
    value_b = multiply(normed_b, value_full).astype(jnp.bfloat16)
    query_groups = (
        rotate(query_lin, cosine, sine_table)
        .astype(jnp.bfloat16)
        .reshape(tokens_dev, KV_HEADS, group_size, HEAD_DIM)
    )
    key_b = rotate(key_lin, cosine, sine_table).astype(jnp.bfloat16).reshape(tokens_dev, kv_width)
    own_piece = jnp.concatenate([key_b, value_b], axis=1)

    def receive_advance(current, unused):
        shifted = shifted_2(current, "dev", 1)
        return (shifted, shifted)

    last_piece, received = lax.scan(receive_advance, own_piece, None, length=steps_back)
    pieces = jnp.concatenate([own_piece[None], received], axis=0)
    normalizer, attended_f = online_pass(query_groups, pieces, positions)
    attended_b = attended_f.reshape(tokens_dev, HEADS * HEAD_DIM).astype(jnp.bfloat16)
    middle = features + multiply(attended_b, out_full)
    forward_attn = (
        normed_f,
        normed_b,
        query_groups,
        pieces,
        normalizer,
        attended_b,
        attended_f,
        middle,
    )
    mixer_weights = (
        lax.all_gather(norm_second, "dev", axis=0, tiled=True),
        lax.all_gather(gate_weight, "dev", axis=0, tiled=True),
        lax.all_gather(up_weight, "dev", axis=0, tiled=True),
        lax.all_gather(down_weight, "dev", axis=0, tiled=True),
    )
    middle = forward_attn[7]
    gain_full, gate_full, up_full, down_full = mixer_weights
    normed_mb = rms_scale(middle, gain_full.astype(jnp.float32)).astype(jnp.bfloat16)
    gate = multiply(normed_mb, gate_full)
    up_part = multiply(normed_mb, up_full)
    hidden_b = (jax.nn.silu(gate) * up_part).astype(jnp.bfloat16)
    result = middle + multiply(hidden_b, down_full)
    forward_mixer = (normed_mb, gate, up_part, hidden_b, result)
    outputs = forward_mixer[4].astype(jnp.bfloat16)
    gain_second, gate_full, up_full, down_full = mixer_weights
    normed_mb, gate, up_part, hidden_b, unused_result = forward_mixer
    grad_output = cotangent.astype(jnp.float32)
    down_part = inner_rows(hidden_b, cotangent)
    grad_hidden = outer_cols(cotangent, down_full)
    unused_value, swiglu_pull = jax.vjp(
        lambda gate_in, up_in: jax.nn.silu(gate_in) * up_in, gate, up_part
    )
    grad_gate, grad_up = swiglu_pull(grad_hidden)
    grad_gate_b = grad_gate.astype(jnp.bfloat16)
    grad_up_b = grad_up.astype(jnp.bfloat16)
    gate_part = inner_rows(normed_mb, grad_gate_b)
    up_grad_part = inner_rows(normed_mb, grad_up_b)
    grad_normed_second = outer_cols(grad_gate_b, gate_full) + outer_cols(grad_up_b, up_full)
    middle = forward_attn[7]
    unused_norm, norm_pull = jax.vjp(rms_scale, middle, gain_second.astype(jnp.float32))
    grad_middle_norm, second_part = norm_pull(grad_normed_second)
    grad_middle = grad_output + grad_middle_norm
    mixer_grads = (
        lax.psum_scatter(second_part, "dev", scatter_dimension=0, tiled=True),
        lax.psum_scatter(gate_part, "dev", scatter_dimension=0, tiled=True),
        lax.psum_scatter(up_grad_part, "dev", scatter_dimension=0, tiled=True),
        lax.psum_scatter(down_part, "dev", scatter_dimension=0, tiled=True),
    )
    gain_first, query_full, key_full, value_full, out_full = attention_weights
    normed_f, normed_b, query_groups, pieces, normalizer, attended_b, attended_f, unused_middle = (
        forward_attn
    )
    grad_attn_b = grad_middle.astype(jnp.bfloat16)
    out_part = inner_rows(attended_b, grad_attn_b)
    grad_attended_b = outer_cols(grad_attn_b, out_full).astype(jnp.bfloat16)
    grad_groups = grad_attended_b.reshape(tokens_dev, KV_HEADS, group_size, HEAD_DIM)
    delta = jnp.transpose(jnp.sum(grad_groups.astype(jnp.float32) * attended_f, axis=-1), (1, 2, 0))
    grad_query_rot, piece_grads = gradient_pass(
        query_groups, grad_groups, pieces, positions, normalizer, delta
    )

    def send_back(carried, piece_term):
        shifted = shifted_2((carried + piece_term).astype(jnp.bfloat16), "dev", -1).astype(
            jnp.float32
        )
        return (shifted, None)

    returned, unused_steps = lax.scan(
        send_back, jnp.zeros(piece_grads.shape[1:], jnp.float32), piece_grads[1:], reverse=True
    )
    own_grads = piece_grads[0] + returned
    grad_key_rot = own_grads[:, :kv_width].reshape(tokens_dev, KV_HEADS, HEAD_DIM)
    grad_value_b = own_grads[:, kv_width:].astype(jnp.bfloat16)
    grad_key_b = (
        unrotate(grad_key_rot, cosine, sine_table)
        .reshape(tokens_dev, kv_width)
        .astype(jnp.bfloat16)
    )
    grad_query_b = (
        unrotate(grad_query_rot.reshape(tokens_dev, HEADS, HEAD_DIM), cosine, sine_table)
        .reshape(tokens_dev, HEADS * HEAD_DIM)
        .astype(jnp.bfloat16)
    )
    query_part = inner_rows(normed_b, grad_query_b)
    key_part = inner_rows(normed_b, grad_key_b)
    value_part = inner_rows(normed_b, grad_value_b)
    grad_normed_first = (
        outer_cols(grad_query_b, query_full)
        + outer_cols(grad_key_b, key_full)
        + outer_cols(grad_value_b, value_full)
    )
    unused_first, first_pull = jax.vjp(rms_scale, features, gain_first.astype(jnp.float32))
    grad_input_norm, first_part = first_pull(grad_normed_first)
    input_grad = grad_middle + grad_input_norm
    attn_grads = (
        lax.psum_scatter(first_part, "dev", scatter_dimension=0, tiled=True),
        lax.psum_scatter(query_part, "dev", scatter_dimension=0, tiled=True),
        lax.psum_scatter(key_part, "dev", scatter_dimension=0, tiled=True),
        lax.psum_scatter(value_part, "dev", scatter_dimension=0, tiled=True),
        lax.psum_scatter(out_part, "dev", scatter_dimension=0, tiled=True),
    )
    return (
        outputs,
        input_grad,
        attn_grads[0],
        attn_grads[1],
        attn_grads[2],
        attn_grads[3],
        attn_grads[4],
        mixer_grads[0],
        mixer_grads[1],
        mixer_grads[2],
        mixer_grads[3],
    )


def solution(mesh):
    in_specs = (
        P("dev", None),
        P("dev"),
        P("dev"),
        P("dev", None),
        P("dev", None),
        P("dev", None),
        P("dev", None),
        P("dev"),
        P("dev", None),
        P("dev", None),
        P("dev", None),
        P("dev", None),
    )
    out_specs = (
        P("dev", None),
        P("dev", None),
        P("dev"),
        P("dev", None),
        P("dev", None),
        P("dev", None),
        P("dev", None),
        P("dev"),
        P("dev", None),
        P("dev", None),
        P("dev", None),
    )
    return jax.shard_map(
        per_device, mesh=mesh, in_specs=in_specs, out_specs=out_specs, check_vma=False
    )
```

profile of v0, /device:TPU:10, one launch (start us, length us, event | category | flops | bytes accessed | tf_op | source)
XLA Modules:
  0.0 2158.7 jit_solution(12276238668122434051)
XLA Ops:
  13.8 41.5 %all-reduce.5 = (bf16[1536]{0:T(1024)(128)(2,1)S(1)}, bf16[1536]{0:T(1024)(128)(2,1)S(1)}) all-reduce(bf16[1536]{0:T(1024)(128)(2,1)S(1)} %dynamic-update-slice, bf16[1536]{0:T(1024)(128)(2,1)S(1)} %dynamic-update-slice.1), channel_id=1, replica_groups=mesh['dev'=32] {'dev'}, use_global_device_ids=true, to_apply=%add | all-reduce | flops 3072 | bytes 12288
  57.5 10.8 all-gather.8.cloned.1.call-done
  74.4 53.0 %all-gather.10.cloned.1.call-done = bf16[1536,768]{1,0:T(8,128)(2,1)} async-done(((bf16[48,768]{1,0:T(8,128)(2,1)}), bf16[1536,768]{1,0:T(8,128)(2,1)}) %all-gather.10.cloned.1.call-update) | async-done | bytes 2359312 | tf_op jit(solution)/shard_map/all_gather | solution.py:185
  131.2 165.9 %while.55 = (s32[]{:T(128)}, bf16[256,1536]{1,0:T(8,128)(2,1)}, bf16[8,256,1536]{1,2,0:T(8,128)(2,1)}, s32[]{:T(128)}) while((s32[]{:T(128)}, bf16[256,1536]{1,0:T(8,128)(2,1)}, bf16[8,256,1536]{1,2,0:T(8,128)(2,1)}, s32[]{:T(128)}) %tuple.117), condition=%wide.region_2.3_spmd, body=%wide.region_1.2_spmd.sunk | while | flops 2 | bytes 7864425 | solution.py:206
  133.3 12.4 collective-permute-done
  149.8 15.8 collective-permute-done
  169.7 18.6 collective-permute-done
  194.7 9.2 collective-permute-done
  206.0 5.2 collective-permute-start
  211.2 10.8 collective-permute-done
  227.7 14.0 collective-permute-done
  245.7 20.4 collective-permute-done
  270.1 24.9 %collective-permute-done = bf16[256,1536]{1,0:T(8,128)(2,1)S(1)} collective-permute-done((bf16[256,1536]{1,0:T(8,128)(2,1)}, bf16[256,1536]{1,0:T(8,128)(2,1)S(1)}, u32[]{:S(2)}, u32[]{:S(2)}) %collective-permute-start) | collective-permute-done | bytes 786464 | tf_op jit(solution)/shard_map/while/body/eval_jaxpr/ppermute | solution.py:21
  297.1 6.3 pad_maximum_fusion
  303.4 4.3 fusion.70
  309.3 111.2 %while.56 = (s32[]{:T(128)}, f32[8,2,256]{2,1,0:T(2,128)S(1)}, f32[8,2,256]{2,1,0:T(2,128)}, f32[256,8,2,96]{0,3,2,1:T(8,128)S(1)}, s32[9]{0:T(128)S(1)}, /*inde...) while((s32[]{:T(128)}, f32[8,2,256]{2,1,0:T(2,128)S(1)}, ...), condition=%wide.region_6.7_spmd.clone, body=%wide.region_3.6_spmd.clone.sunk | while | flops 415654144 | bytes 38411936 | solution.py:113
  427.8 11.1 fusion.81
  438.9 33.1 %all-gather.18.cloned.1.call-done = bf16[1536,4096]{1,0:T(8,128)(2,1)} async-done(((bf16[48,4096]{1,0:T(8,128)(2,1)}), bf16[1536,4096]{1,0:T(8,128)(2,1)}) %all-gather.18.cloned.1.call-update) | async-done | bytes 12582928 | tf_op jit(solution)/shard_map/all_gather | solution.py:224
  472.1 9.5 fusion.82
  481.6 87.6 %all-gather.20.cloned.1.call-done = bf16[4096,1536]{1,0:T(8,128)(2,1)} async-done(((bf16[128,1536]{1,0:T(8,128)(2,1)}), bf16[4096,1536]{1,0:T(8,128)(2,1)}) %all-gather.20.cloned.1.call-update) | async-done | bytes 12582928 | tf_op jit(solution)/shard_map/all_gather | solution.py:225
  569.2 11.5 multiply_convert_fusion
  580.7 7.4 fusion.83
  588.2 10.8 multiply_reduce_fusion
  606.0 118.4 %while.57 = (s32[]{:T(128)}, f32[256,8,2,96]{0,3,2,1:T(8,128)}, f32[9,256,1536]{1,2,0:T(8,128)}, bf16[9,256,1536]{1,2,0:T(8,128)(2,1)}, s32[9]{0:T(128)S(1)}, /*...) while((s32[]{:T(128)}, f32[256,8,2,96]{0,3,2,1:T(8,128)}, ...), condition=%wide.region_11.12_spmd.clone, body=%wide.region_10.11_spmd.clone.sunk | while | flops 1018757376 | bytes 34459304 | solution.py:154
  724.4 15.1 copy.64
  739.5 10.4 slice.75
  749.9 120.3 %while.58 = (s32[]{:T(128)}, f32[256,1536]{1,0:T(8,128)S(1)}, f32[8,256,1536]{2,1,0:T(8,128)}, s32[]{:T(128)}, s32[]{:T(128)}, /*index=5*/s32[]{:T(128)}) while((s32[]{:T(128)}, f32[256,1536]{1,0:T(8,128)S(1)}, f32[8,256,1536]{2,1,0:T(8,128)}, s32[]{:T(128)}, s32[]{:T(128)}, /*index=5*/s32[]{:T(128)}) %tuple.159), condition=%wide.region_13.14_spmd.clone, body=%wide.region_12.13_spmd.clone.sunk | while | flops 1572868 | bytes 9437319 | solution.py:279
  753.9 9.5 collective-permute-done.1
  769.1 9.5 collective-permute-done.1
  784.3 9.5 collective-permute-done.1
  799.5 9.5 collective-permute-done.1
  814.7 9.5 collective-permute-done.1
  829.9 9.5 collective-permute-done.1
  845.1 9.5 collective-permute-done.1
  860.3 9.5 collective-permute-done.1
  883.3 5.2 fusion.68
  890.2 4.9 fusion.56
  896.2 12.1 fusion.85
  908.4 12.2 fusion.86
  921.8 12.5 fusion.87
  943.8 53.7 %all-reduce.4 = (f32[1536]{0:T(1024)S(1)}, f32[1536]{0:T(1024)S(1)}) all-reduce(f32[1536]{0:T(1024)S(1)} %get-tuple-element.281, f32[1536]{0:T(1024)S(1)} %copy-done.44), channel_id=2, replica_groups=mesh['dev'=32] {'dev'}, use_global_device_ids=true, to_apply=%region_16.17.clone | all-reduce | flops 3072 | bytes 24576
  1001.9 7.5 fusion.42
  1009.4 102.7 %reduce-scatter.12.cloned.1.call-done = f32[48,768]{1,0:T(8,128)} async-done(((f32[1536,768]{1,0:T(8,128)}), f32[48,768]{1,0:T(8,128)}) %reduce-scatter.12.cloned.1.call-update) | async-done | bytes 147472 | tf_op jit(solution)/shard_map/reduce_scatter | solution.py:310
  1112.0 140.9 %reduce-scatter.8.cloned.1.call-done = f32[48,1536]{1,0:T(8,128)} async-done(((f32[1536,1536]{1,0:T(8,128)}), f32[48,1536]{1,0:T(8,128)}) %reduce-scatter.8.cloned.1.call-update) | async-done | bytes 294928 | tf_op jit(solution)/shard_map/reduce_scatter | solution.py:308
  1252.9 142.1 %reduce-scatter.14.cloned.1.call-done = f32[48,1536]{1,0:T(8,128)} async-done(((f32[1536,1536]{1,0:T(8,128)}), f32[48,1536]{1,0:T(8,128)}) %reduce-scatter.14.cloned.1.call-update) | async-done | bytes 294928 | tf_op jit(solution)/shard_map/reduce_scatter | solution.py:311
  1395.0 251.6 %reduce-scatter.16.cloned.1.call-done = f32[48,4096]{1,0:T(8,128)} async-done(((f32[1536,4096]{1,0:T(8,128)}), f32[48,4096]{1,0:T(8,128)}) %reduce-scatter.16.cloned.1.call-update) | async-done | bytes 786448 | tf_op jit(solution)/shard_map/reduce_scatter | solution.py:256
  1646.6 253.2 %reduce-scatter.18.cloned.1.call-done = f32[48,4096]{1,0:T(8,128)} async-done(((f32[1536,4096]{1,0:T(8,128)}), f32[48,4096]{1,0:T(8,128)}) %reduce-scatter.18.cloned.1.call-update) | async-done | bytes 786448 | tf_op jit(solution)/shard_map/reduce_scatter | solution.py:257
  1899.8 251.9 %reduce-scatter.20.cloned.1.call-done = f32[128,1536]{1,0:T(8,128)} async-done(((f32[4096,1536]{1,0:T(8,128)}), f32[128,1536]{1,0:T(8,128)}) %reduce-scatter.20.cloned.1.call-update) | async-done | bytes 786448 | tf_op jit(solution)/shard_map/reduce_scatter | solution.py:258
  (577 shorter events, 358.8 us)
Async XLA Ops:
  7.2 48.1 %copy-start.4 = (bf16[256,1536]{1,0:T(8,128)(2,1)S(1)}, bf16[256,1536]{1,0:T(8,128)(2,1)}, u32[]{:S(2)}) copy-start(bf16[256,1536]{1,0:T(8,128)(2,1)} %param.20) | copy-start | bytes 2359300
  7.2 48.9 %copy-start.37 = (s32[256]{0:T(256)S(1)}, s32[256]{0:T(256)}, u32[]{:S(2)}) copy-start(s32[256]{0:T(256)} %param.21) | copy-start | bytes 3076
  7.2 61.1 %all-gather.8.cloned.1.call-start = ((), (), s32[]{:S(2)}) async-start(), calls=%async_computation.7 | async-start | bytes 2433024 | tf_op jit(solution)/shard_map/all_gather | solution.py:184
  7.9 119.5 %all-gather.10.cloned.1.call-start = ((), (), s32[]{:S(2)}) async-start(), calls=%async_computation.8 | async-start | bytes 2433024 | tf_op jit(solution)/shard_map/all_gather | solution.py:185
  8.7 294.7 %all-gather.12.cloned.1.call-start = ((), (), s32[]{:S(2)}) async-start(), calls=%async_computation.9 | async-start | bytes 4866048 | tf_op jit(solution)/shard_map/all_gather | solution.py:183
  9.4 412.9 %all-gather.14.cloned.1.call-start = ((), (), s32[]{:S(2)}) async-start(), calls=%async_computation.10 | async-start | bytes 4866048 | tf_op jit(solution)/shard_map/all_gather | solution.py:186
  10.0 417.8 %all-gather.16.cloned.1.call-start = ((), (), s32[]{:S(2)}) async-start(), calls=%async_computation.11 | async-start | bytes 12976128 | tf_op jit(solution)/shard_map/all_gather | solution.py:223
  10.6 461.5 %all-gather.18.cloned.1.call-start = ((), (), s32[]{:S(2)}) async-start(), calls=%async_computation.12 | async-start | bytes 12976128 | tf_op jit(solution)/shard_map/all_gather | solution.py:224
  11.2 558.0 %all-gather.20.cloned.1.call-start = ((), (), s32[]{:S(2)}) async-start(), calls=%async_computation.13 | async-start | bytes 12976128 | tf_op jit(solution)/shard_map/all_gather | solution.py:225
  11.9 997.5 %reduce-scatter.10.cloned.1.call-start = ((), (), s32[]{:S(2)}) async-start(), calls=%async_computation.15 | async-start | bytes 4866048 | tf_op jit(solution)/shard_map/reduce_scatter | solution.py:309
  55.3 248.1 %copy-start.35 = (f32[1536]{0:T(1024)}, f32[1536]{0:T(1024)S(1)}, u32[]{:S(2)}) copy-start(f32[1536]{0:T(1024)S(1)} %convert_element_type.96) | copy-start | bytes 18436
  56.1 247.3 %copy-start.40 = (f32[256]{0:T(256)}, f32[256]{0:T(256)S(1)}, u32[]{:S(2)}) copy-start(f32[256]{0:T(256)S(1)} %fusion.62) | copy-start | bytes 3076
  56.5 251.4 %copy-start.23 = (f32[256,96]{0,1:T(8,128)}, f32[256,96]{0,1:T(8,128)S(1)}, u32[]{:S(2)}) copy-start(f32[256,96]{0,1:T(8,128)S(1)} %get-tuple-element.357) | copy-start | bytes 294916
  56.6 251.4 %copy-start.26 = (f32[256,96]{0,1:T(8,128)}, f32[256,96]{0,1:T(8,128)S(1)}, u32[]{:S(2)}) copy-start(f32[256,96]{0,1:T(8,128)S(1)} %get-tuple-element.356) | copy-start | bytes 294916
  74.4 55.5 %copy-start.31 = (bf16[256,768]{1,0:T(8,128)(2,1)S(1)}, bf16[256,768]{1,0:T(8,128)(2,1)}, u32[]{:S(2)}) copy-start(bf16[256,768]{1,0:T(8,128)(2,1)} %add_convert_fusion) | copy-start | bytes 1179652
  131.2 14.6 collective-permute-start
  147.9 17.7 collective-permute-start
  167.7 20.6 collective-permute-start
  190.4 13.5 collective-permute-start
  206.0 16.0 collective-permute-start
  224.1 17.6 collective-permute-start
  243.8 22.3 %collective-permute-start = (bf16[256,1536]{1,0:T(8,128)(2,1)}, bf16[256,1536]{1,0:T(8,128)(2,1)S(1)}, u32[]{:S(2)}, u32[]{:S(2)}) collective-permute-start(bf16[256,1536]{1,0:T(8,128)(2,1)} %get-tuple-element.531), channel_id=1, source_target_pairs={{0,1},{1,2},{2,3},{3,4},{4,5},{5,6},{6,7},{7,8},{8,9},{9,10},{10,1... | collective-permute-start | bytes 2359304 | tf_op jit(solution)/shard_map/while/body/eval_jaxpr/ppermute | solution.py:21
  268.2 26.8 %collective-permute-start = (bf16[256,1536]{1,0:T(8,128)(2,1)}, bf16[256,1536]{1,0:T(8,128)(2,1)S(1)}, u32[]{:S(2)}, u32[]{:S(2)}) collective-permute-start(bf16[256,1536]{1,0:T(8,128)(2,1)} %get-tuple-element.531), channel_id=1, source_target_pairs={{0,1},{1,2},{2,3},{3,4},{4,5},{5,6},{6,7},{7,8},{8,9},{9,10},{10,1... | collective-permute-start | bytes 2359304 | tf_op jit(solution)/shard_map/while/body/eval_jaxpr/ppermute | solution.py:21
  335.2 4.9 copy-start.6
  384.5 4.9 copy-start.6
  422.3 5.3 copy-start.39
  427.8 44.3 %copy-start.16 = (bf16[256,1536]{1,0:T(8,128)(2,1)}, bf16[256,1536]{1,0:T(8,128)(2,1)S(1)}, u32[]{:S(2)}) copy-start(bf16[256,1536]{1,0:T(8,128)(2,1)S(1)} %multiply_convert_fusion.2) | copy-start | bytes 2359300
  580.7 7.5 copy-start.9
  580.7 21.3 slice-start
  588.2 10.9 copy-start.21
  588.2 13.9 slice-start.1
  739.5 10.4 copy-start.2
  751.5 11.9 collective-permute-start.1
  765.3 13.3 collective-permute-start.1
  780.5 13.3 collective-permute-start.1
  795.7 13.3 collective-permute-start.1
  810.9 13.3 collective-permute-start.1
  826.1 13.3 collective-permute-start.1
  841.3 13.3 collective-permute-start.1
  856.5 13.3 collective-permute-start.1
  877.1 234.9 %reduce-scatter.12.cloned.1.call-start = ((), (), s32[]{:S(2)}) async-start(), calls=%async_computation.16 | async-start | bytes 4866048 | tf_op jit(solution)/shard_map/reduce_scatter | solution.py:310
  880.3 372.6 %reduce-scatter.8.cloned.1.call-start = ((), (), s32[]{:S(2)}) async-start(), calls=%async_computation.14 | async-start | bytes 9732096 | tf_op jit(solution)/shard_map/reduce_scatter | solution.py:308
  883.3 5.2 copy-start.19
  888.6 506.5 %reduce-scatter.14.cloned.1.call-start = ((), (), s32[]{:S(2)}) async-start(), calls=%async_computation.17 | async-start | bytes 9732096 | tf_op jit(solution)/shard_map/reduce_scatter | solution.py:311
  895.1 751.5 %reduce-scatter.16.cloned.1.call-start = ((), (), s32[]{:S(2)}) async-start(), calls=%async_computation.18 | async-start | bytes 25952256 | tf_op jit(solution)/shard_map/reduce_scatter | solution.py:256
  908.4 991.4 %reduce-scatter.18.cloned.1.call-start = ((), (), s32[]{:S(2)}) async-start(), calls=%async_computation.19 | async-start | bytes 25952256 | tf_op jit(solution)/shard_map/reduce_scatter | solution.py:257
  920.6 1231.1 %reduce-scatter.20.cloned.1.call-start = ((), (), s32[]{:S(2)}) async-start(), calls=%async_computation.20 | async-start | bytes 25952256 | tf_op jit(solution)/shard_map/reduce_scatter | solution.py:258
  941.6 57.2 %copy-start.43 = (f32[256]{0:T(256)S(1)}, f32[256]{0:T(256)}, u32[]{:S(2)}) copy-start(f32[256]{0:T(256)} %copy-done.42) | copy-start | bytes 3076
  (95 other events, 201.4 us)
Sparse Core Ops, SparseCore 0:
  10.9 57.3 all-gather.7
  71.2 56.1 all-gather.9
  130.3 68.9 all-gather.11
  202.0 67.5 all-gather.13
  272.3 102.6 all-gather.15
  377.8 94.2 all-gather.17
  474.9 94.2 all-gather.19
  877.3 121.6 reduce-scatter.9
  1005.9 106.0 reduce-scatter.11
  1118.3 134.4 reduce-scatter.7
  1260.4 134.6 reduce-scatter.13
  1401.9 244.7 reduce-scatter.15
  1654.8 245.0 reduce-scatter.17
  1906.7 245.0 reduce-scatter.19
where the time goes:
time: 2170 us; the launch traced here: 2160 us
  waiting for transfers between devices  1530 us (71%)
  matrix products  281 us (13%)
  local copies, waits for them, and re-layouts  101 us (5%)
  blocking collectives  95.3 us (4%)
  other arithmetic  65.2 us (3%)
  starting transfers between devices  52.6 us (2%)
    reduce_scatter x1, waiting for transfers between devices, per_device(): lax.psum_scatter(up_grad_part, 'dev', scatter_dimension=0, tiled=True)  253 us
    reduce_scatter x1, waiting for transfers between devices, per_device(): lax.psum_scatter(down_part, 'dev', scatter_dimension=0, tiled=True)  252 us
    reduce_scatter x1, waiting for transfers between devices, per_device(): lax.psum_scatter(gate_part, 'dev', scatter_dimension=0, tiled=True)  252 us
    ppermute x16, waiting for transfers between devices, shifted_2(): lax.ppermute(value, axis, [(source, source + steps) for source in range(l...  202 us
    reduce_scatter x1, waiting for transfers between devices, per_device(): lax.psum_scatter(out_part, 'dev', scatter_dimension=0, tiled=True)  142 us
    reduce_scatter x1, waiting for transfers between devices, per_device(): lax.psum_scatter(query_part, 'dev', scatter_dimension=0, tiled=True)  141 us
    reduce_scatter x1, waiting for transfers between devices, per_device(): lax.psum_scatter(value_part, 'dev', scatter_dimension=0, tiled=True)  103 us
    unnamed x2, blocking collectives  95.3 us
  transfers between devices with their start and end apart: 30, of which 26 were waited for; matrix products, arithmetic and copies ran while one was open for 11% of the time, Pallas kernels for 0%

commit v1 on v0

v1 whole, which is shorter than its diff:
```python
import math

import jax
import jax.numpy as jnp
from jax import lax
from jax.experimental import pallas as pl
from jax.experimental.pallas import tpu as pltpu
from jax.sharding import PartitionSpec as P

HEADS = 16
KV_HEADS = 8
HEAD_DIM = 96
TEAM = 8

eps_norm = 1e-05
rope_base = 100000.0
masked_score = -1e30

OWN_HEADS = HEADS // TEAM
OWN_KV = KV_HEADS // TEAM
GROUP = HEADS // KV_HEADS
BLOCK = 256
LANES = 128
score_scale = 1.0 / math.sqrt(HEAD_DIM)
log2_scale = score_scale / math.log(2.0)
kernel_vmem = 56 * 1024 * 1024
small_cost = pl.CostEstimate(flops=1000, bytes_accessed=1000, transcendentals=0)

Q_WIDTH = OWN_HEADS * HEAD_DIM
KV_WIDTH = OWN_KV * HEAD_DIM
LINED = Q_WIDTH + 2 * KV_WIDTH


def relative(position):
    return 2 * (position % 4) + position // 4


def visible_mask(block, starts, ends):
    key = block * BLOCK + lax.broadcasted_iota(jnp.int32, (BLOCK, 1), 0)
    return (key >= starts) & (key <= ends)


def chunk_lanes(ref, chunk):
    spot = pl.ds(chunk * BLOCK, BLOCK)
    return jnp.concatenate([ref[head, :, spot] for head in range(GROUP)], axis=1)


def chunk_range(chunk, starts_ref, last):
    starts = starts_ref[:, pl.ds(chunk * BLOCK, BLOCK)]
    ends = last * BLOCK + lax.broadcasted_iota(jnp.int32, (1, BLOCK), 1)
    return (
        jnp.concatenate([starts] * GROUP, axis=1),
        jnp.concatenate([ends] * GROUP, axis=1),
    )


def attend_kernel(low_ref, starts_ref, query_ref, *refs):
    count = len(refs) - 4
    member = low_ref[TEAM]
    pieces = refs[:count]
    out_ref, norm_ref, keys, values = refs[count:]
    per_piece = pieces[0].shape[-1] // BLOCK
    for back, piece in enumerate(pieces):
        for part in range(per_piece):
            block = (count - 1 - back) * per_piece + (relative(part) ^ member)
            spot = pl.ds(part * BLOCK, BLOCK)
            keys[block] = piece[0, 0, :, spot].T
            values[block] = piece[1, 0, :, spot]
    own_block = (count - 1) * per_piece
    for chunk in range(per_piece):
        queries = chunk_lanes(query_ref, chunk)
        last = own_block + (relative(chunk) ^ member)
        starts, ends = chunk_range(chunk, starts_ref, last)

        def advance(step, running):
            top, total, summed = running
            block = last - step
            scores = (
                jnp.dot(keys[block], queries, preferred_element_type=jnp.float32) * log2_scale
            )
            scores = jnp.where(visible_mask(block, starts, ends), scores, masked_score)
            new_top = jnp.maximum(top, jnp.max(scores, axis=0, keepdims=True))
            factor = jnp.exp2(top - new_top)
            weights = jnp.exp2(scores - new_top)
            total = total * factor + jnp.sum(weights, axis=0, keepdims=True)
            summed = summed * factor + jnp.dot(
                values[block], weights.astype(jnp.bfloat16), preferred_element_type=jnp.float32
            )
            return new_top, total, summed

        lanes = GROUP * BLOCK
        top, total, summed = lax.fori_loop(
            0,
            last - low_ref[chunk] + 1,
            advance,
            (
                jnp.full((1, lanes), masked_score, jnp.float32),
                jnp.zeros((1, lanes), jnp.float32),
                jnp.zeros((HEAD_DIM, lanes), jnp.float32),
            ),
        )
        attended = summed / total
        norm = top + jnp.log2(total)
        spot = pl.ds(chunk * BLOCK, BLOCK)
        for head in range(GROUP):
            out_ref[head, :, spot] = attended[:, head * BLOCK : (head + 1) * BLOCK]
            norm_ref[head, :, spot] = norm[:, head * BLOCK : (head + 1) * BLOCK]


def gradient_kernel(low_ref, starts_ref, query_ref, grad_ref, out_ref, norm_ref, *refs):
    count = len(refs) - 8
    member = low_ref[TEAM]
    pieces = refs[:count]
    query_grad, own_grad, back_grad, keys, keys_t, values, key_sum, value_sum = refs[count:]
    per_piece = pieces[0].shape[-1] // BLOCK
    for back, piece in enumerate(pieces):
        for part in range(per_piece):
            block = (count - 1 - back) * per_piece + (relative(part) ^ member)
            spot = pl.ds(part * BLOCK, BLOCK)
            keys_t[block] = piece[0, 0, :, spot]
            keys[block] = piece[0, 0, :, spot].T
            values[block] = piece[1, 0, :, spot].T
    key_sum[...] = jnp.zeros_like(key_sum)
    value_sum[...] = jnp.zeros_like(value_sum)
    own_block = (count - 1) * per_piece
    rows_rows = (((1,), (1,)), ((), ()))
    for chunk in range(per_piece):
        queries = chunk_lanes(query_ref, chunk)
        grads = chunk_lanes(grad_ref, chunk)
        norm = chunk_lanes(norm_ref, chunk)
        delta = jnp.sum(
            grads.astype(jnp.float32) * chunk_lanes(out_ref, chunk), axis=0, keepdims=True
        )
        last = own_block + (relative(chunk) ^ member)
        starts, ends = chunk_range(chunk, starts_ref, last)

        def advance(block, summed):
            scores = (
                jnp.dot(keys[block], queries, preferred_element_type=jnp.float32) * log2_scale
            )
            scores = jnp.where(visible_mask(block, starts, ends), scores - norm, masked_score)
            probs = jnp.exp2(scores)
            slopes = jnp.dot(values[block], grads, preferred_element_type=jnp.float32)
            grad_scores = (probs * (slopes - delta)).astype(jnp.bfloat16)
            key_sum[block] += lax.dot_general(
                queries, grad_scores, rows_rows, preferred_element_type=jnp.float32
            )
            value_sum[block] += lax.dot_general(
                grads, probs.astype(jnp.bfloat16), rows_rows, preferred_element_type=jnp.float32
            )
            return summed + jnp.dot(
                keys_t[block], grad_scores, preferred_element_type=jnp.float32
            )

        summed = lax.fori_loop(
            low_ref[chunk],
            last + 1,
            advance,
            jnp.zeros((HEAD_DIM, GROUP * BLOCK), jnp.float32),
        )
        spot = pl.ds(chunk * BLOCK, BLOCK)
        for head in range(GROUP):
            query_grad[head, :, spot] = (
                summed[:, head * BLOCK : (head + 1) * BLOCK] * score_scale
            )
    for back in range(count):
        for part in range(per_piece):
            block = (count - 1 - back) * per_piece + (relative(part) ^ member)
            spot = pl.ds(part * BLOCK, BLOCK)
            key_part = key_sum[block] * score_scale
            value_part = value_sum[block]
            if back == 0:
                own_grad[0, 0, :, spot] = key_part
                own_grad[1, 0, :, spot] = value_part
            else:
                back_grad[back - 1, 0, 0, :, spot] = key_part.astype(jnp.bfloat16)
                back_grad[back - 1, 1, 0, :, spot] = value_part.astype(jnp.bfloat16)


def attention_specs(tokens, pieces, first_head):
    whole = pl.BlockSpec((1, tokens), lambda head: (0, 0))
    low = pl.BlockSpec(memory_space=pltpu.SMEM)
    heads = pl.BlockSpec(
        (GROUP, HEAD_DIM, tokens), lambda head: (first_head + head, 0, 0)
    )
    norm = pl.BlockSpec((GROUP, 1, tokens), lambda head: (first_head + head, 0, 0))
    kv = pl.BlockSpec((2, 1, HEAD_DIM, tokens), lambda head: (0, first_head + head, 0, 0))
    return low, whole, heads, norm, [kv] * len(pieces)


def attend(low, starts, queries, pieces, first_head, count):
    tokens = queries.shape[-1]
    blocks = len(pieces) * tokens // BLOCK
    low_spec, whole, heads, norm, kv = attention_specs(tokens, pieces, first_head)
    return pl.pallas_call(
        attend_kernel,
        grid=(count,),
        in_specs=[low_spec, whole, heads] + kv,
        out_specs=[
            pl.BlockSpec((GROUP, HEAD_DIM, tokens), lambda head: (head, 0, 0)),
            pl.BlockSpec((GROUP, 1, tokens), lambda head: (head, 0, 0)),
        ],
        out_shape=[
            jax.ShapeDtypeStruct((count * GROUP, HEAD_DIM, tokens), jnp.float32),
            jax.ShapeDtypeStruct((count * GROUP, 1, tokens), jnp.float32),
        ],
        scratch_shapes=[
            pltpu.VMEM((blocks, BLOCK, HEAD_DIM), jnp.bfloat16),
            pltpu.VMEM((blocks, HEAD_DIM, BLOCK), jnp.bfloat16),
        ],
        compiler_params=pltpu.CompilerParams(vmem_limit_bytes=kernel_vmem),
        cost_estimate=small_cost,
    )(low, starts, queries, *pieces)


def attend_back(low, starts, queries, grads, attended, norm, pieces, first_head, count):
    tokens = queries.shape[-1]
    blocks = len(pieces) * tokens // BLOCK
    low_spec, whole, heads, norm_spec, kv = attention_specs(tokens, pieces, first_head)
    back = len(pieces) - 1
    return pl.pallas_call(
        gradient_kernel,
        grid=(count,),
        in_specs=[low_spec, whole, heads, heads, heads, norm_spec] + kv,
        out_specs=[
            pl.BlockSpec((GROUP, HEAD_DIM, tokens), lambda head: (head, 0, 0)),
            pl.BlockSpec((2, 1, HEAD_DIM, tokens), lambda head: (0, head, 0, 0)),
            pl.BlockSpec((back, 2, 1, HEAD_DIM, tokens), lambda head: (0, 0, head, 0, 0)),
        ],
        out_shape=[
            jax.ShapeDtypeStruct((count * GROUP, HEAD_DIM, tokens), jnp.float32),
            jax.ShapeDtypeStruct((2, count, HEAD_DIM, tokens), jnp.float32),
            jax.ShapeDtypeStruct((back, 2, count, HEAD_DIM, tokens), jnp.bfloat16),
        ],
        scratch_shapes=[
            pltpu.VMEM((blocks, BLOCK, HEAD_DIM), jnp.bfloat16),
            pltpu.VMEM((blocks, HEAD_DIM, BLOCK), jnp.bfloat16),
            pltpu.VMEM((blocks, BLOCK, HEAD_DIM), jnp.bfloat16),
            pltpu.VMEM((blocks, HEAD_DIM, BLOCK), jnp.float32),
            pltpu.VMEM((blocks, HEAD_DIM, BLOCK), jnp.float32),
        ],
        compiler_params=pltpu.CompilerParams(vmem_limit_bytes=kernel_vmem),
        cost_estimate=small_cost,
    )(low, starts, queries, grads, attended, norm, *pieces)

class Order:
    def __init__(self, token):
        self.token = token

    def step(self, *values):
        self.token, tied = lax.optimization_barrier((self.token, values))
        return tied[0] if len(tied) == 1 else tied


class Grid:
    def __init__(self):
        self.count = lax.axis_size("dev")
        self.teams = self.count // TEAM
        index = lax.axis_index("dev")
        self.member = index % TEAM
        self.team = index // TEAM

    def places(self):
        return jnp.stack([self.team, self.member]).astype(jnp.int32)

    def turn(self, value, bits):
        return lax.ppermute(value, "dev", [(d, d ^ bits) for d in range(self.count)])

    def shift(self, value, steps, around=True):
        pairs = []
        for device in range(self.count):
            target = device + steps * TEAM
            if around or 0 <= target < self.count:
                pairs.append((device, target % self.count))
        return lax.ppermute(value, "dev", pairs)

    def spread(self, value):
        return [value] + [self.shift(value, steps) for steps in range(1, self.teams)]

    def both_ways(self, ahead, behind):
        return self.shift(ahead, 1, False), self.shift(behind, -1, False)

    def gather_team(self, blocks):
        return list(blocks) + [self.turn(block, 1) for block in blocks]

    def chips(self, block):
        return [block] + [self.turn(block, 2 * chip) for chip in range(1, 4)]

    def to_members(self, value):
        pairs = [
            (owner, owner % self.teams * TEAM + owner // self.teams)
            for owner in range(self.count)
        ]
        return lax.ppermute(value, "dev", pairs)

    def to_owners(self, value):
        pairs = [
            (owner % self.teams * TEAM + owner // self.teams, owner)
            for owner in range(self.count)
        ]
        return lax.ppermute(value, "dev", pairs)

    def send_chips(self, blocks):
        return [self.turn(block, 2 * chip) for chip, block in enumerate(blocks, 1)]


def call(kernel, grid, in_specs, out_specs, out_shape, scratch=(), prefetch=0):
    return pl.pallas_call(
        kernel,
        out_shape=out_shape,
        grid_spec=pltpu.PrefetchScalarGridSpec(
            num_scalar_prefetch=prefetch,
            grid=grid,
            in_specs=in_specs,
            out_specs=out_specs,
            scratch_shapes=list(scratch),
        ),
        compiler_params=pltpu.CompilerParams(vmem_limit_bytes=kernel_vmem),
        cost_estimate=small_cost,
    )


def fixed(array):
    return pl.BlockSpec(array.shape, lambda *unused: (0,) * array.ndim)


def lanes_at(rows, step_width):
    return pl.BlockSpec((rows, step_width), lambda p, *unused: (0, p))


def rows_at(step_rows, width):
    return pl.BlockSpec((step_rows, width), lambda p, *unused: (p, 0))


def kept_given(rows, width, axis):
    def index(at):
        return (0, at) if axis else (at, 0)

    specs = [
        pl.BlockSpec((rows, width), lambda p, *unused: index(jnp.minimum(p, 3))),
        pl.BlockSpec((rows, width), lambda p, *unused: index(jnp.maximum(p - 4, 0))),
    ]
    shape = (rows, 4 * width) if axis else (4 * rows, width)
    shapes = [
        jax.ShapeDtypeStruct(shape, jnp.float32),
        jax.ShapeDtypeStruct(shape, jnp.bfloat16),
    ]
    return specs, shapes


def keep_or_give(position, keep_ref, give_ref, value):
    @pl.when(position < 4)
    def keep():
        keep_ref[...] = value

    @pl.when(position >= 4)
    def give():
        give_ref[...] = value.astype(give_ref.dtype)


def pick(position, refs, target):
    for number in range(TEAM):

        @pl.when(position == number)
        def move():
            if len(refs) == TEAM:
                target[...] = refs[number][...]
            else:
                target[...] = refs[number // 4][number % 4]


def dot_rows(left, right):
    return lax.dot_general(
        left, right, (((1,), (1,)), ((), ())), preferred_element_type=jnp.float32
    )


def dot(left, right):
    return jnp.dot(left, right, preferred_element_type=jnp.float32)


def place_rows(grid, blocks, start, stop):
    count = len(blocks)
    positions, rows = blocks[0].shape[:2]
    width = stop - start

    def kernel(places_ref, *refs):
        target = refs[-1]
        for number, ref in enumerate(refs[:-1]):

            @pl.when(pl.program_id(0) == number)
            def move():
                for position in range(positions):
                    at = relative(position) ^ places_ref[1] if positions > 1 else 0
                    target[0, pl.ds(at, 1)] = ref[position : position + 1, :, start:stop]

    def target_map(step, places_ref):
        return ((places_ref[0] + count - step) % count, 0, 0, 0)

    return call(
        kernel,
        (count,),
        [fixed(block) for block in blocks],
        pl.BlockSpec((1, positions, rows, width), target_map),
        jax.ShapeDtypeStruct((count, positions, rows, width), blocks[0].dtype),
        prefetch=1,
    )(grid.places(), *blocks)


def place_mixer(grid, own, hops, units, unit_rows):
    count = grid.teams
    positions, rows, wide = own.shape
    third = wide - 2 * units
    sources = [own] + [block for hop in hops for block in hop]

    def kernel(places_ref, *refs):
        mixer_ref, down_ref = refs[-2:]
        team = places_ref[0]

        def move(ref):
            for position in range(positions):
                at = relative(position) ^ places_ref[1]
                mixer_ref[0, pl.ds(at, 1)] = ref[position : position + 1, :, : 2 * units]
                row = position * rows
                while row < (position + 1) * rows:
                    part = row // unit_rows
                    stop = min((part + 1) * unit_rows, (position + 1) * rows)
                    down_ref[
                        0,
                        row - part * unit_rows : stop - part * unit_rows,
                        part * third : (part + 1) * third,
                    ] = ref[position, row - position * rows : stop - position * rows, 2 * units :]
                    row = stop

        for steps in range(count):
            here = pl.program_id(0) == steps
            if steps == 0:
                pl.when(here)(lambda: move(refs[0]))
            else:
                ahead, behind = refs[2 * steps - 1], refs[2 * (count - steps)]
                pl.when(here & (team >= steps))(lambda ahead=ahead: move(ahead))
                pl.when(here & (team < steps))(lambda behind=behind: move(behind))

    def target_map(step, places_ref):
        return (places_ref[0] + count - step) % count

    return call(
        kernel,
        (count,),
        [fixed(source) for source in sources],
        [
            pl.BlockSpec(
                (1, positions, rows, 2 * units), lambda s, p: (target_map(s, p), 0, 0, 0)
            ),
            pl.BlockSpec((1, unit_rows, 3 * third), lambda s, p: (target_map(s, p), 0, 0)),
        ],
        [
            jax.ShapeDtypeStruct((count, positions, rows, 2 * units), own.dtype),
            jax.ShapeDtypeStruct((count, unit_rows, 3 * third), own.dtype),
        ],
        prefetch=1,
    )(grid.places(), *sources)


def project(inputs_t, weights, cosine, sine_table):
    width, own = inputs_t[0].shape
    tokens = TEAM * own
    half = HEAD_DIM // 2

    def kernel(weights_ref, cosine_ref, sine_ref, *refs):
        sources = refs[:TEAM]
        normed_ref, query_ref, kv_ref, chosen, turned = refs[TEAM:]
        position = pl.program_id(0)

        @pl.when(position == 0)
        def prepare():
            turned[...] = weights_ref[:, :LINED].T

        pick(position, sources, chosen)
        values = chosen[...].astype(jnp.float32)
        scale = lax.rsqrt(jnp.mean(values * values, axis=0, keepdims=True) + eps_norm)
        gain = weights_ref[:, LINED : LINED + 1].astype(jnp.float32)
        normed = (values * scale * gain).astype(jnp.bfloat16)
        normed_ref[...] = normed
        lined = dot(turned[...], normed)
        cosines, sines = cosine_ref[...], sine_ref[...]

        def rotated(head):
            block = lined[head * HEAD_DIM : (head + 1) * HEAD_DIM]
            shifted = jnp.concatenate([-block[half:], block[:half]], axis=0)
            return (block * cosines + shifted * sines).astype(jnp.bfloat16)

        for head in range(OWN_HEADS):
            query_ref[head] = rotated(head)
        for head in range(OWN_KV):
            kv_ref[0, head] = rotated(OWN_HEADS + head)
            start = Q_WIDTH + KV_WIDTH + head * HEAD_DIM
            kv_ref[1, head] = lined[start : start + HEAD_DIM].astype(jnp.bfloat16)

    return call(
        kernel,
        (TEAM,),
        [fixed(weights), lanes_at(HEAD_DIM, own), lanes_at(HEAD_DIM, own)]
        + [fixed(block) for block in inputs_t],
        [
            lanes_at(width, own),
            pl.BlockSpec((OWN_HEADS, HEAD_DIM, own), lambda p: (0, 0, p)),
            pl.BlockSpec((2, OWN_KV, HEAD_DIM, own), lambda p: (0, 0, 0, p)),
        ],
        [
            jax.ShapeDtypeStruct((width, tokens), jnp.bfloat16),
            jax.ShapeDtypeStruct((OWN_HEADS, HEAD_DIM, tokens), jnp.bfloat16),
            jax.ShapeDtypeStruct((2, OWN_KV, HEAD_DIM, tokens), jnp.bfloat16),
        ],
        [
            pltpu.VMEM((width, own), jnp.bfloat16),
            pltpu.VMEM((LINED, width), jnp.bfloat16),
        ],
    )(weights, cosine, sine_table, *inputs_t)


def project_out(attended, out_rows):
    tokens = attended.shape[-1]
    own = tokens // TEAM
    width = out_rows.shape[1]
    specs, shapes = kept_given(width, own, 1)

    def kernel(attended_ref, rows_ref, keep_ref, give_ref, turned):
        position = pl.program_id(0)

        @pl.when(position == 0)
        def prepare():
            turned[...] = rows_ref[...].T

        block = attended_ref[...].reshape(Q_WIDTH, own).astype(jnp.bfloat16)
        keep_or_give(position, keep_ref, give_ref, dot(turned[...], block))

    return call(
        kernel,
        (TEAM,),
        [pl.BlockSpec((OWN_HEADS, HEAD_DIM, own), lambda p: (0, 0, p)), fixed(out_rows)],
        specs,
        shapes,
        [pltpu.VMEM((width, Q_WIDTH), jnp.bfloat16)],
    )(attended, out_rows)


def mixer_forward(normed, cotangent, weights, down):
    own, width = cotangent[0].shape[1:]
    units = down.shape[0]
    tokens = TEAM * own

    def kernel(weights_ref, down_ref, *refs):
        normed_refs, cotangent_refs = refs[:TEAM], refs[TEAM : TEAM + 2]
        hidden_ref, grad_ref, chosen, turned, wanted = refs[TEAM + 2 :]
        position = pl.program_id(0)
        pick(position, normed_refs, chosen)
        pick(position, cotangent_refs, wanted)
        turned[...] = chosen[...].T
        gate = dot(turned[...], weights_ref[:, :units])
        up = dot(turned[...], weights_ref[:, units:])
        logistic = 1.0 / (1.0 + jnp.exp(-gate))
        silu = gate * logistic
        hidden_ref[...] = (silu * up).astype(jnp.bfloat16)
        grad_hidden = dot_rows(wanted[...], down_ref[...])
        grad_ref[:, :units] = (
            grad_hidden * up * (logistic * (1.0 + gate * (1.0 - logistic)))
        ).astype(jnp.bfloat16)
        grad_ref[:, units:] = (grad_hidden * silu).astype(jnp.bfloat16)

    return call(
        kernel,
        (TEAM,),
        [fixed(weights), fixed(down)]
        + [fixed(block) for block in normed]
        + [fixed(block) for block in cotangent],
        [rows_at(own, units), rows_at(own, 2 * units)],
        [
            jax.ShapeDtypeStruct((tokens, units), jnp.bfloat16),
            jax.ShapeDtypeStruct((tokens, 2 * units), jnp.bfloat16),
        ],
        [
            pltpu.VMEM((width, own), jnp.bfloat16),
            pltpu.VMEM((own, width), jnp.bfloat16),
            pltpu.VMEM((own, width), jnp.bfloat16),
        ],
    )(weights, down, *normed, *cotangent)


def mixer_backward(grads, weights):
    tokens, columns = grads.shape
    own = tokens // TEAM
    specs, shapes = kept_given(weights.shape[0], own, 1)

    def kernel(grads_ref, weights_ref, keep_ref, give_ref):
        keep_or_give(
            pl.program_id(0), keep_ref, give_ref, dot_rows(weights_ref[...], grads_ref[...])
        )

    return call(
        kernel, (TEAM,), [rows_at(own, columns), fixed(weights)], specs, shapes
    )(grads, weights)


def mixer_output(hidden, down):
    tokens, units = hidden.shape
    own = tokens // TEAM
    specs, shapes = kept_given(own, down.shape[1], 0)

    def kernel(hidden_ref, down_ref, keep_ref, give_ref):
        keep_or_give(pl.program_id(0), keep_ref, give_ref, dot(hidden_ref[...], down_ref[...]))

    return call(kernel, (TEAM,), [rows_at(own, units), fixed(down)], specs, shapes)(hidden, down)


def write_teams(places_ref, total, out_ref, teams):
    rows = total.shape[0] // teams
    for team in range(teams):
        steps = (team + teams - places_ref[0]) % teams
        block = total[team * rows : (team + 1) * rows, :].astype(out_ref.dtype)
        out_ref[pl.ds(steps, 1)] = block[None]


def token_product(grid, lefts, right, by_rows, width):
    own = right.shape[0] // TEAM
    rows = lefts[0].shape[0] if by_rows else lefts.shape[1]
    teams = grid.teams

    def kernel(places_ref, right_ref, *refs):
        sources, (out_ref, total) = refs[:-2], refs[-2:]
        position = pl.program_id(0)

        def add(value):
            @pl.when(position == 0)
            def first():
                total[...] = value

            @pl.when(position > 0)
            def later():
                total[...] += value

        for number, source in enumerate(sources):

            @pl.when(position == number)
            def block():
                add(dot(source[...], right_ref[...]))

        @pl.when(position == TEAM - 1)
        def last():
            write_teams(places_ref, total, out_ref, teams)

    return call(
        kernel,
        (TEAM,),
        [rows_at(own, width)] + [fixed(left) for left in lefts],
        pl.BlockSpec((teams, rows // teams, width), lambda p, *unused: (0, 0, 0)),
        jax.ShapeDtypeStruct((teams, rows // teams, width), jnp.bfloat16),
        [pltpu.VMEM((rows, width), jnp.float32)],
        prefetch=1,
    )(grid.places(), right, *lefts)


def down_product(grid, hidden, cotangent):
    tokens, units = hidden.shape
    own, width = cotangent[0].shape[1:]
    teams = grid.teams

    def kernel(places_ref, hidden_ref, *refs):
        sources, (out_ref, total, wanted) = refs[:2], refs[2:]
        position = pl.program_id(0)
        pick(position, sources, wanted)
        value = dot(hidden_ref[...].T, wanted[...])

        @pl.when(position == 0)
        def first():
            total[...] = value

        @pl.when(position > 0)
        def later():
            total[...] += value

        @pl.when(position == TEAM - 1)
        def last():
            write_teams(places_ref, total, out_ref, teams)

    return call(
        kernel,
        (TEAM,),
        [rows_at(own, units)] + [fixed(block) for block in cotangent],
        pl.BlockSpec((teams, units // teams, width), lambda p, *unused: (0, 0, 0)),
        jax.ShapeDtypeStruct((teams, units // teams, width), jnp.bfloat16),
        [pltpu.VMEM((units, width), jnp.float32), pltpu.VMEM((own, width), jnp.bfloat16)],
        prefetch=1,
    )(grid.places(), hidden, *cotangent)


def project_out_back(grid, grads, out_rows, attended):
    teams = grid.teams
    tokens = attended.shape[-1]
    own = tokens // TEAM
    width = out_rows.shape[1]

    def kernel(places_ref, rows_ref, attended_ref, *refs):
        sources, (grad_ref, out_ref, chosen, total) = refs[:TEAM], refs[TEAM:]
        position = pl.program_id(0)
        pick(position, sources, chosen)
        grad_ref[...] = (
            dot(rows_ref[...], chosen[...])
            .astype(jnp.bfloat16)
            .reshape(OWN_HEADS, HEAD_DIM, own)
        )
        block = attended_ref[...].reshape(Q_WIDTH, own).astype(jnp.bfloat16)
        value = dot_rows(block, chosen[...])

        @pl.when(position == 0)
        def first():
            total[...] = value

        @pl.when(position > 0)
        def later():
            total[...] += value

        @pl.when(position == TEAM - 1)
        def last():
            write_teams(places_ref, total, out_ref, teams)

    heads = pl.BlockSpec((OWN_HEADS, HEAD_DIM, own), lambda p, *unused: (0, 0, p))
    shape = (teams, Q_WIDTH // teams, width)
    return call(
        kernel,
        (TEAM,),
        [fixed(out_rows), heads] + [fixed(block) for block in grads],
        [heads, pl.BlockSpec(shape, lambda p, *unused: (0, 0, 0))],
        [
            jax.ShapeDtypeStruct((OWN_HEADS, HEAD_DIM, tokens), jnp.bfloat16),
            jax.ShapeDtypeStruct(shape, jnp.bfloat16),
        ],
        [pltpu.VMEM((width, own), jnp.bfloat16), pltpu.VMEM((Q_WIDTH, width), jnp.float32)],
        prefetch=1,
    )(grid.places(), out_rows, attended, *grads)


def project_back(grid, normed, query_rot, own_grads, returned, cosine, sine_table, weights):
    width, tokens = normed.shape
    own = tokens // TEAM
    half = HEAD_DIM // 2
    teams = grid.teams
    specs, shapes = kept_given(width, own, 1)

    def kernel(places_ref, normed_ref, query_ref, cosine_ref, sine_ref, weights_ref, *refs):
        kv_refs = refs[: 1 + len(returned)]
        keep_ref, give_ref, out_ref, total, grad_ref = refs[1 + len(returned) :]
        position = pl.program_id(0)
        cosines, sines = cosine_ref[...], sine_ref[...]

        def unrotated(block):
            scaled = block * sines
            shifted = jnp.concatenate([scaled[half:], -scaled[:half]], axis=0)
            return (block * cosines + shifted).astype(jnp.bfloat16)

        for head in range(OWN_HEADS):
            grad_ref[head * HEAD_DIM : (head + 1) * HEAD_DIM] = unrotated(query_ref[head])
        kv = kv_refs[0][...]
        for ref in kv_refs[1:]:
            kv = kv + ref[...].astype(jnp.float32)
        for head in range(OWN_KV):
            start = Q_WIDTH + head * HEAD_DIM
            grad_ref[start : start + HEAD_DIM] = unrotated(kv[0, head])
            start = start + KV_WIDTH
            grad_ref[start : start + HEAD_DIM] = kv[1, head].astype(jnp.bfloat16)
        grad = grad_ref[...]
        keep_or_give(position, keep_ref, give_ref, dot(weights_ref[:, :LINED], grad))
        value = dot_rows(normed_ref[...], grad)

        @pl.when(position == 0)
        def first():
            total[...] = value

        @pl.when(position > 0)
        def later():
            total[...] += value

        @pl.when(position == TEAM - 1)
        def last():
            write_teams(places_ref, total, out_ref, teams)

    heads = pl.BlockSpec((OWN_HEADS, HEAD_DIM, own), lambda p, *unused: (0, 0, p))
    kv_heads = pl.BlockSpec((2, OWN_KV, HEAD_DIM, own), lambda p, *unused: (0, 0, 0, p))
    return call(
        kernel,
        (TEAM,),
        [
            lanes_at(width, own),
            heads,
            lanes_at(HEAD_DIM, own),
            lanes_at(HEAD_DIM, own),
            fixed(weights),
        ]
        + [kv_heads] * (1 + len(returned)),
        specs + [pl.BlockSpec((teams, width // teams, LINED), lambda p, *unused: (0, 0, 0))],
        shapes + [jax.ShapeDtypeStruct((teams, width // teams, LINED), jnp.bfloat16)],
        [pltpu.VMEM((width, LINED), jnp.float32), pltpu.VMEM((LINED, own), jnp.bfloat16)],
        prefetch=1,
    )(grid.places(), normed, query_rot, cosine, sine_table, weights, own_grads, *returned)


def combine(keep, arrived, axis):
    size = keep.shape[axis] // 4
    shape = (keep.shape[0], size) if axis else (size, keep.shape[1])

    def kernel(keep_ref, arrived_ref, own_ref, *block_refs):
        position = pl.program_id(0)
        total = keep_ref[...] + arrived_ref[...].astype(jnp.float32)

        @pl.when(position == 0)
        def own():
            own_ref[...] = total

        for number, ref in enumerate(block_refs, 1):

            @pl.when(position == number)
            def other():
                ref[...] = total.astype(jnp.bfloat16)

    part = pl.BlockSpec(shape, (lambda p: (0, p)) if axis else (lambda p: (p, 0)))
    whole = pl.BlockSpec(shape, lambda p: (0, 0))
    own, *blocks = call(
        kernel,
        (4,),
        [part, part],
        [whole] * 4,
        [jax.ShapeDtypeStruct(shape, jnp.float32)]
        + [jax.ShapeDtypeStruct(shape, jnp.bfloat16)] * 3,
    )(keep, arrived)
    return own, blocks


def summed(refs):
    total = refs[0][...]
    for ref in refs[1:]:
        total = total + ref[...].astype(jnp.float32)
    return total


def finish(kernel, arrays, shapes):
    return call(
        kernel,
        (1,),
        [fixed(array) for array in arrays],
        [pl.BlockSpec(shape.shape, lambda p: (0, 0)) for shape in shapes],
        shapes,
    )(*arrays)


def finish_middle(terms, inputs_t, gain):
    def kernel(*refs):
        inputs_ref, gain_ref, middle_ref, normed_ref = refs[len(terms) :]
        middle = inputs_ref[...].astype(jnp.float32) + summed(refs[: len(terms)])
        middle_ref[...] = middle
        scale = lax.rsqrt(jnp.mean(middle * middle, axis=0, keepdims=True) + eps_norm)
        normed_ref[...] = (middle * scale * gain_ref[...]).astype(jnp.bfloat16)

    shape = inputs_t.shape
    return finish(
        kernel,
        list(terms) + [inputs_t, gain],
        [jax.ShapeDtypeStruct(shape, jnp.float32), jax.ShapeDtypeStruct(shape, jnp.bfloat16)],
    )


def norm_back(values, gain, grad):
    inverse = lax.rsqrt(jnp.mean(values * values, axis=0, keepdims=True) + eps_norm)
    normal = values * inverse
    scaled = grad * gain
    inner = jnp.mean(scaled * normal, axis=0, keepdims=True)
    return inverse * (scaled - normal * inner), jnp.sum(grad * normal, axis=1, keepdims=True)


def finish_second(terms, middle, cotangent, gain):
    def kernel(*refs):
        middle_ref, cotangent_ref, gain_ref, grad_ref, attn_ref, gain_out = refs[len(terms) :]
        norm_grad, gain_part = norm_back(
            middle_ref[...], gain_ref[...], summed(refs[: len(terms)])
        )
        grad = cotangent_ref[...].T.astype(jnp.float32) + norm_grad
        grad_ref[...] = grad
        attn_ref[...] = grad.astype(jnp.bfloat16)
        gain_out[...] = gain_part

    shape = middle.shape
    return finish(
        kernel,
        list(terms) + [middle, cotangent, gain],
        [
            jax.ShapeDtypeStruct(shape, jnp.float32),
            jax.ShapeDtypeStruct(shape, jnp.bfloat16),
            jax.ShapeDtypeStruct((shape[0], 1), jnp.float32),
        ],
    )


def finish_first(terms, inputs_t, grad_middle, gain):
    def kernel(*refs):
        inputs_ref, grad_ref, gain_ref, out_ref, gain_out = refs[len(terms) :]
        norm_grad, gain_part = norm_back(
            inputs_ref[...].astype(jnp.float32), gain_ref[...], summed(refs[: len(terms)])
        )
        out_ref[...] = (grad_ref[...] + norm_grad).T
        gain_out[...] = gain_part

    width, own = inputs_t.shape
    return finish(
        kernel,
        list(terms) + [inputs_t, grad_middle, gain],
        [
            jax.ShapeDtypeStruct((own, width), jnp.float32),
            jax.ShapeDtypeStruct((width, 1), jnp.float32),
        ],
    )


def finish_output(terms, middle):
    def kernel(*refs):
        middle_ref, out_ref = refs[len(terms) :]
        out_ref[...] = (middle_ref[...].T + summed(refs[: len(terms)])).astype(jnp.bfloat16)

    return finish(
        kernel, list(terms) + [middle], [jax.ShapeDtypeStruct(terms[0].shape, jnp.bfloat16)]
    )[0]


def sum_teams(product, parts, kind):
    def kernel(own_ref, *refs):
        total = own_ref[0].astype(jnp.float32)
        for ref in refs[:-1]:
            total = total + ref[...].astype(jnp.float32)
        refs[-1][...] = total.astype(kind)

    shape = product.shape[1:]
    return call(
        kernel,
        (1,),
        [pl.BlockSpec((1,) + shape, lambda p: (0, 0, 0))] + [fixed(part) for part in parts],
        pl.BlockSpec(shape, lambda p: (0, 0)),
        jax.ShapeDtypeStruct(shape, kind),
    )(product, *parts)


def rope_tables(positions):
    half_dim = HEAD_DIM // 2
    frequency = rope_base ** (-(jnp.arange(half_dim, dtype=jnp.float32) * 2.0 / HEAD_DIM))
    angles = frequency[:, None] * positions.astype(jnp.float32)[None, :]
    angles = jnp.concatenate([angles, angles], axis=0)
    return (jnp.cos(angles), jnp.sin(angles))


def per_device(
    inputs,
    positions,
    norm_first,
    query_weight,
    key_weight,
    value_weight,
    out_weight,
    norm_second,
    gate_weight,
    up_weight,
    down_weight,
    cotangent,
):
    grid = Grid()
    member, teams = grid.member, grid.teams
    chip, core = member // 2, member % 2
    own, width = inputs.shape
    tokens = own * TEAM
    rows = query_weight.shape[0]
    unit_rows = down_weight.shape[0]
    units = unit_rows * teams
    longest = own * grid.count // 4
    steps_back = min((longest - 2) // tokens + 1, teams - 1)
    bf16, f32 = jnp.bfloat16, jnp.float32
    order = Order(jnp.zeros((8, 128), jnp.int32))

    def dynamic(array, index, axis=0):
        return lax.dynamic_index_in_dim(array, index, axis, keepdims=False)

    def by_member(weight):
        return jnp.transpose(weight.reshape(rows, TEAM, -1), (1, 0, 2))

    def units_by_member(weight):
        blocks = jnp.transpose(weight.reshape(rows, teams, TEAM, unit_rows), (2, 0, 1, 3))
        return blocks.reshape(TEAM, rows, units)

    gains = jnp.pad(jnp.stack([norm_first, norm_second], axis=1), ((0, 0), (0, LANES - 2)))
    columns = jnp.concatenate(
        [
            by_member(query_weight),
            by_member(key_weight),
            by_member(value_weight),
            jnp.broadcast_to(gains[None], (TEAM, rows, LANES)),
            units_by_member(gate_weight),
            units_by_member(up_weight),
        ],
        axis=-1,
    )
    attn_wide = LINED + LANES
    columns = columns.reshape(TEAM // 2, 2, rows, attn_wide + 2 * units)
    position_chips = jnp.stack(grid.chips(positions))
    all_positions = jnp.concatenate([position_chips, grid.turn(position_chips, 1)]).reshape(tokens)
    inputs_t = inputs.T
    columns, inputs_t = order.step(columns, inputs_t)
    pairs = [
        dynamic(columns, chip)
        if other == 0
        else grid.turn(dynamic(columns, chip ^ other), 2 * other)
        for other in range(4)
    ]
    inputs_two = [grid.turn(inputs_t, 2), grid.turn(inputs_t, 4)]
    cosine, sine_table = rope_tables(all_positions)
    block_index = steps_back * TEAM + (
        jnp.array([relative(p) for p in range(TEAM)], jnp.int32) ^ member
    )
    token_index = (block_index[:, None] * own + jnp.arange(own, dtype=jnp.int32)).reshape(tokens)
    starts = token_index - all_positions
    low = jnp.concatenate([starts[::own] // BLOCK, member[None]]).astype(jnp.int32)
    starts = starts[None]
    third = width // 3
    down_thirds = jnp.concatenate(
        [down_weight[:, part * third : (part + 1) * third] for part in range(3)], axis=0
    ).reshape(TEAM, rows, third)
    cosine, sine_table, starts, low, down_thirds, pairs, inputs_two, inputs_t = order.step(
        cosine, sine_table, starts, low, down_thirds, pairs, inputs_two, inputs_t
    )
    inputs_three = grid.turn(inputs_t, 6)
    pairs = jnp.stack(pairs)
    pairs_keep, pairs_give = dynamic(pairs, core, 1), dynamic(pairs, 1 - core, 1)
    team_rows = jnp.concatenate([pairs_keep, grid.turn(pairs_give, 1)], axis=0)
    attn_rows, team_rows, out_weight = order.step(
        team_rows[..., :attn_wide], team_rows, out_weight
    )
    attn_z = grid.spread(attn_rows)
    inputs_others = [grid.turn(block, 1) for block in [inputs_t] + inputs_two]
    attn_z, inputs_three = order.step(attn_z, inputs_three)
    inputs_others = inputs_others + [grid.turn(inputs_three, 1)]
    inputs_team = [inputs_t] + inputs_two + [inputs_three] + inputs_others
    out_own = grid.to_members(out_weight)
    attn_w = place_rows(grid, attn_z, 0, attn_wide).reshape(width, attn_wide)
    attn_w, inputs_team, out_own = order.step(attn_w, inputs_team, out_own)

    out_z = grid.spread(out_own)
    normed_first, queries, own_piece = project(inputs_team, attn_w, cosine, sine_table)
    own_piece, out_z, cotangent, attn_w = order.step(own_piece, out_z, cotangent, attn_w)
    arrived = [grid.shift(own_piece, step, False) for step in range(1, steps_back + 1)]
    cotangent_chips = grid.chips(cotangent)
    out_rows = place_rows(grid, [block[None] for block in out_z], 0, width)
    out_rows = out_rows.reshape(Q_WIDTH, width)
    gain_first = attn_w[:, LINED : LINED + 1].astype(f32)
    gain_second = attn_w[:, LINED + 1 : LINED + 2].astype(f32)
    mixer_own = jnp.concatenate([team_rows[..., attn_wide:], down_thirds], axis=-1)
    arrived, out_rows, gain_first, gain_second, mixer_own = order.step(
        arrived, out_rows, gain_first, gain_second, mixer_own
    )

    mixer_hops = [grid.both_ways(mixer_own, mixer_own)]

    def next_hop():
        mixer_hops[-1] = order.step(mixer_hops[-1])
        if len(mixer_hops) < teams - 1:
            mixer_hops.append(grid.both_ways(*mixer_hops[-1]))

    pieces = [own_piece] + arrived
    attended, normalizer = attend(low, starts, queries, pieces, 0, OWN_KV)
    keep, give = project_out(attended, out_rows)
    give, cotangent_chips, mixer_hops[0] = order.step(give, cotangent_chips, mixer_hops[0])
    other = grid.turn(give, 1)
    if len(mixer_hops) < teams - 1:
        mixer_hops.append(grid.both_ways(*mixer_hops[-1]))
    other = order.step(other)
    total, blocks = combine(keep, other, 1)
    blocks = order.step(blocks)
    terms = grid.send_chips(blocks)
    cotangent_stack = order.step(jnp.stack(cotangent_chips))
    terms, mixer_hops[-1] = order.step(terms, mixer_hops[-1])
    if len(mixer_hops) < teams - 1:
        mixer_hops.append(grid.both_ways(*mixer_hops[-1]))
    cotangent_other = grid.turn(cotangent_stack, 1)
    middle, normed_second = finish_middle([total] + terms, inputs_t, gain_second)
    normed_second, cotangent_other = order.step(normed_second, cotangent_other)
    cotangent_team = [cotangent_stack, cotangent_other]
    second_chips = grid.chips(normed_second)
    while len(mixer_hops) < teams - 1:
        next_hop()
    second_chips, mixer_hops[-1] = order.step(second_chips, mixer_hops[-1])
    second_team = grid.gather_team(second_chips)
    mixer_w, down_w = place_mixer(grid, mixer_own, mixer_hops, units, unit_rows)
    mixer_w = mixer_w.reshape(width, 2 * units)
    down_w = down_w.reshape(units, width)
    mixer_w, down_w, second_team = order.step(mixer_w, down_w, second_team)

    early = max(1, teams // 2)

    def send_teams(product, first, last):
        return [grid.shift(product[steps], steps) for steps in range(first, last)]

    hidden, grads = mixer_forward(second_team, cotangent_team, mixer_w, down_w)
    keep, give = mixer_backward(grads, mixer_w)
    give, grads = order.step(give, grads)
    other = order.step(grid.turn(give, 1))
    total, blocks = combine(keep, other, 1)
    blocks, hidden, grads = order.step(blocks, hidden, grads)
    terms = grid.send_chips(blocks)
    mixer_part = token_product(grid, second_team, grads, True, 2 * units)
    mixer_part, hidden = order.step(mixer_part, hidden)
    mixer_parts = send_teams(mixer_part, 1, early + 1)
    down_part = down_product(grid, hidden, cotangent_team)
    terms, down_part = order.step(terms, down_part)
    grad_middle, grad_attn, second_part = finish_second(
        [total] + terms, middle, cotangent, gain_second
    )
    grad_attn, hidden = order.step(grad_attn, hidden)
    attn_chips = grid.chips(grad_attn)
    out_keep, out_give = mixer_output(hidden, down_w)
    attn_chips, out_give, mixer_parts = order.step(attn_chips, out_give, mixer_parts)
    late_parts = send_teams(mixer_part, early + 1, teams)
    attn_team = order.step(grid.gather_team(attn_chips))

    grad_attended, out_part = project_out_back(grid, attn_team, out_rows, attended)
    grad_attended, down_part, out_give = order.step(grad_attended, down_part, out_give)
    down_parts = send_teams(down_part, 1, early + 1)
    out_other = grid.turn(out_give, 1)
    query_rot, own_grads, back_grads = attend_back(
        low, starts, queries, grad_attended, attended, normalizer, pieces, 0, OWN_KV
    )
    query_rot, own_grads, back_grads, late_parts, out_other = order.step(
        query_rot, own_grads, back_grads, late_parts, out_other
    )
    returned = [
        grid.shift(back_grads[step - 1], -step, False) for step in range(1, steps_back + 1)
    ]
    out_total, out_blocks = combine(out_keep, out_other, 0)
    out_blocks = order.step(out_blocks)
    out_terms = grid.send_chips(out_blocks)
    mixer_total = sum_teams(mixer_part, mixer_parts + late_parts, bf16)
    returned, down_parts, mixer_total = order.step(returned, down_parts, mixer_total)
    down_late = send_teams(down_part, early + 1, teams)
    keep, give, attn_part = project_back(
        grid, normed_first, query_rot, own_grads, returned, cosine, sine_table, attn_w
    )
    attn_part, give, out_terms, down_late = order.step(attn_part, give, out_terms, down_late)
    other = grid.turn(give, 1)
    attn_parts = send_teams(attn_part, 1, early + 1)
    other = order.step(other)
    total, blocks = combine(keep, other, 1)
    blocks, out_part = order.step(blocks, out_part)
    terms = grid.send_chips(blocks)
    outputs = finish_output([out_total] + out_terms, middle)
    down_grad = sum_teams(down_part, down_parts + down_late, f32)
    attn_parts, outputs, down_grad = order.step(attn_parts, outputs, down_grad)
    attn_late = send_teams(attn_part, early + 1, teams)
    out_parts = send_teams(out_part, 1, teams)

    def members_rows(total):
        blocks = total.reshape(TEAM // 2, 2, rows, -1)
        return dynamic(blocks, core, 1), grid.turn(dynamic(blocks, 1 - core, 1), 1)

    def owner_columns(mine, others):
        both = jnp.stack([mine, others])
        first = jnp.where(core == 0, both[0], both[1])
        second = jnp.where(core == 0, both[1], both[0])
        both = jnp.stack([first, second], axis=1)
        found = [
            dynamic(both, chip) if other == 0 else grid.turn(dynamic(both, chip ^ other), 2 * other)
            for other in range(4)
        ]
        return found

    def in_order(found):
        stacked = jnp.stack(found)
        return jnp.stack([dynamic(stacked, chip ^ other) for other in range(4)]).reshape(
            (TEAM,) + found[0].shape[1:]
        )

    mixer_mine, mixer_others = members_rows(mixer_total)
    mixer_mine, mixer_others, terms = order.step(mixer_mine, mixer_others, terms)
    mixer_found = owner_columns(mixer_mine, mixer_others)
    input_grad, first_part = finish_first([total] + terms, inputs_t, grad_middle, gain_first)
    gain_parts = jnp.concatenate([first_part, second_part], axis=1).T
    attn_late, gain_parts, out_parts = order.step(attn_late, gain_parts, out_parts)
    attn_total = sum_teams(attn_part, attn_parts + attn_late, bf16)
    out_own = sum_teams(out_part, out_parts, bf16)
    attn_mine, attn_others = members_rows(attn_total)
    gain_parts = gain_parts + grid.turn(gain_parts, 1)
    attn_mine, attn_others, gain_parts, out_own = order.step(
        attn_mine, attn_others, gain_parts, out_own
    )
    attn_found = owner_columns(attn_mine, attn_others)
    out_grad = grid.to_owners(out_own).astype(f32)
    gain_parts = gain_parts + grid.turn(gain_parts, 2)
    mixer_found, gain_parts = order.step(mixer_found, gain_parts)
    mixer_columns = in_order(mixer_found)

    def whole_units(blocks):
        blocks = blocks.reshape(TEAM, rows, teams, unit_rows)
        return jnp.transpose(blocks, (1, 2, 0, 3)).reshape(rows, TEAM * units).astype(f32)

    def whole(blocks):
        return jnp.transpose(blocks, (1, 0, 2)).reshape(rows, -1).astype(f32)

    gate_grad = whole_units(mixer_columns[..., :units])
    up_grad = whole_units(mixer_columns[..., units:])
    gain_parts = gain_parts + grid.turn(gain_parts, 4)
    gain_blocks = gain_parts.reshape(2, teams, TEAM, rows)
    gain_sums = dynamic(dynamic(gain_blocks, grid.team, 1), member, 1)
    for steps in range(1, teams):
        block = dynamic(dynamic(gain_blocks, (grid.team + steps) % teams, 1), member, 1)
        gain_sums = gain_sums + grid.shift(block, steps)
    attn_found, gain_sums = order.step(attn_found, gain_sums)
    attn_columns = in_order(attn_found)
    gain_sums = gain_sums + order.token[0, 0].astype(f32)
    return (
        outputs,
        input_grad,
        gain_sums[0],
        whole(attn_columns[..., :Q_WIDTH]),
        whole(attn_columns[..., Q_WIDTH : Q_WIDTH + KV_WIDTH]),
        whole(attn_columns[..., Q_WIDTH + KV_WIDTH :]),
        out_grad,
        gain_sums[1],
        gate_grad,
        up_grad,
        down_grad,
    )


def solution(mesh):
    matrix, vector = P("dev", None), P("dev")
    in_specs = (matrix, vector, vector) + (matrix,) * 4 + (vector,) + (matrix,) * 4
    out_specs = (matrix, matrix, vector) + (matrix,) * 4 + (vector,) + (matrix,) * 3
    return jax.shard_map(
        per_device, mesh=mesh, in_specs=in_specs, out_specs=out_specs, check_vma=False
    )
```

time: 2170 us -> 651 us (0.30)
  waiting for transfers between devices: 1530 us -> 219 us
  matrix products: 281 us -> 0 us
  Pallas kernels: 0 us -> 258 us
  blocking collectives: 95.3 us -> 0 us
  local copies, waits for them, and re-layouts: 101 us -> 35.8 us
  starting transfers between devices: 52.6 us -> 111 us
  other arithmetic: 65.2 us -> 11 us
    reduce_scatter x7 -> x0, waiting for transfers between devices: 1140 us -> none  [the longest x1 253 us: per_device(): lax.psum_scatter(up_grad_part, 'dev', scatter_dimension=0, tiled=True)]
    dot_general x84 -> x0, matrix products: 281 us -> none  [the longest x7 53 us: inner_rows(): lax.dot_general(operand, weights, (((0,), (0,)), ((), ())), preferred_ele...]
    pallas_call x0 -> x26, Pallas kernels: none -> 258 us  [the longest x1 30.7 us: attend_back(): pl.pallas_call(gradient_kernel, grid=(count,), in_specs=[low_spec, whole,...]
    all_gather x7 -> x0, waiting for transfers between devices: 185 us -> none  [the longest x1 87.6 us: per_device(): lax.all_gather(down_weight, 'dev', axis=0, tiled=True)]
    unnamed x2 -> x0, blocking collectives: 95.3 us -> none
    ppermute x16 -> x91, starting transfers between devices: 52 us -> 111 us  [the longest x29 61.8 us: shift(): return lax.ppermute(value, 'dev', pairs)]
    while x163 -> x0, local copies, waits for them, and re-layouts: 28.4 us -> none  [the longest x1 15.1 us: gradient_pass(): lax.scan(gradient_advance, jnp.zeros(query_groups.shape, jnp.float32), (o...]
    ppermute x16 -> x91, waiting for transfers between devices: 202 us -> 219 us  [the longest x29 118 us: shift(): return lax.ppermute(value, 'dev', pairs)]
  transfers between devices with their start and end apart: 30 -> 91, of which waited for: 26 -> 33; matrix products, arithmetic and copies ran while one was open for 11% -> 5% of each run, Pallas kernels for 0% -> 30%
where the time goes in v1:
time: 651 us; the launch traced here: 638 us
  Pallas kernels  258 us (40%)
  waiting for transfers between devices  219 us (34%)
  starting transfers between devices  111 us (17%)
  local copies, waits for them, and re-layouts  35.8 us (5%)
  other arithmetic  11 us (2%)
    ppermute x29, waiting for transfers between devices, shift(): return lax.ppermute(value, 'dev', pairs)  118 us
    ppermute x60, waiting for transfers between devices, turn(): lax.ppermute(value, 'dev', [(d, d ^ bits) for d in range(self.count)])  97.6 us
    ppermute x29, starting transfers between devices, shift(): return lax.ppermute(value, 'dev', pairs)  61.8 us
    ppermute x60, starting transfers between devices, turn(): lax.ppermute(value, 'dev', [(d, d ^ bits) for d in range(self.count)])  45.9 us
    pallas_call x1, Pallas kernels, attend_back(): pl.pallas_call(gradient_kernel, grid=(count,), in_specs=[low_spec, whole,...  30.7 us
    pallas_call x4, Pallas kernels, combine(): call(kernel, (4,), [part, part], [whole] * 4, [jax.ShapeDtypeStruct(shape...  27.1 us
    pallas_call x1, Pallas kernels, attend(): pl.pallas_call(attend_kernel, grid=(count,), in_specs=[low_spec, whole, h...  24.5 us
    pallas_call x1, Pallas kernels, project_back(): call(kernel, (TEAM,), [lanes_at(width, own), heads, lanes_at(HEAD_DIM, ow...  23.6 us
  transfers between devices with their start and end apart: 91, of which 33 were waited for; matrix products, arithmetic and copies ran while one was open for 5% of the time, Pallas kernels for 30%

profile of v1, /device:TPU:10, one launch (start us, length us, event | category | flops | bytes accessed | tf_op | source)
XLA Modules:
  0.0 638.2 jit_solution(2465797738896981961)
XLA Ops:
  21.0 3.6 fusion
  24.6 12.8 %collective-permute-done.4 = bf16[2,48,1536]{2,1,0:T(8,128)(2,1)S(1)} collective-permute-done((bf16[2,48,1536]{2,1,0:T(8,128)(2,1)}, bf16[2,48,1536]{2,1,0:T(8,128)(2,1)S(1)}, u32[]{:S(2)}, u32[]{:S(2)}) %collective-permute-start.4) | collective-permute-done | bytes 294944 | tf_op jit(solution)/shard_map/ppermute | solution.py:267
  37.4 3.7 collective-permute-done.5
  49.8 14.1 %collective-permute-done.13.refs_3_ = bf16[1536,256]{1,0:T(8,128)(2,1)} collective-permute-done((bf16[1536,256]{1,0:T(8,128)(2,1)S(1)}, bf16[1536,256]{1,0:T(8,128)(2,1)}, u32[]{:S(2)}, u32[]{:S(2)}) %collective-permute-start.13) | collective-permute-done | bytes 786464 | tf_op jit(solution)/shard_map/ppermute | solution.py:267
  63.9 9.2 %collective-permute-done.10.refs_1_ = bf16[8,48,512]{2,1,0:T(8,128)(2,1)S(1)} collective-permute-done((bf16[8,48,512]{2,1,0:T(8,128)(2,1)S(1)}, bf16[8,48,512]{2,1,0:T(8,128)(2,1)S(1)}, u32[]{:S(2)}, u32[]{:S(2)}) %collective-permute-start.10) | collective-permute-done | bytes 393248 | tf_op jit(solution)/shard_map/ppermute | solution.py:275
  73.1 7.6 %collective-permute-done.11.refs_2_ = bf16[8,48,512]{2,1,0:T(8,128)(2,1)S(1)} collective-permute-done((bf16[8,48,512]{2,1,0:T(8,128)(2,1)S(1)}, bf16[8,48,512]{2,1,0:T(8,128)(2,1)S(1)}, u32[]{:S(2)}, u32[]{:S(2)}) %collective-permute-start.11) | collective-permute-done | bytes 393248 | tf_op jit(solution)/shard_map/ppermute | solution.py:275
  85.8 3.8 shard_map.212
  98.0 11.8 %shard_map.213 = (bf16[1536,2048]{1,0:T(8,128)(2,1)}, bf16[2,96,2048]{2,1,0:T(8,128)(2,1)}, bf16[2,1,96,2048]{3,2,1,0:T(8,128)(2,1)}) custom-call(bf16[1536,512]{1,0:T(8,128)(2,1)} %bitcast.175, f32[96,2048]{1,0:T(8,128)} %get-tuple-element.279.cosine_ref, f32[96,2048]{1,0:T(8,128)} %get-tuple-element.280.sine_ref, bf16[1536,256]{1,0:T(8,128)(2,1)} %bitcast.182, ...), custom_call_target="tpu_custom_call" | custom-call | flops 1000 | bytes 1000 | tf_op jit(solution)/shard_map/pallas_call | solution.py:500
  112.1 3.5 shard_map.214
  117.0 14.2 %collective-permute-done.22.refs_1_ = bf16[2,1,96,2048]{3,2,1,0:T(8,128)(2,1)S(1)} collective-permute-done((bf16[2,1,96,2048]{3,2,1,0:T(8,128)(2,1)}, bf16[2,1,96,2048]{3,2,1,0:T(8,128)(2,1)S(1)}, u32[]{:S(2)}, u32[]{:S(2)}) %collective-permute-start.22) | collective-permute-done | bytes 786464 | tf_op jit(solution)/shard_map/ppermute | solution.py:275
  133.4 3.7 collective-permute-start.27
  137.3 3.4 collective-permute-start.25
  140.7 24.5 %shard_map.215 = (f32[2,96,2048]{2,1,0:T(8,128)}, f32[2,1,2048]{2,1,0:T(1,128)}) custom-call(s32[9]{0:T(128)} %pad_add_fusion.1.low_ref, s32[1,2048]{1,0:T(1,128)} %bitcast.227, bf16[2,96,2048]{2,1,0:T(8,128)(2,1)} %get-tuple-element.303.query_ref, bf16[2,1,96,2048]{3,2,1,0:T(8,128)(2,1)} %get-tuple-element.292.refs_0_, bf16[2,1,96,2048]{3,2,1,0:T(8,128)(2,1)} %copy-done.15), custom_call_target="tpu_custom_call" | custom-call | flops 1000 | bytes 1000 | tf_op jit(solution)/shard_map/pallas_call | solution.py:195
  165.3 9.4 %shard_map.216 = (f32[1536,1024]{1,0:T(8,128)}, bf16[1536,1024]{1,0:T(8,128)(2,1)}) custom-call(f32[2,96,2048]{2,1,0:T(8,128)} %get-tuple-element.305.attended_ref.out_ref, bf16[192,1536]{1,0:T(8,128)(2,1)} %bitcast.189), custom_call_target="tpu_custom_call" | custom-call | flops 1000 | bytes 1000 | tf_op jit(solution)/shard_map/pallas_call | solution.py:538
  182.3 6.8 %shard_map.217 = (f32[1536,256]{1,0:T(8,128)}, bf16[1536,256]{1,0:T(8,128)(2,1)}, bf16[1536,256]{1,0:T(8,128)(2,1)}, bf16[1536,256]{1,0:T(8,128)(2,1)}) custom-call(f32[1536,1024]{1,0:T(8,128)} %get-tuple-element.313.keep_ref, bf16[1536,1024]{1,0:T(8,128)(2,1)} %copy-done.18), custom_call_target="tpu_custom_call" | custom-call | flops 1000 | bytes 1000 | tf_op jit(solution)/shard_map/pallas_call | solution.py:827
  191.2 5.0 collective-permute-start.33
  196.8 22.7 %collective-permute-done.32.refs_3_ = bf16[8,48,1536]{2,1,0:T(8,128)(2,1)} collective-permute-done((bf16[8,48,1536]{2,1,0:T(8,128)(2,1)S(1)}, bf16[8,48,1536]{2,1,0:T(8,128)(2,1)}, u32[]{:S(2)}, u32[]{:S(2)}) %collective-permute-start.32) | collective-permute-done | bytes 1179680 | tf_op jit(solution)/shard_map/ppermute | solution.py:275
  222.8 16.9 %collective-permute-done.31.refs_3_ = bf16[1536,256]{1,0:T(8,128)(2,1)} collective-permute-done((bf16[1536,256]{1,0:T(8,128)(2,1)}, bf16[1536,256]{1,0:T(8,128)(2,1)}, u32[]{:S(2)}, u32[]{:S(2)}) %collective-permute-start.31) | collective-permute-done | bytes 786464 | tf_op jit(solution)/shard_map/ppermute | solution.py:267
  242.2 3.5 collective-permute-start.39
  245.6 4.8 shard_map.218
  254.0 14.3 %collective-permute-done.38.refs_5_ = bf16[8,48,1536]{2,1,0:T(8,128)(2,1)S(1)} collective-permute-done((bf16[8,48,1536]{2,1,0:T(8,128)(2,1)}, bf16[8,48,1536]{2,1,0:T(8,128)(2,1)S(1)}, u32[]{:S(2)}, u32[]{:S(2)}) %collective-permute-start.38) | collective-permute-done | bytes 1179680 | tf_op jit(solution)/shard_map/ppermute | solution.py:275
  271.2 14.0 %collective-permute-done.36.refs_2_ = bf16[1536,256]{1,0:T(8,128)(2,1)S(1)} collective-permute-done((bf16[1536,256]{1,0:T(8,128)(2,1)}, bf16[1536,256]{1,0:T(8,128)(2,1)S(1)}, u32[]{:S(2)}, u32[]{:S(2)}) %collective-permute-start.36) | collective-permute-done | bytes 786464 | tf_op jit(solution)/shard_map/ppermute | solution.py:267
  286.3 6.7 %shard_map.219 = (bf16[4,8,48,1024]{3,2,1,0:T(8,128)(2,1)}, bf16[4,128,1536]{2,1,0:T(8,128)(2,1)}) custom-call(s32[2]{0:T(128)} %pad_add_fusion.2.places_ref, bf16[8,48,1536]{2,1,0:T(8,128)(2,1)} %copy-done.6, bf16[8,48,1536]{2,1,0:T(8,128)(2,1)} %copy-done.23, bf16[8,48,1536]{2,1,0:T(8,128)(2,1)} %collective-permute-done.27.refs_2_, ...), custom_call_target="tpu_custom_call" | custom-call | flops 1000 | bytes 1000 | tf_op jit(solution)/shard_map/pallas_call | solution.py:447
  294.5 20.5 %shard_map.220 = (bf16[2048,512]{1,0:T(8,128)(2,1)}, bf16[2048,1024]{1,0:T(8,128)(2,1)}) custom-call(bf16[1536,1024]{1,0:T(8,128)(2,1)} %bitcast.185, bf16[512,1536]{1,0:T(8,128)(2,1)} %bitcast.187, bf16[1536,256]{1,0:T(8,128)(2,1)} %get-tuple-element.353.refs_0_, bf16[1536,256]{1,0:T(8,128)(2,1)} %copy-done.9, bf16[1536,256]{1,0:T(8,128)(2,1)} %copy-done.10, ...), custom_call_target="tpu_custom_call" | custom-call | flops 1000 | bytes 1000 | tf_op jit(solution)/shard_map/pallas_call | solution.py:571
  314.9 13.4 %shard_map.221 = (f32[1536,1024]{1,0:T(8,128)}, bf16[1536,1024]{1,0:T(8,128)(2,1)}) custom-call(bf16[2048,1024]{1,0:T(8,128)(2,1)} %get-tuple-element.375.grads_ref.right_ref, bf16[1536,1024]{1,0:T(8,128)(2,1)} %bitcast.186), custom_call_target="tpu_custom_call" | custom-call | flops 1000 | bytes 1000 | tf_op jit(solution)/shard_map/pallas_call | solution.py:600
  328.5 5.8 collective-permute-done.44.arrived_ref
  335.9 6.7 %shard_map.222 = (f32[1536,256]{1,0:T(8,128)}, bf16[1536,256]{1,0:T(8,128)(2,1)}, bf16[1536,256]{1,0:T(8,128)(2,1)}, bf16[1536,256]{1,0:T(8,128)(2,1)}) custom-call(f32[1536,1024]{1,0:T(8,128)} %get-tuple-element.367.keep_ref, bf16[1536,1024]{1,0:T(8,128)(2,1)} %copy-done.19), custom_call_target="tpu_custom_call" | custom-call | flops 1000 | bytes 1000 | tf_op jit(solution)/shard_map/pallas_call | solution.py:827
  346.1 18.8 %shard_map.223.own_ref = bf16[4,384,1024]{2,1,0:T(8,128)(2,1)} custom-call(s32[2]{0:T(128)} %pad_add_fusion.2.places_ref, bf16[2048,1024]{1,0:T(8,128)(2,1)} %get-tuple-element.375.grads_ref.right_ref, bf16[1536,256]{1,0:T(8,128)(2,1)} %get-tuple-element.353.refs_0_, bf16[1536,256]{1,0:T(8,128)(2,1)} %copy-done.9, bf16[1536,256]{1,0:T(8,128)(2,1)} %copy-done.10, ...), custom_call_target="tpu_custom_call" | custom-call | flops 1000 | bytes 1000 | tf_op jit(solution)/shard_map/pallas_call | solution.py:652
  364.9 13.1 %shard_map.224.own_ref = bf16[4,128,1536]{2,1,0:T(8,128)(2,1)} custom-call(s32[2]{0:T(128)} %pad_add_fusion.2.places_ref, bf16[2048,512]{1,0:T(8,128)(2,1)} %get-tuple-element.391.hidden_ref, bf16[4,256,1536]{2,1,0:T(8,128)(2,1)} %copy-done, bf16[4,256,1536]{2,1,0:T(8,128)(2,1)} %copy-done.4), custom_call_target="tpu_custom_call" | custom-call | flops 1000 | bytes 1000 | tf_op jit(solution)/shard_map/pallas_call | solution.py:686
  381.8 5.9 shard_map.225
  391.2 10.0 %shard_map.226 = (f32[1024,1536]{1,0:T(8,128)}, bf16[1024,1536]{1,0:T(8,128)(2,1)}) custom-call(bf16[2048,512]{1,0:T(8,128)(2,1)} %get-tuple-element.391.hidden_ref, bf16[512,1536]{1,0:T(8,128)(2,1)} %bitcast.188), custom_call_target="tpu_custom_call" | custom-call | flops 1000 | bytes 1000 | tf_op jit(solution)/shard_map/pallas_call | solution.py:613
  401.2 12.6 %collective-permute-done.51.refs_0_ = bf16[384,1024]{1,0:T(8,128)(2,1)S(1)} collective-permute-done((bf16[384,1024]{1,0:T(8,128)(2,1)S(1)}, bf16[384,1024]{1,0:T(8,128)(2,1)S(1)}, u32[]{:S(2)}, u32[]{:S(2)}) %collective-permute-start.51) | collective-permute-done | bytes 786464 | tf_op jit(solution)/shard_map/ppermute | solution.py:275
  413.9 15.1 %collective-permute-done.52.refs_1_ = bf16[384,1024]{1,0:T(8,128)(2,1)S(1)} collective-permute-done((bf16[384,1024]{1,0:T(8,128)(2,1)S(1)}, bf16[384,1024]{1,0:T(8,128)(2,1)S(1)}, u32[]{:S(2)}, u32[]{:S(2)}) %collective-permute-start.52) | collective-permute-done | bytes 786464 | tf_op jit(solution)/shard_map/ppermute | solution.py:275
  435.7 11.3 %shard_map.227 = (bf16[2,96,2048]{2,1,0:T(8,128)(2,1)}, bf16[4,48,1536]{2,1,0:T(8,128)(2,1)}) custom-call(s32[2]{0:T(128)} %pad_add_fusion.2.places_ref, bf16[192,1536]{1,0:T(8,128)(2,1)} %bitcast.190, f32[2,96,2048]{2,1,0:T(8,128)} %get-tuple-element.305.attended_ref.out_ref, bf16[1536,256]{1,0:T(8,128)(2,1)} %get-tuple-element.400.refs_0_, ...), custom_call_target="tpu_custom_call" | custom-call | flops 1000 | bytes 1000 | tf_op jit(solution)/shard_map/pallas_call | solution.py:729
  447.2 4.0 collective-permute-start.57
  455.5 30.7 %shard_map.228 = (f32[2,96,2048]{2,1,0:T(8,128)}, f32[2,1,96,2048]{3,2,1,0:T(8,128)}, bf16[1,2,1,96,2048]{4,3,2,1,0:T(8,128)(2,1)}) custom-call(s32[9]{0:T(128)} %pad_add_fusion.1.low_ref, s32[1,2048]{1,0:T(1,128)} %bitcast.228, bf16[2,96,2048]{2,1,0:T(8,128)(2,1)} %get-tuple-element.303.query_ref, bf16[2,96,2048]{2,1,0:T(8,128)(2,1)} %get-tuple-element.412.grad_ref, ...), custom_call_target="tpu_custom_call" | custom-call | flops 1000 | bytes 1000 | tf_op jit(solution)/shard_map/pallas_call | solution.py:221
  488.2 6.9 %shard_map.229 = (f32[256,1536]{1,0:T(8,128)}, bf16[256,1536]{1,0:T(8,128)(2,1)}, bf16[256,1536]{1,0:T(8,128)(2,1)}, bf16[256,1536]{1,0:T(8,128)(2,1)}) custom-call(f32[1024,1536]{1,0:T(8,128)} %get-tuple-element.419.keep_ref, bf16[1024,1536]{1,0:T(8,128)(2,1)} %copy-done.17), custom_call_target="tpu_custom_call" | custom-call | flops 1000 | bytes 1000 | tf_op jit(solution)/shard_map/pallas_call | solution.py:827
  501.8 8.1 %collective-permute-done.59.refs_1_ = bf16[2,1,96,2048]{3,2,1,0:T(8,128)(2,1)S(1)} collective-permute-done((bf16[2,1,96,2048]{3,2,1,0:T(8,128)(2,1)}, bf16[2,1,96,2048]{3,2,1,0:T(8,128)(2,1)S(1)}, u32[]{:S(2)}, u32[]{:S(2)}) %collective-permute-start.59) | collective-permute-done | bytes 786464 | tf_op jit(solution)/shard_map/ppermute | solution.py:275
  510.8 23.6 %shard_map.231 = (f32[1536,1024]{1,0:T(8,128)}, bf16[1536,1024]{1,0:T(8,128)(2,1)}, bf16[4,384,384]{2,1,0:T(8,128)(2,1)}) custom-call(s32[2]{0:T(128)} %pad_add_fusion.2.places_ref, bf16[1536,2048]{1,0:T(8,128)(2,1)} %get-tuple-element.431.normed_ref, f32[2,96,2048]{2,1,0:T(8,128)} %get-tuple-element.432.query_ref, ...), custom_call_target="tpu_custom_call" | custom-call | flops 1000 | bytes 1000 | tf_op jit(solution)/shard_map/pallas_call | solution.py:789
  534.6 5.9 collective-permute-done.66.arrived_ref
  542.1 6.8 %shard_map.232 = (f32[1536,256]{1,0:T(8,128)}, bf16[1536,256]{1,0:T(8,128)(2,1)}, bf16[1536,256]{1,0:T(8,128)(2,1)}, bf16[1536,256]{1,0:T(8,128)(2,1)}) custom-call(f32[1536,1024]{1,0:T(8,128)} %get-tuple-element.443.keep_ref, bf16[1536,1024]{1,0:T(8,128)(2,1)} %copy-done.20), custom_call_target="tpu_custom_call" | custom-call | flops 1000 | bytes 1000 | tf_op jit(solution)/shard_map/pallas_call | solution.py:827
  553.4 3.5 collective-permute-start.68
  560.8 4.1 shard_map.233
  565.0 7.4 %collective-permute-done.68.refs_1_ = bf16[384,384]{1,0:T(8,128)(2,1)} collective-permute-done((bf16[384,384]{1,0:T(8,128)(2,1)}, bf16[384,384]{1,0:T(8,128)(2,1)}, u32[]{:S(2)}, u32[]{:S(2)}) %collective-permute-start.68) | collective-permute-done | bytes 294944 | tf_op jit(solution)/shard_map/ppermute | solution.py:275
  572.4 4.8 collective-permute-start.73
  580.4 6.6 %collective-permute-done.71.refs_2_ = bf16[1536,256]{1,0:T(8,128)(2,1)S(1)} collective-permute-done((bf16[1536,256]{1,0:T(8,128)(2,1)}, bf16[1536,256]{1,0:T(8,128)(2,1)S(1)}, u32[]{:S(2)}, u32[]{:S(2)}) %collective-permute-start.71) | collective-permute-done | bytes 786464 | tf_op jit(solution)/shard_map/ppermute | solution.py:267
  589.1 5.5 shard_map.235
  607.8 4.5 collective-permute-done.82
  (383 shorter events, 159.6 us)
Async XLA Ops:
  10.5 32.1 %collective-permute-start.7 = (bf16[1536,256]{1,0:T(8,128)(2,1)S(1)}, bf16[1536,256]{1,0:T(8,128)(2,1)}, u32[]{:S(2)}, u32[]{:S(2)}) collective-permute-start(bf16[1536,256]{1,0:T(8,128)(2,1)S(1)} %bitcast.178), channel_id=1, source_target_pairs={{0,2},{1,3},{2,0},{3,1},{4,6},{5,7},{6,4},{7,5},{8,10},{9,11},{10,... | collective-permute-start | bytes 2359304 | tf_op jit(solution)/shard_map/ppermute | solution.py:267
  11.1 31.5 %collective-permute-start.8 = (bf16[1536,256]{1,0:T(8,128)(2,1)S(1)}, bf16[1536,256]{1,0:T(8,128)(2,1)}, u32[]{:S(2)}, u32[]{:S(2)}) collective-permute-start(bf16[1536,256]{1,0:T(8,128)(2,1)S(1)} %bitcast.179), channel_id=1, source_target_pairs={{0,4},{1,5},{2,6},{3,7},{4,0},{5,1},{6,2},{7,3},{8,12},{9,13},{10,... | collective-permute-start | bytes 2359304 | tf_op jit(solution)/shard_map/ppermute | solution.py:267
  14.7 22.7 %collective-permute-start.4 = (bf16[2,48,1536]{2,1,0:T(8,128)(2,1)}, bf16[2,48,1536]{2,1,0:T(8,128)(2,1)S(1)}, u32[]{:S(2)}, u32[]{:S(2)}) collective-permute-start(bf16[2,48,1536]{2,1,0:T(8,128)(2,1)} %get-tuple-element.518), channel_id=1, source_target_pairs={{0,2},{1,3},{2,0},{3,1},{4,6},{5,7},{6,4},{7,5},{8,10},{9,11},{10,... | collective-permute-start | bytes 884744 | tf_op jit(solution)/shard_map/ppermute | solution.py:267
  16.2 24.8 %collective-permute-start.5 = (bf16[2,48,1536]{2,1,0:T(8,128)(2,1)}, bf16[2,48,1536]{2,1,0:T(8,128)(2,1)S(1)}, u32[]{:S(2)}, u32[]{:S(2)}) collective-permute-start(bf16[2,48,1536]{2,1,0:T(8,128)(2,1)} %get-tuple-element.517), channel_id=1, source_target_pairs={{0,4},{1,5},{2,6},{3,7},{4,0},{5,1},{6,2},{7,3},{8,12},{9,13},{10,... | collective-permute-start | bytes 884744 | tf_op jit(solution)/shard_map/ppermute | solution.py:267
  18.0 24.6 %collective-permute-start.6 = (bf16[2,48,1536]{2,1,0:T(8,128)(2,1)S(1)}, bf16[2,48,1536]{2,1,0:T(8,128)(2,1)S(1)}, u32[]{:S(2)}, u32[]{:S(2)}) collective-permute-start(bf16[2,48,1536]{2,1,0:T(8,128)(2,1)S(1)} %get-tuple-element.516), channel_id=1, source_target_pairs={{0,6},{1,7},{2,4},{3,5},{4,2},{5,3},{6,0},{7,1},{8,14},{9,15},{10,... | collective-permute-start | bytes 884744 | tf_op jit(solution)/shard_map/ppermute | solution.py:267
  42.9 21.0 %collective-permute-start.13 = (bf16[1536,256]{1,0:T(8,128)(2,1)S(1)}, bf16[1536,256]{1,0:T(8,128)(2,1)}, u32[]{:S(2)}, u32[]{:S(2)}) collective-permute-start(bf16[1536,256]{1,0:T(8,128)(2,1)S(1)} %bitcast.180), channel_id=1, source_target_pairs={{0,6},{1,7},{2,4},{3,5},{4,2},{5,3},{6,0},{7,1},{8,14},{9,15},{10,... | collective-permute-start | bytes 2359304 | tf_op jit(solution)/shard_map/ppermute | solution.py:267
  45.1 28.0 %collective-permute-start.10 = (bf16[8,48,512]{2,1,0:T(8,128)(2,1)S(1)}, bf16[8,48,512]{2,1,0:T(8,128)(2,1)S(1)}, u32[]{:S(2)}, u32[]{:S(2)}) collective-permute-start(bf16[8,48,512]{2,1,0:T(8,128)(2,1)S(1)} %fusion.2.refs_0_), channel_id=1, source_target_pairs={{0,8},{1,9},{2,10},{3,11},{4,12},{5,13},{6,14},{7,15},{8,16},{9,17... | collective-permute-start | bytes 1179656 | tf_op jit(solution)/shard_map/ppermute | solution.py:275
  46.7 34.0 %collective-permute-start.11 = (bf16[8,48,512]{2,1,0:T(8,128)(2,1)S(1)}, bf16[8,48,512]{2,1,0:T(8,128)(2,1)S(1)}, u32[]{:S(2)}, u32[]{:S(2)}) collective-permute-start(bf16[8,48,512]{2,1,0:T(8,128)(2,1)S(1)} %fusion.2.refs_0_), channel_id=1, source_target_pairs={{0,16},{1,17},{2,18},{3,19},{4,20},{5,21},{6,22},{7,23},{8,24},{9,... | collective-permute-start | bytes 1179656 | tf_op jit(solution)/shard_map/ppermute | solution.py:275
  48.0 34.5 %collective-permute-start.12 = (bf16[8,48,512]{2,1,0:T(8,128)(2,1)S(1)}, bf16[8,48,512]{2,1,0:T(8,128)(2,1)S(1)}, u32[]{:S(2)}, u32[]{:S(2)}) collective-permute-start(bf16[8,48,512]{2,1,0:T(8,128)(2,1)S(1)} %fusion.2.refs_0_), channel_id=1, source_target_pairs={{0,24},{1,25},{2,26},{3,27},{4,28},{5,29},{6,30},{7,31},{8,0},{9,1... | collective-permute-start | bytes 1179656 | tf_op jit(solution)/shard_map/ppermute | solution.py:275
  49.8 41.9 %collective-permute-start.14 = (bf16[1536,256]{1,0:T(8,128)(2,1)S(1)}, bf16[1536,256]{1,0:T(8,128)(2,1)}, u32[]{:S(2)}, u32[]{:S(2)}) collective-permute-start(bf16[1536,256]{1,0:T(8,128)(2,1)S(1)} %bitcast.181), channel_id=1, source_target_pairs={{0,1},{1,0},{2,3},{3,2},{4,5},{5,4},{6,7},{7,6},{8,9},{9,8},{10,11... | collective-permute-start | bytes 2359304 | tf_op jit(solution)/shard_map/ppermute | solution.py:267
  63.9 27.8 %collective-permute-start.15 = (bf16[1536,256]{1,0:T(8,128)(2,1)}, bf16[1536,256]{1,0:T(8,128)(2,1)}, u32[]{:S(2)}, u32[]{:S(2)}) collective-permute-start(bf16[1536,256]{1,0:T(8,128)(2,1)} %collective-permute-done.7.refs_1_), channel_id=1, source_target_pairs={{0,1},{1,0},{2,3},{3,2},{4,5},{5,4},{6,7},{7,6},{8,9},{9,8},{10,11... | collective-permute-start | bytes 2359304 | tf_op jit(solution)/shard_map/ppermute | solution.py:267
  109.9 21.3 %collective-permute-start.22 = (bf16[2,1,96,2048]{3,2,1,0:T(8,128)(2,1)}, bf16[2,1,96,2048]{3,2,1,0:T(8,128)(2,1)S(1)}, u32[]{:S(2)}, u32[]{:S(2)}) collective-permute-start(bf16[2,1,96,2048]{3,2,1,0:T(8,128)(2,1)} %get-tuple-element.292.refs_0_), channel_id=1, source_target_pairs={{0,8},{1,9},{2,10},{3,11},{4,12},{5,13},{6,14},{7,15},{8,16},{9,17... | collective-permute-start | bytes 2359304 | tf_op jit(solution)/shard_map/ppermute | solution.py:275
  131.2 43.5 %collective-permute-start.26 = (bf16[8,48,1536]{2,1,0:T(8,128)(2,1)S(1)}, bf16[8,48,1536]{2,1,0:T(8,128)(2,1)S(1)}, u32[]{:S(2)}, u32[]{:S(2)}) collective-permute-start(bf16[8,48,1536]{2,1,0:T(8,128)(2,1)S(1)} %pad_maximum_fusion.3.refs_0_), channel_id=1, source_target_pairs={{0,8},{1,9},{2,10},{3,11},{4,12},{5,13},{6,14},{7,15},{8,16},{9,17... | collective-permute-start | bytes 3538952 | tf_op jit(solution)/shard_map/ppermute | solution.py:275
  133.4 41.3 %collective-permute-start.27 = (bf16[8,48,1536]{2,1,0:T(8,128)(2,1)S(1)}, bf16[8,48,1536]{2,1,0:T(8,128)(2,1)}, u32[]{:S(2)}, u32[]{:S(2)}) collective-permute-start(bf16[8,48,1536]{2,1,0:T(8,128)(2,1)S(1)} %pad_maximum_fusion.3.refs_0_), channel_id=1, source_target_pairs={{8,0},{9,1},{10,2},{11,3},{12,4},{13,5},{14,6},{15,7},{16,8},{17,9... | collective-permute-start | bytes 3538952 | tf_op jit(solution)/shard_map/ppermute | solution.py:275
  137.2 37.5 %collective-permute-start.23 = (bf16[256,1536]{1,0:T(8,128)(2,1)S(1)}, bf16[256,1536]{1,0:T(8,128)(2,1)}, u32[]{:S(2)}, u32[]{:S(2)}) collective-permute-start(bf16[256,1536]{1,0:T(8,128)(2,1)S(1)} %copy-done.8), channel_id=1, source_target_pairs={{0,2},{1,3},{2,0},{3,1},{4,6},{5,7},{6,4},{7,5},{8,10},{9,11},{10,... | collective-permute-start | bytes 2359304 | tf_op jit(solution)/shard_map/ppermute | solution.py:267
  137.2 37.4 %collective-permute-start.24 = (bf16[256,1536]{1,0:T(8,128)(2,1)S(1)}, bf16[256,1536]{1,0:T(8,128)(2,1)}, u32[]{:S(2)}, u32[]{:S(2)}) collective-permute-start(bf16[256,1536]{1,0:T(8,128)(2,1)S(1)} %copy-done.8), channel_id=1, source_target_pairs={{0,4},{1,5},{2,6},{3,7},{4,0},{5,1},{6,2},{7,3},{8,12},{9,13},{10,... | collective-permute-start | bytes 2359304 | tf_op jit(solution)/shard_map/ppermute | solution.py:267
  137.3 37.4 %collective-permute-start.25 = (bf16[256,1536]{1,0:T(8,128)(2,1)S(1)}, bf16[256,1536]{1,0:T(8,128)(2,1)}, u32[]{:S(2)}, u32[]{:S(2)}) collective-permute-start(bf16[256,1536]{1,0:T(8,128)(2,1)S(1)} %copy-done.8), channel_id=1, source_target_pairs={{0,6},{1,7},{2,4},{3,5},{4,2},{5,3},{6,0},{7,1},{8,14},{9,15},{10,... | collective-permute-start | bytes 2359304 | tf_op jit(solution)/shard_map/ppermute | solution.py:267
  189.1 61.3 %collective-permute-start.34 = (bf16[4,256,1536]{2,1,0:T(8,128)(2,1)S(1)}, bf16[4,256,1536]{2,1,0:T(8,128)(2,1)S(1)}, u32[]{:S(2)}, u32[]{:S(2)}) collective-permute-start(bf16[4,256,1536]{2,1,0:T(8,128)(2,1)S(1)} %pad_maximum_fusion.refs_8_.refs_0_), channel_id=1, source_target_pairs={{0,1},{1,0},{2,3},{3,2},{4,5},{5,4},{6,7},{7,6},{8,9},{9,8},{10,11... | collective-permute-start | bytes 9437192 | tf_op jit(solution)/shard_map/ppermute | solution.py:267
  189.3 30.2 %collective-permute-start.32 = (bf16[8,48,1536]{2,1,0:T(8,128)(2,1)S(1)}, bf16[8,48,1536]{2,1,0:T(8,128)(2,1)}, u32[]{:S(2)}, u32[]{:S(2)}) collective-permute-start(bf16[8,48,1536]{2,1,0:T(8,128)(2,1)S(1)} %copy-done.24), channel_id=1, source_target_pairs={{0,8},{1,9},{2,10},{3,11},{4,12},{5,13},{6,14},{7,15},{8,16},{9,17... | collective-permute-start | bytes 3538952 | tf_op jit(solution)/shard_map/ppermute | solution.py:275
  191.2 30.7 %collective-permute-start.33 = (bf16[8,48,1536]{2,1,0:T(8,128)(2,1)}, bf16[8,48,1536]{2,1,0:T(8,128)(2,1)}, u32[]{:S(2)}, u32[]{:S(2)}) collective-permute-start(bf16[8,48,1536]{2,1,0:T(8,128)(2,1)} %collective-permute-done.27.refs_2_), channel_id=1, source_target_pairs={{8,0},{9,1},{10,2},{11,3},{12,4},{13,5},{14,6},{15,7},{16,8},{17,9... | collective-permute-start | bytes 3538952 | tf_op jit(solution)/shard_map/ppermute | solution.py:275
  196.2 25.8 %collective-permute-start.29 = (bf16[1536,256]{1,0:T(8,128)(2,1)}, bf16[1536,256]{1,0:T(8,128)(2,1)S(1)}, u32[]{:S(2)}, u32[]{:S(2)}) collective-permute-start(bf16[1536,256]{1,0:T(8,128)(2,1)} %get-tuple-element.324), channel_id=1, source_target_pairs={{0,2},{1,3},{2,0},{3,1},{4,6},{5,7},{6,4},{7,5},{8,10},{9,11},{10,... | collective-permute-start | bytes 2359304 | tf_op jit(solution)/shard_map/ppermute | solution.py:267
  196.2 25.7 %collective-permute-start.30 = (bf16[1536,256]{1,0:T(8,128)(2,1)}, bf16[1536,256]{1,0:T(8,128)(2,1)S(1)}, u32[]{:S(2)}, u32[]{:S(2)}) collective-permute-start(bf16[1536,256]{1,0:T(8,128)(2,1)} %get-tuple-element.325), channel_id=1, source_target_pairs={{0,4},{1,5},{2,6},{3,7},{4,0},{5,1},{6,2},{7,3},{8,12},{9,13},{10,... | collective-permute-start | bytes 2359304 | tf_op jit(solution)/shard_map/ppermute | solution.py:267
  239.7 28.6 %collective-permute-start.38 = (bf16[8,48,1536]{2,1,0:T(8,128)(2,1)}, bf16[8,48,1536]{2,1,0:T(8,128)(2,1)S(1)}, u32[]{:S(2)}, u32[]{:S(2)}) collective-permute-start(bf16[8,48,1536]{2,1,0:T(8,128)(2,1)} %collective-permute-done.32.refs_3_), channel_id=1, source_target_pairs={{0,8},{1,9},{2,10},{3,11},{4,12},{5,13},{6,14},{7,15},{8,16},{9,17... | collective-permute-start | bytes 3538952 | tf_op jit(solution)/shard_map/ppermute | solution.py:275
  242.2 28.7 %collective-permute-start.39 = (bf16[8,48,1536]{2,1,0:T(8,128)(2,1)}, bf16[8,48,1536]{2,1,0:T(8,128)(2,1)}, u32[]{:S(2)}, u32[]{:S(2)}) collective-permute-start(bf16[8,48,1536]{2,1,0:T(8,128)(2,1)} %collective-permute-done.33.refs_4_), channel_id=1, source_target_pairs={{8,0},{9,1},{10,2},{11,3},{12,4},{13,5},{14,6},{15,7},{16,8},{17,9... | collective-permute-start | bytes 3538952 | tf_op jit(solution)/shard_map/ppermute | solution.py:275
  250.5 34.7 %collective-permute-start.36 = (bf16[1536,256]{1,0:T(8,128)(2,1)}, bf16[1536,256]{1,0:T(8,128)(2,1)S(1)}, u32[]{:S(2)}, u32[]{:S(2)}) collective-permute-start(bf16[1536,256]{1,0:T(8,128)(2,1)} %get-tuple-element.353.refs_0_), channel_id=1, source_target_pairs={{0,4},{1,5},{2,6},{3,7},{4,0},{5,1},{6,2},{7,3},{8,12},{9,13},{10,... | collective-permute-start | bytes 2359304 | tf_op jit(solution)/shard_map/ppermute | solution.py:267
  251.3 33.8 %collective-permute-start.37 = (bf16[1536,256]{1,0:T(8,128)(2,1)}, bf16[1536,256]{1,0:T(8,128)(2,1)S(1)}, u32[]{:S(2)}, u32[]{:S(2)}) collective-permute-start(bf16[1536,256]{1,0:T(8,128)(2,1)} %get-tuple-element.353.refs_0_), channel_id=1, source_target_pairs={{0,6},{1,7},{2,4},{3,5},{4,2},{5,3},{6,0},{7,1},{8,14},{9,15},{10,... | collective-permute-start | bytes 2359304 | tf_op jit(solution)/shard_map/ppermute | solution.py:267
  342.6 38.2 %collective-permute-start.45 = (bf16[1536,256]{1,0:T(8,128)(2,1)}, bf16[1536,256]{1,0:T(8,128)(2,1)S(1)}, u32[]{:S(2)}, u32[]{:S(2)}) collective-permute-start(bf16[1536,256]{1,0:T(8,128)(2,1)} %get-tuple-element.378), channel_id=1, source_target_pairs={{0,2},{1,3},{2,0},{3,1},{4,6},{5,7},{6,4},{7,5},{8,10},{9,11},{10,... | collective-permute-start | bytes 2359304 | tf_op jit(solution)/shard_map/ppermute | solution.py:267
  344.3 36.6 %collective-permute-start.46 = (bf16[1536,256]{1,0:T(8,128)(2,1)}, bf16[1536,256]{1,0:T(8,128)(2,1)}, u32[]{:S(2)}, u32[]{:S(2)}) collective-permute-start(bf16[1536,256]{1,0:T(8,128)(2,1)} %get-tuple-element.379), channel_id=1, source_target_pairs={{0,4},{1,5},{2,6},{3,7},{4,0},{5,1},{6,2},{7,3},{8,12},{9,13},{10,... | collective-permute-start | bytes 2359304 | tf_op jit(solution)/shard_map/ppermute | solution.py:267
  344.6 36.3 %collective-permute-start.47 = (bf16[1536,256]{1,0:T(8,128)(2,1)}, bf16[1536,256]{1,0:T(8,128)(2,1)}, u32[]{:S(2)}, u32[]{:S(2)}) collective-permute-start(bf16[1536,256]{1,0:T(8,128)(2,1)} %get-tuple-element.380), channel_id=1, source_target_pairs={{0,6},{1,7},{2,4},{3,5},{4,2},{5,3},{6,0},{7,1},{8,14},{9,15},{10,... | collective-permute-start | bytes 2359304 | tf_op jit(solution)/shard_map/ppermute | solution.py:267
  378.2 35.6 %collective-permute-start.51 = (bf16[384,1024]{1,0:T(8,128)(2,1)S(1)}, bf16[384,1024]{1,0:T(8,128)(2,1)S(1)}, u32[]{:S(2)}, u32[]{:S(2)}) collective-permute-start(bf16[384,1024]{1,0:T(8,128)(2,1)S(1)} %get-tuple-element.505), channel_id=1, source_target_pairs={{0,8},{1,9},{2,10},{3,11},{4,12},{5,13},{6,14},{7,15},{8,16},{9,17... | collective-permute-start | bytes 2359304 | tf_op jit(solution)/shard_map/ppermute | solution.py:275
  379.0 50.0 %collective-permute-start.52 = (bf16[384,1024]{1,0:T(8,128)(2,1)S(1)}, bf16[384,1024]{1,0:T(8,128)(2,1)S(1)}, u32[]{:S(2)}, u32[]{:S(2)}) collective-permute-start(bf16[384,1024]{1,0:T(8,128)(2,1)S(1)} %get-tuple-element.504), channel_id=1, source_target_pairs={{0,16},{1,17},{2,18},{3,19},{4,20},{5,21},{6,22},{7,23},{8,24},{9,... | collective-permute-start | bytes 2359304 | tf_op jit(solution)/shard_map/ppermute | solution.py:275
  387.7 41.2 %collective-permute-start.48 = (bf16[1536,256]{1,0:T(8,128)(2,1)}, bf16[1536,256]{1,0:T(8,128)(2,1)S(1)}, u32[]{:S(2)}, u32[]{:S(2)}) collective-permute-start(bf16[1536,256]{1,0:T(8,128)(2,1)} %get-tuple-element.400.refs_0_), channel_id=1, source_target_pairs={{0,2},{1,3},{2,0},{3,1},{4,6},{5,7},{6,4},{7,5},{8,10},{9,11},{10,... | collective-permute-start | bytes 2359304 | tf_op jit(solution)/shard_map/ppermute | solution.py:267
  389.4 39.6 %collective-permute-start.49 = (bf16[1536,256]{1,0:T(8,128)(2,1)}, bf16[1536,256]{1,0:T(8,128)(2,1)S(1)}, u32[]{:S(2)}, u32[]{:S(2)}) collective-permute-start(bf16[1536,256]{1,0:T(8,128)(2,1)} %get-tuple-element.400.refs_0_), channel_id=1, source_target_pairs={{0,4},{1,5},{2,6},{3,7},{4,0},{5,1},{6,2},{7,3},{8,12},{9,13},{10,... | collective-permute-start | bytes 2359304 | tf_op jit(solution)/shard_map/ppermute | solution.py:267
  389.7 39.3 %collective-permute-start.50 = (bf16[1536,256]{1,0:T(8,128)(2,1)}, bf16[1536,256]{1,0:T(8,128)(2,1)S(1)}, u32[]{:S(2)}, u32[]{:S(2)}) collective-permute-start(bf16[1536,256]{1,0:T(8,128)(2,1)} %get-tuple-element.400.refs_0_), channel_id=1, source_target_pairs={{0,6},{1,7},{2,4},{3,5},{4,2},{5,3},{6,0},{7,1},{8,14},{9,15},{10,... | collective-permute-start | bytes 2359304 | tf_op jit(solution)/shard_map/ppermute | solution.py:267
  447.0 39.2 %collective-permute-start.58 = (bf16[1024,1536]{1,0:T(8,128)(2,1)}, bf16[1024,1536]{1,0:T(8,128)(2,1)S(1)}, u32[]{:S(2)}, u32[]{:S(2)}) collective-permute-start(bf16[1024,1536]{1,0:T(8,128)(2,1)} %get-tuple-element.417), channel_id=1, source_target_pairs={{0,1},{1,0},{2,3},{3,2},{4,5},{5,4},{6,7},{7,6},{8,9},{9,8},{10,11... | collective-permute-start | bytes 9437192 | tf_op jit(solution)/shard_map/ppermute | solution.py:267
  447.2 39.0 %collective-permute-start.57 = (bf16[384,1024]{1,0:T(8,128)(2,1)S(1)}, bf16[384,1024]{1,0:T(8,128)(2,1)S(1)}, u32[]{:S(2)}, u32[]{:S(2)}) collective-permute-start(bf16[384,1024]{1,0:T(8,128)(2,1)S(1)} %get-tuple-element.503), channel_id=1, source_target_pairs={{0,24},{1,25},{2,26},{3,27},{4,28},{5,29},{6,30},{7,31},{8,0},{9,1... | collective-permute-start | bytes 2359304 | tf_op jit(solution)/shard_map/ppermute | solution.py:275
  452.2 44.8 %collective-permute-start.60 = (bf16[128,1536]{1,0:T(8,128)(2,1)S(1)}, bf16[128,1536]{1,0:T(8,128)(2,1)S(1)}, u32[]{:S(2)}, u32[]{:S(2)}) collective-permute-start(bf16[128,1536]{1,0:T(8,128)(2,1)S(1)} %get-tuple-element.508), channel_id=1, source_target_pairs={{0,8},{1,9},{2,10},{3,11},{4,12},{5,13},{6,14},{7,15},{8,16},{9,17... | collective-permute-start | bytes 1179656 | tf_op jit(solution)/shard_map/ppermute | solution.py:275
  452.2 46.3 %collective-permute-start.61 = (bf16[128,1536]{1,0:T(8,128)(2,1)}, bf16[128,1536]{1,0:T(8,128)(2,1)S(1)}, u32[]{:S(2)}, u32[]{:S(2)}) collective-permute-start(bf16[128,1536]{1,0:T(8,128)(2,1)} %get-tuple-element.507), channel_id=1, source_target_pairs={{0,16},{1,17},{2,18},{3,19},{4,20},{5,21},{6,22},{7,23},{8,24},{9,... | collective-permute-start | bytes 1179656 | tf_op jit(solution)/shard_map/ppermute | solution.py:275
  486.2 23.7 %collective-permute-start.59 = (bf16[2,1,96,2048]{3,2,1,0:T(8,128)(2,1)}, bf16[2,1,96,2048]{3,2,1,0:T(8,128)(2,1)S(1)}, u32[]{:S(2)}, u32[]{:S(2)}) collective-permute-start(bf16[2,1,96,2048]{3,2,1,0:T(8,128)(2,1)} %bitcast.243), channel_id=1, source_target_pairs={{8,0},{9,1},{10,2},{11,3},{12,4},{13,5},{14,6},{15,7},{16,8},{17,9... | collective-permute-start | bytes 2359304 | tf_op jit(solution)/shard_map/ppermute | solution.py:275
  495.0 39.4 %collective-permute-start.62 = (bf16[256,1536]{1,0:T(8,128)(2,1)}, bf16[256,1536]{1,0:T(8,128)(2,1)S(1)}, u32[]{:S(2)}, u32[]{:S(2)}) collective-permute-start(bf16[256,1536]{1,0:T(8,128)(2,1)} %get-tuple-element.437), channel_id=1, source_target_pairs={{0,2},{1,3},{2,0},{3,1},{4,6},{5,7},{6,4},{7,5},{8,10},{9,11},{10,... | collective-permute-start | bytes 2359304 | tf_op jit(solution)/shard_map/ppermute | solution.py:267
  496.7 37.8 %collective-permute-start.63 = (bf16[256,1536]{1,0:T(8,128)(2,1)}, bf16[256,1536]{1,0:T(8,128)(2,1)S(1)}, u32[]{:S(2)}, u32[]{:S(2)}) collective-permute-start(bf16[256,1536]{1,0:T(8,128)(2,1)} %get-tuple-element.438), channel_id=1, source_target_pairs={{0,4},{1,5},{2,6},{3,7},{4,0},{5,1},{6,2},{7,3},{8,12},{9,13},{10,... | collective-permute-start | bytes 2359304 | tf_op jit(solution)/shard_map/ppermute | solution.py:267
  497.0 37.5 %collective-permute-start.64 = (bf16[256,1536]{1,0:T(8,128)(2,1)}, bf16[256,1536]{1,0:T(8,128)(2,1)S(1)}, u32[]{:S(2)}, u32[]{:S(2)}) collective-permute-start(bf16[256,1536]{1,0:T(8,128)(2,1)} %get-tuple-element.439), channel_id=1, source_target_pairs={{0,6},{1,7},{2,4},{3,5},{4,2},{5,3},{6,0},{7,1},{8,14},{9,15},{10,... | collective-permute-start | bytes 2359304 | tf_op jit(solution)/shard_map/ppermute | solution.py:267
  498.5 35.9 %collective-permute-start.65 = (bf16[128,1536]{1,0:T(8,128)(2,1)}, bf16[128,1536]{1,0:T(8,128)(2,1)S(1)}, u32[]{:S(2)}, u32[]{:S(2)}) collective-permute-start(bf16[128,1536]{1,0:T(8,128)(2,1)} %get-tuple-element.506), channel_id=1, source_target_pairs={{0,24},{1,25},{2,26},{3,27},{4,28},{5,29},{6,30},{7,31},{8,0},{9,1... | collective-permute-start | bytes 1179656 | tf_op jit(solution)/shard_map/ppermute | solution.py:275
  548.9 29.1 %collective-permute-start.70 = (bf16[1536,256]{1,0:T(8,128)(2,1)}, bf16[1536,256]{1,0:T(8,128)(2,1)S(1)}, u32[]{:S(2)}, u32[]{:S(2)}) collective-permute-start(bf16[1536,256]{1,0:T(8,128)(2,1)} %get-tuple-element.462), channel_id=1, source_target_pairs={{0,2},{1,3},{2,0},{3,1},{4,6},{5,7},{6,4},{7,5},{8,10},{9,11},{10,... | collective-permute-start | bytes 2359304 | tf_op jit(solution)/shard_map/ppermute | solution.py:267
  550.7 36.4 %collective-permute-start.71 = (bf16[1536,256]{1,0:T(8,128)(2,1)}, bf16[1536,256]{1,0:T(8,128)(2,1)S(1)}, u32[]{:S(2)}, u32[]{:S(2)}) collective-permute-start(bf16[1536,256]{1,0:T(8,128)(2,1)} %get-tuple-element.463), channel_id=1, source_target_pairs={{0,4},{1,5},{2,6},{3,7},{4,0},{5,1},{6,2},{7,3},{8,12},{9,13},{10,... | collective-permute-start | bytes 2359304 | tf_op jit(solution)/shard_map/ppermute | solution.py:267
  551.0 37.2 %collective-permute-start.72 = (bf16[1536,256]{1,0:T(8,128)(2,1)}, bf16[1536,256]{1,0:T(8,128)(2,1)S(1)}, u32[]{:S(2)}, u32[]{:S(2)}) collective-permute-start(bf16[1536,256]{1,0:T(8,128)(2,1)} %get-tuple-element.464), channel_id=1, source_target_pairs={{0,6},{1,7},{2,4},{3,5},{4,2},{5,3},{6,0},{7,1},{8,14},{9,15},{10,... | collective-permute-start | bytes 2359304 | tf_op jit(solution)/shard_map/ppermute | solution.py:267
  572.4 23.6 %collective-permute-start.73 = (bf16[384,384]{1,0:T(8,128)(2,1)}, bf16[384,384]{1,0:T(8,128)(2,1)}, u32[]{:S(2)}, u32[]{:S(2)}) collective-permute-start(bf16[384,384]{1,0:T(8,128)(2,1)} %get-tuple-element.511), channel_id=1, source_target_pairs={{0,24},{1,25},{2,26},{3,27},{4,28},{5,29},{6,30},{7,31},{8,0},{9,1... | collective-permute-start | bytes 884744 | tf_op jit(solution)/shard_map/ppermute | solution.py:275
  607.2 22.7 %collective-permute-start.83 = (bf16[2,48,384]{2,1,0:T(8,128)(2,1)S(1)}, bf16[2,48,384]{2,1,0:T(8,128)(2,1)S(1)}, u32[]{:S(2)}, u32[]{:S(2)}) collective-permute-start(bf16[2,48,384]{2,1,0:T(8,128)(2,1)S(1)} %get-tuple-element.550), channel_id=1, source_target_pairs={{0,2},{1,3},{2,0},{3,1},{4,6},{5,7},{6,4},{7,5},{8,10},{9,11},{10,... | collective-permute-start | bytes 221192 | tf_op jit(solution)/shard_map/ppermute | solution.py:267
  (111 other events, 1124.7 us)

commit v2 on v1

--- a/solution.py
+++ b/solution.py
@@ -1,3 +1,4 @@
+import functools
 import math
 
 import jax
@@ -54,7 +55,7 @@
     )
 
 
-def attend_kernel(low_ref, starts_ref, query_ref, *refs):
+def attend_kernel(chunks, low_ref, starts_ref, query_ref, *refs):
     count = len(refs) - 4
     member = low_ref[TEAM]
     pieces = refs[:count]
@@ -67,7 +68,7 @@
             keys[block] = piece[0, 0, :, spot].T
             values[block] = piece[1, 0, :, spot]
     own_block = (count - 1) * per_piece
-    for chunk in range(per_piece):
+    for place, chunk in enumerate(chunks):
         queries = chunk_lanes(query_ref, chunk)
         last = own_block + (relative(chunk) ^ member)
         starts, ends = chunk_range(chunk, starts_ref, last)
@@ -101,13 +102,14 @@
         )
         attended = summed / total
         norm = top + jnp.log2(total)
-        spot = pl.ds(chunk * BLOCK, BLOCK)
+        spot = pl.ds(place * BLOCK, BLOCK)
         for head in range(GROUP):
             out_ref[head, :, spot] = attended[:, head * BLOCK : (head + 1) * BLOCK]
             norm_ref[head, :, spot] = norm[:, head * BLOCK : (head + 1) * BLOCK]
 
 
-def gradient_kernel(low_ref, starts_ref, query_ref, grad_ref, out_ref, norm_ref, *refs):
+def gradient_kernel(low_ref, starts_ref, query_ref, grad_ref, *refs):
+    out_refs, norm_refs, refs = refs[:4], refs[4:8], refs[8:]
     count = len(refs) - 8
     member = low_ref[TEAM]
     pieces = refs[:count]
@@ -127,9 +129,11 @@
     for chunk in range(per_piece):
         queries = chunk_lanes(query_ref, chunk)
         grads = chunk_lanes(grad_ref, chunk)
-        norm = chunk_lanes(norm_ref, chunk)
+        norm = chunk_lanes(norm_refs[chunk % 4], chunk // 4)
         delta = jnp.sum(
-            grads.astype(jnp.float32) * chunk_lanes(out_ref, chunk), axis=0, keepdims=True
+            grads.astype(jnp.float32) * chunk_lanes(out_refs[chunk % 4], chunk // 4),
+            axis=0,
+            keepdims=True,
         )
         last = own_block + (relative(chunk) ^ member)
         starts, ends = chunk_range(chunk, starts_ref, last)
@@ -188,21 +192,23 @@
     return low, whole, heads, norm, [kv] * len(pieces)
 
 
-def attend(low, starts, queries, pieces, first_head, count):
+def attend(low, starts, queries, pieces, chip):
     tokens = queries.shape[-1]
     blocks = len(pieces) * tokens // BLOCK
-    low_spec, whole, heads, norm, kv = attention_specs(tokens, pieces, first_head)
+    chunks = (chip, chip + 4)
+    wide = len(chunks) * BLOCK
+    low_spec, whole, heads, norm, kv = attention_specs(tokens, pieces, 0)
     return pl.pallas_call(
-        attend_kernel,
-        grid=(count,),
+        functools.partial(attend_kernel, chunks),
+        grid=(OWN_KV,),
         in_specs=[low_spec, whole, heads] + kv,
         out_specs=[
-            pl.BlockSpec((GROUP, HEAD_DIM, tokens), lambda head: (head, 0, 0)),
-            pl.BlockSpec((GROUP, 1, tokens), lambda head: (head, 0, 0)),
+            pl.BlockSpec((GROUP, HEAD_DIM, wide), lambda head: (head, 0, 0)),
+            pl.BlockSpec((GROUP, 1, wide), lambda head: (head, 0, 0)),
         ],
         out_shape=[
-            jax.ShapeDtypeStruct((count * GROUP, HEAD_DIM, tokens), jnp.float32),
-            jax.ShapeDtypeStruct((count * GROUP, 1, tokens), jnp.float32),
+            jax.ShapeDtypeStruct((OWN_HEADS, HEAD_DIM, wide), jnp.float32),
+            jax.ShapeDtypeStruct((OWN_HEADS, 1, wide), jnp.float32),
         ],
         scratch_shapes=[
             pltpu.VMEM((blocks, BLOCK, HEAD_DIM), jnp.bfloat16),
@@ -221,7 +227,12 @@
     return pl.pallas_call(
         gradient_kernel,
         grid=(count,),
-        in_specs=[low_spec, whole, heads, heads, heads, norm_spec] + kv,
+        in_specs=[low_spec, whole, heads, heads]
+        + [
+            pl.BlockSpec((GROUP,) + block.shape[1:], lambda head: (head, 0, 0))
+            for block in list(attended) + list(norm)
+        ]
+        + kv,
         out_specs=[
             pl.BlockSpec((GROUP, HEAD_DIM, tokens), lambda head: (head, 0, 0)),
             pl.BlockSpec((2, 1, HEAD_DIM, tokens), lambda head: (0, head, 0, 0)),
@@ -241,7 +252,7 @@
         ],
         compiler_params=pltpu.CompilerParams(vmem_limit_bytes=kernel_vmem),
         cost_estimate=small_cost,
-    )(low, starts, queries, grads, attended, norm, *pieces)
+    )(low, starts, queries, grads, *attended, *norm, *pieces)
 
 class Order:
     def __init__(self, token):
@@ -520,43 +531,62 @@
 
 
 def project_out(attended, out_rows):
-    tokens = attended.shape[-1]
-    own = tokens // TEAM
+    own = attended.shape[-1] // 2
     width = out_rows.shape[1]
-    specs, shapes = kept_given(width, own, 1)
 
     def kernel(attended_ref, rows_ref, keep_ref, give_ref, turned):
-        position = pl.program_id(0)
-
-        @pl.when(position == 0)
+        @pl.when(pl.program_id(0) == 0)
         def prepare():
             turned[...] = rows_ref[...].T
 
         block = attended_ref[...].reshape(Q_WIDTH, own).astype(jnp.bfloat16)
-        keep_or_give(position, keep_ref, give_ref, dot(turned[...], block))
+        first_or_second(keep_ref, give_ref, dot(turned[...], block))
 
     return call(
         kernel,
-        (TEAM,),
+        (2,),
         [pl.BlockSpec((OWN_HEADS, HEAD_DIM, own), lambda p: (0, 0, p)), fixed(out_rows)],
-        specs,
-        shapes,
+        [pl.BlockSpec((width, own), lambda p: (0, 0))] * 2,
+        two_blocks(width, own),
         [pltpu.VMEM((width, Q_WIDTH), jnp.bfloat16)],
     )(attended, out_rows)
 
 
-def mixer_forward(normed, cotangent, weights, down):
-    own, width = cotangent[0].shape[1:]
+def two_blocks(width, own):
+    return [
+        jax.ShapeDtypeStruct((width, own), jnp.float32),
+        jax.ShapeDtypeStruct((width, own), jnp.bfloat16),
+    ]
+
+
+def first_or_second(keep_ref, give_ref, value):
+    @pl.when(pl.program_id(0) == 0)
+    def keep():
+        keep_ref[...] = value
+
+    @pl.when(pl.program_id(0) == 1)
+    def give():
+        give_ref[...] = value.astype(jnp.bfloat16)
+
+
+def mixer(chip, normed, cotangent, weights, down):
+    width, own = normed[0].shape
     units = down.shape[0]
-    tokens = TEAM * own
-
-    def kernel(weights_ref, down_ref, *refs):
-        normed_refs, cotangent_refs = refs[:TEAM], refs[TEAM : TEAM + 2]
-        hidden_ref, grad_ref, chosen, turned, wanted = refs[TEAM + 2 :]
-        position = pl.program_id(0)
-        pick(position, normed_refs, chosen)
-        pick(position, cotangent_refs, wanted)
-        turned[...] = chosen[...].T
+
+    def kernel(first_ref, second_ref, wanted_a, wanted_b, weights_ref, down_ref, *refs):
+        hidden_ref, grad_ref, keep_ref, give_ref, turned, wanted = refs
+        step = pl.program_id(0)
+
+        @pl.when(step == 0)
+        def first():
+            turned[...] = first_ref[...].T
+            wanted[...] = wanted_a[0]
+
+        @pl.when(step == 1)
+        def second():
+            turned[...] = second_ref[...].T
+            wanted[...] = wanted_b[0]
+
         gate = dot(turned[...], weights_ref[:, :units])
         up = dot(turned[...], weights_ref[:, units:])
         logistic = 1.0 / (1.0 + jnp.exp(-gate))
@@ -567,50 +597,71 @@
             grad_hidden * up * (logistic * (1.0 + gate * (1.0 - logistic)))
         ).astype(jnp.bfloat16)
         grad_ref[:, units:] = (grad_hidden * silu).astype(jnp.bfloat16)
-
+        term = dot_rows(weights_ref[...], grad_ref[...])
+
+        @pl.when(step == 0)
+        def keep():
+            keep_ref[...] = term
+
+        @pl.when(step == 1)
+        def give():
+            give_ref[...] = term.astype(jnp.bfloat16)
+
+    block = pl.BlockSpec((1, own, width), lambda p: (chip, 0, 0))
+    whole = pl.BlockSpec((width, own), lambda p: (0, 0))
     return call(
         kernel,
+        (2,),
+        [fixed(normed[0]), fixed(normed[1]), block, block, fixed(weights), fixed(down)],
+        [rows_at(own, units), rows_at(own, 2 * units), whole, whole],
+        [
+            jax.ShapeDtypeStruct((2 * own, units), jnp.bfloat16),
+            jax.ShapeDtypeStruct((2 * own, 2 * units), jnp.bfloat16),
+            jax.ShapeDtypeStruct((width, own), jnp.float32),
+            jax.ShapeDtypeStruct((width, own), jnp.bfloat16),
+        ],
+        [pltpu.VMEM((own, width), jnp.bfloat16), pltpu.VMEM((own, width), jnp.bfloat16)],
+    )(normed[0], normed[1], cotangent[0], cotangent[1], weights, down)
+
+
+def add_block(keep, arrived):
+    def kernel(keep_ref, arrived_ref, out_ref):
+        out_ref[...] = (keep_ref[...] + arrived_ref[...].astype(jnp.float32)).astype(jnp.bfloat16)
+
+    rows = keep.shape[0] // 2
+    part = rows_at(rows, keep.shape[1])
+    return call(
+        kernel, (2,), [part, part], part, jax.ShapeDtypeStruct(keep.shape, jnp.bfloat16)
+    )(keep, arrived)
+
+
+def pair_rows(position, refs, target):
+    own = target.shape[0]
+    for number in range(TEAM):
+
+        @pl.when(position == number)
+        def move():
+            start = number // 4 * own
+            target[...] = refs[number % 4][start : start + own]
+
+
+def mixer_output(hidden, down):
+    own, units = hidden[0].shape[0] // 2, hidden[0].shape[1]
+    specs, shapes = kept_given(own, down.shape[1], 0)
+
+    def kernel(down_ref, *refs):
+        keep_ref, give_ref, chosen = refs[4:]
+        pair_rows(pl.program_id(0), refs[:4], chosen)
+        keep_or_give(pl.program_id(0), keep_ref, give_ref, dot(chosen[...], down_ref[...]))
+
+    return call(
+        kernel,
         (TEAM,),
-        [fixed(weights), fixed(down)]
-        + [fixed(block) for block in normed]
-        + [fixed(block) for block in cotangent],
-        [rows_at(own, units), rows_at(own, 2 * units)],
-        [
-            jax.ShapeDtypeStruct((tokens, units), jnp.bfloat16),
-            jax.ShapeDtypeStruct((tokens, 2 * units), jnp.bfloat16),
-        ],
-        [
-            pltpu.VMEM((width, own), jnp.bfloat16),
-            pltpu.VMEM((own, width), jnp.bfloat16),
-            pltpu.VMEM((own, width), jnp.bfloat16),
-        ],
-    )(weights, down, *normed, *cotangent)
-
-
-def mixer_backward(grads, weights):
-    tokens, columns = grads.shape
-    own = tokens // TEAM
-    specs, shapes = kept_given(weights.shape[0], own, 1)
-
-    def kernel(grads_ref, weights_ref, keep_ref, give_ref):
-        keep_or_give(
-            pl.program_id(0), keep_ref, give_ref, dot_rows(weights_ref[...], grads_ref[...])
-        )
-
-    return call(
-        kernel, (TEAM,), [rows_at(own, columns), fixed(weights)], specs, shapes
-    )(grads, weights)
-
-
-def mixer_output(hidden, down):
-    tokens, units = hidden.shape
-    own = tokens // TEAM
-    specs, shapes = kept_given(own, down.shape[1], 0)
-
-    def kernel(hidden_ref, down_ref, keep_ref, give_ref):
-        keep_or_give(pl.program_id(0), keep_ref, give_ref, dot(hidden_ref[...], down_ref[...]))
-
-    return call(kernel, (TEAM,), [rows_at(own, units), fixed(down)], specs, shapes)(hidden, down)
+        [fixed(down)] + [fixed(block) for block in hidden],
+        specs,
+        shapes,
+        [pltpu.VMEM((own, units), jnp.bfloat16)],
+    )(down, *hidden)
 
 
 def write_teams(places_ref, total, out_ref, teams):
@@ -621,14 +672,16 @@
         out_ref[pl.ds(steps, 1)] = block[None]
 
 
-def token_product(grid, lefts, right, by_rows, width):
-    own = right.shape[0] // TEAM
-    rows = lefts[0].shape[0] if by_rows else lefts.shape[1]
+def token_product(grid, lefts, rights):
+    rows, own = lefts[0].shape
+    width = rights[0].shape[1]
     teams = grid.teams
 
-    def kernel(places_ref, right_ref, *refs):
-        sources, (out_ref, total) = refs[:-2], refs[-2:]
+    def kernel(places_ref, *refs):
+        left_refs, right_refs = refs[:TEAM], refs[TEAM : TEAM + 4]
+        out_ref, total, chosen = refs[TEAM + 4 :]
         position = pl.program_id(0)
+        pair_rows(position, right_refs, chosen)
 
         def add(value):
             @pl.when(position == 0)
@@ -639,11 +692,11 @@
             def later():
                 total[...] += value
 
-        for number, source in enumerate(sources):
+        for number, source in enumerate(left_refs):
 
             @pl.when(position == number)
             def block():
-                add(dot(source[...], right_ref[...]))
+                add(dot(source[...], chosen[...]))
 
         @pl.when(position == TEAM - 1)
         def last():
@@ -652,24 +705,25 @@
     return call(
         kernel,
         (TEAM,),
-        [rows_at(own, width)] + [fixed(left) for left in lefts],
+        [fixed(block) for block in list(lefts) + list(rights)],
         pl.BlockSpec((teams, rows // teams, width), lambda p, *unused: (0, 0, 0)),
         jax.ShapeDtypeStruct((teams, rows // teams, width), jnp.bfloat16),
-        [pltpu.VMEM((rows, width), jnp.float32)],
+        [pltpu.VMEM((rows, width), jnp.float32), pltpu.VMEM((own, width), jnp.bfloat16)],
         prefetch=1,
-    )(grid.places(), right, *lefts)
+    )(grid.places(), *lefts, *rights)
 
 
 def down_product(grid, hidden, cotangent):
-    tokens, units = hidden.shape
+    units = hidden[0].shape[1]
     own, width = cotangent[0].shape[1:]
     teams = grid.teams
 
-    def kernel(places_ref, hidden_ref, *refs):
-        sources, (out_ref, total, wanted) = refs[:2], refs[2:]
+    def kernel(places_ref, *refs):
+        hidden_refs, sources, (out_ref, total, wanted, chosen) = refs[:4], refs[4:6], refs[6:]
         position = pl.program_id(0)
         pick(position, sources, wanted)
-        value = dot(hidden_ref[...].T, wanted[...])
+        pair_rows(position, hidden_refs, chosen)
+        value = dot(chosen[...].T, wanted[...])
 
         @pl.when(position == 0)
         def first():
@@ -686,31 +740,44 @@
     return call(
         kernel,
         (TEAM,),
-        [rows_at(own, units)] + [fixed(block) for block in cotangent],
+        [fixed(block) for block in list(hidden) + list(cotangent)],
         pl.BlockSpec((teams, units // teams, width), lambda p, *unused: (0, 0, 0)),
         jax.ShapeDtypeStruct((teams, units // teams, width), jnp.bfloat16),
-        [pltpu.VMEM((units, width), jnp.float32), pltpu.VMEM((own, width), jnp.bfloat16)],
+        [
+            pltpu.VMEM((units, width), jnp.float32),
+            pltpu.VMEM((own, width), jnp.bfloat16),
+            pltpu.VMEM((own, units), jnp.bfloat16),
+        ],
         prefetch=1,
-    )(grid.places(), hidden, *cotangent)
+    )(grid.places(), *hidden, *cotangent)
 
 
 def project_out_back(grid, grads, out_rows, attended):
     teams = grid.teams
-    tokens = attended.shape[-1]
-    own = tokens // TEAM
+    own = attended[0].shape[-1] // 2
+    tokens = TEAM * own
     width = out_rows.shape[1]
 
-    def kernel(places_ref, rows_ref, attended_ref, *refs):
-        sources, (grad_ref, out_ref, chosen, total) = refs[:TEAM], refs[TEAM:]
+    def kernel(places_ref, rows_ref, *refs):
+        attended_refs, sources = refs[:4], refs[4 : 4 + TEAM]
+        grad_ref, out_ref, chosen, total, wanted = refs[4 + TEAM :]
         position = pl.program_id(0)
         pick(position, sources, chosen)
+        for number in range(TEAM):
+
+            @pl.when(position == number)
+            def move():
+                start = number // 4 * own
+                wanted[...] = attended_refs[number % 4][:, :, start : start + own].astype(
+                    jnp.bfloat16
+                )
+
         grad_ref[...] = (
             dot(rows_ref[...], chosen[...])
             .astype(jnp.bfloat16)
             .reshape(OWN_HEADS, HEAD_DIM, own)
         )
-        block = attended_ref[...].reshape(Q_WIDTH, own).astype(jnp.bfloat16)
-        value = dot_rows(block, chosen[...])
+        value = dot_rows(wanted[...].reshape(Q_WIDTH, own), chosen[...])
 
         @pl.when(position == 0)
         def first():
@@ -729,28 +796,29 @@
     return call(
         kernel,
         (TEAM,),
-        [fixed(out_rows), heads] + [fixed(block) for block in grads],
+        [fixed(out_rows)] + [fixed(block) for block in list(attended) + list(grads)],
         [heads, pl.BlockSpec(shape, lambda p, *unused: (0, 0, 0))],
         [
             jax.ShapeDtypeStruct((OWN_HEADS, HEAD_DIM, tokens), jnp.bfloat16),
             jax.ShapeDtypeStruct(shape, jnp.bfloat16),
         ],
-        [pltpu.VMEM((width, own), jnp.bfloat16), pltpu.VMEM((Q_WIDTH, width), jnp.float32)],
+        [
+            pltpu.VMEM((width, own), jnp.bfloat16),
+            pltpu.VMEM((Q_WIDTH, width), jnp.float32),
+            pltpu.VMEM((OWN_HEADS, HEAD_DIM, own), jnp.bfloat16),
+        ],
         prefetch=1,
-    )(grid.places(), out_rows, attended, *grads)
-
-
-def project_back(grid, normed, query_rot, own_grads, returned, cosine, sine_table, weights):
-    width, tokens = normed.shape
-    own = tokens // TEAM
+    )(grid.places(), out_rows, *attended, *grads)
+
+
+def project_back(chip, query_rot, own_grads, returned, cosine, sine_table, weights):
+    width = weights.shape[0]
+    own = query_rot.shape[-1] // TEAM
     half = HEAD_DIM // 2
-    teams = grid.teams
-    specs, shapes = kept_given(width, own, 1)
-
-    def kernel(places_ref, normed_ref, query_ref, cosine_ref, sine_ref, weights_ref, *refs):
+
+    def kernel(query_ref, cosine_ref, sine_ref, weights_ref, *refs):
         kv_refs = refs[: 1 + len(returned)]
-        keep_ref, give_ref, out_ref, total, grad_ref = refs[1 + len(returned) :]
-        position = pl.program_id(0)
+        keep_ref, give_ref, grad_ref = refs[1 + len(returned) :]
         cosines, sines = cosine_ref[...], sine_ref[...]
 
         def unrotated(block):
@@ -768,9 +836,44 @@
             grad_ref[start : start + HEAD_DIM] = unrotated(kv[0, head])
             start = start + KV_WIDTH
             grad_ref[start : start + HEAD_DIM] = kv[1, head].astype(jnp.bfloat16)
-        grad = grad_ref[...]
-        keep_or_give(position, keep_ref, give_ref, dot(weights_ref[:, :LINED], grad))
-        value = dot_rows(normed_ref[...], grad)
+        first_or_second(keep_ref, give_ref, dot(weights_ref[:, :LINED], grad_ref[...]))
+
+    def at(p):
+        return chip + 4 * p
+
+    tables = pl.BlockSpec((HEAD_DIM, own), lambda p: (0, at(p)))
+    kv_heads = pl.BlockSpec((2, OWN_KV, HEAD_DIM, own), lambda p: (0, 0, 0, at(p)))
+    return call(
+        kernel,
+        (2,),
+        [
+            pl.BlockSpec((OWN_HEADS, HEAD_DIM, own), lambda p: (0, 0, at(p))),
+            tables,
+            tables,
+            fixed(weights),
+        ]
+        + [kv_heads] * (1 + len(returned)),
+        [pl.BlockSpec((width, own), lambda p: (0, 0))] * 2 + [lanes_at(LINED, own)],
+        two_blocks(width, own) + [jax.ShapeDtypeStruct((LINED, 2 * own), jnp.bfloat16)],
+    )(query_rot, cosine, sine_table, weights, own_grads, *returned)
+
+
+def lined_product(grid, normed, grads):
+    width, tokens = normed.shape
+    own = tokens // TEAM
+    teams = grid.teams
+
+    def kernel(places_ref, normed_ref, *refs):
+        grad_refs, (out_ref, total, chosen) = refs[:4], refs[4:]
+        position = pl.program_id(0)
+        for number in range(TEAM):
+
+            @pl.when(position == number)
+            def move():
+                start = number // 4 * own
+                chosen[...] = grad_refs[number % 4][:, start : start + own]
+
+        value = dot_rows(normed_ref[...], chosen[...])
 
         @pl.when(position == 0)
         def first():
@@ -784,24 +887,15 @@
         def last():
             write_teams(places_ref, total, out_ref, teams)
 
-    heads = pl.BlockSpec((OWN_HEADS, HEAD_DIM, own), lambda p, *unused: (0, 0, p))
-    kv_heads = pl.BlockSpec((2, OWN_KV, HEAD_DIM, own), lambda p, *unused: (0, 0, 0, p))
     return call(
         kernel,
         (TEAM,),
-        [
-            lanes_at(width, own),
-            heads,
-            lanes_at(HEAD_DIM, own),
-            lanes_at(HEAD_DIM, own),
-            fixed(weights),
-        ]
-        + [kv_heads] * (1 + len(returned)),
-        specs + [pl.BlockSpec((teams, width // teams, LINED), lambda p, *unused: (0, 0, 0))],
-        shapes + [jax.ShapeDtypeStruct((teams, width // teams, LINED), jnp.bfloat16)],
+        [lanes_at(width, own)] + [fixed(block) for block in grads],
+        pl.BlockSpec((teams, width // teams, LINED), lambda p, *unused: (0, 0, 0)),
+        jax.ShapeDtypeStruct((teams, width // teams, LINED), jnp.bfloat16),
         [pltpu.VMEM((width, LINED), jnp.float32), pltpu.VMEM((LINED, own), jnp.bfloat16)],
         prefetch=1,
-    )(grid.places(), normed, query_rot, cosine, sine_table, weights, own_grads, *returned)
+    )(grid.places(), normed, *grads)
 
 
 def combine(keep, arrived, axis):
@@ -1047,118 +1141,157 @@
     attn_w = place_rows(grid, attn_z, 0, attn_wide).reshape(width, attn_wide)
     attn_w, inputs_team, out_own = order.step(attn_w, inputs_team, out_own)
 
+    mixer_own = jnp.concatenate([team_rows[..., attn_wide:], down_thirds], axis=-1)
+
+    out_own, mixer_own = order.step(out_own, mixer_own)
     out_z = grid.spread(out_own)
+    mixer_hops = [grid.both_ways(mixer_own, mixer_own)]
+
+    def next_hop():
+        if len(mixer_hops) < teams - 1:
+            mixer_hops.append(grid.both_ways(*mixer_hops[-1]))
+
     normed_first, queries, own_piece = project(inputs_team, attn_w, cosine, sine_table)
-    own_piece, out_z, cotangent, attn_w = order.step(own_piece, out_z, cotangent, attn_w)
+    own_piece, out_z, mixer_hops[-1], attn_w, cotangent = order.step(
+        own_piece, out_z, mixer_hops[-1], attn_w, cotangent
+    )
     arrived = [grid.shift(own_piece, step, False) for step in range(1, steps_back + 1)]
-    cotangent_chips = grid.chips(cotangent)
+    cotangent_chips = [cotangent, grid.turn(cotangent, 2), grid.turn(cotangent, 4)]
     out_rows = place_rows(grid, [block[None] for block in out_z], 0, width)
     out_rows = out_rows.reshape(Q_WIDTH, width)
     gain_first = attn_w[:, LINED : LINED + 1].astype(f32)
     gain_second = attn_w[:, LINED + 1 : LINED + 2].astype(f32)
-    mixer_own = jnp.concatenate([team_rows[..., attn_wide:], down_thirds], axis=-1)
-    arrived, out_rows, gain_first, gain_second, mixer_own = order.step(
-        arrived, out_rows, gain_first, gain_second, mixer_own
-    )
-
-    mixer_hops = [grid.both_ways(mixer_own, mixer_own)]
-
-    def next_hop():
-        mixer_hops[-1] = order.step(mixer_hops[-1])
-        if len(mixer_hops) < teams - 1:
-            mixer_hops.append(grid.both_ways(*mixer_hops[-1]))
+    arrived, gain_first, gain_second, out_rows, cotangent_chips, mixer_hops[-1] = order.step(
+        arrived, gain_first, gain_second, out_rows, cotangent_chips, mixer_hops[-1]
+    )
+    cotangent_chips = cotangent_chips + [grid.turn(cotangent_chips[0], 6)]
+    next_hop()
 
     pieces = [own_piece] + arrived
-    attended, normalizer = attend(low, starts, queries, pieces, 0, OWN_KV)
-    keep, give = project_out(attended, out_rows)
-    give, cotangent_chips, mixer_hops[0] = order.step(give, cotangent_chips, mixer_hops[0])
-    other = grid.turn(give, 1)
-    if len(mixer_hops) < teams - 1:
-        mixer_hops.append(grid.both_ways(*mixer_hops[-1]))
-    other = order.step(other)
-    total, blocks = combine(keep, other, 1)
-    blocks = order.step(blocks)
-    terms = grid.send_chips(blocks)
-    cotangent_stack = order.step(jnp.stack(cotangent_chips))
-    terms, mixer_hops[-1] = order.step(terms, mixer_hops[-1])
-    if len(mixer_hops) < teams - 1:
-        mixer_hops.append(grid.both_ways(*mixer_hops[-1]))
+    attended, normalizer = [None] * 4, [None] * 4
+
+    def run_attention(other_chip):
+        attended[other_chip], normalizer[other_chip] = attend(
+            low, starts, order.step(queries), pieces, other_chip
+        )
+        keep, give = project_out(attended[other_chip], out_rows)
+        return keep, order.step(give)
+
+    keep_one, give = run_attention(1)
+    passed_one = grid.turn(give, 1)
+    keep_two, give = run_attention(2)
+    passed_one, cotangent_chips = order.step(passed_one, cotangent_chips)
+    passed_two = grid.turn(give, 1)
+    block_one = order.step(add_block(keep_one, passed_one))
+    keep_three, give = run_attention(3)
+    passed_two, mixer_hops[-1] = order.step(passed_two, mixer_hops[-1])
+    passed_three = grid.turn(give, 1)
+    block_one, block_two = order.step(block_one, add_block(keep_two, passed_two))
+    terms = [grid.turn(block_one, 2), grid.turn(block_two, 4)]
+    keep_own, give = run_attention(0)
+    passed_three, terms[0] = order.step(passed_three, terms[0])
+    block_three = order.step(add_block(keep_three, passed_three))
+    terms.append(grid.turn(block_three, 6))
+    passed_own = grid.turn(give, 1)
+    passed_own, cotangent_stack = order.step(passed_own, jnp.stack(cotangent_chips))
     cotangent_other = grid.turn(cotangent_stack, 1)
+    terms[1], cotangent_other = order.step(terms[1], cotangent_other)
+    cotangent_team = [cotangent_stack, cotangent_other]
+    next_hop()
+    total = keep_own
+    terms = order.step([passed_own] + terms)
     middle, normed_second = finish_middle([total] + terms, inputs_t, gain_second)
-    normed_second, cotangent_other = order.step(normed_second, cotangent_other)
-    cotangent_team = [cotangent_stack, cotangent_other]
-    second_chips = grid.chips(normed_second)
+    normed_second = order.step(normed_second)
+    second_chips = [normed_second, grid.turn(normed_second, 2), grid.turn(normed_second, 4)]
+    second_other = [grid.turn(normed_second, 1)]
+    mixer_hops[-1] = order.step(mixer_hops[-1])
     while len(mixer_hops) < teams - 1:
         next_hop()
-    second_chips, mixer_hops[-1] = order.step(second_chips, mixer_hops[-1])
-    second_team = grid.gather_team(second_chips)
+        mixer_hops[-1] = order.step(mixer_hops[-1])
     mixer_w, down_w = place_mixer(grid, mixer_own, mixer_hops, units, unit_rows)
     mixer_w = mixer_w.reshape(width, 2 * units)
     down_w = down_w.reshape(units, width)
-    mixer_w, down_w, second_team = order.step(mixer_w, down_w, second_team)
-
-    early = max(1, teams // 2)
-
-    def send_teams(product, first, last):
+    mixer_w, down_w, second_other[0] = order.step(mixer_w, down_w, second_other[0])
+
+    def send_teams(product, first=1, last=teams):
         return [grid.shift(product[steps], steps) for steps in range(first, last)]
 
-    hidden, grads = mixer_forward(second_team, cotangent_team, mixer_w, down_w)
-    keep, give = mixer_backward(grads, mixer_w)
-    give, grads = order.step(give, grads)
-    other = order.step(grid.turn(give, 1))
-    total, blocks = combine(keep, other, 1)
-    blocks, hidden, grads = order.step(blocks, hidden, grads)
-    terms = grid.send_chips(blocks)
-    mixer_part = token_product(grid, second_team, grads, True, 2 * units)
-    mixer_part, hidden = order.step(mixer_part, hidden)
-    mixer_parts = send_teams(mixer_part, 1, early + 1)
-    down_part = down_product(grid, hidden, cotangent_team)
-    terms, down_part = order.step(terms, down_part)
-    grad_middle, grad_attn, second_part = finish_second(
-        [total] + terms, middle, cotangent, gain_second
-    )
+    def run_mixer(other_chip):
+        hidden_part, grads_part, keep, give = mixer(
+            other_chip,
+            (second_chips[other_chip], second_other[other_chip]),
+            cotangent_team,
+            mixer_w,
+            down_w,
+        )
+        return hidden_part, grads_part, keep, order.step(give)
+
+    parts = [run_mixer(0)]
+    passed = [grid.turn(parts[0][3], 1)]
+    second_chips = order.step(second_chips)
+    second_chips = second_chips + [grid.turn(second_chips[0], 6)]
+    second_other += order.step([grid.turn(second_chips[1], 1), grid.turn(second_chips[2], 1)])
+    parts.append(run_mixer(1))
+    passed.append(grid.turn(parts[1][3], 1))
+    second_chips[3], passed[0] = order.step(second_chips[3], passed[0])
+    second_other.append(grid.turn(second_chips[3], 1))
+    parts.append(run_mixer(2))
+    passed[1], second_other[3] = order.step(passed[1], second_other[3])
+    block = order.step(add_block(parts[1][2], passed[1]))
+    terms = [parts[0][2], passed[0], grid.turn(block, 2)]
+    second_other[3] = order.step(second_other[3])
+    passed.append(grid.turn(parts[2][3], 1))
+    parts.append(run_mixer(3))
+    passed[2] = order.step(passed[2])
+    passed.append(grid.turn(parts[3][3], 1))
+    block = order.step(add_block(parts[2][2], passed[2]))
+    terms.append(grid.turn(block, 4))
+    passed[3] = order.step(passed[3])
+    hidden, grads = [part[0] for part in parts], [part[1] for part in parts]
+    block, grads, hidden = order.step(add_block(parts[3][2], passed[3]), grads, hidden)
+    terms.append(grid.turn(block, 6))
+    second_team = second_chips + second_other
+    down_part = order.step(down_product(grid, hidden, cotangent_team))
+    down_parts = send_teams(down_part, 1, 3)
+    second_team, grads = order.step(second_team, grads)
+    mixer_part = token_product(grid, second_team, grads)
+    mixer_part, terms, down_parts = order.step(mixer_part, terms, down_parts)
+    mixer_parts = send_teams(mixer_part, 1, 2)
+    down_parts += send_teams(down_part, 3)
+    grad_middle, grad_attn, second_part = finish_second(terms, middle, cotangent, gain_second)
     grad_attn, hidden = order.step(grad_attn, hidden)
-    attn_chips = grid.chips(grad_attn)
+    attn_chips = [grad_attn, grid.turn(grad_attn, 2), grid.turn(grad_attn, 4)]
+    attn_chips, hidden, mixer_parts, down_parts = order.step(
+        attn_chips, hidden, mixer_parts, down_parts
+    )
+    attn_chips = attn_chips + [grid.turn(attn_chips[0], 6)]
+    mixer_parts += send_teams(mixer_part, 3)
+    attn_other = [grid.turn(attn_chips[0], 1)]
     out_keep, out_give = mixer_output(hidden, down_w)
-    attn_chips, out_give, mixer_parts = order.step(attn_chips, out_give, mixer_parts)
-    late_parts = send_teams(mixer_part, early + 1, teams)
-    attn_team = order.step(grid.gather_team(attn_chips))
+    out_give, attn_other = order.step(out_give, attn_other)
+    attn_other += order.step([grid.turn(attn_chips[1], 1), grid.turn(attn_chips[2], 1)])
+    attn_chips[3], mixer_parts = order.step(attn_chips[3], mixer_parts)
+    mixer_late = send_teams(mixer_part, 2, 3)
+    attn_other.append(order.step(grid.turn(attn_chips[3], 1)))
+    attn_team = attn_chips + attn_other
 
     grad_attended, out_part = project_out_back(grid, attn_team, out_rows, attended)
-    grad_attended, down_part, out_give = order.step(grad_attended, down_part, out_give)
-    down_parts = send_teams(down_part, 1, early + 1)
+    grad_attended, out_give = order.step(grad_attended, out_give)
     out_other = grid.turn(out_give, 1)
     query_rot, own_grads, back_grads = attend_back(
         low, starts, queries, grad_attended, attended, normalizer, pieces, 0, OWN_KV
     )
-    query_rot, own_grads, back_grads, late_parts, out_other = order.step(
-        query_rot, own_grads, back_grads, late_parts, out_other
-    )
+    query_rot, own_grads, back_grads, out_other, mixer_late = order.step(
+        query_rot, own_grads, back_grads, out_other, mixer_late
+    )
+    mixer_parts = mixer_parts + mixer_late
     returned = [
         grid.shift(back_grads[step - 1], -step, False) for step in range(1, steps_back + 1)
     ]
     out_total, out_blocks = combine(out_keep, out_other, 0)
     out_blocks = order.step(out_blocks)
-    out_terms = grid.send_chips(out_blocks)
-    mixer_total = sum_teams(mixer_part, mixer_parts + late_parts, bf16)
-    returned, down_parts, mixer_total = order.step(returned, down_parts, mixer_total)
-    down_late = send_teams(down_part, early + 1, teams)
-    keep, give, attn_part = project_back(
-        grid, normed_first, query_rot, own_grads, returned, cosine, sine_table, attn_w
-    )
-    attn_part, give, out_terms, down_late = order.step(attn_part, give, out_terms, down_late)
-    other = grid.turn(give, 1)
-    attn_parts = send_teams(attn_part, 1, early + 1)
-    other = order.step(other)
-    total, blocks = combine(keep, other, 1)
-    blocks, out_part = order.step(blocks, out_part)
-    terms = grid.send_chips(blocks)
-    outputs = finish_output([out_total] + out_terms, middle)
-    down_grad = sum_teams(down_part, down_parts + down_late, f32)
-    attn_parts, outputs, down_grad = order.step(attn_parts, outputs, down_grad)
-    attn_late = send_teams(attn_part, early + 1, teams)
-    out_parts = send_teams(out_part, 1, teams)
-
+    out_terms = [grid.turn(out_blocks[0], 2), grid.turn(out_blocks[1], 4)]
+    mixer_total = sum_teams(mixer_part, mixer_parts, bf16)
     def members_rows(total):
         blocks = total.reshape(TEAM // 2, 2, rows, -1)
         return dynamic(blocks, core, 1), grid.turn(dynamic(blocks, 1 - core, 1), 1)
@@ -1180,23 +1313,59 @@
             (TEAM,) + found[0].shape[1:]
         )
 
+    returned, mixer_total = order.step(returned, mixer_total)
     mixer_mine, mixer_others = members_rows(mixer_total)
-    mixer_mine, mixer_others, terms = order.step(mixer_mine, mixer_others, terms)
+    lined_grads = [None] * 4
+
+    def run_back(other_chip):
+        keep, give, lined_grads[other_chip] = project_back(
+            other_chip, order.step(query_rot), own_grads, returned, cosine, sine_table, attn_w
+        )
+        return keep, order.step(give)
+
+    keep_one, give = run_back(1)
+    passed_one = grid.turn(give, 1)
+    keep_two, give = run_back(2)
+    passed_one, out_terms = order.step(passed_one, out_terms)
+    passed_two = grid.turn(give, 1)
+    block_one = order.step(add_block(keep_one, passed_one))
+    keep_three, give = run_back(3)
+    passed_two, mixer_others = order.step(passed_two, mixer_others)
+    passed_three = grid.turn(give, 1)
+    block_one, block_two = order.step(block_one, add_block(keep_two, passed_two))
+    terms = [grid.turn(block_one, 2), grid.turn(block_two, 4)]
+    keep_own, give = run_back(0)
+    passed_three = order.step(passed_three)
+    block_three = order.step(add_block(keep_three, passed_three))
+    terms.append(grid.turn(block_three, 6))
+    passed_own = grid.turn(give, 1)
+    attn_part = lined_product(grid, normed_first, lined_grads)
+    attn_part, passed_own, terms[:2] = order.step(attn_part, passed_own, terms[:2])
+    attn_parts = send_teams(attn_part)
+    out_terms = out_terms + [grid.turn(out_blocks[2], 6)]
+    total = keep_own
+    terms = order.step([passed_own] + terms)
+    down_grad = sum_teams(down_part, down_parts, f32)
+    attn_parts, down_grad, out_part = order.step(attn_parts, down_grad, out_part)
+    attn_total = sum_teams(attn_part, attn_parts, bf16)
+    attn_mine, attn_others = members_rows(attn_total)
+    out_parts = send_teams(out_part)
+    outputs = finish_output([out_total] + out_terms, middle)
+    attn_others, outputs = order.step(attn_others, outputs)
     mixer_found = owner_columns(mixer_mine, mixer_others)
     input_grad, first_part = finish_first([total] + terms, inputs_t, grad_middle, gain_first)
     gain_parts = jnp.concatenate([first_part, second_part], axis=1).T
-    attn_late, gain_parts, out_parts = order.step(attn_late, gain_parts, out_parts)
-    attn_total = sum_teams(attn_part, attn_parts + attn_late, bf16)
+    gain_parts, out_parts = order.step(gain_parts, out_parts)
+    gain_other = grid.turn(gain_parts, 1)
     out_own = sum_teams(out_part, out_parts, bf16)
-    attn_mine, attn_others = members_rows(attn_total)
-    gain_parts = gain_parts + grid.turn(gain_parts, 1)
-    attn_mine, attn_others, gain_parts, out_own = order.step(
-        attn_mine, attn_others, gain_parts, out_own
-    )
+    mixer_found, gain_other, out_own = order.step(mixer_found, gain_other, out_own)
+    gain_parts = gain_parts + gain_other
+    gain_chips = [grid.turn(gain_parts, 2 * other) for other in range(1, 4)]
+    gain_chips = order.step(gain_chips)
     attn_found = owner_columns(attn_mine, attn_others)
-    out_grad = grid.to_owners(out_own).astype(f32)
-    gain_parts = gain_parts + grid.turn(gain_parts, 2)
-    mixer_found, gain_parts = order.step(mixer_found, gain_parts)
+    out_grad = grid.to_owners(out_own)
+    for other in gain_chips:
+        gain_parts = gain_parts + other
     mixer_columns = in_order(mixer_found)
 
     def whole_units(blocks):
@@ -1208,13 +1377,13 @@
 
     gate_grad = whole_units(mixer_columns[..., :units])
     up_grad = whole_units(mixer_columns[..., units:])
-    gain_parts = gain_parts + grid.turn(gain_parts, 4)
+    attn_found, out_grad, gain_parts = order.step(attn_found, out_grad, gain_parts)
     gain_blocks = gain_parts.reshape(2, teams, TEAM, rows)
     gain_sums = dynamic(dynamic(gain_blocks, grid.team, 1), member, 1)
     for steps in range(1, teams):
         block = dynamic(dynamic(gain_blocks, (grid.team + steps) % teams, 1), member, 1)
         gain_sums = gain_sums + grid.shift(block, steps)
-    attn_found, gain_sums = order.step(attn_found, gain_sums)
+    out_grad = out_grad.astype(f32)
     attn_columns = in_order(attn_found)
     gain_sums = gain_sums + order.token[0, 0].astype(f32)
     return (

time: 651 us -> 737 us (1.13)
  Pallas kernels: 258 us -> 292 us
  waiting for transfers between devices: 219 us -> 252 us
  starting transfers between devices: 111 us -> 135 us
    pallas_call x9 -> x30, Pallas kernels: 145 us -> 206 us  [the longest x4 56.1 us: mixer(): call(kernel, (2,), [fixed(normed[0]), fixed(normed[1]), block, block, fix...]
    ppermute x60 -> x70, waiting for transfers between devices: 97.6 us -> 122 us  [turn(): lax.ppermute(value, 'dev', [(d, d ^ bits) for d in range(self.count)])]
    ppermute x60 -> x70, starting transfers between devices: 45.9 us -> 66.7 us  [turn(): lax.ppermute(value, 'dev', [(d, d ^ bits) for d in range(self.count)])]
    pallas_call x4 -> x1, Pallas kernels: 27.1 us -> 6.83 us  [combine(): call(kernel, (4,), [part, part], [whole] * 4, [jax.ShapeDtypeStruct(shape...]
    pallas_call x1, Pallas kernels: 30.7 us -> 22.3 us  [attend_back(): pl.pallas_call(gradient_kernel, grid=(count,), in_specs=[low_spec, whole,...]
  transfers between devices with their start and end apart: 91 -> 101, of which waited for: 33 -> 35; matrix products, arithmetic and copies ran while one was open for 5% -> 5% of each run, Pallas kernels for 30% -> 38%
where the time goes in v2:
time: 737 us; the launch traced here: 730 us
  Pallas kernels  292 us (40%)
  waiting for transfers between devices  252 us (34%)
  starting transfers between devices  135 us (18%)
  local copies, waits for them, and re-layouts  36.6 us (5%)
  other arithmetic  11.7 us (2%)
    ppermute x70, waiting for transfers between devices, turn(): lax.ppermute(value, 'dev', [(d, d ^ bits) for d in range(self.count)])  122 us
    ppermute x29, waiting for transfers between devices, shift(): return lax.ppermute(value, 'dev', pairs)  120 us
    ppermute x70, starting transfers between devices, turn(): lax.ppermute(value, 'dev', [(d, d ^ bits) for d in range(self.count)])  66.7 us
    ppermute x29, starting transfers between devices, shift(): return lax.ppermute(value, 'dev', pairs)  64 us
    pallas_call x4, Pallas kernels, mixer(): call(kernel, (2,), [fixed(normed[0]), fixed(normed[1]), block, block, fix...  56.1 us
    pallas_call x4, Pallas kernels, attend(): pl.pallas_call(functools.partial(attend_kernel, chunks), grid=(OWN_KV,),...  25.5 us
    pallas_call x9, Pallas kernels, add_block(): call(kernel, (2,), [part, part], part, jax.ShapeDtypeStruct(keep.shape, j...  22.9 us
    pallas_call x1, Pallas kernels, attend_back(): pl.pallas_call(gradient_kernel, grid=(count,), in_specs=[low_spec, whole,...  22.3 us
  transfers between devices with their start and end apart: 101, of which 35 were waited for; matrix products, arithmetic and copies ran while one was open for 5% of the time, Pallas kernels for 38%

profile of v2, /device:TPU:10, one launch (start us, length us, event | category | flops | bytes accessed | tf_op | source)
XLA Modules:
  0.0 730.0 jit_solution(7218493067760231922)
XLA Ops:
  25.7 11.7 %collective-permute-done.4 = bf16[2,48,1536]{2,1,0:T(8,128)(2,1)S(1)} collective-permute-done((bf16[2,48,1536]{2,1,0:T(8,128)(2,1)}, bf16[2,48,1536]{2,1,0:T(8,128)(2,1)S(1)}, u32[]{:S(2)}, u32[]{:S(2)}) %collective-permute-start.4) | collective-permute-done | bytes 294944 | tf_op jit(solution)/shard_map/ppermute | solution.py:278
  49.8 14.1 %collective-permute-done.13.refs_3_ = bf16[1536,256]{1,0:T(8,128)(2,1)} collective-permute-done((bf16[1536,256]{1,0:T(8,128)(2,1)S(1)}, bf16[1536,256]{1,0:T(8,128)(2,1)}, u32[]{:S(2)}, u32[]{:S(2)}) %collective-permute-start.13) | collective-permute-done | bytes 786464 | tf_op jit(solution)/shard_map/ppermute | solution.py:278
  63.9 9.1 %collective-permute-done.10.refs_1_ = bf16[8,48,512]{2,1,0:T(8,128)(2,1)S(1)} collective-permute-done((bf16[8,48,512]{2,1,0:T(8,128)(2,1)S(1)}, bf16[8,48,512]{2,1,0:T(8,128)(2,1)S(1)}, u32[]{:S(2)}, u32[]{:S(2)}) %collective-permute-start.10) | collective-permute-done | bytes 393248 | tf_op jit(solution)/shard_map/ppermute | solution.py:286
  73.1 7.6 %collective-permute-done.11.refs_2_ = bf16[8,48,512]{2,1,0:T(8,128)(2,1)S(1)} collective-permute-done((bf16[8,48,512]{2,1,0:T(8,128)(2,1)S(1)}, bf16[8,48,512]{2,1,0:T(8,128)(2,1)S(1)}, u32[]{:S(2)}, u32[]{:S(2)}) %collective-permute-start.11) | collective-permute-done | bytes 393248 | tf_op jit(solution)/shard_map/ppermute | solution.py:286
  92.7 4.4 collective-permute-start.22
  105.0 11.9 %shard_map.213 = (bf16[1536,2048]{1,0:T(8,128)(2,1)}, bf16[2,96,2048]{2,1,0:T(8,128)(2,1)}, bf16[2,1,96,2048]{3,2,1,0:T(8,128)(2,1)}) custom-call(bf16[1536,512]{1,0:T(8,128)(2,1)} %bitcast.185, f32[96,2048]{1,0:T(8,128)} %get-tuple-element.405.cosine_ref, f32[96,2048]{1,0:T(8,128)} %get-tuple-element.406.sine_ref, bf16[1536,256]{1,0:T(8,128)(2,1)} %bitcast.209, ...), custom_call_target="tpu_custom_call" | custom-call | flops 1000 | bytes 1000 | tf_op jit(solution)/shard_map/pallas_call | solution.py:511
  116.9 15.8 %collective-permute-done.19 = bf16[48,1536]{1,0:T(8,128)(2,1)S(1)} collective-permute-done((bf16[48,1536]{1,0:T(8,128)(2,1)S(1)}, bf16[48,1536]{1,0:T(8,128)(2,1)S(1)}, u32[]{:S(2)}, u32[]{:S(2)}) %collective-permute-start.19) | collective-permute-done | bytes 147488 | tf_op jit(solution)/shard_map/ppermute | solution.py:286
  135.9 4.2 collective-permute-done.21
  148.0 13.9 %collective-permute-done.24.refs_1_.refs_9_ = bf16[2,1,96,2048]{3,2,1,0:T(8,128)(2,1)S(1)} collective-permute-done((bf16[2,1,96,2048]{3,2,1,0:T(8,128)(2,1)}, bf16[2,1,96,2048]{3,2,1,0:T(8,128)(2,1)S(1)}, u32[]{:S(2)}, u32[]{:S(2)}) %collective-permute-start.24) | collective-permute-done | bytes 786464 | tf_op jit(solution)/shard_map/ppermute | solution.py:286
  168.1 5.2 shard_map.215
  179.2 6.4 shard_map.217
  189.6 8.4 %collective-permute-done.28 = bf16[256,1536]{1,0:T(8,128)(2,1)S(1)} collective-permute-done((bf16[256,1536]{1,0:T(8,128)(2,1)S(1)}, bf16[256,1536]{1,0:T(8,128)(2,1)S(1)}, u32[]{:S(2)}, u32[]{:S(2)}) %collective-permute-start.28) | collective-permute-done | bytes 786464 | tf_op jit(solution)/shard_map/ppermute | solution.py:278
  200.6 6.6 shard_map.220
  217.2 7.2 shard_map.223
  228.8 6.8 collective-permute-done.33.refs_2_
  241.5 4.7 collective-permute-start.38
  248.4 26.8 %collective-permute-done.35.refs_3_ = bf16[1536,256]{1,0:T(8,128)(2,1)S(1)} collective-permute-done((bf16[1536,256]{1,0:T(8,128)(2,1)}, bf16[1536,256]{1,0:T(8,128)(2,1)S(1)}, u32[]{:S(2)}, u32[]{:S(2)}) %collective-permute-start.35) | collective-permute-done | bytes 786464 | tf_op jit(solution)/shard_map/ppermute | solution.py:278
  276.1 5.6 shard_map.226
  283.9 6.7 shard_map.227
  291.5 10.6 %shard_map.228 = (bf16[512,512]{1,0:T(8,128)(2,1)}, bf16[512,1024]{1,0:T(8,128)(2,1)}, f32[1536,256]{1,0:T(8,128)}, bf16[1536,256]{1,0:T(8,128)(2,1)}) custom-call(bf16[1536,256]{1,0:T(8,128)(2,1)} %get-tuple-element.565.first_ref.refs_0_, bf16[1536,256]{1,0:T(8,128)(2,1)} %copy-done.12, bf16[4,256,1536]{2,1,0:T(8,128)(2,1)} %copy-done, ...), custom_call_target="tpu_custom_call" | custom-call | flops 1000 | bytes 1000 | tf_op jit(solution)/shard_map/pallas_call | solution.py:612
  307.9 10.9 %shard_map.229 = (bf16[512,512]{1,0:T(8,128)(2,1)}, bf16[512,1024]{1,0:T(8,128)(2,1)}, f32[1536,256]{1,0:T(8,128)}, bf16[1536,256]{1,0:T(8,128)(2,1)}) custom-call(bf16[1536,256]{1,0:T(8,128)(2,1)} %copy-done.13, bf16[1536,256]{1,0:T(8,128)(2,1)} %copy-done.15, bf16[4,256,1536]{2,1,0:T(8,128)(2,1)} %copy-done, bf16[4,256,1536]{2,1,0:T(8,128)(2,1)} %copy-done.1, ...), custom_call_target="tpu_custom_call" | custom-call | flops 1000 | bytes 1000 | tf_op jit(solution)/shard_map/pallas_call | solution.py:612
  318.9 5.4 collective-permute-done.45.first_ref.refs_3_
  324.8 10.6 %shard_map.230 = (bf16[512,512]{1,0:T(8,128)(2,1)}, bf16[512,1024]{1,0:T(8,128)(2,1)}, f32[1536,256]{1,0:T(8,128)}, bf16[1536,256]{1,0:T(8,128)(2,1)}) custom-call(bf16[1536,256]{1,0:T(8,128)(2,1)} %copy-done.14, bf16[1536,256]{1,0:T(8,128)(2,1)} %copy-done.16, bf16[4,256,1536]{2,1,0:T(8,128)(2,1)} %copy-done, bf16[4,256,1536]{2,1,0:T(8,128)(2,1)} %copy-done.1, ...), custom_call_target="tpu_custom_call" | custom-call | flops 1000 | bytes 1000 | tf_op jit(solution)/shard_map/pallas_call | solution.py:612
  338.9 24.0 %shard_map.232 = (bf16[512,512]{1,0:T(8,128)(2,1)}, bf16[512,1024]{1,0:T(8,128)(2,1)}, f32[1536,256]{1,0:T(8,128)}, bf16[1536,256]{1,0:T(8,128)(2,1)}) custom-call(bf16[1536,256]{1,0:T(8,128)(2,1)} %copy-done.17, bf16[1536,256]{1,0:T(8,128)(2,1)} %copy-done.18, bf16[4,256,1536]{2,1,0:T(8,128)(2,1)} %copy-done, bf16[4,256,1536]{2,1,0:T(8,128)(2,1)} %copy-done.1, ...), custom_call_target="tpu_custom_call" | custom-call | flops 1000 | bytes 1000 | tf_op jit(solution)/shard_map/pallas_call | solution.py:612
  371.1 13.9 %shard_map.235.own_ref = bf16[4,128,1536]{2,1,0:T(8,128)(2,1)} custom-call(s32[2]{0:T(128)} %pad_add_fusion.2.places_ref, bf16[512,512]{1,0:T(8,128)(2,1)} %get-tuple-element.601.refs_0_, bf16[512,512]{1,0:T(8,128)(2,1)} %get-tuple-element.602.refs_1_, bf16[512,512]{1,0:T(8,128)(2,1)} %get-tuple-element.603.refs_2_, ...), custom_call_target="tpu_custom_call" | custom-call | flops 1000 | bytes 1000 | tf_op jit(solution)/shard_map/pallas_call | solution.py:740
  394.2 20.1 %shard_map.236.own_ref = bf16[4,384,1024]{2,1,0:T(8,128)(2,1)} custom-call(s32[2]{0:T(128)} %pad_add_fusion.2.places_ref, bf16[1536,256]{1,0:T(8,128)(2,1)} %get-tuple-element.565.first_ref.refs_0_, bf16[1536,256]{1,0:T(8,128)(2,1)} %copy-done.13, bf16[1536,256]{1,0:T(8,128)(2,1)} %copy-done.14, bf16[1536,256]{1,0:T(8,128)(2,1)} %copy-done.17, ...), custom_call_target="tpu_custom_call" | custom-call | flops 1000 | bytes 1000 | tf_op jit(solution)/shard_map/pallas_call | solution.py:705
  418.1 6.4 shard_map.237
  430.6 25.3 %collective-permute-done.59.refs_2_ = bf16[128,1536]{1,0:T(8,128)(2,1)S(1)} collective-permute-done((bf16[128,1536]{1,0:T(8,128)(2,1)S(1)}, bf16[128,1536]{1,0:T(8,128)(2,1)S(1)}, u32[]{:S(2)}, u32[]{:S(2)}) %collective-permute-start.59) | collective-permute-done | bytes 393248 | tf_op jit(solution)/shard_map/ppermute | solution.py:286
  459.0 10.0 %shard_map.238 = (f32[1024,1536]{1,0:T(8,128)}, bf16[1024,1536]{1,0:T(8,128)(2,1)}) custom-call(bf16[512,1536]{1,0:T(8,128)(2,1)} %bitcast.199, bf16[512,512]{1,0:T(8,128)(2,1)} %get-tuple-element.601.refs_0_, bf16[512,512]{1,0:T(8,128)(2,1)} %get-tuple-element.602.refs_1_, bf16[512,512]{1,0:T(8,128)(2,1)} %get-tuple-element.603.refs_2_, ...), custom_call_target="tpu_custom_call" | custom-call | flops 1000 | bytes 1000 | tf_op jit(solution)/shard_map/pallas_call | solution.py:657
  469.1 8.2 %collective-permute-done.64.refs_1_ = bf16[384,1024]{1,0:T(8,128)(2,1)S(1)} collective-permute-done((bf16[384,1024]{1,0:T(8,128)(2,1)}, bf16[384,1024]{1,0:T(8,128)(2,1)S(1)}, u32[]{:S(2)}, u32[]{:S(2)}) %collective-permute-start.64) | collective-permute-done | bytes 786464 | tf_op jit(solution)/shard_map/ppermute | solution.py:286
  481.8 11.6 %shard_map.239 = (bf16[2,96,2048]{2,1,0:T(8,128)(2,1)}, bf16[4,48,1536]{2,1,0:T(8,128)(2,1)}) custom-call(s32[2]{0:T(128)} %pad_add_fusion.2.places_ref, bf16[192,1536]{1,0:T(8,128)(2,1)} %bitcast.204, f32[2,96,512]{2,1,0:T(8,128)} %get-tuple-element.467.attended_ref.refs_0_, f32[2,96,512]{2,1,0:T(8,128)} %get-tuple-element.435.attended_ref.refs_1_, ...), custom_call_target="tpu_custom_call" | custom-call | flops 1000 | bytes 1000 | tf_op jit(solution)/shard_map/pallas_call | solution.py:796
  495.9 22.3 %shard_map.240 = (f32[2,96,2048]{2,1,0:T(8,128)}, f32[2,1,96,2048]{3,2,1,0:T(8,128)}, bf16[1,2,1,96,2048]{4,3,2,1,0:T(8,128)(2,1)}) custom-call(s32[9]{0:T(128)} %pad_add_fusion.1.low_ref, s32[1,2048]{1,0:T(1,128)} %bitcast.247, bf16[2,96,2048]{2,1,0:T(8,128)(2,1)} %get-tuple-element.466.query_ref, bf16[2,96,2048]{2,1,0:T(8,128)(2,1)} %get-tuple-element.622.grad_ref, ...), custom_call_target="tpu_custom_call" | custom-call | flops 1000 | bytes 1000 | tf_op jit(solution)/shard_map/pallas_call | solution.py:227
  518.2 11.6 %collective-permute-done.67.refs_2_ = bf16[384,1024]{1,0:T(8,128)(2,1)S(1)} collective-permute-done((bf16[384,1024]{1,0:T(8,128)(2,1)S(1)}, bf16[384,1024]{1,0:T(8,128)(2,1)S(1)}, u32[]{:S(2)}, u32[]{:S(2)}) %collective-permute-start.67) | collective-permute-done | bytes 786464 | tf_op jit(solution)/shard_map/ppermute | solution.py:286
  529.9 4.7 collective-permute-start.68
  534.5 6.8 shard_map.241
  545.9 5.9 collective-permute-done.68.refs_1_
  552.7 4.8 shard_map.243
  557.6 4.8 shard_map.244
  566.4 4.8 shard_map.246
  574.9 4.8 shard_map.248
  590.2 11.2 %shard_map.250.own_ref = bf16[4,384,384]{2,1,0:T(8,128)(2,1)} custom-call(s32[2]{0:T(128)} %pad_add_fusion.2.places_ref, bf16[1536,2048]{1,0:T(8,128)(2,1)} %get-tuple-element.681.normed_ref, bf16[384,512]{1,0:T(8,128)(2,1)} %get-tuple-element.682.refs_0_, bf16[384,512]{1,0:T(8,128)(2,1)} %get-tuple-element.683.refs_1_, ...), custom_call_target="tpu_custom_call" | custom-call | flops 1000 | bytes 1000 | tf_op jit(solution)/shard_map/pallas_call | solution.py:890
  601.5 32.2 %collective-permute-done.77.refs_3_ = bf16[1536,256]{1,0:T(8,128)(2,1)} collective-permute-done((bf16[1536,256]{1,0:T(8,128)(2,1)}, bf16[1536,256]{1,0:T(8,128)(2,1)}, u32[]{:S(2)}, u32[]{:S(2)}) %collective-permute-start.77) | collective-permute-done | bytes 786464 | tf_op jit(solution)/shard_map/ppermute | solution.py:278
  642.3 4.0 shard_map.253
  657.0 5.9 shard_map.254
  671.0 9.9 %collective-permute-start.89 = (bf16[2,48,1024]{2,1,0:T(8,128)(2,1)S(1)}, bf16[2,48,1024]{2,1,0:T(8,128)(2,1)S(1)}, u32[]{:S(2)}, u32[]{:S(2)}) collective-permute-start(bf16[2,48,1024]{2,1,0:T(8,128)(2,1)S(1)} %get-tuple-element.772), channel_id=1, source_target_pairs={{0,6},{1,7},{2,4},{3,5},{4,2},{5,3},{6,0},{7,1},{8,14},{9,15},{10,... | collective-permute-start | bytes 589832 | tf_op jit(solution)/shard_map/ppermute | solution.py:278
  681.8 10.1 %collective-permute-start.94 = (bf16[2,48,384]{2,1,0:T(8,128)(2,1)}, bf16[2,48,384]{2,1,0:T(8,128)(2,1)S(1)}, u32[]{:S(2)}, u32[]{:S(2)}) collective-permute-start(bf16[2,48,384]{2,1,0:T(8,128)(2,1)} %get-tuple-element.794), channel_id=1, source_target_pairs={{0,2},{1,3},{2,0},{3,1},{4,6},{5,7},{6,4},{7,5},{8,10},{9,11},{10,... | collective-permute-start | bytes 221192 | tf_op jit(solution)/shard_map/ppermute | solution.py:278
  706.9 7.2 collective-permute-done.97
  716.0 5.7 collective-permute-start.99
  (453 shorter events, 235.9 us)
Async XLA Ops:
  10.5 32.1 %collective-permute-start.7 = (bf16[1536,256]{1,0:T(8,128)(2,1)S(1)}, bf16[1536,256]{1,0:T(8,128)(2,1)S(1)}, u32[]{:S(2)}, u32[]{:S(2)}) collective-permute-start(bf16[1536,256]{1,0:T(8,128)(2,1)S(1)} %bitcast.205), channel_id=1, source_target_pairs={{0,2},{1,3},{2,0},{3,1},{4,6},{5,7},{6,4},{7,5},{8,10},{9,11},{10,... | collective-permute-start | bytes 2359304 | tf_op jit(solution)/shard_map/ppermute | solution.py:278
  11.1 31.5 %collective-permute-start.8 = (bf16[1536,256]{1,0:T(8,128)(2,1)S(1)}, bf16[1536,256]{1,0:T(8,128)(2,1)}, u32[]{:S(2)}, u32[]{:S(2)}) collective-permute-start(bf16[1536,256]{1,0:T(8,128)(2,1)S(1)} %bitcast.206), channel_id=1, source_target_pairs={{0,4},{1,5},{2,6},{3,7},{4,0},{5,1},{6,2},{7,3},{8,12},{9,13},{10,... | collective-permute-start | bytes 2359304 | tf_op jit(solution)/shard_map/ppermute | solution.py:278
  15.8 21.6 %collective-permute-start.4 = (bf16[2,48,1536]{2,1,0:T(8,128)(2,1)}, bf16[2,48,1536]{2,1,0:T(8,128)(2,1)S(1)}, u32[]{:S(2)}, u32[]{:S(2)}) collective-permute-start(bf16[2,48,1536]{2,1,0:T(8,128)(2,1)} %get-tuple-element.764), channel_id=1, source_target_pairs={{0,2},{1,3},{2,0},{3,1},{4,6},{5,7},{6,4},{7,5},{8,10},{9,11},{10,... | collective-permute-start | bytes 884744 | tf_op jit(solution)/shard_map/ppermute | solution.py:278
  17.3 23.7 %collective-permute-start.5 = (bf16[2,48,1536]{2,1,0:T(8,128)(2,1)}, bf16[2,48,1536]{2,1,0:T(8,128)(2,1)S(1)}, u32[]{:S(2)}, u32[]{:S(2)}) collective-permute-start(bf16[2,48,1536]{2,1,0:T(8,128)(2,1)} %get-tuple-element.763), channel_id=1, source_target_pairs={{0,4},{1,5},{2,6},{3,7},{4,0},{5,1},{6,2},{7,3},{8,12},{9,13},{10,... | collective-permute-start | bytes 884744 | tf_op jit(solution)/shard_map/ppermute | solution.py:278
  19.1 23.5 %collective-permute-start.6 = (bf16[2,48,1536]{2,1,0:T(8,128)(2,1)}, bf16[2,48,1536]{2,1,0:T(8,128)(2,1)S(1)}, u32[]{:S(2)}, u32[]{:S(2)}) collective-permute-start(bf16[2,48,1536]{2,1,0:T(8,128)(2,1)} %get-tuple-element.762), channel_id=1, source_target_pairs={{0,6},{1,7},{2,4},{3,5},{4,2},{5,3},{6,0},{7,1},{8,14},{9,15},{10,... | collective-permute-start | bytes 884744 | tf_op jit(solution)/shard_map/ppermute | solution.py:278
  45.1 28.0 %collective-permute-start.10 = (bf16[8,48,512]{2,1,0:T(8,128)(2,1)S(1)}, bf16[8,48,512]{2,1,0:T(8,128)(2,1)S(1)}, u32[]{:S(2)}, u32[]{:S(2)}) collective-permute-start(bf16[8,48,512]{2,1,0:T(8,128)(2,1)S(1)} %fusion.2.refs_0_), channel_id=1, source_target_pairs={{0,8},{1,9},{2,10},{3,11},{4,12},{5,13},{6,14},{7,15},{8,16},{9,17... | collective-permute-start | bytes 1179656 | tf_op jit(solution)/shard_map/ppermute | solution.py:286
  46.7 34.0 %collective-permute-start.11 = (bf16[8,48,512]{2,1,0:T(8,128)(2,1)S(1)}, bf16[8,48,512]{2,1,0:T(8,128)(2,1)S(1)}, u32[]{:S(2)}, u32[]{:S(2)}) collective-permute-start(bf16[8,48,512]{2,1,0:T(8,128)(2,1)S(1)} %fusion.2.refs_0_), channel_id=1, source_target_pairs={{0,16},{1,17},{2,18},{3,19},{4,20},{5,21},{6,22},{7,23},{8,24},{9,... | collective-permute-start | bytes 1179656 | tf_op jit(solution)/shard_map/ppermute | solution.py:286
  48.0 34.5 %collective-permute-start.12 = (bf16[8,48,512]{2,1,0:T(8,128)(2,1)S(1)}, bf16[8,48,512]{2,1,0:T(8,128)(2,1)S(1)}, u32[]{:S(2)}, u32[]{:S(2)}) collective-permute-start(bf16[8,48,512]{2,1,0:T(8,128)(2,1)S(1)} %fusion.2.refs_0_), channel_id=1, source_target_pairs={{0,24},{1,25},{2,26},{3,27},{4,28},{5,29},{6,30},{7,31},{8,0},{9,1... | collective-permute-start | bytes 1179656 | tf_op jit(solution)/shard_map/ppermute | solution.py:286
  49.8 42.9 %collective-permute-start.14 = (bf16[1536,256]{1,0:T(8,128)(2,1)S(1)}, bf16[1536,256]{1,0:T(8,128)(2,1)}, u32[]{:S(2)}, u32[]{:S(2)}) collective-permute-start(bf16[1536,256]{1,0:T(8,128)(2,1)S(1)} %bitcast.208), channel_id=1, source_target_pairs={{0,1},{1,0},{2,3},{3,2},{4,5},{5,4},{6,7},{7,6},{8,9},{9,8},{10,11... | collective-permute-start | bytes 2359304 | tf_op jit(solution)/shard_map/ppermute | solution.py:278
  63.9 28.7 %collective-permute-start.15 = (bf16[1536,256]{1,0:T(8,128)(2,1)S(1)}, bf16[1536,256]{1,0:T(8,128)(2,1)}, u32[]{:S(2)}, u32[]{:S(2)}) collective-permute-start(bf16[1536,256]{1,0:T(8,128)(2,1)S(1)} %collective-permute-done.7.refs_1_), channel_id=1, source_target_pairs={{0,1},{1,0},{2,3},{3,2},{4,5},{5,4},{6,7},{7,6},{8,9},{9,8},{10,11... | collective-permute-start | bytes 2359304 | tf_op jit(solution)/shard_map/ppermute | solution.py:278
  92.7 47.5 %collective-permute-start.22 = (bf16[8,48,1536]{2,1,0:T(8,128)(2,1)S(1)}, bf16[8,48,1536]{2,1,0:T(8,128)(2,1)S(1)}, u32[]{:S(2)}, u32[]{:S(2)}) collective-permute-start(bf16[8,48,1536]{2,1,0:T(8,128)(2,1)S(1)} %pad_maximum_fusion.3.refs_0_), channel_id=1, source_target_pairs={{0,8},{1,9},{2,10},{3,11},{4,12},{5,13},{6,14},{7,15},{8,16},{9,17... | collective-permute-start | bytes 3538952 | tf_op jit(solution)/shard_map/ppermute | solution.py:286
  97.1 43.1 %collective-permute-start.23 = (bf16[8,48,1536]{2,1,0:T(8,128)(2,1)S(1)}, bf16[8,48,1536]{2,1,0:T(8,128)(2,1)S(1)}, u32[]{:S(2)}, u32[]{:S(2)}) collective-permute-start(bf16[8,48,1536]{2,1,0:T(8,128)(2,1)S(1)} %pad_maximum_fusion.3.refs_0_), channel_id=1, source_target_pairs={{8,0},{9,1},{10,2},{11,3},{12,4},{13,5},{14,6},{15,7},{16,8},{17,9... | collective-permute-start | bytes 3538952 | tf_op jit(solution)/shard_map/ppermute | solution.py:286
  99.0 33.7 %collective-permute-start.19 = (bf16[48,1536]{1,0:T(8,128)(2,1)S(1)}, bf16[48,1536]{1,0:T(8,128)(2,1)S(1)}, u32[]{:S(2)}, u32[]{:S(2)}) collective-permute-start(bf16[48,1536]{1,0:T(8,128)(2,1)S(1)} %collective-permute-done.18), channel_id=1, source_target_pairs={{0,8},{1,9},{2,10},{3,11},{4,12},{5,13},{6,14},{7,15},{8,16},{9,17... | collective-permute-start | bytes 442376 | tf_op jit(solution)/shard_map/ppermute | solution.py:286
  101.4 34.5 %collective-permute-start.20 = (bf16[48,1536]{1,0:T(8,128)(2,1)S(1)}, bf16[48,1536]{1,0:T(8,128)(2,1)S(1)}, u32[]{:S(2)}, u32[]{:S(2)}) collective-permute-start(bf16[48,1536]{1,0:T(8,128)(2,1)S(1)} %collective-permute-done.18), channel_id=1, source_target_pairs={{0,16},{1,17},{2,18},{3,19},{4,20},{5,21},{6,22},{7,23},{8,24},{9,... | collective-permute-start | bytes 442376 | tf_op jit(solution)/shard_map/ppermute | solution.py:286
  103.0 37.2 %collective-permute-start.21 = (bf16[48,1536]{1,0:T(8,128)(2,1)S(1)}, bf16[48,1536]{1,0:T(8,128)(2,1)S(1)}, u32[]{:S(2)}, u32[]{:S(2)}) collective-permute-start(bf16[48,1536]{1,0:T(8,128)(2,1)S(1)} %collective-permute-done.18), channel_id=1, source_target_pairs={{0,24},{1,25},{2,26},{3,27},{4,28},{5,29},{6,30},{7,31},{8,0},{9,1... | collective-permute-start | bytes 442376 | tf_op jit(solution)/shard_map/ppermute | solution.py:286
  162.2 48.9 %collective-permute-start.30 = (bf16[8,48,1536]{2,1,0:T(8,128)(2,1)S(1)}, bf16[8,48,1536]{2,1,0:T(8,128)(2,1)S(1)}, u32[]{:S(2)}, u32[]{:S(2)}) collective-permute-start(bf16[8,48,1536]{2,1,0:T(8,128)(2,1)S(1)} %collective-permute-done.22.refs_1_), channel_id=1, source_target_pairs={{0,8},{1,9},{2,10},{3,11},{4,12},{5,13},{6,14},{7,15},{8,16},{9,17... | collective-permute-start | bytes 3538952 | tf_op jit(solution)/shard_map/ppermute | solution.py:286
  164.2 46.9 %collective-permute-start.31 = (bf16[8,48,1536]{2,1,0:T(8,128)(2,1)S(1)}, bf16[8,48,1536]{2,1,0:T(8,128)(2,1)S(1)}, u32[]{:S(2)}, u32[]{:S(2)}) collective-permute-start(bf16[8,48,1536]{2,1,0:T(8,128)(2,1)S(1)} %collective-permute-done.23.refs_2_), channel_id=1, source_target_pairs={{8,0},{9,1},{10,2},{11,3},{12,4},{13,5},{14,6},{15,7},{16,8},{17,9... | collective-permute-start | bytes 3538952 | tf_op jit(solution)/shard_map/ppermute | solution.py:286
  189.3 21.7 %collective-permute-start.29 = (bf16[1536,256]{1,0:T(8,128)(2,1)}, bf16[1536,256]{1,0:T(8,128)(2,1)}, u32[]{:S(2)}, u32[]{:S(2)}) collective-permute-start(bf16[1536,256]{1,0:T(8,128)(2,1)} %get-tuple-element.457), channel_id=1, source_target_pairs={{0,1},{1,0},{2,3},{3,2},{4,5},{5,4},{6,7},{7,6},{8,9},{9,8},{10,11... | collective-permute-start | bytes 2359304 | tf_op jit(solution)/shard_map/ppermute | solution.py:278
  214.4 21.3 %collective-permute-start.33 = (bf16[1536,256]{1,0:T(8,128)(2,1)}, bf16[1536,256]{1,0:T(8,128)(2,1)}, u32[]{:S(2)}, u32[]{:S(2)}) collective-permute-start(bf16[1536,256]{1,0:T(8,128)(2,1)} %shard_map.219), channel_id=1, source_target_pairs={{0,2},{1,3},{2,0},{3,1},{4,6},{5,7},{6,4},{7,5},{8,10},{9,11},{10,... | collective-permute-start | bytes 2359304 | tf_op jit(solution)/shard_map/ppermute | solution.py:278
  238.1 37.1 %collective-permute-start.36 = (bf16[4,256,1536]{2,1,0:T(8,128)(2,1)S(1)}, bf16[4,256,1536]{2,1,0:T(8,128)(2,1)S(1)}, u32[]{:S(2)}, u32[]{:S(2)}) collective-permute-start(bf16[4,256,1536]{2,1,0:T(8,128)(2,1)S(1)} %pad_maximum_fusion.wanted_a.refs_4_), channel_id=1, source_target_pairs={{0,1},{1,0},{2,3},{3,2},{4,5},{5,4},{6,7},{7,6},{8,9},{9,8},{10,11... | collective-permute-start | bytes 9437192 | tf_op jit(solution)/shard_map/ppermute | solution.py:278
  238.2 37.0 %collective-permute-start.35 = (bf16[1536,256]{1,0:T(8,128)(2,1)}, bf16[1536,256]{1,0:T(8,128)(2,1)S(1)}, u32[]{:S(2)}, u32[]{:S(2)}) collective-permute-start(bf16[1536,256]{1,0:T(8,128)(2,1)} %shard_map.222), channel_id=1, source_target_pairs={{0,4},{1,5},{2,6},{3,7},{4,0},{5,1},{6,2},{7,3},{8,12},{9,13},{10,... | collective-permute-start | bytes 2359304 | tf_op jit(solution)/shard_map/ppermute | solution.py:278
  238.5 36.7 %collective-permute-start.37 = (bf16[1536,256]{1,0:T(8,128)(2,1)}, bf16[1536,256]{1,0:T(8,128)(2,1)}, u32[]{:S(2)}, u32[]{:S(2)}) collective-permute-start(bf16[1536,256]{1,0:T(8,128)(2,1)} %shard_map.225), channel_id=1, source_target_pairs={{0,6},{1,7},{2,4},{3,5},{4,2},{5,3},{6,0},{7,1},{8,14},{9,15},{10,... | collective-permute-start | bytes 2359304 | tf_op jit(solution)/shard_map/ppermute | solution.py:278
  241.5 42.4 %collective-permute-start.38 = (bf16[8,48,1536]{2,1,0:T(8,128)(2,1)S(1)}, bf16[8,48,1536]{2,1,0:T(8,128)(2,1)}, u32[]{:S(2)}, u32[]{:S(2)}) collective-permute-start(bf16[8,48,1536]{2,1,0:T(8,128)(2,1)S(1)} %collective-permute-done.30.refs_3_), channel_id=1, source_target_pairs={{0,8},{1,9},{2,10},{3,11},{4,12},{5,13},{6,14},{7,15},{8,16},{9,17... | collective-permute-start | bytes 3538952 | tf_op jit(solution)/shard_map/ppermute | solution.py:286
  246.2 37.7 %collective-permute-start.39 = (bf16[8,48,1536]{2,1,0:T(8,128)(2,1)}, bf16[8,48,1536]{2,1,0:T(8,128)(2,1)}, u32[]{:S(2)}, u32[]{:S(2)}) collective-permute-start(bf16[8,48,1536]{2,1,0:T(8,128)(2,1)} %copy-done.25), channel_id=1, source_target_pairs={{8,0},{9,1},{10,2},{11,3},{12,4},{13,5},{14,6},{15,7},{16,8},{17,9... | collective-permute-start | bytes 3538952 | tf_op jit(solution)/shard_map/ppermute | solution.py:286
  335.4 28.0 %collective-permute-start.49 = (bf16[1536,256]{1,0:T(8,128)(2,1)}, bf16[1536,256]{1,0:T(8,128)(2,1)S(1)}, u32[]{:S(2)}, u32[]{:S(2)}) collective-permute-start(bf16[1536,256]{1,0:T(8,128)(2,1)} %get-tuple-element.537), channel_id=1, source_target_pairs={{0,1},{1,0},{2,3},{3,2},{4,5},{5,4},{6,7},{7,6},{8,9},{9,8},{10,11... | collective-permute-start | bytes 2359304 | tf_op jit(solution)/shard_map/ppermute | solution.py:278
  366.8 47.5 %collective-permute-start.51 = (bf16[1536,256]{1,0:T(8,128)(2,1)S(1)}, bf16[1536,256]{1,0:T(8,128)(2,1)S(1)}, u32[]{:S(2)}, u32[]{:S(2)}) collective-permute-start(bf16[1536,256]{1,0:T(8,128)(2,1)S(1)} %copy-done.47), channel_id=1, source_target_pairs={{0,2},{1,3},{2,0},{3,1},{4,6},{5,7},{6,4},{7,5},{8,10},{9,11},{10,... | collective-permute-start | bytes 2359304 | tf_op jit(solution)/shard_map/ppermute | solution.py:278
  367.2 47.1 %collective-permute-start.52 = (bf16[1536,256]{1,0:T(8,128)(2,1)}, bf16[1536,256]{1,0:T(8,128)(2,1)S(1)}, u32[]{:S(2)}, u32[]{:S(2)}) collective-permute-start(bf16[1536,256]{1,0:T(8,128)(2,1)} %shard_map.233), channel_id=1, source_target_pairs={{0,4},{1,5},{2,6},{3,7},{4,0},{5,1},{6,2},{7,3},{8,12},{9,13},{10,... | collective-permute-start | bytes 2359304 | tf_op jit(solution)/shard_map/ppermute | solution.py:278
  385.0 32.1 %collective-permute-start.53 = (bf16[1536,256]{1,0:T(8,128)(2,1)S(1)}, bf16[1536,256]{1,0:T(8,128)(2,1)S(1)}, u32[]{:S(2)}, u32[]{:S(2)}) collective-permute-start(bf16[1536,256]{1,0:T(8,128)(2,1)S(1)} %copy-done.48), channel_id=1, source_target_pairs={{0,6},{1,7},{2,4},{3,5},{4,2},{5,3},{6,0},{7,1},{8,14},{9,15},{10,... | collective-permute-start | bytes 2359304 | tf_op jit(solution)/shard_map/ppermute | solution.py:278
  389.5 24.8 %collective-permute-start.54 = (bf16[128,1536]{1,0:T(8,128)(2,1)S(1)}, bf16[128,1536]{1,0:T(8,128)(2,1)S(1)}, u32[]{:S(2)}, u32[]{:S(2)}) collective-permute-start(bf16[128,1536]{1,0:T(8,128)(2,1)S(1)} %get-tuple-element.752), channel_id=1, source_target_pairs={{0,8},{1,9},{2,10},{3,11},{4,12},{5,13},{6,14},{7,15},{8,16},{9,17... | collective-permute-start | bytes 1179656 | tf_op jit(solution)/shard_map/ppermute | solution.py:286
  392.4 24.6 %collective-permute-start.55 = (bf16[128,1536]{1,0:T(8,128)(2,1)S(1)}, bf16[128,1536]{1,0:T(8,128)(2,1)S(1)}, u32[]{:S(2)}, u32[]{:S(2)}) collective-permute-start(bf16[128,1536]{1,0:T(8,128)(2,1)S(1)} %get-tuple-element.751), channel_id=1, source_target_pairs={{0,16},{1,17},{2,18},{3,19},{4,20},{5,21},{6,22},{7,23},{8,24},{9,... | collective-permute-start | bytes 1179656 | tf_op jit(solution)/shard_map/ppermute | solution.py:286
  424.5 31.3 %collective-permute-start.56 = (bf16[1536,256]{1,0:T(8,128)(2,1)}, bf16[1536,256]{1,0:T(8,128)(2,1)S(1)}, u32[]{:S(2)}, u32[]{:S(2)}) collective-permute-start(bf16[1536,256]{1,0:T(8,128)(2,1)} %get-tuple-element.606.refs_4_), channel_id=1, source_target_pairs={{0,2},{1,3},{2,0},{3,1},{4,6},{5,7},{6,4},{7,5},{8,10},{9,11},{10,... | collective-permute-start | bytes 2359304 | tf_op jit(solution)/shard_map/ppermute | solution.py:278
  425.9 30.0 %collective-permute-start.57 = (bf16[1536,256]{1,0:T(8,128)(2,1)}, bf16[1536,256]{1,0:T(8,128)(2,1)S(1)}, u32[]{:S(2)}, u32[]{:S(2)}) collective-permute-start(bf16[1536,256]{1,0:T(8,128)(2,1)} %get-tuple-element.606.refs_4_), channel_id=1, source_target_pairs={{0,4},{1,5},{2,6},{3,7},{4,0},{5,1},{6,2},{7,3},{8,12},{9,13},{10,... | collective-permute-start | bytes 2359304 | tf_op jit(solution)/shard_map/ppermute | solution.py:278
  428.3 27.6 %collective-permute-start.58 = (bf16[384,1024]{1,0:T(8,128)(2,1)S(1)}, bf16[384,1024]{1,0:T(8,128)(2,1)S(1)}, u32[]{:S(2)}, u32[]{:S(2)}) collective-permute-start(bf16[384,1024]{1,0:T(8,128)(2,1)S(1)} %get-tuple-element.749), channel_id=1, source_target_pairs={{0,8},{1,9},{2,10},{3,11},{4,12},{5,13},{6,14},{7,15},{8,16},{9,17... | collective-permute-start | bytes 2359304 | tf_op jit(solution)/shard_map/ppermute | solution.py:286
  428.6 27.3 %collective-permute-start.59 = (bf16[128,1536]{1,0:T(8,128)(2,1)S(1)}, bf16[128,1536]{1,0:T(8,128)(2,1)S(1)}, u32[]{:S(2)}, u32[]{:S(2)}) collective-permute-start(bf16[128,1536]{1,0:T(8,128)(2,1)S(1)} %copy-done.65), channel_id=1, source_target_pairs={{0,24},{1,25},{2,26},{3,27},{4,28},{5,29},{6,30},{7,31},{8,0},{9,1... | collective-permute-start | bytes 1179656 | tf_op jit(solution)/shard_map/ppermute | solution.py:286
  493.4 36.5 %collective-permute-start.66 = (bf16[1024,1536]{1,0:T(8,128)(2,1)}, bf16[1024,1536]{1,0:T(8,128)(2,1)S(1)}, u32[]{:S(2)}, u32[]{:S(2)}) collective-permute-start(bf16[1024,1536]{1,0:T(8,128)(2,1)} %get-tuple-element.630), channel_id=1, source_target_pairs={{0,1},{1,0},{2,3},{3,2},{4,5},{5,4},{6,7},{7,6},{8,9},{9,8},{10,11... | collective-permute-start | bytes 9437192 | tf_op jit(solution)/shard_map/ppermute | solution.py:278
  493.6 36.3 %collective-permute-start.67 = (bf16[384,1024]{1,0:T(8,128)(2,1)S(1)}, bf16[384,1024]{1,0:T(8,128)(2,1)S(1)}, u32[]{:S(2)}, u32[]{:S(2)}) collective-permute-start(bf16[384,1024]{1,0:T(8,128)(2,1)S(1)} %get-tuple-element.747), channel_id=1, source_target_pairs={{0,16},{1,17},{2,18},{3,19},{4,20},{5,21},{6,22},{7,23},{8,24},{9,... | collective-permute-start | bytes 2359304 | tf_op jit(solution)/shard_map/ppermute | solution.py:286
  529.9 22.0 %collective-permute-start.68 = (bf16[2,1,96,2048]{3,2,1,0:T(8,128)(2,1)}, bf16[2,1,96,2048]{3,2,1,0:T(8,128)(2,1)S(1)}, u32[]{:S(2)}, u32[]{:S(2)}) collective-permute-start(bf16[2,1,96,2048]{3,2,1,0:T(8,128)(2,1)} %bitcast.271), channel_id=1, source_target_pairs={{8,0},{9,1},{10,2},{11,3},{12,4},{13,5},{14,6},{15,7},{16,8},{17,9... | collective-permute-start | bytes 2359304 | tf_op jit(solution)/shard_map/ppermute | solution.py:286
  541.4 21.6 %collective-permute-start.70 = (bf16[256,1536]{1,0:T(8,128)(2,1)}, bf16[256,1536]{1,0:T(8,128)(2,1)S(1)}, u32[]{:S(2)}, u32[]{:S(2)}) collective-permute-start(bf16[256,1536]{1,0:T(8,128)(2,1)} %get-tuple-element.655), channel_id=1, source_target_pairs={{0,2},{1,3},{2,0},{3,1},{4,6},{5,7},{6,4},{7,5},{8,10},{9,11},{10,... | collective-permute-start | bytes 2359304 | tf_op jit(solution)/shard_map/ppermute | solution.py:278
  541.7 21.3 %collective-permute-start.71 = (bf16[256,1536]{1,0:T(8,128)(2,1)}, bf16[256,1536]{1,0:T(8,128)(2,1)S(1)}, u32[]{:S(2)}, u32[]{:S(2)}) collective-permute-start(bf16[256,1536]{1,0:T(8,128)(2,1)} %get-tuple-element.656), channel_id=1, source_target_pairs={{0,4},{1,5},{2,6},{3,7},{4,0},{5,1},{6,2},{7,3},{8,12},{9,13},{10,... | collective-permute-start | bytes 2359304 | tf_op jit(solution)/shard_map/ppermute | solution.py:278
  579.7 21.7 %collective-permute-start.75 = (bf16[1536,256]{1,0:T(8,128)(2,1)}, bf16[1536,256]{1,0:T(8,128)(2,1)}, u32[]{:S(2)}, u32[]{:S(2)}) collective-permute-start(bf16[1536,256]{1,0:T(8,128)(2,1)} %get-tuple-element.686), channel_id=1, source_target_pairs={{0,1},{1,0},{2,3},{3,2},{4,5},{5,4},{6,7},{7,6},{8,9},{9,8},{10,11... | collective-permute-start | bytes 2359304 | tf_op jit(solution)/shard_map/ppermute | solution.py:278
  579.8 21.6 %collective-permute-start.76 = (bf16[1536,256]{1,0:T(8,128)(2,1)S(1)}, bf16[1536,256]{1,0:T(8,128)(2,1)}, u32[]{:S(2)}, u32[]{:S(2)}) collective-permute-start(bf16[1536,256]{1,0:T(8,128)(2,1)S(1)} %copy-done.46), channel_id=1, source_target_pairs={{0,2},{1,3},{2,0},{3,1},{4,6},{5,7},{6,4},{7,5},{8,10},{9,11},{10,... | collective-permute-start | bytes 2359304 | tf_op jit(solution)/shard_map/ppermute | solution.py:278
  580.2 53.5 %collective-permute-start.77 = (bf16[1536,256]{1,0:T(8,128)(2,1)}, bf16[1536,256]{1,0:T(8,128)(2,1)}, u32[]{:S(2)}, u32[]{:S(2)}) collective-permute-start(bf16[1536,256]{1,0:T(8,128)(2,1)} %shard_map.247), channel_id=1, source_target_pairs={{0,4},{1,5},{2,6},{3,7},{4,0},{5,1},{6,2},{7,3},{8,12},{9,13},{10,... | collective-permute-start | bytes 2359304 | tf_op jit(solution)/shard_map/ppermute | solution.py:278
  581.3 59.3 %collective-permute-start.83 = (bf16[256,1536]{1,0:T(8,128)(2,1)}, bf16[256,1536]{1,0:T(8,128)(2,1)S(1)}, u32[]{:S(2)}, u32[]{:S(2)}) collective-permute-start(bf16[256,1536]{1,0:T(8,128)(2,1)} %get-tuple-element.707), channel_id=1, source_target_pairs={{0,6},{1,7},{2,4},{3,5},{4,2},{5,3},{6,0},{7,1},{8,14},{9,15},{10,... | collective-permute-start | bytes 2359304 | tf_op jit(solution)/shard_map/ppermute | solution.py:278
  586.7 59.7 %collective-permute-start.78 = (bf16[1536,256]{1,0:T(8,128)(2,1)}, bf16[1536,256]{1,0:T(8,128)(2,1)}, u32[]{:S(2)}, u32[]{:S(2)}) collective-permute-start(bf16[1536,256]{1,0:T(8,128)(2,1)} %shard_map.249), channel_id=1, source_target_pairs={{0,6},{1,7},{2,4},{3,5},{4,2},{5,3},{6,0},{7,1},{8,14},{9,15},{10,... | collective-permute-start | bytes 2359304 | tf_op jit(solution)/shard_map/ppermute | solution.py:278
  640.6 53.2 %collective-permute-start.87 = (bf16[2,48,1024]{2,1,0:T(8,128)(2,1)}, bf16[2,48,1024]{2,1,0:T(8,128)(2,1)S(1)}, u32[]{:S(2)}, u32[]{:S(2)}) collective-permute-start(bf16[2,48,1024]{2,1,0:T(8,128)(2,1)} %get-tuple-element.774), channel_id=1, source_target_pairs={{0,2},{1,3},{2,0},{3,1},{4,6},{5,7},{6,4},{7,5},{8,10},{9,11},{10,... | collective-permute-start | bytes 589832 | tf_op jit(solution)/shard_map/ppermute | solution.py:278
  667.2 26.5 %collective-permute-start.88 = (bf16[2,48,1024]{2,1,0:T(8,128)(2,1)S(1)}, bf16[2,48,1024]{2,1,0:T(8,128)(2,1)S(1)}, u32[]{:S(2)}, u32[]{:S(2)}) collective-permute-start(bf16[2,48,1024]{2,1,0:T(8,128)(2,1)S(1)} %get-tuple-element.775), channel_id=1, source_target_pairs={{0,4},{1,5},{2,6},{3,7},{4,0},{5,1},{6,2},{7,3},{8,12},{9,13},{10,... | collective-permute-start | bytes 589832 | tf_op jit(solution)/shard_map/ppermute | solution.py:278
  671.0 22.8 %collective-permute-start.89 = (bf16[2,48,1024]{2,1,0:T(8,128)(2,1)S(1)}, bf16[2,48,1024]{2,1,0:T(8,128)(2,1)S(1)}, u32[]{:S(2)}, u32[]{:S(2)}) collective-permute-start(bf16[2,48,1024]{2,1,0:T(8,128)(2,1)S(1)} %get-tuple-element.772), channel_id=1, source_target_pairs={{0,6},{1,7},{2,4},{3,5},{4,2},{5,3},{6,0},{7,1},{8,14},{9,15},{10,... | collective-permute-start | bytes 589832 | tf_op jit(solution)/shard_map/ppermute | solution.py:278
  681.8 23.7 %collective-permute-start.94 = (bf16[2,48,384]{2,1,0:T(8,128)(2,1)}, bf16[2,48,384]{2,1,0:T(8,128)(2,1)S(1)}, u32[]{:S(2)}, u32[]{:S(2)}) collective-permute-start(bf16[2,48,384]{2,1,0:T(8,128)(2,1)} %get-tuple-element.794), channel_id=1, source_target_pairs={{0,2},{1,3},{2,0},{3,1},{4,6},{5,7},{6,4},{7,5},{8,10},{9,11},{10,... | collective-permute-start | bytes 221192 | tf_op jit(solution)/shard_map/ppermute | solution.py:278
  (138 other events, 1445.2 us)

commit v3 on v1

--- a/solution.py
+++ b/solution.py
@@ -545,18 +545,24 @@
     )(attended, out_rows)
 
 
-def mixer_forward(normed, cotangent, weights, down):
-    own, width = cotangent[0].shape[1:]
+def mixer(chip, normed, cotangent, weights, down):
+    width, own = normed[0].shape
     units = down.shape[0]
-    tokens = TEAM * own
-
-    def kernel(weights_ref, down_ref, *refs):
-        normed_refs, cotangent_refs = refs[:TEAM], refs[TEAM : TEAM + 2]
-        hidden_ref, grad_ref, chosen, turned, wanted = refs[TEAM + 2 :]
-        position = pl.program_id(0)
-        pick(position, normed_refs, chosen)
-        pick(position, cotangent_refs, wanted)
-        turned[...] = chosen[...].T
+
+    def kernel(first_ref, second_ref, wanted_a, wanted_b, weights_ref, down_ref, *refs):
+        hidden_ref, grad_ref, keep_ref, give_ref, turned, wanted = refs
+        step = pl.program_id(0)
+
+        @pl.when(step == 0)
+        def first():
+            turned[...] = first_ref[...].T
+            wanted[...] = wanted_a[0]
+
+        @pl.when(step == 1)
+        def second():
+            turned[...] = second_ref[...].T
+            wanted[...] = wanted_b[0]
+
         gate = dot(turned[...], weights_ref[:, :units])
         up = dot(turned[...], weights_ref[:, units:])
         logistic = 1.0 / (1.0 + jnp.exp(-gate))
@@ -567,50 +573,71 @@
             grad_hidden * up * (logistic * (1.0 + gate * (1.0 - logistic)))
         ).astype(jnp.bfloat16)
         grad_ref[:, units:] = (grad_hidden * silu).astype(jnp.bfloat16)
-
+        term = dot_rows(weights_ref[...], grad_ref[...])
+
+        @pl.when(step == 0)
+        def keep():
+            keep_ref[...] = term
+
+        @pl.when(step == 1)
+        def give():
+            give_ref[...] = term.astype(jnp.bfloat16)
+
+    block = pl.BlockSpec((1, own, width), lambda p: (chip, 0, 0))
+    whole = pl.BlockSpec((width, own), lambda p: (0, 0))
     return call(
         kernel,
+        (2,),
+        [fixed(normed[0]), fixed(normed[1]), block, block, fixed(weights), fixed(down)],
+        [rows_at(own, units), rows_at(own, 2 * units), whole, whole],
+        [
+            jax.ShapeDtypeStruct((2 * own, units), jnp.bfloat16),
+            jax.ShapeDtypeStruct((2 * own, 2 * units), jnp.bfloat16),
+            jax.ShapeDtypeStruct((width, own), jnp.float32),
+            jax.ShapeDtypeStruct((width, own), jnp.bfloat16),
+        ],
+        [pltpu.VMEM((own, width), jnp.bfloat16), pltpu.VMEM((own, width), jnp.bfloat16)],
+    )(normed[0], normed[1], cotangent[0], cotangent[1], weights, down)
+
+
+def add_block(keep, arrived):
+    def kernel(keep_ref, arrived_ref, out_ref):
+        out_ref[...] = (keep_ref[...] + arrived_ref[...].astype(jnp.float32)).astype(jnp.bfloat16)
+
+    rows = keep.shape[0] // 2
+    part = rows_at(rows, keep.shape[1])
+    return call(
+        kernel, (2,), [part, part], part, jax.ShapeDtypeStruct(keep.shape, jnp.bfloat16)
+    )(keep, arrived)
+
+
+def pair_rows(position, refs, target):
+    own = target.shape[0]
+    for number in range(TEAM):
+
+        @pl.when(position == number)
+        def move():
+            start = number // 4 * own
+            target[...] = refs[number % 4][start : start + own]
+
+
+def mixer_output(hidden, down):
+    own, units = hidden[0].shape[0] // 2, hidden[0].shape[1]
+    specs, shapes = kept_given(own, down.shape[1], 0)
+
+    def kernel(down_ref, *refs):
+        keep_ref, give_ref, chosen = refs[4:]
+        pair_rows(pl.program_id(0), refs[:4], chosen)
+        keep_or_give(pl.program_id(0), keep_ref, give_ref, dot(chosen[...], down_ref[...]))
+
+    return call(
+        kernel,
         (TEAM,),
-        [fixed(weights), fixed(down)]
-        + [fixed(block) for block in normed]
-        + [fixed(block) for block in cotangent],
-        [rows_at(own, units), rows_at(own, 2 * units)],
-        [
-            jax.ShapeDtypeStruct((tokens, units), jnp.bfloat16),
-            jax.ShapeDtypeStruct((tokens, 2 * units), jnp.bfloat16),
-        ],
-        [
-            pltpu.VMEM((width, own), jnp.bfloat16),
-            pltpu.VMEM((own, width), jnp.bfloat16),
-            pltpu.VMEM((own, width), jnp.bfloat16),
-        ],
-    )(weights, down, *normed, *cotangent)
-
-
-def mixer_backward(grads, weights):
-    tokens, columns = grads.shape
-    own = tokens // TEAM
-    specs, shapes = kept_given(weights.shape[0], own, 1)
-
-    def kernel(grads_ref, weights_ref, keep_ref, give_ref):
-        keep_or_give(
-            pl.program_id(0), keep_ref, give_ref, dot_rows(weights_ref[...], grads_ref[...])
-        )
-
-    return call(
-        kernel, (TEAM,), [rows_at(own, columns), fixed(weights)], specs, shapes
-    )(grads, weights)
-
-
-def mixer_output(hidden, down):
-    tokens, units = hidden.shape
-    own = tokens // TEAM
-    specs, shapes = kept_given(own, down.shape[1], 0)
-
-    def kernel(hidden_ref, down_ref, keep_ref, give_ref):
-        keep_or_give(pl.program_id(0), keep_ref, give_ref, dot(hidden_ref[...], down_ref[...]))
-
-    return call(kernel, (TEAM,), [rows_at(own, units), fixed(down)], specs, shapes)(hidden, down)
+        [fixed(down)] + [fixed(block) for block in hidden],
+        specs,
+        shapes,
+        [pltpu.VMEM((own, units), jnp.bfloat16)],
+    )(down, *hidden)
 
 
 def write_teams(places_ref, total, out_ref, teams):
@@ -621,14 +648,16 @@
         out_ref[pl.ds(steps, 1)] = block[None]
 
 
-def token_product(grid, lefts, right, by_rows, width):
-    own = right.shape[0] // TEAM
-    rows = lefts[0].shape[0] if by_rows else lefts.shape[1]
+def token_product(grid, lefts, rights):
+    rows, own = lefts[0].shape
+    width = rights[0].shape[1]
     teams = grid.teams
 
-    def kernel(places_ref, right_ref, *refs):
-        sources, (out_ref, total) = refs[:-2], refs[-2:]
+    def kernel(places_ref, *refs):
+        left_refs, right_refs = refs[:TEAM], refs[TEAM : TEAM + 4]
+        out_ref, total, chosen = refs[TEAM + 4 :]
         position = pl.program_id(0)
+        pair_rows(position, right_refs, chosen)
 
         def add(value):
             @pl.when(position == 0)
@@ -639,11 +668,11 @@
             def later():
                 total[...] += value
 
-        for number, source in enumerate(sources):
+        for number, source in enumerate(left_refs):
 
             @pl.when(position == number)
             def block():
-                add(dot(source[...], right_ref[...]))
+                add(dot(source[...], chosen[...]))
 
         @pl.when(position == TEAM - 1)
         def last():
@@ -652,24 +681,25 @@
     return call(
         kernel,
         (TEAM,),
-        [rows_at(own, width)] + [fixed(left) for left in lefts],
+        [fixed(block) for block in list(lefts) + list(rights)],
         pl.BlockSpec((teams, rows // teams, width), lambda p, *unused: (0, 0, 0)),
         jax.ShapeDtypeStruct((teams, rows // teams, width), jnp.bfloat16),
-        [pltpu.VMEM((rows, width), jnp.float32)],
+        [pltpu.VMEM((rows, width), jnp.float32), pltpu.VMEM((own, width), jnp.bfloat16)],
         prefetch=1,
-    )(grid.places(), right, *lefts)
+    )(grid.places(), *lefts, *rights)
 
 
 def down_product(grid, hidden, cotangent):
-    tokens, units = hidden.shape
+    units = hidden[0].shape[1]
     own, width = cotangent[0].shape[1:]
     teams = grid.teams
 
-    def kernel(places_ref, hidden_ref, *refs):
-        sources, (out_ref, total, wanted) = refs[:2], refs[2:]
+    def kernel(places_ref, *refs):
+        hidden_refs, sources, (out_ref, total, wanted, chosen) = refs[:4], refs[4:6], refs[6:]
         position = pl.program_id(0)
         pick(position, sources, wanted)
-        value = dot(hidden_ref[...].T, wanted[...])
+        pair_rows(position, hidden_refs, chosen)
+        value = dot(chosen[...].T, wanted[...])
 
         @pl.when(position == 0)
         def first():
@@ -686,12 +716,16 @@
     return call(
         kernel,
         (TEAM,),
-        [rows_at(own, units)] + [fixed(block) for block in cotangent],
+        [fixed(block) for block in list(hidden) + list(cotangent)],
         pl.BlockSpec((teams, units // teams, width), lambda p, *unused: (0, 0, 0)),
         jax.ShapeDtypeStruct((teams, units // teams, width), jnp.bfloat16),
-        [pltpu.VMEM((units, width), jnp.float32), pltpu.VMEM((own, width), jnp.bfloat16)],
+        [
+            pltpu.VMEM((units, width), jnp.float32),
+            pltpu.VMEM((own, width), jnp.bfloat16),
+            pltpu.VMEM((own, units), jnp.bfloat16),
+        ],
         prefetch=1,
-    )(grid.places(), hidden, *cotangent)
+    )(grid.places(), *hidden, *cotangent)
 
 
 def project_out_back(grid, grads, out_rows, attended):
@@ -1047,76 +1081,102 @@
     attn_w = place_rows(grid, attn_z, 0, attn_wide).reshape(width, attn_wide)
     attn_w, inputs_team, out_own = order.step(attn_w, inputs_team, out_own)
 
+    out_own, cotangent = order.step(out_own, cotangent)
     out_z = grid.spread(out_own)
+    cotangent_chips = [cotangent, grid.turn(cotangent, 2), grid.turn(cotangent, 4)]
     normed_first, queries, own_piece = project(inputs_team, attn_w, cosine, sine_table)
-    own_piece, out_z, cotangent, attn_w = order.step(own_piece, out_z, cotangent, attn_w)
+    own_piece, out_z, attn_w = order.step(own_piece, out_z, attn_w)
     arrived = [grid.shift(own_piece, step, False) for step in range(1, steps_back + 1)]
-    cotangent_chips = grid.chips(cotangent)
+    cotangent_chips = order.step(cotangent_chips)
+    cotangent_chips = cotangent_chips + [grid.turn(cotangent_chips[0], 6)]
     out_rows = place_rows(grid, [block[None] for block in out_z], 0, width)
     out_rows = out_rows.reshape(Q_WIDTH, width)
     gain_first = attn_w[:, LINED : LINED + 1].astype(f32)
     gain_second = attn_w[:, LINED + 1 : LINED + 2].astype(f32)
     mixer_own = jnp.concatenate([team_rows[..., attn_wide:], down_thirds], axis=-1)
-    arrived, out_rows, gain_first, gain_second, mixer_own = order.step(
-        arrived, out_rows, gain_first, gain_second, mixer_own
+    arrived, gain_first, gain_second, mixer_own, out_rows = order.step(
+        arrived, gain_first, gain_second, mixer_own, out_rows
     )
 
     mixer_hops = [grid.both_ways(mixer_own, mixer_own)]
 
     def next_hop():
-        mixer_hops[-1] = order.step(mixer_hops[-1])
         if len(mixer_hops) < teams - 1:
             mixer_hops.append(grid.both_ways(*mixer_hops[-1]))
 
     pieces = [own_piece] + arrived
     attended, normalizer = attend(low, starts, queries, pieces, 0, OWN_KV)
     keep, give = project_out(attended, out_rows)
-    give, cotangent_chips, mixer_hops[0] = order.step(give, cotangent_chips, mixer_hops[0])
+    give, mixer_hops[0], cotangent_chips = order.step(give, mixer_hops[0], cotangent_chips)
     other = grid.turn(give, 1)
-    if len(mixer_hops) < teams - 1:
-        mixer_hops.append(grid.both_ways(*mixer_hops[-1]))
-    other = order.step(other)
+    next_hop()
+    cotangent_stack = jnp.stack(cotangent_chips)
+    other, cotangent_stack = order.step(other, cotangent_stack)
+    cotangent_other = grid.turn(cotangent_stack, 1)
     total, blocks = combine(keep, other, 1)
-    blocks = order.step(blocks)
-    terms = grid.send_chips(blocks)
-    cotangent_stack = order.step(jnp.stack(cotangent_chips))
-    terms, mixer_hops[-1] = order.step(terms, mixer_hops[-1])
-    if len(mixer_hops) < teams - 1:
-        mixer_hops.append(grid.both_ways(*mixer_hops[-1]))
-    cotangent_other = grid.turn(cotangent_stack, 1)
+    blocks, cotangent_other = order.step(blocks, cotangent_other)
+    cotangent_team = [cotangent_stack, cotangent_other]
+    near = [grid.turn(blocks[0], 2), grid.turn(blocks[1], 4)]
+    near, far, mixer_hops[-1] = order.step(near, blocks[2], mixer_hops[-1])
+    terms = near + [grid.turn(far, 6)]
+    next_hop()
+    terms = order.step(terms)
     middle, normed_second = finish_middle([total] + terms, inputs_t, gain_second)
-    normed_second, cotangent_other = order.step(normed_second, cotangent_other)
-    cotangent_team = [cotangent_stack, cotangent_other]
-    second_chips = grid.chips(normed_second)
+    normed_second, mixer_hops[-1] = order.step(normed_second, mixer_hops[-1])
     while len(mixer_hops) < teams - 1:
         next_hop()
-    second_chips, mixer_hops[-1] = order.step(second_chips, mixer_hops[-1])
-    second_team = grid.gather_team(second_chips)
+        mixer_hops[-1] = order.step(mixer_hops[-1])
+    second_chips = [normed_second, grid.turn(normed_second, 2), grid.turn(normed_second, 4)]
+    second_other = [grid.turn(normed_second, 1)]
     mixer_w, down_w = place_mixer(grid, mixer_own, mixer_hops, units, unit_rows)
     mixer_w = mixer_w.reshape(width, 2 * units)
     down_w = down_w.reshape(units, width)
-    mixer_w, down_w, second_team = order.step(mixer_w, down_w, second_team)
-
+    mixer_w, down_w, second_other[0] = order.step(mixer_w, down_w, second_other[0])
+
+    def send_teams(product, first=1, last=teams):
+        return [grid.shift(product[steps], steps) for steps in range(first, last)]
+
+    def run_mixer(other_chip):
+        hidden_part, grads_part, keep, give = mixer(
+            other_chip,
+            (second_chips[other_chip], second_other[other_chip]),
+            cotangent_team,
+            mixer_w,
+            down_w,
+        )
+        return hidden_part, grads_part, keep, order.step(give)
+
+    parts = [run_mixer(0)]
+    passed = [grid.turn(parts[0][3], 1)]
+    second_chips = order.step(second_chips)
+    second_chips = second_chips + [grid.turn(second_chips[0], 6)]
+    second_other += order.step([grid.turn(second_chips[1], 1), grid.turn(second_chips[2], 1)])
+    parts.append(run_mixer(1))
+    passed.append(grid.turn(parts[1][3], 1))
+    second_chips[3], passed[0] = order.step(second_chips[3], passed[0])
+    second_other.append(grid.turn(second_chips[3], 1))
+    parts.append(run_mixer(2))
+    passed[1], second_other[3] = order.step(passed[1], second_other[3])
+    block = order.step(add_block(parts[1][2], passed[1]))
+    terms = [parts[0][2], passed[0], grid.turn(block, 2)]
+    passed.append(grid.turn(parts[2][3], 1))
+    parts.append(run_mixer(3))
+    passed[2] = order.step(passed[2])
+    passed.append(grid.turn(parts[3][3], 1))
+    block = order.step(add_block(parts[2][2], passed[2]))
+    terms.append(grid.turn(block, 4))
+    passed[3] = order.step(passed[3])
+    hidden, grads = [part[0] for part in parts], [part[1] for part in parts]
+    block, grads, hidden = order.step(add_block(parts[3][2], passed[3]), grads, hidden)
+    terms.append(grid.turn(block, 6))
+    second_team = second_chips + second_other
     early = max(1, teams // 2)
-
-    def send_teams(product, first, last):
-        return [grid.shift(product[steps], steps) for steps in range(first, last)]
-
-    hidden, grads = mixer_forward(second_team, cotangent_team, mixer_w, down_w)
-    keep, give = mixer_backward(grads, mixer_w)
-    give, grads = order.step(give, grads)
-    other = order.step(grid.turn(give, 1))
-    total, blocks = combine(keep, other, 1)
-    blocks, hidden, grads = order.step(blocks, hidden, grads)
-    terms = grid.send_chips(blocks)
-    mixer_part = token_product(grid, second_team, grads, True, 2 * units)
+    mixer_part = token_product(grid, second_team, grads)
     mixer_part, hidden = order.step(mixer_part, hidden)
     mixer_parts = send_teams(mixer_part, 1, early + 1)
     down_part = down_product(grid, hidden, cotangent_team)
     terms, down_part = order.step(terms, down_part)
-    grad_middle, grad_attn, second_part = finish_second(
-        [total] + terms, middle, cotangent, gain_second
-    )
+    grad_middle, grad_attn, second_part = finish_second(terms, middle, cotangent, gain_second)
     grad_attn, hidden = order.step(grad_attn, hidden)
     attn_chips = grid.chips(grad_attn)
     out_keep, out_give = mixer_output(hidden, down_w)

time: 651 us -> 638 us (0.980)
  waiting for transfers between devices: 219 us -> 185 us
  Pallas kernels: 258 us -> 280 us
    ppermute x29, waiting for transfers between devices: 118 us -> 81.9 us  [shift(): return lax.ppermute(value, 'dev', pairs)]
    pallas_call x5 -> x10, Pallas kernels: 75.7 us -> 104 us  [the longest x4 42.8 us: mixer(): call(kernel, (2,), [fixed(normed[0]), fixed(normed[1]), block, block, fix...]
    pallas_call x4 -> x3, Pallas kernels: 27.1 us -> 20.5 us  [combine(): call(kernel, (4,), [part, part], [whole] * 4, [jax.ShapeDtypeStruct(shape...]
    ppermute x60 -> x63, waiting for transfers between devices: 97.6 us -> 100 us  [turn(): lax.ppermute(value, 'dev', [(d, d ^ bits) for d in range(self.count)])]
    ppermute x60 -> x63, starting transfers between devices: 45.9 us -> 47.9 us  [turn(): lax.ppermute(value, 'dev', [(d, d ^ bits) for d in range(self.count)])]
    unnamed x143 -> x155, local copies, waits for them, and re-layouts: 14.6 us -> 13.7 us
  transfers between devices with their start and end apart: 91 -> 94, of which waited for: 33 -> 38; matrix products, arithmetic and copies ran while one was open for 5% -> 5% of each run, Pallas kernels for 30% -> 42%
where the time goes in v3:
time: 638 us; the launch traced here: 625 us
  Pallas kernels  280 us (44%)
  waiting for transfers between devices  185 us (29%)
  starting transfers between devices  112 us (18%)
  local copies, waits for them, and re-layouts  34.4 us (5%)
  other arithmetic  11 us (2%)
    ppermute x63, waiting for transfers between devices, turn(): lax.ppermute(value, 'dev', [(d, d ^ bits) for d in range(self.count)])  100 us
    ppermute x29, waiting for transfers between devices, shift(): return lax.ppermute(value, 'dev', pairs)  81.9 us
    ppermute x29, starting transfers between devices, shift(): return lax.ppermute(value, 'dev', pairs)  59.9 us
    ppermute x63, starting transfers between devices, turn(): lax.ppermute(value, 'dev', [(d, d ^ bits) for d in range(self.count)])  47.9 us
    pallas_call x4, Pallas kernels, mixer(): call(kernel, (2,), [fixed(normed[0]), fixed(normed[1]), block, block, fix...  42.8 us
    pallas_call x1, Pallas kernels, attend_back(): pl.pallas_call(gradient_kernel, grid=(count,), in_specs=[low_spec, whole,...  30.7 us
    pallas_call x1, Pallas kernels, token_product(): call(kernel, (TEAM,), [fixed(block) for block in list(lefts) + list(right...  30.3 us
    pallas_call x1, Pallas kernels, attend(): pl.pallas_call(attend_kernel, grid=(count,), in_specs=[low_spec, whole, h...  24.6 us
  transfers between devices with their start and end apart: 94, of which 38 were waited for; matrix products, arithmetic and copies ran while one was open for 5% of the time, Pallas kernels for 42%

profile of v3, /device:TPU:10, one launch (start us, length us, event | category | flops | bytes accessed | tf_op | source)
XLA Modules:
  0.0 625.4 jit_solution(443807192342507922)
XLA Ops:
  21.1 3.6 fusion
  24.6 12.7 %collective-permute-done.4 = bf16[2,48,1536]{2,1,0:T(8,128)(2,1)S(1)} collective-permute-done((bf16[2,48,1536]{2,1,0:T(8,128)(2,1)}, bf16[2,48,1536]{2,1,0:T(8,128)(2,1)S(1)}, u32[]{:S(2)}, u32[]{:S(2)}) %collective-permute-start.4) | collective-permute-done | bytes 294944 | tf_op jit(solution)/shard_map/ppermute | solution.py:267
  37.4 3.7 collective-permute-done.5
  49.8 14.1 %collective-permute-done.13.refs_3_ = bf16[1536,256]{1,0:T(8,128)(2,1)} collective-permute-done((bf16[1536,256]{1,0:T(8,128)(2,1)S(1)}, bf16[1536,256]{1,0:T(8,128)(2,1)}, u32[]{:S(2)}, u32[]{:S(2)}) %collective-permute-start.13) | collective-permute-done | bytes 786464 | tf_op jit(solution)/shard_map/ppermute | solution.py:267
  63.9 9.1 %collective-permute-done.10.refs_1_ = bf16[8,48,512]{2,1,0:T(8,128)(2,1)S(1)} collective-permute-done((bf16[8,48,512]{2,1,0:T(8,128)(2,1)S(1)}, bf16[8,48,512]{2,1,0:T(8,128)(2,1)S(1)}, u32[]{:S(2)}, u32[]{:S(2)}) %collective-permute-start.10) | collective-permute-done | bytes 393248 | tf_op jit(solution)/shard_map/ppermute | solution.py:275
  73.0 7.6 %collective-permute-done.11.refs_2_ = bf16[8,48,512]{2,1,0:T(8,128)(2,1)S(1)} collective-permute-done((bf16[8,48,512]{2,1,0:T(8,128)(2,1)S(1)}, bf16[8,48,512]{2,1,0:T(8,128)(2,1)S(1)}, u32[]{:S(2)}, u32[]{:S(2)}) %collective-permute-start.11) | collective-permute-done | bytes 393248 | tf_op jit(solution)/shard_map/ppermute | solution.py:275
  85.8 4.0 shard_map.212
  100.2 11.8 %shard_map.213 = (bf16[1536,2048]{1,0:T(8,128)(2,1)}, bf16[2,96,2048]{2,1,0:T(8,128)(2,1)}, bf16[2,1,96,2048]{3,2,1,0:T(8,128)(2,1)}) custom-call(bf16[1536,512]{1,0:T(8,128)(2,1)} %bitcast.184, f32[96,2048]{1,0:T(8,128)} %get-tuple-element.322.cosine_ref, f32[96,2048]{1,0:T(8,128)} %get-tuple-element.323.sine_ref, bf16[1536,256]{1,0:T(8,128)(2,1)} %bitcast.191, ...), custom_call_target="tpu_custom_call" | custom-call | flops 1000 | bytes 1000 | tf_op jit(solution)/shard_map/pallas_call | solution.py:500
  115.0 3.4 shard_map.214
  119.7 12.9 %collective-permute-done.24.refs_1_ = bf16[2,1,96,2048]{3,2,1,0:T(8,128)(2,1)S(1)} collective-permute-done((bf16[2,1,96,2048]{3,2,1,0:T(8,128)(2,1)}, bf16[2,1,96,2048]{3,2,1,0:T(8,128)(2,1)S(1)}, u32[]{:S(2)}, u32[]{:S(2)}) %collective-permute-start.24) | collective-permute-done | bytes 786464 | tf_op jit(solution)/shard_map/ppermute | solution.py:275
  134.8 3.7 collective-permute-start.26
  140.7 24.6 %shard_map.215 = (f32[2,96,2048]{2,1,0:T(8,128)}, f32[2,1,2048]{2,1,0:T(1,128)}) custom-call(s32[9]{0:T(128)} %pad_add_fusion.1.low_ref, s32[1,2048]{1,0:T(1,128)} %bitcast.233, bf16[2,96,2048]{2,1,0:T(8,128)(2,1)} %get-tuple-element.348.query_ref, bf16[2,1,96,2048]{3,2,1,0:T(8,128)(2,1)} %get-tuple-element.337.refs_0_, bf16[2,1,96,2048]{3,2,1,0:T(8,128)(2,1)} %copy-done.7), custom_call_target="tpu_custom_call" | custom-call | flops 1000 | bytes 1000 | tf_op jit(solution)/shard_map/pallas_call | solution.py:195
  165.3 9.4 %shard_map.216 = (f32[1536,1024]{1,0:T(8,128)}, bf16[1536,1024]{1,0:T(8,128)(2,1)}) custom-call(f32[2,96,2048]{2,1,0:T(8,128)} %get-tuple-element.350.attended_ref.out_ref, bf16[192,1536]{1,0:T(8,128)(2,1)} %bitcast.194), custom_call_target="tpu_custom_call" | custom-call | flops 1000 | bytes 1000 | tf_op jit(solution)/shard_map/pallas_call | solution.py:538
  176.7 4.1 collective-permute-done.28.arrived_ref
  182.8 4.9 collective-permute-start.33
  187.8 6.8 %shard_map.217 = (f32[1536,256]{1,0:T(8,128)}, bf16[1536,256]{1,0:T(8,128)(2,1)}, bf16[1536,256]{1,0:T(8,128)(2,1)}, bf16[1536,256]{1,0:T(8,128)(2,1)}) custom-call(f32[1536,1024]{1,0:T(8,128)} %get-tuple-element.364.keep_ref, bf16[1536,1024]{1,0:T(8,128)(2,1)} %collective-permute-done.28.arrived_ref), custom_call_target="tpu_custom_call" | custom-call | flops 1000 | bytes 1000 | tf_op jit(solution)/shard_map/pallas_call | solution.py:861
  195.9 15.3 %collective-permute-done.32.refs_3_ = bf16[8,48,1536]{2,1,0:T(8,128)(2,1)} collective-permute-done((bf16[8,48,1536]{2,1,0:T(8,128)(2,1)S(1)}, bf16[8,48,1536]{2,1,0:T(8,128)(2,1)}, u32[]{:S(2)}, u32[]{:S(2)}) %collective-permute-start.32) | collective-permute-done | bytes 1179680 | tf_op jit(solution)/shard_map/ppermute | solution.py:275
  216.1 4.0 collective-permute-start.36
  221.6 17.5 %collective-permute-done.34.refs_3_ = bf16[1536,256]{1,0:T(8,128)(2,1)S(1)} collective-permute-done((bf16[1536,256]{1,0:T(8,128)(2,1)}, bf16[1536,256]{1,0:T(8,128)(2,1)S(1)}, u32[]{:S(2)}, u32[]{:S(2)}) %collective-permute-start.34) | collective-permute-done | bytes 786464 | tf_op jit(solution)/shard_map/ppermute | solution.py:267
  240.0 4.7 shard_map.218
  246.6 6.7 %shard_map.219 = (bf16[4,8,48,1024]{3,2,1,0:T(8,128)(2,1)}, bf16[4,128,1536]{2,1,0:T(8,128)(2,1)}) custom-call(s32[2]{0:T(128)} %pad_add_fusion.2.places_ref, bf16[8,48,1536]{2,1,0:T(8,128)(2,1)} %copy-done.5, bf16[8,48,1536]{2,1,0:T(8,128)(2,1)} %copy-done.23, bf16[8,48,1536]{2,1,0:T(8,128)(2,1)} %collective-permute-done.26.refs_2_, ...), custom_call_target="tpu_custom_call" | custom-call | flops 1000 | bytes 1000 | tf_op jit(solution)/shard_map/pallas_call | solution.py:447
  254.2 10.6 %shard_map.220 = (bf16[512,512]{1,0:T(8,128)(2,1)}, bf16[512,1024]{1,0:T(8,128)(2,1)}, f32[1536,256]{1,0:T(8,128)}, bf16[1536,256]{1,0:T(8,128)(2,1)}) custom-call(bf16[1536,256]{1,0:T(8,128)(2,1)} %get-tuple-element.409.first_ref.refs_0_, bf16[1536,256]{1,0:T(8,128)(2,1)} %copy-done.14, bf16[4,256,1536]{2,1,0:T(8,128)(2,1)} %copy-done, ...), custom_call_target="tpu_custom_call" | custom-call | flops 1000 | bytes 1000 | tf_op jit(solution)/shard_map/pallas_call | solution.py:588
  269.6 10.9 %shard_map.221 = (bf16[512,512]{1,0:T(8,128)(2,1)}, bf16[512,1024]{1,0:T(8,128)(2,1)}, f32[1536,256]{1,0:T(8,128)}, bf16[1536,256]{1,0:T(8,128)(2,1)}) custom-call(bf16[1536,256]{1,0:T(8,128)(2,1)} %copy-done.15, bf16[1536,256]{1,0:T(8,128)(2,1)} %copy-done.17, bf16[4,256,1536]{2,1,0:T(8,128)(2,1)} %copy-done, bf16[4,256,1536]{2,1,0:T(8,128)(2,1)} %copy-done.1, ...), custom_call_target="tpu_custom_call" | custom-call | flops 1000 | bytes 1000 | tf_op jit(solution)/shard_map/pallas_call | solution.py:588
  280.6 6.5 %collective-permute-done.42.first_ref.refs_3_ = bf16[1536,256]{1,0:T(8,128)(2,1)S(1)} collective-permute-done((bf16[1536,256]{1,0:T(8,128)(2,1)S(1)}, bf16[1536,256]{1,0:T(8,128)(2,1)S(1)}, u32[]{:S(2)}, u32[]{:S(2)}) %collective-permute-start.42) | collective-permute-done | bytes 786464 | tf_op jit(solution)/shard_map/ppermute | solution.py:267
  287.7 10.6 %shard_map.222 = (bf16[512,512]{1,0:T(8,128)(2,1)}, bf16[512,1024]{1,0:T(8,128)(2,1)}, f32[1536,256]{1,0:T(8,128)}, bf16[1536,256]{1,0:T(8,128)(2,1)}) custom-call(bf16[1536,256]{1,0:T(8,128)(2,1)} %copy-done.16, bf16[1536,256]{1,0:T(8,128)(2,1)} %copy-done.18, bf16[4,256,1536]{2,1,0:T(8,128)(2,1)} %copy-done, bf16[4,256,1536]{2,1,0:T(8,128)(2,1)} %copy-done.1, ...), custom_call_target="tpu_custom_call" | custom-call | flops 1000 | bytes 1000 | tf_op jit(solution)/shard_map/pallas_call | solution.py:588
  299.3 10.6 %shard_map.224 = (bf16[512,512]{1,0:T(8,128)(2,1)}, bf16[512,1024]{1,0:T(8,128)(2,1)}, f32[1536,256]{1,0:T(8,128)}, bf16[1536,256]{1,0:T(8,128)(2,1)}) custom-call(bf16[1536,256]{1,0:T(8,128)(2,1)} %copy-done.19, bf16[1536,256]{1,0:T(8,128)(2,1)} %copy-done.20, bf16[4,256,1536]{2,1,0:T(8,128)(2,1)} %copy-done, bf16[4,256,1536]{2,1,0:T(8,128)(2,1)} %copy-done.1, ...), custom_call_target="tpu_custom_call" | custom-call | flops 1000 | bytes 1000 | tf_op jit(solution)/shard_map/pallas_call | solution.py:588
  323.2 30.3 %shard_map.227.own_ref = bf16[4,384,1024]{2,1,0:T(8,128)(2,1)} custom-call(s32[2]{0:T(128)} %pad_add_fusion.2.places_ref, bf16[1536,256]{1,0:T(8,128)(2,1)} %get-tuple-element.409.first_ref.refs_0_, bf16[1536,256]{1,0:T(8,128)(2,1)} %copy-done.15, bf16[1536,256]{1,0:T(8,128)(2,1)} %copy-done.16, bf16[1536,256]{1,0:T(8,128)(2,1)} %copy-done.19, ...), custom_call_target="tpu_custom_call" | custom-call | flops 1000 | bytes 1000 | tf_op jit(solution)/shard_map/pallas_call | solution.py:681
  355.4 4.1 collective-permute-start.55
  359.5 13.8 %shard_map.228.own_ref = bf16[4,128,1536]{2,1,0:T(8,128)(2,1)} custom-call(s32[2]{0:T(128)} %pad_add_fusion.2.places_ref, bf16[512,512]{1,0:T(8,128)(2,1)} %get-tuple-element.470.refs_0_, bf16[512,512]{1,0:T(8,128)(2,1)} %get-tuple-element.471.refs_1_, bf16[512,512]{1,0:T(8,128)(2,1)} %get-tuple-element.472.refs_2_, ...), custom_call_target="tpu_custom_call" | custom-call | flops 1000 | bytes 1000 | tf_op jit(solution)/shard_map/pallas_call | solution.py:716
  374.8 6.2 shard_map.229
  384.5 10.0 %shard_map.230 = (f32[1024,1536]{1,0:T(8,128)}, bf16[1024,1536]{1,0:T(8,128)(2,1)}) custom-call(bf16[512,1536]{1,0:T(8,128)(2,1)} %bitcast.183, bf16[512,512]{1,0:T(8,128)(2,1)} %get-tuple-element.470.refs_0_, bf16[512,512]{1,0:T(8,128)(2,1)} %get-tuple-element.471.refs_1_, bf16[512,512]{1,0:T(8,128)(2,1)} %get-tuple-element.472.refs_2_, ...), custom_call_target="tpu_custom_call" | custom-call | flops 1000 | bytes 1000 | tf_op jit(solution)/shard_map/pallas_call | solution.py:633
  394.5 11.0 %collective-permute-done.55.refs_1_ = bf16[384,1024]{1,0:T(8,128)(2,1)S(1)} collective-permute-done((bf16[384,1024]{1,0:T(8,128)(2,1)S(1)}, bf16[384,1024]{1,0:T(8,128)(2,1)S(1)}, u32[]{:S(2)}, u32[]{:S(2)}) %collective-permute-start.55) | collective-permute-done | bytes 786464 | tf_op jit(solution)/shard_map/ppermute | solution.py:275
  405.5 11.1 %collective-permute-done.52.refs_2_ = bf16[1536,256]{1,0:T(8,128)(2,1)S(1)} collective-permute-done((bf16[1536,256]{1,0:T(8,128)(2,1)}, bf16[1536,256]{1,0:T(8,128)(2,1)S(1)}, u32[]{:S(2)}, u32[]{:S(2)}) %collective-permute-start.52) | collective-permute-done | bytes 786464 | tf_op jit(solution)/shard_map/ppermute | solution.py:267
  423.3 11.3 %shard_map.231 = (bf16[2,96,2048]{2,1,0:T(8,128)(2,1)}, bf16[4,48,1536]{2,1,0:T(8,128)(2,1)}) custom-call(s32[2]{0:T(128)} %pad_add_fusion.2.places_ref, bf16[192,1536]{1,0:T(8,128)(2,1)} %bitcast.195, f32[2,96,2048]{2,1,0:T(8,128)} %get-tuple-element.350.attended_ref.out_ref, bf16[1536,256]{1,0:T(8,128)(2,1)} %get-tuple-element.482.refs_0_, ...), custom_call_target="tpu_custom_call" | custom-call | flops 1000 | bytes 1000 | tf_op jit(solution)/shard_map/pallas_call | solution.py:763
  439.1 30.7 %shard_map.232 = (f32[2,96,2048]{2,1,0:T(8,128)}, f32[2,1,96,2048]{3,2,1,0:T(8,128)}, bf16[1,2,1,96,2048]{4,3,2,1,0:T(8,128)(2,1)}) custom-call(s32[9]{0:T(128)} %pad_add_fusion.1.low_ref, s32[1,2048]{1,0:T(1,128)} %bitcast.234, bf16[2,96,2048]{2,1,0:T(8,128)(2,1)} %get-tuple-element.348.query_ref, bf16[2,96,2048]{2,1,0:T(8,128)(2,1)} %get-tuple-element.494.grad_ref, ...), custom_call_target="tpu_custom_call" | custom-call | flops 1000 | bytes 1000 | tf_op jit(solution)/shard_map/pallas_call | solution.py:221
  474.0 6.8 %shard_map.233 = (f32[256,1536]{1,0:T(8,128)}, bf16[256,1536]{1,0:T(8,128)(2,1)}, bf16[256,1536]{1,0:T(8,128)(2,1)}, bf16[256,1536]{1,0:T(8,128)(2,1)}) custom-call(f32[1024,1536]{1,0:T(8,128)} %get-tuple-element.501.keep_ref, bf16[1024,1536]{1,0:T(8,128)(2,1)} %copy-done.9), custom_call_target="tpu_custom_call" | custom-call | flops 1000 | bytes 1000 | tf_op jit(solution)/shard_map/pallas_call | solution.py:861
  487.6 9.7 %collective-permute-done.62.refs_1_ = bf16[2,1,96,2048]{3,2,1,0:T(8,128)(2,1)S(1)} collective-permute-done((bf16[2,1,96,2048]{3,2,1,0:T(8,128)(2,1)}, bf16[2,1,96,2048]{3,2,1,0:T(8,128)(2,1)S(1)}, u32[]{:S(2)}, u32[]{:S(2)}) %collective-permute-start.62) | collective-permute-done | bytes 786464 | tf_op jit(solution)/shard_map/ppermute | solution.py:275
  498.3 23.6 %shard_map.235 = (f32[1536,1024]{1,0:T(8,128)}, bf16[1536,1024]{1,0:T(8,128)(2,1)}, bf16[4,384,384]{2,1,0:T(8,128)(2,1)}) custom-call(s32[2]{0:T(128)} %pad_add_fusion.2.places_ref, bf16[1536,2048]{1,0:T(8,128)(2,1)} %get-tuple-element.513.normed_ref, f32[2,96,2048]{2,1,0:T(8,128)} %get-tuple-element.514.query_ref, ...), custom_call_target="tpu_custom_call" | custom-call | flops 1000 | bytes 1000 | tf_op jit(solution)/shard_map/pallas_call | solution.py:823
  522.0 5.9 collective-permute-done.69.arrived_ref
  529.6 6.9 %shard_map.236 = (f32[1536,256]{1,0:T(8,128)}, bf16[1536,256]{1,0:T(8,128)(2,1)}, bf16[1536,256]{1,0:T(8,128)(2,1)}, bf16[1536,256]{1,0:T(8,128)(2,1)}) custom-call(f32[1536,1024]{1,0:T(8,128)} %get-tuple-element.525.keep_ref, bf16[1536,1024]{1,0:T(8,128)(2,1)} %copy-done.10), custom_call_target="tpu_custom_call" | custom-call | flops 1000 | bytes 1000 | tf_op jit(solution)/shard_map/pallas_call | solution.py:861
  541.0 3.3 collective-permute-start.71
  547.0 4.1 shard_map.237
  551.2 8.7 %collective-permute-done.71.refs_1_ = bf16[384,384]{1,0:T(8,128)(2,1)} collective-permute-done((bf16[384,384]{1,0:T(8,128)(2,1)}, bf16[384,384]{1,0:T(8,128)(2,1)}, u32[]{:S(2)}, u32[]{:S(2)}) %collective-permute-start.71) | collective-permute-done | bytes 294944 | tf_op jit(solution)/shard_map/ppermute | solution.py:275
  559.9 4.8 collective-permute-start.76
  567.9 6.3 %collective-permute-done.74.refs_2_ = bf16[1536,256]{1,0:T(8,128)(2,1)S(1)} collective-permute-done((bf16[1536,256]{1,0:T(8,128)(2,1)}, bf16[1536,256]{1,0:T(8,128)(2,1)S(1)}, u32[]{:S(2)}, u32[]{:S(2)}) %collective-permute-start.74) | collective-permute-done | bytes 786464 | tf_op jit(solution)/shard_map/ppermute | solution.py:267
  576.1 5.5 shard_map.239
  595.4 4.6 collective-permute-done.85
  604.9 3.4 collective-permute-start.91
  (405 shorter events, 166.6 us)
Async XLA Ops:
  10.5 32.1 %collective-permute-start.7 = (bf16[1536,256]{1,0:T(8,128)(2,1)S(1)}, bf16[1536,256]{1,0:T(8,128)(2,1)}, u32[]{:S(2)}, u32[]{:S(2)}) collective-permute-start(bf16[1536,256]{1,0:T(8,128)(2,1)S(1)} %bitcast.187), channel_id=1, source_target_pairs={{0,2},{1,3},{2,0},{3,1},{4,6},{5,7},{6,4},{7,5},{8,10},{9,11},{10,... | collective-permute-start | bytes 2359304 | tf_op jit(solution)/shard_map/ppermute | solution.py:267
  11.1 31.5 %collective-permute-start.8 = (bf16[1536,256]{1,0:T(8,128)(2,1)S(1)}, bf16[1536,256]{1,0:T(8,128)(2,1)}, u32[]{:S(2)}, u32[]{:S(2)}) collective-permute-start(bf16[1536,256]{1,0:T(8,128)(2,1)S(1)} %bitcast.188), channel_id=1, source_target_pairs={{0,4},{1,5},{2,6},{3,7},{4,0},{5,1},{6,2},{7,3},{8,12},{9,13},{10,... | collective-permute-start | bytes 2359304 | tf_op jit(solution)/shard_map/ppermute | solution.py:267
  14.7 22.7 %collective-permute-start.4 = (bf16[2,48,1536]{2,1,0:T(8,128)(2,1)}, bf16[2,48,1536]{2,1,0:T(8,128)(2,1)S(1)}, u32[]{:S(2)}, u32[]{:S(2)}) collective-permute-start(bf16[2,48,1536]{2,1,0:T(8,128)(2,1)} %get-tuple-element.600), channel_id=1, source_target_pairs={{0,2},{1,3},{2,0},{3,1},{4,6},{5,7},{6,4},{7,5},{8,10},{9,11},{10,... | collective-permute-start | bytes 884744 | tf_op jit(solution)/shard_map/ppermute | solution.py:267
  16.2 24.8 %collective-permute-start.5 = (bf16[2,48,1536]{2,1,0:T(8,128)(2,1)}, bf16[2,48,1536]{2,1,0:T(8,128)(2,1)S(1)}, u32[]{:S(2)}, u32[]{:S(2)}) collective-permute-start(bf16[2,48,1536]{2,1,0:T(8,128)(2,1)} %get-tuple-element.599), channel_id=1, source_target_pairs={{0,4},{1,5},{2,6},{3,7},{4,0},{5,1},{6,2},{7,3},{8,12},{9,13},{10,... | collective-permute-start | bytes 884744 | tf_op jit(solution)/shard_map/ppermute | solution.py:267
  18.0 24.6 %collective-permute-start.6 = (bf16[2,48,1536]{2,1,0:T(8,128)(2,1)S(1)}, bf16[2,48,1536]{2,1,0:T(8,128)(2,1)S(1)}, u32[]{:S(2)}, u32[]{:S(2)}) collective-permute-start(bf16[2,48,1536]{2,1,0:T(8,128)(2,1)S(1)} %get-tuple-element.598), channel_id=1, source_target_pairs={{0,6},{1,7},{2,4},{3,5},{4,2},{5,3},{6,0},{7,1},{8,14},{9,15},{10,... | collective-permute-start | bytes 884744 | tf_op jit(solution)/shard_map/ppermute | solution.py:267
  42.9 21.0 %collective-permute-start.13 = (bf16[1536,256]{1,0:T(8,128)(2,1)S(1)}, bf16[1536,256]{1,0:T(8,128)(2,1)}, u32[]{:S(2)}, u32[]{:S(2)}) collective-permute-start(bf16[1536,256]{1,0:T(8,128)(2,1)S(1)} %bitcast.189), channel_id=1, source_target_pairs={{0,6},{1,7},{2,4},{3,5},{4,2},{5,3},{6,0},{7,1},{8,14},{9,15},{10,... | collective-permute-start | bytes 2359304 | tf_op jit(solution)/shard_map/ppermute | solution.py:267
  45.1 28.0 %collective-permute-start.10 = (bf16[8,48,512]{2,1,0:T(8,128)(2,1)S(1)}, bf16[8,48,512]{2,1,0:T(8,128)(2,1)S(1)}, u32[]{:S(2)}, u32[]{:S(2)}) collective-permute-start(bf16[8,48,512]{2,1,0:T(8,128)(2,1)S(1)} %fusion.2.refs_0_), channel_id=1, source_target_pairs={{0,8},{1,9},{2,10},{3,11},{4,12},{5,13},{6,14},{7,15},{8,16},{9,17... | collective-permute-start | bytes 1179656 | tf_op jit(solution)/shard_map/ppermute | solution.py:275
  46.7 34.0 %collective-permute-start.11 = (bf16[8,48,512]{2,1,0:T(8,128)(2,1)S(1)}, bf16[8,48,512]{2,1,0:T(8,128)(2,1)S(1)}, u32[]{:S(2)}, u32[]{:S(2)}) collective-permute-start(bf16[8,48,512]{2,1,0:T(8,128)(2,1)S(1)} %fusion.2.refs_0_), channel_id=1, source_target_pairs={{0,16},{1,17},{2,18},{3,19},{4,20},{5,21},{6,22},{7,23},{8,24},{9,... | collective-permute-start | bytes 1179656 | tf_op jit(solution)/shard_map/ppermute | solution.py:275
  47.9 34.5 %collective-permute-start.12 = (bf16[8,48,512]{2,1,0:T(8,128)(2,1)S(1)}, bf16[8,48,512]{2,1,0:T(8,128)(2,1)S(1)}, u32[]{:S(2)}, u32[]{:S(2)}) collective-permute-start(bf16[8,48,512]{2,1,0:T(8,128)(2,1)S(1)} %fusion.2.refs_0_), channel_id=1, source_target_pairs={{0,24},{1,25},{2,26},{3,27},{4,28},{5,29},{6,30},{7,31},{8,0},{9,1... | collective-permute-start | bytes 1179656 | tf_op jit(solution)/shard_map/ppermute | solution.py:275
  49.8 42.3 %collective-permute-start.14 = (bf16[1536,256]{1,0:T(8,128)(2,1)S(1)}, bf16[1536,256]{1,0:T(8,128)(2,1)}, u32[]{:S(2)}, u32[]{:S(2)}) collective-permute-start(bf16[1536,256]{1,0:T(8,128)(2,1)S(1)} %bitcast.190), channel_id=1, source_target_pairs={{0,1},{1,0},{2,3},{3,2},{4,5},{5,4},{6,7},{7,6},{8,9},{9,8},{10,11... | collective-permute-start | bytes 2359304 | tf_op jit(solution)/shard_map/ppermute | solution.py:267
  63.9 28.2 %collective-permute-start.15 = (bf16[1536,256]{1,0:T(8,128)(2,1)}, bf16[1536,256]{1,0:T(8,128)(2,1)}, u32[]{:S(2)}, u32[]{:S(2)}) collective-permute-start(bf16[1536,256]{1,0:T(8,128)(2,1)} %collective-permute-done.7.refs_1_), channel_id=1, source_target_pairs={{0,1},{1,0},{2,3},{3,2},{4,5},{5,4},{6,7},{7,6},{8,9},{9,8},{10,11... | collective-permute-start | bytes 2359304 | tf_op jit(solution)/shard_map/ppermute | solution.py:267
  92.1 19.8 %collective-permute-start.19 = (bf16[48,1536]{1,0:T(8,128)(2,1)}, bf16[48,1536]{1,0:T(8,128)(2,1)S(1)}, u32[]{:S(2)}, u32[]{:S(2)}) collective-permute-start(bf16[48,1536]{1,0:T(8,128)(2,1)} %collective-permute-done.18), channel_id=1, source_target_pairs={{0,8},{1,9},{2,10},{3,11},{4,12},{5,13},{6,14},{7,15},{8,16},{9,17... | collective-permute-start | bytes 442376 | tf_op jit(solution)/shard_map/ppermute | solution.py:275
  98.4 21.3 %collective-permute-start.22 = (bf16[256,1536]{1,0:T(8,128)(2,1)S(1)}, bf16[256,1536]{1,0:T(8,128)(2,1)S(1)}, u32[]{:S(2)}, u32[]{:S(2)}) collective-permute-start(bf16[256,1536]{1,0:T(8,128)(2,1)S(1)} %copy-done.11), channel_id=1, source_target_pairs={{0,2},{1,3},{2,0},{3,1},{4,6},{5,7},{6,4},{7,5},{8,10},{9,11},{10,... | collective-permute-start | bytes 2359304 | tf_op jit(solution)/shard_map/ppermute | solution.py:267
  98.4 21.3 %collective-permute-start.23 = (bf16[256,1536]{1,0:T(8,128)(2,1)S(1)}, bf16[256,1536]{1,0:T(8,128)(2,1)}, u32[]{:S(2)}, u32[]{:S(2)}) collective-permute-start(bf16[256,1536]{1,0:T(8,128)(2,1)S(1)} %copy-done.11), channel_id=1, source_target_pairs={{0,4},{1,5},{2,6},{3,7},{4,0},{5,1},{6,2},{7,3},{8,12},{9,13},{10,... | collective-permute-start | bytes 2359304 | tf_op jit(solution)/shard_map/ppermute | solution.py:267
  112.7 19.8 %collective-permute-start.24 = (bf16[2,1,96,2048]{3,2,1,0:T(8,128)(2,1)}, bf16[2,1,96,2048]{3,2,1,0:T(8,128)(2,1)S(1)}, u32[]{:S(2)}, u32[]{:S(2)}) collective-permute-start(bf16[2,1,96,2048]{3,2,1,0:T(8,128)(2,1)} %get-tuple-element.337.refs_0_), channel_id=1, source_target_pairs={{0,8},{1,9},{2,10},{3,11},{4,12},{5,13},{6,14},{7,15},{8,16},{9,17... | collective-permute-start | bytes 2359304 | tf_op jit(solution)/shard_map/ppermute | solution.py:275
  132.6 42.1 %collective-permute-start.25 = (bf16[8,48,1536]{2,1,0:T(8,128)(2,1)S(1)}, bf16[8,48,1536]{2,1,0:T(8,128)(2,1)S(1)}, u32[]{:S(2)}, u32[]{:S(2)}) collective-permute-start(bf16[8,48,1536]{2,1,0:T(8,128)(2,1)S(1)} %pad_maximum_fusion.3.refs_0_), channel_id=1, source_target_pairs={{0,8},{1,9},{2,10},{3,11},{4,12},{5,13},{6,14},{7,15},{8,16},{9,17... | collective-permute-start | bytes 3538952 | tf_op jit(solution)/shard_map/ppermute | solution.py:275
  134.8 39.9 %collective-permute-start.26 = (bf16[8,48,1536]{2,1,0:T(8,128)(2,1)S(1)}, bf16[8,48,1536]{2,1,0:T(8,128)(2,1)}, u32[]{:S(2)}, u32[]{:S(2)}) collective-permute-start(bf16[8,48,1536]{2,1,0:T(8,128)(2,1)S(1)} %pad_maximum_fusion.3.refs_0_), channel_id=1, source_target_pairs={{8,0},{9,1},{10,2},{11,3},{12,4},{13,5},{14,6},{15,7},{16,8},{17,9... | collective-permute-start | bytes 3538952 | tf_op jit(solution)/shard_map/ppermute | solution.py:275
  138.5 36.2 %collective-permute-start.27 = (bf16[256,1536]{1,0:T(8,128)(2,1)S(1)}, bf16[256,1536]{1,0:T(8,128)(2,1)S(1)}, u32[]{:S(2)}, u32[]{:S(2)}) collective-permute-start(bf16[256,1536]{1,0:T(8,128)(2,1)S(1)} %copy-done.11), channel_id=1, source_target_pairs={{0,6},{1,7},{2,4},{3,5},{4,2},{5,3},{6,0},{7,1},{8,14},{9,15},{10,... | collective-permute-start | bytes 2359304 | tf_op jit(solution)/shard_map/ppermute | solution.py:267
  180.9 30.2 %collective-permute-start.32 = (bf16[8,48,1536]{2,1,0:T(8,128)(2,1)S(1)}, bf16[8,48,1536]{2,1,0:T(8,128)(2,1)}, u32[]{:S(2)}, u32[]{:S(2)}) collective-permute-start(bf16[8,48,1536]{2,1,0:T(8,128)(2,1)S(1)} %collective-permute-done.25.refs_1_), channel_id=1, source_target_pairs={{0,8},{1,9},{2,10},{3,11},{4,12},{5,13},{6,14},{7,15},{8,16},{9,17... | collective-permute-start | bytes 3538952 | tf_op jit(solution)/shard_map/ppermute | solution.py:275
  182.8 30.7 %collective-permute-start.33 = (bf16[8,48,1536]{2,1,0:T(8,128)(2,1)}, bf16[8,48,1536]{2,1,0:T(8,128)(2,1)}, u32[]{:S(2)}, u32[]{:S(2)}) collective-permute-start(bf16[8,48,1536]{2,1,0:T(8,128)(2,1)} %collective-permute-done.26.refs_2_), channel_id=1, source_target_pairs={{8,0},{9,1},{10,2},{11,3},{12,4},{13,5},{14,6},{15,7},{16,8},{17,9... | collective-permute-start | bytes 3538952 | tf_op jit(solution)/shard_map/ppermute | solution.py:275
  214.2 30.6 %collective-permute-start.35 = (bf16[8,48,1536]{2,1,0:T(8,128)(2,1)}, bf16[8,48,1536]{2,1,0:T(8,128)(2,1)S(1)}, u32[]{:S(2)}, u32[]{:S(2)}) collective-permute-start(bf16[8,48,1536]{2,1,0:T(8,128)(2,1)} %collective-permute-done.32.refs_3_), channel_id=1, source_target_pairs={{0,8},{1,9},{2,10},{3,11},{4,12},{5,13},{6,14},{7,15},{8,16},{9,17... | collective-permute-start | bytes 3538952 | tf_op jit(solution)/shard_map/ppermute | solution.py:275
  216.1 28.9 %collective-permute-start.36 = (bf16[8,48,1536]{2,1,0:T(8,128)(2,1)}, bf16[8,48,1536]{2,1,0:T(8,128)(2,1)S(1)}, u32[]{:S(2)}, u32[]{:S(2)}) collective-permute-start(bf16[8,48,1536]{2,1,0:T(8,128)(2,1)} %collective-permute-done.33.refs_4_), channel_id=1, source_target_pairs={{8,0},{9,1},{10,2},{11,3},{12,4},{13,5},{14,6},{15,7},{16,8},{17,9... | collective-permute-start | bytes 3538952 | tf_op jit(solution)/shard_map/ppermute | solution.py:275
  245.0 20.2 %collective-permute-start.38 = (bf16[1536,256]{1,0:T(8,128)(2,1)}, bf16[1536,256]{1,0:T(8,128)(2,1)S(1)}, u32[]{:S(2)}, u32[]{:S(2)}) collective-permute-start(bf16[1536,256]{1,0:T(8,128)(2,1)} %get-tuple-element.409.first_ref.refs_0_), channel_id=1, source_target_pairs={{0,2},{1,3},{2,0},{3,1},{4,6},{5,7},{6,4},{7,5},{8,10},{9,11},{10,... | collective-permute-start | bytes 2359304 | tf_op jit(solution)/shard_map/ppermute | solution.py:267
  246.3 19.9 %collective-permute-start.39 = (bf16[1536,256]{1,0:T(8,128)(2,1)}, bf16[1536,256]{1,0:T(8,128)(2,1)S(1)}, u32[]{:S(2)}, u32[]{:S(2)}) collective-permute-start(bf16[1536,256]{1,0:T(8,128)(2,1)} %get-tuple-element.409.first_ref.refs_0_), channel_id=1, source_target_pairs={{0,4},{1,5},{2,6},{3,7},{4,0},{5,1},{6,2},{7,3},{8,12},{9,13},{10,... | collective-permute-start | bytes 2359304 | tf_op jit(solution)/shard_map/ppermute | solution.py:267
  266.7 20.3 %collective-permute-start.42 = (bf16[1536,256]{1,0:T(8,128)(2,1)S(1)}, bf16[1536,256]{1,0:T(8,128)(2,1)S(1)}, u32[]{:S(2)}, u32[]{:S(2)}) collective-permute-start(bf16[1536,256]{1,0:T(8,128)(2,1)S(1)} %copy-done.13), channel_id=1, source_target_pairs={{0,6},{1,7},{2,4},{3,5},{4,2},{5,3},{6,0},{7,1},{8,14},{9,15},{10,... | collective-permute-start | bytes 2359304 | tf_op jit(solution)/shard_map/ppermute | solution.py:267
  267.5 19.6 %collective-permute-start.43 = (bf16[1536,256]{1,0:T(8,128)(2,1)}, bf16[1536,256]{1,0:T(8,128)(2,1)S(1)}, u32[]{:S(2)}, u32[]{:S(2)}) collective-permute-start(bf16[1536,256]{1,0:T(8,128)(2,1)} %get-tuple-element.410), channel_id=1, source_target_pairs={{0,1},{1,0},{2,3},{3,2},{4,5},{5,4},{6,7},{7,6},{8,9},{9,8},{10,11... | collective-permute-start | bytes 2359304 | tf_op jit(solution)/shard_map/ppermute | solution.py:267
  316.4 57.0 %collective-permute-start.48 = (bf16[1536,256]{1,0:T(8,128)(2,1)S(1)}, bf16[1536,256]{1,0:T(8,128)(2,1)S(1)}, u32[]{:S(2)}, u32[]{:S(2)}) collective-permute-start(bf16[1536,256]{1,0:T(8,128)(2,1)S(1)} %copy-done.46), channel_id=1, source_target_pairs={{0,2},{1,3},{2,0},{3,1},{4,6},{5,7},{6,4},{7,5},{8,10},{9,11},{10,... | collective-permute-start | bytes 2359304 | tf_op jit(solution)/shard_map/ppermute | solution.py:267
  317.1 56.3 %collective-permute-start.49 = (bf16[1536,256]{1,0:T(8,128)(2,1)}, bf16[1536,256]{1,0:T(8,128)(2,1)S(1)}, u32[]{:S(2)}, u32[]{:S(2)}) collective-permute-start(bf16[1536,256]{1,0:T(8,128)(2,1)} %shard_map.225), channel_id=1, source_target_pairs={{0,4},{1,5},{2,6},{3,7},{4,0},{5,1},{6,2},{7,3},{8,12},{9,13},{10,... | collective-permute-start | bytes 2359304 | tf_op jit(solution)/shard_map/ppermute | solution.py:267
  321.0 52.3 %collective-permute-start.50 = (bf16[1536,256]{1,0:T(8,128)(2,1)}, bf16[1536,256]{1,0:T(8,128)(2,1)S(1)}, u32[]{:S(2)}, u32[]{:S(2)}) collective-permute-start(bf16[1536,256]{1,0:T(8,128)(2,1)} %shard_map.226), channel_id=1, source_target_pairs={{0,6},{1,7},{2,4},{3,5},{4,2},{5,3},{6,0},{7,1},{8,14},{9,15},{10,... | collective-permute-start | bytes 2359304 | tf_op jit(solution)/shard_map/ppermute | solution.py:267
  355.3 39.2 %collective-permute-start.54 = (bf16[384,1024]{1,0:T(8,128)(2,1)S(1)}, bf16[384,1024]{1,0:T(8,128)(2,1)S(1)}, u32[]{:S(2)}, u32[]{:S(2)}) collective-permute-start(bf16[384,1024]{1,0:T(8,128)(2,1)S(1)} %get-tuple-element.587), channel_id=1, source_target_pairs={{0,8},{1,9},{2,10},{3,11},{4,12},{5,13},{6,14},{7,15},{8,16},{9,17... | collective-permute-start | bytes 2359304 | tf_op jit(solution)/shard_map/ppermute | solution.py:275
  355.4 50.1 %collective-permute-start.55 = (bf16[384,1024]{1,0:T(8,128)(2,1)S(1)}, bf16[384,1024]{1,0:T(8,128)(2,1)S(1)}, u32[]{:S(2)}, u32[]{:S(2)}) collective-permute-start(bf16[384,1024]{1,0:T(8,128)(2,1)S(1)} %get-tuple-element.586), channel_id=1, source_target_pairs={{0,16},{1,17},{2,18},{3,19},{4,20},{5,21},{6,22},{7,23},{8,24},{9,... | collective-permute-start | bytes 2359304 | tf_op jit(solution)/shard_map/ppermute | solution.py:275
  381.0 24.5 %collective-permute-start.51 = (bf16[1536,256]{1,0:T(8,128)(2,1)}, bf16[1536,256]{1,0:T(8,128)(2,1)S(1)}, u32[]{:S(2)}, u32[]{:S(2)}) collective-permute-start(bf16[1536,256]{1,0:T(8,128)(2,1)} %get-tuple-element.482.refs_0_), channel_id=1, source_target_pairs={{0,2},{1,3},{2,0},{3,1},{4,6},{5,7},{6,4},{7,5},{8,10},{9,11},{10,... | collective-permute-start | bytes 2359304 | tf_op jit(solution)/shard_map/ppermute | solution.py:267
  381.7 34.9 %collective-permute-start.52 = (bf16[1536,256]{1,0:T(8,128)(2,1)}, bf16[1536,256]{1,0:T(8,128)(2,1)S(1)}, u32[]{:S(2)}, u32[]{:S(2)}) collective-permute-start(bf16[1536,256]{1,0:T(8,128)(2,1)} %get-tuple-element.482.refs_0_), channel_id=1, source_target_pairs={{0,4},{1,5},{2,6},{3,7},{4,0},{5,1},{6,2},{7,3},{8,12},{9,13},{10,... | collective-permute-start | bytes 2359304 | tf_op jit(solution)/shard_map/ppermute | solution.py:267
  382.3 34.3 %collective-permute-start.53 = (bf16[1536,256]{1,0:T(8,128)(2,1)}, bf16[1536,256]{1,0:T(8,128)(2,1)S(1)}, u32[]{:S(2)}, u32[]{:S(2)}) collective-permute-start(bf16[1536,256]{1,0:T(8,128)(2,1)} %get-tuple-element.482.refs_0_), channel_id=1, source_target_pairs={{0,6},{1,7},{2,4},{3,5},{4,2},{5,3},{6,0},{7,1},{8,14},{9,15},{10,... | collective-permute-start | bytes 2359304 | tf_op jit(solution)/shard_map/ppermute | solution.py:267
  434.6 37.4 %collective-permute-start.61 = (bf16[1024,1536]{1,0:T(8,128)(2,1)}, bf16[1024,1536]{1,0:T(8,128)(2,1)S(1)}, u32[]{:S(2)}, u32[]{:S(2)}) collective-permute-start(bf16[1024,1536]{1,0:T(8,128)(2,1)} %get-tuple-element.499), channel_id=1, source_target_pairs={{0,1},{1,0},{2,3},{3,2},{4,5},{5,4},{6,7},{7,6},{8,9},{9,8},{10,11... | collective-permute-start | bytes 9437192 | tf_op jit(solution)/shard_map/ppermute | solution.py:267
  434.8 37.2 %collective-permute-start.60 = (bf16[384,1024]{1,0:T(8,128)(2,1)S(1)}, bf16[384,1024]{1,0:T(8,128)(2,1)S(1)}, u32[]{:S(2)}, u32[]{:S(2)}) collective-permute-start(bf16[384,1024]{1,0:T(8,128)(2,1)S(1)} %get-tuple-element.585), channel_id=1, source_target_pairs={{0,24},{1,25},{2,26},{3,27},{4,28},{5,29},{6,30},{7,31},{8,0},{9,1... | collective-permute-start | bytes 2359304 | tf_op jit(solution)/shard_map/ppermute | solution.py:275
  434.9 47.8 %collective-permute-start.63 = (bf16[128,1536]{1,0:T(8,128)(2,1)S(1)}, bf16[128,1536]{1,0:T(8,128)(2,1)S(1)}, u32[]{:S(2)}, u32[]{:S(2)}) collective-permute-start(bf16[128,1536]{1,0:T(8,128)(2,1)S(1)} %get-tuple-element.590), channel_id=1, source_target_pairs={{0,8},{1,9},{2,10},{3,11},{4,12},{5,13},{6,14},{7,15},{8,16},{9,17... | collective-permute-start | bytes 1179656 | tf_op jit(solution)/shard_map/ppermute | solution.py:275
  437.0 47.3 %collective-permute-start.64 = (bf16[128,1536]{1,0:T(8,128)(2,1)S(1)}, bf16[128,1536]{1,0:T(8,128)(2,1)S(1)}, u32[]{:S(2)}, u32[]{:S(2)}) collective-permute-start(bf16[128,1536]{1,0:T(8,128)(2,1)S(1)} %get-tuple-element.589), channel_id=1, source_target_pairs={{0,16},{1,17},{2,18},{3,19},{4,20},{5,21},{6,22},{7,23},{8,24},{9,... | collective-permute-start | bytes 1179656 | tf_op jit(solution)/shard_map/ppermute | solution.py:275
  472.0 25.3 %collective-permute-start.62 = (bf16[2,1,96,2048]{3,2,1,0:T(8,128)(2,1)}, bf16[2,1,96,2048]{3,2,1,0:T(8,128)(2,1)S(1)}, u32[]{:S(2)}, u32[]{:S(2)}) collective-permute-start(bf16[2,1,96,2048]{3,2,1,0:T(8,128)(2,1)} %bitcast.249), channel_id=1, source_target_pairs={{8,0},{9,1},{10,2},{11,3},{12,4},{13,5},{14,6},{15,7},{16,8},{17,9... | collective-permute-start | bytes 2359304 | tf_op jit(solution)/shard_map/ppermute | solution.py:275
  480.8 41.1 %collective-permute-start.65 = (bf16[256,1536]{1,0:T(8,128)(2,1)}, bf16[256,1536]{1,0:T(8,128)(2,1)S(1)}, u32[]{:S(2)}, u32[]{:S(2)}) collective-permute-start(bf16[256,1536]{1,0:T(8,128)(2,1)} %get-tuple-element.519), channel_id=1, source_target_pairs={{0,2},{1,3},{2,0},{3,1},{4,6},{5,7},{6,4},{7,5},{8,10},{9,11},{10,... | collective-permute-start | bytes 2359304 | tf_op jit(solution)/shard_map/ppermute | solution.py:267
  482.1 39.8 %collective-permute-start.66 = (bf16[256,1536]{1,0:T(8,128)(2,1)}, bf16[256,1536]{1,0:T(8,128)(2,1)S(1)}, u32[]{:S(2)}, u32[]{:S(2)}) collective-permute-start(bf16[256,1536]{1,0:T(8,128)(2,1)} %get-tuple-element.520), channel_id=1, source_target_pairs={{0,4},{1,5},{2,6},{3,7},{4,0},{5,1},{6,2},{7,3},{8,12},{9,13},{10,... | collective-permute-start | bytes 2359304 | tf_op jit(solution)/shard_map/ppermute | solution.py:267
  482.7 39.2 %collective-permute-start.67 = (bf16[256,1536]{1,0:T(8,128)(2,1)}, bf16[256,1536]{1,0:T(8,128)(2,1)S(1)}, u32[]{:S(2)}, u32[]{:S(2)}) collective-permute-start(bf16[256,1536]{1,0:T(8,128)(2,1)} %get-tuple-element.521), channel_id=1, source_target_pairs={{0,6},{1,7},{2,4},{3,5},{4,2},{5,3},{6,0},{7,1},{8,14},{9,15},{10,... | collective-permute-start | bytes 2359304 | tf_op jit(solution)/shard_map/ppermute | solution.py:267
  484.3 37.6 %collective-permute-start.68 = (bf16[128,1536]{1,0:T(8,128)(2,1)S(1)}, bf16[128,1536]{1,0:T(8,128)(2,1)S(1)}, u32[]{:S(2)}, u32[]{:S(2)}) collective-permute-start(bf16[128,1536]{1,0:T(8,128)(2,1)S(1)} %get-tuple-element.588), channel_id=1, source_target_pairs={{0,24},{1,25},{2,26},{3,27},{4,28},{5,29},{6,30},{7,31},{8,0},{9,1... | collective-permute-start | bytes 1179656 | tf_op jit(solution)/shard_map/ppermute | solution.py:275
  536.5 29.1 %collective-permute-start.73 = (bf16[1536,256]{1,0:T(8,128)(2,1)}, bf16[1536,256]{1,0:T(8,128)(2,1)S(1)}, u32[]{:S(2)}, u32[]{:S(2)}) collective-permute-start(bf16[1536,256]{1,0:T(8,128)(2,1)} %get-tuple-element.544), channel_id=1, source_target_pairs={{0,2},{1,3},{2,0},{3,1},{4,6},{5,7},{6,4},{7,5},{8,10},{9,11},{10,... | collective-permute-start | bytes 2359304 | tf_op jit(solution)/shard_map/ppermute | solution.py:267
  537.8 36.4 %collective-permute-start.74 = (bf16[1536,256]{1,0:T(8,128)(2,1)}, bf16[1536,256]{1,0:T(8,128)(2,1)S(1)}, u32[]{:S(2)}, u32[]{:S(2)}) collective-permute-start(bf16[1536,256]{1,0:T(8,128)(2,1)} %get-tuple-element.545), channel_id=1, source_target_pairs={{0,4},{1,5},{2,6},{3,7},{4,0},{5,1},{6,2},{7,3},{8,12},{9,13},{10,... | collective-permute-start | bytes 2359304 | tf_op jit(solution)/shard_map/ppermute | solution.py:267
  538.4 36.8 %collective-permute-start.75 = (bf16[1536,256]{1,0:T(8,128)(2,1)}, bf16[1536,256]{1,0:T(8,128)(2,1)S(1)}, u32[]{:S(2)}, u32[]{:S(2)}) collective-permute-start(bf16[1536,256]{1,0:T(8,128)(2,1)} %get-tuple-element.546), channel_id=1, source_target_pairs={{0,6},{1,7},{2,4},{3,5},{4,2},{5,3},{6,0},{7,1},{8,14},{9,15},{10,... | collective-permute-start | bytes 2359304 | tf_op jit(solution)/shard_map/ppermute | solution.py:267
  559.9 23.1 %collective-permute-start.76 = (bf16[384,384]{1,0:T(8,128)(2,1)}, bf16[384,384]{1,0:T(8,128)(2,1)}, u32[]{:S(2)}, u32[]{:S(2)}) collective-permute-start(bf16[384,384]{1,0:T(8,128)(2,1)} %get-tuple-element.593), channel_id=1, source_target_pairs={{0,24},{1,25},{2,26},{3,27},{4,28},{5,29},{6,30},{7,31},{8,0},{9,1... | collective-permute-start | bytes 884744 | tf_op jit(solution)/shard_map/ppermute | solution.py:275
  594.6 22.7 %collective-permute-start.86 = (bf16[2,48,384]{2,1,0:T(8,128)(2,1)S(1)}, bf16[2,48,384]{2,1,0:T(8,128)(2,1)S(1)}, u32[]{:S(2)}, u32[]{:S(2)}) collective-permute-start(bf16[2,48,384]{2,1,0:T(8,128)(2,1)S(1)} %get-tuple-element.632), channel_id=1, source_target_pairs={{0,2},{1,3},{2,0},{3,1},{4,6},{5,7},{6,4},{7,5},{8,10},{9,11},{10,... | collective-permute-start | bytes 221192 | tf_op jit(solution)/shard_map/ppermute | solution.py:267
  (120 other events, 1244.4 us)

commit v4 on v3

--- a/solution.py
+++ b/solution.py
@@ -72,26 +72,35 @@
         last = own_block + (relative(chunk) ^ member)
         starts, ends = chunk_range(chunk, starts_ref, last)
 
+        def masked(block):
+            held = jnp.maximum(block, 0)
+            scores = jnp.dot(keys[held], queries, preferred_element_type=jnp.float32) * log2_scale
+            return held, jnp.where(visible_mask(block, starts, ends), scores, masked_score)
+
         def advance(step, running):
             top, total, summed = running
-            block = last - step
-            scores = (
-                jnp.dot(keys[block], queries, preferred_element_type=jnp.float32) * log2_scale
+            one, scores = masked(last - 2 * step)
+            two, more = masked(last - 2 * step - 1)
+            new_top = jnp.maximum(
+                top, jnp.max(jnp.maximum(scores, more), axis=0, keepdims=True)
             )
-            scores = jnp.where(visible_mask(block, starts, ends), scores, masked_score)
-            new_top = jnp.maximum(top, jnp.max(scores, axis=0, keepdims=True))
             factor = jnp.exp2(top - new_top)
-            weights = jnp.exp2(scores - new_top)
-            total = total * factor + jnp.sum(weights, axis=0, keepdims=True)
-            summed = summed * factor + jnp.dot(
-                values[block], weights.astype(jnp.bfloat16), preferred_element_type=jnp.float32
+            weights, others = jnp.exp2(scores - new_top), jnp.exp2(more - new_top)
+            total = total * factor + jnp.sum(weights + others, axis=0, keepdims=True)
+            summed = summed * factor + (
+                jnp.dot(
+                    values[one], weights.astype(jnp.bfloat16), preferred_element_type=jnp.float32
+                )
+                + jnp.dot(
+                    values[two], others.astype(jnp.bfloat16), preferred_element_type=jnp.float32
+                )
             )
             return new_top, total, summed
 
         lanes = GROUP * BLOCK
         top, total, summed = lax.fori_loop(
             0,
-            last - low_ref[chunk] + 1,
+            (last - low_ref[chunk] + 2) // 2,
             advance,
             (
                 jnp.full((1, lanes), masked_score, jnp.float32),
@@ -134,27 +143,32 @@
         last = own_block + (relative(chunk) ^ member)
         starts, ends = chunk_range(chunk, starts_ref, last)
 
-        def advance(block, summed):
-            scores = (
-                jnp.dot(keys[block], queries, preferred_element_type=jnp.float32) * log2_scale
-            )
+        def part(block):
+            held = jnp.minimum(block, last)
+            scores = jnp.dot(keys[held], queries, preferred_element_type=jnp.float32) * log2_scale
             scores = jnp.where(visible_mask(block, starts, ends), scores - norm, masked_score)
             probs = jnp.exp2(scores)
-            slopes = jnp.dot(values[block], grads, preferred_element_type=jnp.float32)
+            slopes = jnp.dot(values[held], grads, preferred_element_type=jnp.float32)
             grad_scores = (probs * (slopes - delta)).astype(jnp.bfloat16)
-            key_sum[block] += lax.dot_general(
-                queries, grad_scores, rows_rows, preferred_element_type=jnp.float32
-            )
-            value_sum[block] += lax.dot_general(
-                grads, probs.astype(jnp.bfloat16), rows_rows, preferred_element_type=jnp.float32
-            )
-            return summed + jnp.dot(
-                keys_t[block], grad_scores, preferred_element_type=jnp.float32
-            )
+            return held, probs.astype(jnp.bfloat16), grad_scores
+
+        def advance(step, summed):
+            found = [part(low_ref[chunk] + 2 * step), part(low_ref[chunk] + 2 * step + 1)]
+            for held, probs, grad_scores in found:
+                key_sum[held] += lax.dot_general(
+                    queries, grad_scores, rows_rows, preferred_element_type=jnp.float32
+                )
+                value_sum[held] += lax.dot_general(
+                    grads, probs, rows_rows, preferred_element_type=jnp.float32
+                )
+                summed = summed + jnp.dot(
+                    keys_t[held], grad_scores, preferred_element_type=jnp.float32
+                )
+            return summed
 
         summed = lax.fori_loop(
-            low_ref[chunk],
-            last + 1,
+            0,
+            (last - low_ref[chunk] + 2) // 2,
             advance,
             jnp.zeros((HEAD_DIM, GROUP * BLOCK), jnp.float32),
         )
@@ -1186,13 +1200,13 @@
 
     grad_attended, out_part = project_out_back(grid, attn_team, out_rows, attended)
     grad_attended, down_part, out_give = order.step(grad_attended, down_part, out_give)
-    down_parts = send_teams(down_part, 1, early + 1)
+    down_late = send_teams(down_part, early + 1, teams)
     out_other = grid.turn(out_give, 1)
     query_rot, own_grads, back_grads = attend_back(
         low, starts, queries, grad_attended, attended, normalizer, pieces, 0, OWN_KV
     )
-    query_rot, own_grads, back_grads, late_parts, out_other = order.step(
-        query_rot, own_grads, back_grads, late_parts, out_other
+    query_rot, own_grads, back_grads, late_parts, down_late, out_other = order.step(
+        query_rot, own_grads, back_grads, late_parts, down_late, out_other
     )
     returned = [
         grid.shift(back_grads[step - 1], -step, False) for step in range(1, steps_back + 1)
@@ -1201,24 +1215,6 @@
     out_blocks = order.step(out_blocks)
     out_terms = grid.send_chips(out_blocks)
     mixer_total = sum_teams(mixer_part, mixer_parts + late_parts, bf16)
-    returned, down_parts, mixer_total = order.step(returned, down_parts, mixer_total)
-    down_late = send_teams(down_part, early + 1, teams)
-    keep, give, attn_part = project_back(
-        grid, normed_first, query_rot, own_grads, returned, cosine, sine_table, attn_w
-    )
-    attn_part, give, out_terms, down_late = order.step(attn_part, give, out_terms, down_late)
-    other = grid.turn(give, 1)
-    attn_parts = send_teams(attn_part, 1, early + 1)
-    other = order.step(other)
-    total, blocks = combine(keep, other, 1)
-    blocks, out_part = order.step(blocks, out_part)
-    terms = grid.send_chips(blocks)
-    outputs = finish_output([out_total] + out_terms, middle)
-    down_grad = sum_teams(down_part, down_parts + down_late, f32)
-    attn_parts, outputs, down_grad = order.step(attn_parts, outputs, down_grad)
-    attn_late = send_teams(attn_part, early + 1, teams)
-    out_parts = send_teams(out_part, 1, teams)
-
     def members_rows(total):
         blocks = total.reshape(TEAM // 2, 2, rows, -1)
         return dynamic(blocks, core, 1), grid.turn(dynamic(blocks, 1 - core, 1), 1)
@@ -1240,24 +1236,45 @@
             (TEAM,) + found[0].shape[1:]
         )
 
+    returned, mixer_total = order.step(returned, mixer_total)
+    down_parts = send_teams(down_part, 1, early + 1)
     mixer_mine, mixer_others = members_rows(mixer_total)
-    mixer_mine, mixer_others, terms = order.step(mixer_mine, mixer_others, terms)
+    keep, give, attn_part = project_back(
+        grid, normed_first, query_rot, own_grads, returned, cosine, sine_table, attn_w
+    )
+    attn_part, give, out_terms, down_parts, mixer_others = order.step(
+        attn_part, give, out_terms, down_parts, mixer_others
+    )
+    other = grid.turn(give, 1)
     mixer_found = owner_columns(mixer_mine, mixer_others)
+    other = order.step(other)
+    total, blocks = combine(keep, other, 1)
+    blocks, mixer_found, out_part = order.step(blocks, mixer_found, out_part)
+    terms = grid.send_chips(blocks)
+    attn_parts = send_teams(attn_part, 1, early + 1)
+    outputs = finish_output([out_total] + out_terms, middle)
+    down_grad = sum_teams(down_part, down_parts + down_late, f32)
+    mixer_columns = in_order(mixer_found)
+    attn_parts, outputs, down_grad = order.step(attn_parts, outputs, down_grad)
+    attn_late = send_teams(attn_part, early + 1, teams)
+    terms, attn_late = order.step(terms, attn_late)
+    out_parts = send_teams(out_part, 1, teams)
     input_grad, first_part = finish_first([total] + terms, inputs_t, grad_middle, gain_first)
     gain_parts = jnp.concatenate([first_part, second_part], axis=1).T
-    attn_late, gain_parts, out_parts = order.step(attn_late, gain_parts, out_parts)
     attn_total = sum_teams(attn_part, attn_parts + attn_late, bf16)
+    attn_mine, attn_others = members_rows(attn_total)
+    gain_parts, attn_total = order.step(gain_parts, attn_total)
+    gain_other = grid.turn(gain_parts, 1)
+    gain_other, attn_others, out_parts = order.step(gain_other, attn_others, out_parts)
+    gain_parts = gain_parts + gain_other
+    gain_parts = order.step(gain_parts)
+    gain_chips = [grid.turn(gain_parts, 2 * other) for other in range(1, 4)]
     out_own = sum_teams(out_part, out_parts, bf16)
-    attn_mine, attn_others = members_rows(attn_total)
-    gain_parts = gain_parts + grid.turn(gain_parts, 1)
-    attn_mine, attn_others, gain_parts, out_own = order.step(
-        attn_mine, attn_others, gain_parts, out_own
-    )
+    gain_chips, out_own = order.step(gain_chips, out_own)
+    for other in gain_chips:
+        gain_parts = gain_parts + other
     attn_found = owner_columns(attn_mine, attn_others)
-    out_grad = grid.to_owners(out_own).astype(f32)
-    gain_parts = gain_parts + grid.turn(gain_parts, 2)
-    mixer_found, gain_parts = order.step(mixer_found, gain_parts)
-    mixer_columns = in_order(mixer_found)
+    out_grad = grid.to_owners(out_own)
 
     def whole_units(blocks):
         blocks = blocks.reshape(TEAM, rows, teams, unit_rows)
@@ -1268,13 +1285,13 @@
 
     gate_grad = whole_units(mixer_columns[..., :units])
     up_grad = whole_units(mixer_columns[..., units:])
-    gain_parts = gain_parts + grid.turn(gain_parts, 4)
+    attn_found, out_grad, gain_parts = order.step(attn_found, out_grad, gain_parts)
     gain_blocks = gain_parts.reshape(2, teams, TEAM, rows)
     gain_sums = dynamic(dynamic(gain_blocks, grid.team, 1), member, 1)
     for steps in range(1, teams):
         block = dynamic(dynamic(gain_blocks, (grid.team + steps) % teams, 1), member, 1)
         gain_sums = gain_sums + grid.shift(block, steps)
-    attn_found, gain_sums = order.step(attn_found, gain_sums)
+    out_grad = out_grad.astype(f32)
     attn_columns = in_order(attn_found)
     gain_sums = gain_sums + order.token[0, 0].astype(f32)
     return (

time: 638 us -> 629 us (0.986)
  Pallas kernels: 280 us -> 264 us
    pallas_call x1, Pallas kernels: 30.7 us -> 22.6 us  [attend_back(): pl.pallas_call(gradient_kernel, grid=(count,), in_specs=[low_spec, whole,...]
    pallas_call x1, Pallas kernels: 24.6 us -> 16.8 us  [attend(): pl.pallas_call(attend_kernel, grid=(count,), in_specs=[low_spec, whole, h...]
    unnamed x155 -> x157, local copies, waits for them, and re-layouts: 13.7 us -> 10.9 us
    ppermute x63 -> x64, waiting for transfers between devices: 100 us -> 102 us  [turn(): lax.ppermute(value, 'dev', [(d, d ^ bits) for d in range(self.count)])]
    ppermute x63 -> x64, starting transfers between devices: 47.9 us -> 48.5 us  [turn(): lax.ppermute(value, 'dev', [(d, d ^ bits) for d in range(self.count)])]
  transfers between devices with their start and end apart: 94 -> 95, of which waited for: 38 -> 33; matrix products, arithmetic and copies ran while one was open for 5% -> 5% of each run, Pallas kernels for 42% -> 41%
where the time goes in v4:
time: 629 us; the launch traced here: 617 us
  Pallas kernels  264 us (42%)
  waiting for transfers between devices  190 us (30%)
  starting transfers between devices  115 us (18%)
  local copies, waits for them, and re-layouts  32.4 us (5%)
  other arithmetic  12.2 us (2%)
    ppermute x64, waiting for transfers between devices, turn(): lax.ppermute(value, 'dev', [(d, d ^ bits) for d in range(self.count)])  102 us
    ppermute x29, waiting for transfers between devices, shift(): return lax.ppermute(value, 'dev', pairs)  78.7 us
    ppermute x29, starting transfers between devices, shift(): return lax.ppermute(value, 'dev', pairs)  62.6 us
    ppermute x64, starting transfers between devices, turn(): lax.ppermute(value, 'dev', [(d, d ^ bits) for d in range(self.count)])  48.5 us
    pallas_call x4, Pallas kernels, mixer(): call(kernel, (2,), [fixed(normed[0]), fixed(normed[1]), block, block, fix...  42.8 us
    pallas_call x1, Pallas kernels, token_product(): call(kernel, (TEAM,), [fixed(block) for block in list(lefts) + list(right...  30.3 us
    pallas_call x1, Pallas kernels, project_back(): call(kernel, (TEAM,), [lanes_at(width, own), heads, lanes_at(HEAD_DIM, ow...  23.7 us
    pallas_call x1, Pallas kernels, attend_back(): pl.pallas_call(gradient_kernel, grid=(count,), in_specs=[low_spec, whole,...  22.6 us
  transfers between devices with their start and end apart: 95, of which 33 were waited for; matrix products, arithmetic and copies ran while one was open for 5% of the time, Pallas kernels for 41%

profile of v4, /device:TPU:10, one launch (start us, length us, event | category | flops | bytes accessed | tf_op | source)
XLA Modules:
  0.0 616.9 jit_solution(6939096892386499459)
XLA Ops:
  21.1 3.6 fusion
  24.6 12.7 %collective-permute-done.4 = bf16[2,48,1536]{2,1,0:T(8,128)(2,1)S(1)} collective-permute-done((bf16[2,48,1536]{2,1,0:T(8,128)(2,1)}, bf16[2,48,1536]{2,1,0:T(8,128)(2,1)S(1)}, u32[]{:S(2)}, u32[]{:S(2)}) %collective-permute-start.4) | collective-permute-done | bytes 294944 | tf_op jit(solution)/shard_map/ppermute | solution.py:281
  37.4 3.7 collective-permute-done.5
  49.8 14.1 %collective-permute-done.13.refs_3_ = bf16[1536,256]{1,0:T(8,128)(2,1)} collective-permute-done((bf16[1536,256]{1,0:T(8,128)(2,1)S(1)}, bf16[1536,256]{1,0:T(8,128)(2,1)}, u32[]{:S(2)}, u32[]{:S(2)}) %collective-permute-start.13) | collective-permute-done | bytes 786464 | tf_op jit(solution)/shard_map/ppermute | solution.py:281
  63.9 9.1 %collective-permute-done.10.refs_1_ = bf16[8,48,512]{2,1,0:T(8,128)(2,1)S(1)} collective-permute-done((bf16[8,48,512]{2,1,0:T(8,128)(2,1)S(1)}, bf16[8,48,512]{2,1,0:T(8,128)(2,1)S(1)}, u32[]{:S(2)}, u32[]{:S(2)}) %collective-permute-start.10) | collective-permute-done | bytes 393248 | tf_op jit(solution)/shard_map/ppermute | solution.py:289
  73.0 7.6 %collective-permute-done.11.refs_2_ = bf16[8,48,512]{2,1,0:T(8,128)(2,1)S(1)} collective-permute-done((bf16[8,48,512]{2,1,0:T(8,128)(2,1)S(1)}, bf16[8,48,512]{2,1,0:T(8,128)(2,1)S(1)}, u32[]{:S(2)}, u32[]{:S(2)}) %collective-permute-start.11) | collective-permute-done | bytes 393248 | tf_op jit(solution)/shard_map/ppermute | solution.py:289
  85.8 4.0 shard_map.212
  100.2 11.8 %shard_map.213 = (bf16[1536,2048]{1,0:T(8,128)(2,1)}, bf16[2,96,2048]{2,1,0:T(8,128)(2,1)}, bf16[2,1,96,2048]{3,2,1,0:T(8,128)(2,1)}) custom-call(bf16[1536,512]{1,0:T(8,128)(2,1)} %bitcast.194, f32[96,2048]{1,0:T(8,128)} %get-tuple-element.325.cosine_ref, f32[96,2048]{1,0:T(8,128)} %get-tuple-element.326.sine_ref, bf16[1536,256]{1,0:T(8,128)(2,1)} %bitcast.201, ...), custom_call_target="tpu_custom_call" | custom-call | flops 1000 | bytes 1000 | tf_op jit(solution)/shard_map/pallas_call | solution.py:514
  115.0 3.4 shard_map.214
  119.7 12.9 %collective-permute-done.24.refs_1_ = bf16[2,1,96,2048]{3,2,1,0:T(8,128)(2,1)S(1)} collective-permute-done((bf16[2,1,96,2048]{3,2,1,0:T(8,128)(2,1)}, bf16[2,1,96,2048]{3,2,1,0:T(8,128)(2,1)S(1)}, u32[]{:S(2)}, u32[]{:S(2)}) %collective-permute-start.24) | collective-permute-done | bytes 786464 | tf_op jit(solution)/shard_map/ppermute | solution.py:289
  134.8 3.7 collective-permute-start.26
  140.7 16.8 %shard_map.215 = (f32[2,96,2048]{2,1,0:T(8,128)}, f32[2,1,2048]{2,1,0:T(1,128)}) custom-call(s32[9]{0:T(128)} %pad_add_fusion.1.low_ref, s32[1,2048]{1,0:T(1,128)} %bitcast.245, bf16[2,96,2048]{2,1,0:T(8,128)(2,1)} %get-tuple-element.351.query_ref, bf16[2,1,96,2048]{3,2,1,0:T(8,128)(2,1)} %get-tuple-element.340.refs_0_, bf16[2,1,96,2048]{3,2,1,0:T(8,128)(2,1)} %copy-done.7), custom_call_target="tpu_custom_call" | custom-call | flops 1000 | bytes 1000 | tf_op jit(solution)/shard_map/pallas_call | solution.py:209
  157.5 9.4 %shard_map.216 = (f32[1536,1024]{1,0:T(8,128)}, bf16[1536,1024]{1,0:T(8,128)(2,1)}) custom-call(f32[2,96,2048]{2,1,0:T(8,128)} %get-tuple-element.353.attended_ref.out_ref, bf16[192,1536]{1,0:T(8,128)(2,1)} %bitcast.204), custom_call_target="tpu_custom_call" | custom-call | flops 1000 | bytes 1000 | tf_op jit(solution)/shard_map/pallas_call | solution.py:552
  168.9 4.1 collective-permute-done.28.arrived_ref
  173.1 4.8 collective-permute-start.32
  180.0 6.8 %shard_map.217 = (f32[1536,256]{1,0:T(8,128)}, bf16[1536,256]{1,0:T(8,128)(2,1)}, bf16[1536,256]{1,0:T(8,128)(2,1)}, bf16[1536,256]{1,0:T(8,128)(2,1)}) custom-call(f32[1536,1024]{1,0:T(8,128)} %get-tuple-element.367.keep_ref, bf16[1536,1024]{1,0:T(8,128)(2,1)} %collective-permute-done.28.arrived_ref), custom_call_target="tpu_custom_call" | custom-call | flops 1000 | bytes 1000 | tf_op jit(solution)/shard_map/pallas_call | solution.py:875
  188.1 15.6 %collective-permute-done.32.refs_3_ = bf16[8,48,1536]{2,1,0:T(8,128)(2,1)} collective-permute-done((bf16[8,48,1536]{2,1,0:T(8,128)(2,1)S(1)}, bf16[8,48,1536]{2,1,0:T(8,128)(2,1)}, u32[]{:S(2)}, u32[]{:S(2)}) %collective-permute-start.32) | collective-permute-done | bytes 1179680 | tf_op jit(solution)/shard_map/ppermute | solution.py:289
  203.7 4.4 collective-permute-done.33.refs_4_
  210.3 3.7 collective-permute-start.36
  214.8 18.6 %collective-permute-done.34.refs_3_ = bf16[1536,256]{1,0:T(8,128)(2,1)S(1)} collective-permute-done((bf16[1536,256]{1,0:T(8,128)(2,1)}, bf16[1536,256]{1,0:T(8,128)(2,1)S(1)}, u32[]{:S(2)}, u32[]{:S(2)}) %collective-permute-start.34) | collective-permute-done | bytes 786464 | tf_op jit(solution)/shard_map/ppermute | solution.py:281
  234.3 4.7 shard_map.218
  240.8 6.7 %shard_map.219 = (bf16[4,8,48,1024]{3,2,1,0:T(8,128)(2,1)}, bf16[4,128,1536]{2,1,0:T(8,128)(2,1)}) custom-call(s32[2]{0:T(128)} %pad_add_fusion.2.places_ref, bf16[8,48,1536]{2,1,0:T(8,128)(2,1)} %copy-done.5, bf16[8,48,1536]{2,1,0:T(8,128)(2,1)} %copy-done.23, bf16[8,48,1536]{2,1,0:T(8,128)(2,1)} %collective-permute-done.26.refs_2_, ...), custom_call_target="tpu_custom_call" | custom-call | flops 1000 | bytes 1000 | tf_op jit(solution)/shard_map/pallas_call | solution.py:461
  248.4 10.6 %shard_map.220 = (bf16[512,512]{1,0:T(8,128)(2,1)}, bf16[512,1024]{1,0:T(8,128)(2,1)}, f32[1536,256]{1,0:T(8,128)}, bf16[1536,256]{1,0:T(8,128)(2,1)}) custom-call(bf16[1536,256]{1,0:T(8,128)(2,1)} %get-tuple-element.412.first_ref.refs_0_, bf16[1536,256]{1,0:T(8,128)(2,1)} %copy-done.13, bf16[4,256,1536]{2,1,0:T(8,128)(2,1)} %copy-done, ...), custom_call_target="tpu_custom_call" | custom-call | flops 1000 | bytes 1000 | tf_op jit(solution)/shard_map/pallas_call | solution.py:602
  263.6 10.9 %shard_map.221 = (bf16[512,512]{1,0:T(8,128)(2,1)}, bf16[512,1024]{1,0:T(8,128)(2,1)}, f32[1536,256]{1,0:T(8,128)}, bf16[1536,256]{1,0:T(8,128)(2,1)}) custom-call(bf16[1536,256]{1,0:T(8,128)(2,1)} %copy-done.14, bf16[1536,256]{1,0:T(8,128)(2,1)} %copy-done.16, bf16[4,256,1536]{2,1,0:T(8,128)(2,1)} %copy-done, bf16[4,256,1536]{2,1,0:T(8,128)(2,1)} %copy-done.1, ...), custom_call_target="tpu_custom_call" | custom-call | flops 1000 | bytes 1000 | tf_op jit(solution)/shard_map/pallas_call | solution.py:602
  274.5 6.5 %collective-permute-done.42.first_ref.refs_3_ = bf16[1536,256]{1,0:T(8,128)(2,1)S(1)} collective-permute-done((bf16[1536,256]{1,0:T(8,128)(2,1)S(1)}, bf16[1536,256]{1,0:T(8,128)(2,1)S(1)}, u32[]{:S(2)}, u32[]{:S(2)}) %collective-permute-start.42) | collective-permute-done | bytes 786464 | tf_op jit(solution)/shard_map/ppermute | solution.py:281
  281.6 10.6 %shard_map.222 = (bf16[512,512]{1,0:T(8,128)(2,1)}, bf16[512,1024]{1,0:T(8,128)(2,1)}, f32[1536,256]{1,0:T(8,128)}, bf16[1536,256]{1,0:T(8,128)(2,1)}) custom-call(bf16[1536,256]{1,0:T(8,128)(2,1)} %copy-done.15, bf16[1536,256]{1,0:T(8,128)(2,1)} %copy-done.17, bf16[4,256,1536]{2,1,0:T(8,128)(2,1)} %copy-done, bf16[4,256,1536]{2,1,0:T(8,128)(2,1)} %copy-done.1, ...), custom_call_target="tpu_custom_call" | custom-call | flops 1000 | bytes 1000 | tf_op jit(solution)/shard_map/pallas_call | solution.py:602
  293.3 10.6 %shard_map.224 = (bf16[512,512]{1,0:T(8,128)(2,1)}, bf16[512,1024]{1,0:T(8,128)(2,1)}, f32[1536,256]{1,0:T(8,128)}, bf16[1536,256]{1,0:T(8,128)(2,1)}) custom-call(bf16[1536,256]{1,0:T(8,128)(2,1)} %copy-done.18, bf16[1536,256]{1,0:T(8,128)(2,1)} %copy-done.19, bf16[4,256,1536]{2,1,0:T(8,128)(2,1)} %copy-done, bf16[4,256,1536]{2,1,0:T(8,128)(2,1)} %copy-done.1, ...), custom_call_target="tpu_custom_call" | custom-call | flops 1000 | bytes 1000 | tf_op jit(solution)/shard_map/pallas_call | solution.py:602
  317.1 30.3 %shard_map.227.own_ref = bf16[4,384,1024]{2,1,0:T(8,128)(2,1)} custom-call(s32[2]{0:T(128)} %pad_add_fusion.2.places_ref, bf16[1536,256]{1,0:T(8,128)(2,1)} %get-tuple-element.412.first_ref.refs_0_, bf16[1536,256]{1,0:T(8,128)(2,1)} %copy-done.14, bf16[1536,256]{1,0:T(8,128)(2,1)} %copy-done.15, bf16[1536,256]{1,0:T(8,128)(2,1)} %copy-done.18, ...), custom_call_target="tpu_custom_call" | custom-call | flops 1000 | bytes 1000 | tf_op jit(solution)/shard_map/pallas_call | solution.py:695
  352.9 13.8 %shard_map.228.own_ref = bf16[4,128,1536]{2,1,0:T(8,128)(2,1)} custom-call(s32[2]{0:T(128)} %pad_add_fusion.2.places_ref, bf16[512,512]{1,0:T(8,128)(2,1)} %get-tuple-element.473.refs_0_, bf16[512,512]{1,0:T(8,128)(2,1)} %get-tuple-element.474.refs_1_, bf16[512,512]{1,0:T(8,128)(2,1)} %get-tuple-element.475.refs_2_, ...), custom_call_target="tpu_custom_call" | custom-call | flops 1000 | bytes 1000 | tf_op jit(solution)/shard_map/pallas_call | solution.py:730
  368.1 6.2 %shard_map.229 = (f32[1536,256]{1,0:T(8,128)}, bf16[1536,256]{1,0:T(8,128)(2,1)}, f32[1536,1]{1,0:T(8,128)}) custom-call(f32[1536,256]{1,0:T(8,128)} %get-tuple-element.464.refs_0_, bf16[1536,256]{1,0:T(8,128)(2,1)} %copy-done.49, bf16[1536,256]{1,0:T(8,128)(2,1)} %copy-done.50, bf16[1536,256]{1,0:T(8,128)(2,1)} %copy-done.51, bf16[1536,256]{1,0:T(8,128)(2,1)} %copy-done.53, ...), custom_call_target="tpu_custom_call" | custom-call | flops 1000 | bytes 1000 | tf_op jit(solution)/shard_map/pallas_call | solution.py:894
  377.9 10.0 %shard_map.230 = (f32[1024,1536]{1,0:T(8,128)}, bf16[1024,1536]{1,0:T(8,128)(2,1)}) custom-call(bf16[512,1536]{1,0:T(8,128)(2,1)} %bitcast.193, bf16[512,512]{1,0:T(8,128)(2,1)} %get-tuple-element.473.refs_0_, bf16[512,512]{1,0:T(8,128)(2,1)} %get-tuple-element.474.refs_1_, bf16[512,512]{1,0:T(8,128)(2,1)} %get-tuple-element.475.refs_2_, ...), custom_call_target="tpu_custom_call" | custom-call | flops 1000 | bytes 1000 | tf_op jit(solution)/shard_map/pallas_call | solution.py:647
  387.9 12.8 %collective-permute-done.55.refs_1_ = bf16[384,1024]{1,0:T(8,128)(2,1)S(1)} collective-permute-done((bf16[384,1024]{1,0:T(8,128)(2,1)S(1)}, bf16[384,1024]{1,0:T(8,128)(2,1)S(1)}, u32[]{:S(2)}, u32[]{:S(2)}) %collective-permute-start.55) | collective-permute-done | bytes 786464 | tf_op jit(solution)/shard_map/ppermute | solution.py:289
  400.7 10.2 %collective-permute-done.52.refs_2_ = bf16[1536,256]{1,0:T(8,128)(2,1)S(1)} collective-permute-done((bf16[1536,256]{1,0:T(8,128)(2,1)}, bf16[1536,256]{1,0:T(8,128)(2,1)S(1)}, u32[]{:S(2)}, u32[]{:S(2)}) %collective-permute-start.52) | collective-permute-done | bytes 786464 | tf_op jit(solution)/shard_map/ppermute | solution.py:281
  417.6 11.3 %shard_map.231 = (bf16[2,96,2048]{2,1,0:T(8,128)(2,1)}, bf16[4,48,1536]{2,1,0:T(8,128)(2,1)}) custom-call(s32[2]{0:T(128)} %pad_add_fusion.2.places_ref, bf16[192,1536]{1,0:T(8,128)(2,1)} %bitcast.205, f32[2,96,2048]{2,1,0:T(8,128)} %get-tuple-element.353.attended_ref.out_ref, bf16[1536,256]{1,0:T(8,128)(2,1)} %get-tuple-element.485.refs_0_, ...), custom_call_target="tpu_custom_call" | custom-call | flops 1000 | bytes 1000 | tf_op jit(solution)/shard_map/pallas_call | solution.py:777
  431.7 22.6 %shard_map.232 = (f32[2,96,2048]{2,1,0:T(8,128)}, f32[2,1,96,2048]{3,2,1,0:T(8,128)}, bf16[1,2,1,96,2048]{4,3,2,1,0:T(8,128)(2,1)}) custom-call(s32[9]{0:T(128)} %pad_add_fusion.1.low_ref, s32[1,2048]{1,0:T(1,128)} %bitcast.246, bf16[2,96,2048]{2,1,0:T(8,128)(2,1)} %get-tuple-element.351.query_ref, bf16[2,96,2048]{2,1,0:T(8,128)(2,1)} %get-tuple-element.497.grad_ref, ...), custom_call_target="tpu_custom_call" | custom-call | flops 1000 | bytes 1000 | tf_op jit(solution)/shard_map/pallas_call | solution.py:235
  461.3 6.7 %shard_map.233 = (f32[256,1536]{1,0:T(8,128)}, bf16[256,1536]{1,0:T(8,128)(2,1)}, bf16[256,1536]{1,0:T(8,128)(2,1)}, bf16[256,1536]{1,0:T(8,128)(2,1)}) custom-call(f32[1024,1536]{1,0:T(8,128)} %get-tuple-element.505.keep_ref, bf16[1024,1536]{1,0:T(8,128)(2,1)} %copy-done.9), custom_call_target="tpu_custom_call" | custom-call | flops 1000 | bytes 1000 | tf_op jit(solution)/shard_map/pallas_call | solution.py:875
  471.6 3.1 shard_map.234
  474.7 4.1 collective-permute-done.63.refs_1_
  481.3 23.7 %shard_map.235 = (f32[1536,1024]{1,0:T(8,128)}, bf16[1536,1024]{1,0:T(8,128)(2,1)}, bf16[4,384,384]{2,1,0:T(8,128)(2,1)}) custom-call(s32[2]{0:T(128)} %pad_add_fusion.2.places_ref, bf16[1536,2048]{1,0:T(8,128)(2,1)} %get-tuple-element.516.normed_ref, f32[2,96,2048]{2,1,0:T(8,128)} %get-tuple-element.517.query_ref, ...), custom_call_target="tpu_custom_call" | custom-call | flops 1000 | bytes 1000 | tf_op jit(solution)/shard_map/pallas_call | solution.py:837
  514.3 4.0 shard_map.237
  518.3 10.5 %collective-permute-start.75 = (bf16[384,384]{1,0:T(8,128)(2,1)S(1)}, bf16[384,384]{1,0:T(8,128)(2,1)S(1)}, u32[]{:S(2)}, u32[]{:S(2)}) collective-permute-start(bf16[384,384]{1,0:T(8,128)(2,1)S(1)} %get-tuple-element.600), channel_id=1, source_target_pairs={{0,16},{1,17},{2,18},{3,19},{4,20},{5,21},{6,22},{7,23},{8,24},{9,... | collective-permute-start | bytes 884744 | tf_op jit(solution)/shard_map/ppermute | solution.py:289
  528.8 6.8 %shard_map.236 = (f32[1536,256]{1,0:T(8,128)}, bf16[1536,256]{1,0:T(8,128)(2,1)}, bf16[1536,256]{1,0:T(8,128)(2,1)}, bf16[1536,256]{1,0:T(8,128)(2,1)}) custom-call(f32[1536,1024]{1,0:T(8,128)} %get-tuple-element.529.keep_ref, bf16[1536,1024]{1,0:T(8,128)(2,1)} %collective-permute-done.70.arrived_ref), custom_call_target="tpu_custom_call" | custom-call | flops 1000 | bytes 1000 | tf_op jit(solution)/shard_map/pallas_call | solution.py:875
  544.0 6.9 %collective-permute-done.79.refs_2_ = bf16[384,384]{1,0:T(8,128)(2,1)S(1)} collective-permute-done((bf16[384,384]{1,0:T(8,128)(2,1)S(1)}, bf16[384,384]{1,0:T(8,128)(2,1)S(1)}, u32[]{:S(2)}, u32[]{:S(2)}) %collective-permute-start.79) | collective-permute-done | bytes 294944 | tf_op jit(solution)/shard_map/ppermute | solution.py:289
  550.9 5.6 collective-permute-done.76.refs_1_
  556.7 14.7 %collective-permute-done.77.refs_2_ = bf16[1536,256]{1,0:T(8,128)(2,1)} collective-permute-done((bf16[1536,256]{1,0:T(8,128)(2,1)}, bf16[1536,256]{1,0:T(8,128)(2,1)}, u32[]{:S(2)}, u32[]{:S(2)}) %collective-permute-start.77) | collective-permute-done | bytes 786464 | tf_op jit(solution)/shard_map/ppermute | solution.py:281
  571.3 5.5 shard_map.239
  597.2 6.9 %collective-permute-done.91 = bf16[48,1536]{1,0:T(8,128)(2,1)S(1)} collective-permute-done((bf16[48,1536]{1,0:T(8,128)(2,1)}, bf16[48,1536]{1,0:T(8,128)(2,1)S(1)}, u32[]{:S(2)}, u32[]{:S(2)}) %collective-permute-start.91) | collective-permute-done | bytes 147488 | tf_op jit(solution)/shard_map/ppermute | solution.py:315
  604.9 3.7 collective-permute-start.93
  (407 shorter events, 163.3 us)
Async XLA Ops:
  10.5 32.1 %collective-permute-start.7 = (bf16[1536,256]{1,0:T(8,128)(2,1)S(1)}, bf16[1536,256]{1,0:T(8,128)(2,1)}, u32[]{:S(2)}, u32[]{:S(2)}) collective-permute-start(bf16[1536,256]{1,0:T(8,128)(2,1)S(1)} %bitcast.197), channel_id=1, source_target_pairs={{0,2},{1,3},{2,0},{3,1},{4,6},{5,7},{6,4},{7,5},{8,10},{9,11},{10,... | collective-permute-start | bytes 2359304 | tf_op jit(solution)/shard_map/ppermute | solution.py:281
  11.1 31.5 %collective-permute-start.8 = (bf16[1536,256]{1,0:T(8,128)(2,1)S(1)}, bf16[1536,256]{1,0:T(8,128)(2,1)}, u32[]{:S(2)}, u32[]{:S(2)}) collective-permute-start(bf16[1536,256]{1,0:T(8,128)(2,1)S(1)} %bitcast.198), channel_id=1, source_target_pairs={{0,4},{1,5},{2,6},{3,7},{4,0},{5,1},{6,2},{7,3},{8,12},{9,13},{10,... | collective-permute-start | bytes 2359304 | tf_op jit(solution)/shard_map/ppermute | solution.py:281
  14.7 22.7 %collective-permute-start.4 = (bf16[2,48,1536]{2,1,0:T(8,128)(2,1)}, bf16[2,48,1536]{2,1,0:T(8,128)(2,1)S(1)}, u32[]{:S(2)}, u32[]{:S(2)}) collective-permute-start(bf16[2,48,1536]{2,1,0:T(8,128)(2,1)} %get-tuple-element.608), channel_id=1, source_target_pairs={{0,2},{1,3},{2,0},{3,1},{4,6},{5,7},{6,4},{7,5},{8,10},{9,11},{10,... | collective-permute-start | bytes 884744 | tf_op jit(solution)/shard_map/ppermute | solution.py:281
  16.2 24.8 %collective-permute-start.5 = (bf16[2,48,1536]{2,1,0:T(8,128)(2,1)}, bf16[2,48,1536]{2,1,0:T(8,128)(2,1)S(1)}, u32[]{:S(2)}, u32[]{:S(2)}) collective-permute-start(bf16[2,48,1536]{2,1,0:T(8,128)(2,1)} %get-tuple-element.607), channel_id=1, source_target_pairs={{0,4},{1,5},{2,6},{3,7},{4,0},{5,1},{6,2},{7,3},{8,12},{9,13},{10,... | collective-permute-start | bytes 884744 | tf_op jit(solution)/shard_map/ppermute | solution.py:281
  18.0 24.6 %collective-permute-start.6 = (bf16[2,48,1536]{2,1,0:T(8,128)(2,1)S(1)}, bf16[2,48,1536]{2,1,0:T(8,128)(2,1)S(1)}, u32[]{:S(2)}, u32[]{:S(2)}) collective-permute-start(bf16[2,48,1536]{2,1,0:T(8,128)(2,1)S(1)} %get-tuple-element.606), channel_id=1, source_target_pairs={{0,6},{1,7},{2,4},{3,5},{4,2},{5,3},{6,0},{7,1},{8,14},{9,15},{10,... | collective-permute-start | bytes 884744 | tf_op jit(solution)/shard_map/ppermute | solution.py:281
  45.1 28.0 %collective-permute-start.10 = (bf16[8,48,512]{2,1,0:T(8,128)(2,1)S(1)}, bf16[8,48,512]{2,1,0:T(8,128)(2,1)S(1)}, u32[]{:S(2)}, u32[]{:S(2)}) collective-permute-start(bf16[8,48,512]{2,1,0:T(8,128)(2,1)S(1)} %fusion.2.refs_0_), channel_id=1, source_target_pairs={{0,8},{1,9},{2,10},{3,11},{4,12},{5,13},{6,14},{7,15},{8,16},{9,17... | collective-permute-start | bytes 1179656 | tf_op jit(solution)/shard_map/ppermute | solution.py:289
  46.7 34.0 %collective-permute-start.11 = (bf16[8,48,512]{2,1,0:T(8,128)(2,1)S(1)}, bf16[8,48,512]{2,1,0:T(8,128)(2,1)S(1)}, u32[]{:S(2)}, u32[]{:S(2)}) collective-permute-start(bf16[8,48,512]{2,1,0:T(8,128)(2,1)S(1)} %fusion.2.refs_0_), channel_id=1, source_target_pairs={{0,16},{1,17},{2,18},{3,19},{4,20},{5,21},{6,22},{7,23},{8,24},{9,... | collective-permute-start | bytes 1179656 | tf_op jit(solution)/shard_map/ppermute | solution.py:289
  47.9 34.5 %collective-permute-start.12 = (bf16[8,48,512]{2,1,0:T(8,128)(2,1)S(1)}, bf16[8,48,512]{2,1,0:T(8,128)(2,1)S(1)}, u32[]{:S(2)}, u32[]{:S(2)}) collective-permute-start(bf16[8,48,512]{2,1,0:T(8,128)(2,1)S(1)} %fusion.2.refs_0_), channel_id=1, source_target_pairs={{0,24},{1,25},{2,26},{3,27},{4,28},{5,29},{6,30},{7,31},{8,0},{9,1... | collective-permute-start | bytes 1179656 | tf_op jit(solution)/shard_map/ppermute | solution.py:289
  49.8 42.3 %collective-permute-start.14 = (bf16[1536,256]{1,0:T(8,128)(2,1)S(1)}, bf16[1536,256]{1,0:T(8,128)(2,1)}, u32[]{:S(2)}, u32[]{:S(2)}) collective-permute-start(bf16[1536,256]{1,0:T(8,128)(2,1)S(1)} %bitcast.200), channel_id=1, source_target_pairs={{0,1},{1,0},{2,3},{3,2},{4,5},{5,4},{6,7},{7,6},{8,9},{9,8},{10,11... | collective-permute-start | bytes 2359304 | tf_op jit(solution)/shard_map/ppermute | solution.py:281
  63.9 28.2 %collective-permute-start.15 = (bf16[1536,256]{1,0:T(8,128)(2,1)}, bf16[1536,256]{1,0:T(8,128)(2,1)}, u32[]{:S(2)}, u32[]{:S(2)}) collective-permute-start(bf16[1536,256]{1,0:T(8,128)(2,1)} %collective-permute-done.7.refs_1_), channel_id=1, source_target_pairs={{0,1},{1,0},{2,3},{3,2},{4,5},{5,4},{6,7},{7,6},{8,9},{9,8},{10,11... | collective-permute-start | bytes 2359304 | tf_op jit(solution)/shard_map/ppermute | solution.py:281
  98.4 21.3 %collective-permute-start.22 = (bf16[256,1536]{1,0:T(8,128)(2,1)S(1)}, bf16[256,1536]{1,0:T(8,128)(2,1)S(1)}, u32[]{:S(2)}, u32[]{:S(2)}) collective-permute-start(bf16[256,1536]{1,0:T(8,128)(2,1)S(1)} %copy-done.10), channel_id=1, source_target_pairs={{0,2},{1,3},{2,0},{3,1},{4,6},{5,7},{6,4},{7,5},{8,10},{9,11},{10,... | collective-permute-start | bytes 2359304 | tf_op jit(solution)/shard_map/ppermute | solution.py:281
  98.4 21.3 %collective-permute-start.23 = (bf16[256,1536]{1,0:T(8,128)(2,1)S(1)}, bf16[256,1536]{1,0:T(8,128)(2,1)}, u32[]{:S(2)}, u32[]{:S(2)}) collective-permute-start(bf16[256,1536]{1,0:T(8,128)(2,1)S(1)} %copy-done.10), channel_id=1, source_target_pairs={{0,4},{1,5},{2,6},{3,7},{4,0},{5,1},{6,2},{7,3},{8,12},{9,13},{10,... | collective-permute-start | bytes 2359304 | tf_op jit(solution)/shard_map/ppermute | solution.py:281
  132.6 34.4 %collective-permute-start.25 = (bf16[8,48,1536]{2,1,0:T(8,128)(2,1)S(1)}, bf16[8,48,1536]{2,1,0:T(8,128)(2,1)S(1)}, u32[]{:S(2)}, u32[]{:S(2)}) collective-permute-start(bf16[8,48,1536]{2,1,0:T(8,128)(2,1)S(1)} %pad_maximum_fusion.3.refs_0_), channel_id=1, source_target_pairs={{0,8},{1,9},{2,10},{3,11},{4,12},{5,13},{6,14},{7,15},{8,16},{9,17... | collective-permute-start | bytes 3538952 | tf_op jit(solution)/shard_map/ppermute | solution.py:289
  134.8 32.2 %collective-permute-start.26 = (bf16[8,48,1536]{2,1,0:T(8,128)(2,1)S(1)}, bf16[8,48,1536]{2,1,0:T(8,128)(2,1)}, u32[]{:S(2)}, u32[]{:S(2)}) collective-permute-start(bf16[8,48,1536]{2,1,0:T(8,128)(2,1)S(1)} %pad_maximum_fusion.3.refs_0_), channel_id=1, source_target_pairs={{8,0},{9,1},{10,2},{11,3},{12,4},{13,5},{14,6},{15,7},{16,8},{17,9... | collective-permute-start | bytes 3538952 | tf_op jit(solution)/shard_map/ppermute | solution.py:289
  138.5 28.4 %collective-permute-start.27 = (bf16[256,1536]{1,0:T(8,128)(2,1)S(1)}, bf16[256,1536]{1,0:T(8,128)(2,1)S(1)}, u32[]{:S(2)}, u32[]{:S(2)}) collective-permute-start(bf16[256,1536]{1,0:T(8,128)(2,1)S(1)} %copy-done.10), channel_id=1, source_target_pairs={{0,6},{1,7},{2,4},{3,5},{4,2},{5,3},{6,0},{7,1},{8,14},{9,15},{10,... | collective-permute-start | bytes 2359304 | tf_op jit(solution)/shard_map/ppermute | solution.py:281
  173.1 30.5 %collective-permute-start.32 = (bf16[8,48,1536]{2,1,0:T(8,128)(2,1)S(1)}, bf16[8,48,1536]{2,1,0:T(8,128)(2,1)}, u32[]{:S(2)}, u32[]{:S(2)}) collective-permute-start(bf16[8,48,1536]{2,1,0:T(8,128)(2,1)S(1)} %collective-permute-done.25.refs_1_), channel_id=1, source_target_pairs={{0,8},{1,9},{2,10},{3,11},{4,12},{5,13},{6,14},{7,15},{8,16},{9,17... | collective-permute-start | bytes 3538952 | tf_op jit(solution)/shard_map/ppermute | solution.py:289
  177.9 30.2 %collective-permute-start.33 = (bf16[8,48,1536]{2,1,0:T(8,128)(2,1)}, bf16[8,48,1536]{2,1,0:T(8,128)(2,1)}, u32[]{:S(2)}, u32[]{:S(2)}) collective-permute-start(bf16[8,48,1536]{2,1,0:T(8,128)(2,1)} %collective-permute-done.26.refs_2_), channel_id=1, source_target_pairs={{8,0},{9,1},{10,2},{11,3},{12,4},{13,5},{14,6},{15,7},{16,8},{17,9... | collective-permute-start | bytes 3538952 | tf_op jit(solution)/shard_map/ppermute | solution.py:289
  186.8 21.3 %collective-permute-start.30 = (bf16[1536,256]{1,0:T(8,128)(2,1)}, bf16[1536,256]{1,0:T(8,128)(2,1)S(1)}, u32[]{:S(2)}, u32[]{:S(2)}) collective-permute-start(bf16[1536,256]{1,0:T(8,128)(2,1)} %get-tuple-element.374), channel_id=1, source_target_pairs={{0,2},{1,3},{2,0},{3,1},{4,6},{5,7},{6,4},{7,5},{8,10},{9,11},{10,... | collective-permute-start | bytes 2359304 | tf_op jit(solution)/shard_map/ppermute | solution.py:281
  208.1 30.9 %collective-permute-start.35 = (bf16[8,48,1536]{2,1,0:T(8,128)(2,1)}, bf16[8,48,1536]{2,1,0:T(8,128)(2,1)S(1)}, u32[]{:S(2)}, u32[]{:S(2)}) collective-permute-start(bf16[8,48,1536]{2,1,0:T(8,128)(2,1)} %collective-permute-done.32.refs_3_), channel_id=1, source_target_pairs={{0,8},{1,9},{2,10},{3,11},{4,12},{5,13},{6,14},{7,15},{8,16},{9,17... | collective-permute-start | bytes 3538952 | tf_op jit(solution)/shard_map/ppermute | solution.py:289
  210.3 29.3 %collective-permute-start.36 = (bf16[8,48,1536]{2,1,0:T(8,128)(2,1)}, bf16[8,48,1536]{2,1,0:T(8,128)(2,1)S(1)}, u32[]{:S(2)}, u32[]{:S(2)}) collective-permute-start(bf16[8,48,1536]{2,1,0:T(8,128)(2,1)} %collective-permute-done.33.refs_4_), channel_id=1, source_target_pairs={{8,0},{9,1},{10,2},{11,3},{12,4},{13,5},{14,6},{15,7},{16,8},{17,9... | collective-permute-start | bytes 3538952 | tf_op jit(solution)/shard_map/ppermute | solution.py:289
  310.3 56.4 %collective-permute-start.48 = (bf16[1536,256]{1,0:T(8,128)(2,1)S(1)}, bf16[1536,256]{1,0:T(8,128)(2,1)S(1)}, u32[]{:S(2)}, u32[]{:S(2)}) collective-permute-start(bf16[1536,256]{1,0:T(8,128)(2,1)S(1)} %copy-done.42), channel_id=1, source_target_pairs={{0,2},{1,3},{2,0},{3,1},{4,6},{5,7},{6,4},{7,5},{8,10},{9,11},{10,... | collective-permute-start | bytes 2359304 | tf_op jit(solution)/shard_map/ppermute | solution.py:281
  311.6 55.1 %collective-permute-start.49 = (bf16[1536,256]{1,0:T(8,128)(2,1)}, bf16[1536,256]{1,0:T(8,128)(2,1)S(1)}, u32[]{:S(2)}, u32[]{:S(2)}) collective-permute-start(bf16[1536,256]{1,0:T(8,128)(2,1)} %shard_map.225), channel_id=1, source_target_pairs={{0,4},{1,5},{2,6},{3,7},{4,0},{5,1},{6,2},{7,3},{8,12},{9,13},{10,... | collective-permute-start | bytes 2359304 | tf_op jit(solution)/shard_map/ppermute | solution.py:281
  315.6 51.2 %collective-permute-start.50 = (bf16[1536,256]{1,0:T(8,128)(2,1)}, bf16[1536,256]{1,0:T(8,128)(2,1)S(1)}, u32[]{:S(2)}, u32[]{:S(2)}) collective-permute-start(bf16[1536,256]{1,0:T(8,128)(2,1)} %shard_map.226), channel_id=1, source_target_pairs={{0,6},{1,7},{2,4},{3,5},{4,2},{5,3},{6,0},{7,1},{8,14},{9,15},{10,... | collective-permute-start | bytes 2359304 | tf_op jit(solution)/shard_map/ppermute | solution.py:281
  349.2 38.7 %collective-permute-start.54 = (bf16[384,1024]{1,0:T(8,128)(2,1)S(1)}, bf16[384,1024]{1,0:T(8,128)(2,1)S(1)}, u32[]{:S(2)}, u32[]{:S(2)}) collective-permute-start(bf16[384,1024]{1,0:T(8,128)(2,1)S(1)} %get-tuple-element.593), channel_id=1, source_target_pairs={{0,8},{1,9},{2,10},{3,11},{4,12},{5,13},{6,14},{7,15},{8,16},{9,17... | collective-permute-start | bytes 2359304 | tf_op jit(solution)/shard_map/ppermute | solution.py:289
  350.8 49.9 %collective-permute-start.55 = (bf16[384,1024]{1,0:T(8,128)(2,1)S(1)}, bf16[384,1024]{1,0:T(8,128)(2,1)S(1)}, u32[]{:S(2)}, u32[]{:S(2)}) collective-permute-start(bf16[384,1024]{1,0:T(8,128)(2,1)S(1)} %get-tuple-element.592), channel_id=1, source_target_pairs={{0,16},{1,17},{2,18},{3,19},{4,20},{5,21},{6,22},{7,23},{8,24},{9,... | collective-permute-start | bytes 2359304 | tf_op jit(solution)/shard_map/ppermute | solution.py:289
  374.4 26.3 %collective-permute-start.51 = (bf16[1536,256]{1,0:T(8,128)(2,1)}, bf16[1536,256]{1,0:T(8,128)(2,1)S(1)}, u32[]{:S(2)}, u32[]{:S(2)}) collective-permute-start(bf16[1536,256]{1,0:T(8,128)(2,1)} %get-tuple-element.485.refs_0_), channel_id=1, source_target_pairs={{0,2},{1,3},{2,0},{3,1},{4,6},{5,7},{6,4},{7,5},{8,10},{9,11},{10,... | collective-permute-start | bytes 2359304 | tf_op jit(solution)/shard_map/ppermute | solution.py:281
  376.0 34.9 %collective-permute-start.52 = (bf16[1536,256]{1,0:T(8,128)(2,1)}, bf16[1536,256]{1,0:T(8,128)(2,1)S(1)}, u32[]{:S(2)}, u32[]{:S(2)}) collective-permute-start(bf16[1536,256]{1,0:T(8,128)(2,1)} %get-tuple-element.485.refs_0_), channel_id=1, source_target_pairs={{0,4},{1,5},{2,6},{3,7},{4,0},{5,1},{6,2},{7,3},{8,12},{9,13},{10,... | collective-permute-start | bytes 2359304 | tf_op jit(solution)/shard_map/ppermute | solution.py:281
  376.6 34.3 %collective-permute-start.53 = (bf16[1536,256]{1,0:T(8,128)(2,1)}, bf16[1536,256]{1,0:T(8,128)(2,1)S(1)}, u32[]{:S(2)}, u32[]{:S(2)}) collective-permute-start(bf16[1536,256]{1,0:T(8,128)(2,1)} %get-tuple-element.485.refs_0_), channel_id=1, source_target_pairs={{0,6},{1,7},{2,4},{3,5},{4,2},{5,3},{6,0},{7,1},{8,14},{9,15},{10,... | collective-permute-start | bytes 2359304 | tf_op jit(solution)/shard_map/ppermute | solution.py:281
  428.9 28.5 %collective-permute-start.62 = (bf16[1024,1536]{1,0:T(8,128)(2,1)}, bf16[1024,1536]{1,0:T(8,128)(2,1)S(1)}, u32[]{:S(2)}, u32[]{:S(2)}) collective-permute-start(bf16[1024,1536]{1,0:T(8,128)(2,1)} %get-tuple-element.503), channel_id=1, source_target_pairs={{0,1},{1,0},{2,3},{3,2},{4,5},{5,4},{6,7},{7,6},{8,9},{9,8},{10,11... | collective-permute-start | bytes 9437192 | tf_op jit(solution)/shard_map/ppermute | solution.py:281
  429.1 25.2 %collective-permute-start.60 = (bf16[384,1024]{1,0:T(8,128)(2,1)S(1)}, bf16[384,1024]{1,0:T(8,128)(2,1)S(1)}, u32[]{:S(2)}, u32[]{:S(2)}) collective-permute-start(bf16[384,1024]{1,0:T(8,128)(2,1)S(1)} %get-tuple-element.591), channel_id=1, source_target_pairs={{0,24},{1,25},{2,26},{3,27},{4,28},{5,29},{6,30},{7,31},{8,0},{9,1... | collective-permute-start | bytes 2359304 | tf_op jit(solution)/shard_map/ppermute | solution.py:289
  429.9 27.4 %collective-permute-start.61 = (bf16[128,1536]{1,0:T(8,128)(2,1)S(1)}, bf16[128,1536]{1,0:T(8,128)(2,1)S(1)}, u32[]{:S(2)}, u32[]{:S(2)}) collective-permute-start(bf16[128,1536]{1,0:T(8,128)(2,1)S(1)} %get-tuple-element.596), channel_id=1, source_target_pairs={{0,24},{1,25},{2,26},{3,27},{4,28},{5,29},{6,30},{7,31},{8,0},{9,1... | collective-permute-start | bytes 1179656 | tf_op jit(solution)/shard_map/ppermute | solution.py:289
  457.3 21.4 %collective-permute-start.63 = (bf16[2,1,96,2048]{3,2,1,0:T(8,128)(2,1)}, bf16[2,1,96,2048]{3,2,1,0:T(8,128)(2,1)S(1)}, u32[]{:S(2)}, u32[]{:S(2)}) collective-permute-start(bf16[2,1,96,2048]{3,2,1,0:T(8,128)(2,1)} %bitcast.261), channel_id=1, source_target_pairs={{8,0},{9,1},{10,2},{11,3},{12,4},{13,5},{14,6},{15,7},{16,8},{17,9... | collective-permute-start | bytes 2359304 | tf_op jit(solution)/shard_map/ppermute | solution.py:289
  459.5 21.0 %collective-permute-start.67 = (bf16[128,1536]{1,0:T(8,128)(2,1)S(1)}, bf16[128,1536]{1,0:T(8,128)(2,1)S(1)}, u32[]{:S(2)}, u32[]{:S(2)}) collective-permute-start(bf16[128,1536]{1,0:T(8,128)(2,1)S(1)} %get-tuple-element.595), channel_id=1, source_target_pairs={{0,8},{1,9},{2,10},{3,11},{4,12},{5,13},{6,14},{7,15},{8,16},{9,17... | collective-permute-start | bytes 1179656 | tf_op jit(solution)/shard_map/ppermute | solution.py:289
  468.0 37.1 %collective-permute-start.64 = (bf16[256,1536]{1,0:T(8,128)(2,1)}, bf16[256,1536]{1,0:T(8,128)(2,1)S(1)}, u32[]{:S(2)}, u32[]{:S(2)}) collective-permute-start(bf16[256,1536]{1,0:T(8,128)(2,1)} %get-tuple-element.522), channel_id=1, source_target_pairs={{0,2},{1,3},{2,0},{3,1},{4,6},{5,7},{6,4},{7,5},{8,10},{9,11},{10,... | collective-permute-start | bytes 2359304 | tf_op jit(solution)/shard_map/ppermute | solution.py:281
  468.5 36.6 %collective-permute-start.65 = (bf16[256,1536]{1,0:T(8,128)(2,1)}, bf16[256,1536]{1,0:T(8,128)(2,1)S(1)}, u32[]{:S(2)}, u32[]{:S(2)}) collective-permute-start(bf16[256,1536]{1,0:T(8,128)(2,1)} %get-tuple-element.523), channel_id=1, source_target_pairs={{0,4},{1,5},{2,6},{3,7},{4,0},{5,1},{6,2},{7,3},{8,12},{9,13},{10,... | collective-permute-start | bytes 2359304 | tf_op jit(solution)/shard_map/ppermute | solution.py:281
  469.7 35.4 %collective-permute-start.66 = (bf16[256,1536]{1,0:T(8,128)(2,1)}, bf16[256,1536]{1,0:T(8,128)(2,1)}, u32[]{:S(2)}, u32[]{:S(2)}) collective-permute-start(bf16[256,1536]{1,0:T(8,128)(2,1)} %get-tuple-element.524), channel_id=1, source_target_pairs={{0,6},{1,7},{2,4},{3,5},{4,2},{5,3},{6,0},{7,1},{8,14},{9,15},{10,... | collective-permute-start | bytes 2359304 | tf_op jit(solution)/shard_map/ppermute | solution.py:281
  478.7 26.3 %collective-permute-start.68 = (bf16[128,1536]{1,0:T(8,128)(2,1)}, bf16[128,1536]{1,0:T(8,128)(2,1)S(1)}, u32[]{:S(2)}, u32[]{:S(2)}) collective-permute-start(bf16[128,1536]{1,0:T(8,128)(2,1)} %get-tuple-element.594), channel_id=1, source_target_pairs={{0,16},{1,17},{2,18},{3,19},{4,20},{5,21},{6,22},{7,23},{8,24},{9,... | collective-permute-start | bytes 1179656 | tf_op jit(solution)/shard_map/ppermute | solution.py:289
  480.6 24.6 %collective-permute-start.69 = (bf16[4,48,1024]{2,1,0:T(8,128)(2,1)S(1)}, bf16[4,48,1024]{2,1,0:T(8,128)(2,1)}, u32[]{:S(2)}, u32[]{:S(2)}) collective-permute-start(bf16[4,48,1024]{2,1,0:T(8,128)(2,1)S(1)} %dynamic-slice_bitcast_fusion.2), channel_id=1, source_target_pairs={{0,1},{1,0},{2,3},{3,2},{4,5},{5,4},{6,7},{7,6},{8,9},{9,8},{10,11... | collective-permute-start | bytes 1179656 | tf_op jit(solution)/shard_map/ppermute | solution.py:281
  507.0 28.6 %collective-permute-start.71 = (bf16[2,48,1024]{2,1,0:T(8,128)(2,1)S(1)}, bf16[2,48,1024]{2,1,0:T(8,128)(2,1)S(1)}, u32[]{:S(2)}, u32[]{:S(2)}) collective-permute-start(bf16[2,48,1024]{2,1,0:T(8,128)(2,1)S(1)} %get-tuple-element.618), channel_id=1, source_target_pairs={{0,2},{1,3},{2,0},{3,1},{4,6},{5,7},{6,4},{7,5},{8,10},{9,11},{10,... | collective-permute-start | bytes 589832 | tf_op jit(solution)/shard_map/ppermute | solution.py:281
  507.4 28.1 %collective-permute-start.72 = (bf16[2,48,1024]{2,1,0:T(8,128)(2,1)S(1)}, bf16[2,48,1024]{2,1,0:T(8,128)(2,1)S(1)}, u32[]{:S(2)}, u32[]{:S(2)}) collective-permute-start(bf16[2,48,1024]{2,1,0:T(8,128)(2,1)S(1)} %get-tuple-element.619), channel_id=1, source_target_pairs={{0,4},{1,5},{2,6},{3,7},{4,0},{5,1},{6,2},{7,3},{8,12},{9,13},{10,... | collective-permute-start | bytes 589832 | tf_op jit(solution)/shard_map/ppermute | solution.py:281
  508.7 26.9 %collective-permute-start.73 = (bf16[2,48,1024]{2,1,0:T(8,128)(2,1)S(1)}, bf16[2,48,1024]{2,1,0:T(8,128)(2,1)S(1)}, u32[]{:S(2)}, u32[]{:S(2)}) collective-permute-start(bf16[2,48,1024]{2,1,0:T(8,128)(2,1)S(1)} %get-tuple-element.616), channel_id=1, source_target_pairs={{0,6},{1,7},{2,4},{3,5},{4,2},{5,3},{6,0},{7,1},{8,14},{9,15},{10,... | collective-permute-start | bytes 589832 | tf_op jit(solution)/shard_map/ppermute | solution.py:281
  510.6 29.3 %collective-permute-start.74 = (bf16[384,384]{1,0:T(8,128)(2,1)S(1)}, bf16[384,384]{1,0:T(8,128)(2,1)S(1)}, u32[]{:S(2)}, u32[]{:S(2)}) collective-permute-start(bf16[384,384]{1,0:T(8,128)(2,1)S(1)} %get-tuple-element.601), channel_id=1, source_target_pairs={{0,8},{1,9},{2,10},{3,11},{4,12},{5,13},{6,14},{7,15},{8,16},{9,17... | collective-permute-start | bytes 884744 | tf_op jit(solution)/shard_map/ppermute | solution.py:289
  518.3 21.7 %collective-permute-start.75 = (bf16[384,384]{1,0:T(8,128)(2,1)S(1)}, bf16[384,384]{1,0:T(8,128)(2,1)S(1)}, u32[]{:S(2)}, u32[]{:S(2)}) collective-permute-start(bf16[384,384]{1,0:T(8,128)(2,1)S(1)} %get-tuple-element.600), channel_id=1, source_target_pairs={{0,16},{1,17},{2,18},{3,19},{4,20},{5,21},{6,22},{7,23},{8,24},{9,... | collective-permute-start | bytes 884744 | tf_op jit(solution)/shard_map/ppermute | solution.py:289
  536.1 35.2 %collective-permute-start.77 = (bf16[1536,256]{1,0:T(8,128)(2,1)}, bf16[1536,256]{1,0:T(8,128)(2,1)}, u32[]{:S(2)}, u32[]{:S(2)}) collective-permute-start(bf16[1536,256]{1,0:T(8,128)(2,1)} %get-tuple-element.549), channel_id=1, source_target_pairs={{0,4},{1,5},{2,6},{3,7},{4,0},{5,1},{6,2},{7,3},{8,12},{9,13},{10,... | collective-permute-start | bytes 2359304 | tf_op jit(solution)/shard_map/ppermute | solution.py:281
  537.3 34.0 %collective-permute-start.78 = (bf16[1536,256]{1,0:T(8,128)(2,1)}, bf16[1536,256]{1,0:T(8,128)(2,1)}, u32[]{:S(2)}, u32[]{:S(2)}) collective-permute-start(bf16[1536,256]{1,0:T(8,128)(2,1)} %get-tuple-element.550), channel_id=1, source_target_pairs={{0,6},{1,7},{2,4},{3,5},{4,2},{5,3},{6,0},{7,1},{8,14},{9,15},{10,... | collective-permute-start | bytes 2359304 | tf_op jit(solution)/shard_map/ppermute | solution.py:281
  540.0 44.1 %collective-permute-start.82 = (bf16[48,1536]{1,0:T(8,128)(2,1)}, bf16[48,1536]{1,0:T(8,128)(2,1)}, u32[]{:S(2)}, u32[]{:S(2)}) collective-permute-start(bf16[48,1536]{1,0:T(8,128)(2,1)} %get-tuple-element.622), channel_id=1, source_target_pairs={{0,8},{1,9},{2,10},{3,11},{4,12},{5,13},{6,14},{7,15},{8,16},{9,17... | collective-permute-start | bytes 442376 | tf_op jit(solution)/shard_map/ppermute | solution.py:289
  550.9 33.2 %collective-permute-start.83 = (bf16[48,1536]{1,0:T(8,128)(2,1)S(1)}, bf16[48,1536]{1,0:T(8,128)(2,1)S(1)}, u32[]{:S(2)}, u32[]{:S(2)}) collective-permute-start(bf16[48,1536]{1,0:T(8,128)(2,1)S(1)} %copy-done.68), channel_id=1, source_target_pairs={{0,16},{1,17},{2,18},{3,19},{4,20},{5,21},{6,22},{7,23},{8,24},{9,... | collective-permute-start | bytes 442376 | tf_op jit(solution)/shard_map/ppermute | solution.py:289
  556.5 27.7 %collective-permute-start.84 = (bf16[48,1536]{1,0:T(8,128)(2,1)S(1)}, bf16[48,1536]{1,0:T(8,128)(2,1)S(1)}, u32[]{:S(2)}, u32[]{:S(2)}) collective-permute-start(bf16[48,1536]{1,0:T(8,128)(2,1)S(1)} %copy-done.67), channel_id=1, source_target_pairs={{0,24},{1,25},{2,26},{3,27},{4,28},{5,29},{6,30},{7,31},{8,0},{9,1... | collective-permute-start | bytes 442376 | tf_op jit(solution)/shard_map/ppermute | solution.py:289
  (122 other events, 1296.7 us)

commit v5 on v4

--- a/solution.py
+++ b/solution.py
@@ -1076,40 +1076,34 @@
     down_thirds = jnp.concatenate(
         [down_weight[:, part * third : (part + 1) * third] for part in range(3)], axis=0
     ).reshape(TEAM, rows, third)
-    cosine, sine_table, starts, low, down_thirds, pairs, inputs_two, inputs_t = order.step(
-        cosine, sine_table, starts, low, down_thirds, pairs, inputs_two, inputs_t
+    cosine, sine_table, starts, low, down_thirds, pairs, inputs_two, inputs_t, out_weight = (
+        order.step(
+            cosine, sine_table, starts, low, down_thirds, pairs, inputs_two, inputs_t, out_weight
+        )
     )
     inputs_three = grid.turn(inputs_t, 6)
+    out_own = grid.to_members(out_weight)
     pairs = jnp.stack(pairs)
     pairs_keep, pairs_give = dynamic(pairs, core, 1), dynamic(pairs, 1 - core, 1)
     team_rows = jnp.concatenate([pairs_keep, grid.turn(pairs_give, 1)], axis=0)
-    attn_rows, team_rows, out_weight = order.step(
-        team_rows[..., :attn_wide], team_rows, out_weight
-    )
+    attn_rows, team_rows = order.step(team_rows[..., :attn_wide], team_rows)
     attn_z = grid.spread(attn_rows)
     inputs_others = [grid.turn(block, 1) for block in [inputs_t] + inputs_two]
-    attn_z, inputs_three = order.step(attn_z, inputs_three)
+    attn_z, inputs_three, out_own = order.step(attn_z, inputs_three, out_own)
     inputs_others = inputs_others + [grid.turn(inputs_three, 1)]
     inputs_team = [inputs_t] + inputs_two + [inputs_three] + inputs_others
-    out_own = grid.to_members(out_weight)
     attn_w = place_rows(grid, attn_z, 0, attn_wide).reshape(width, attn_wide)
-    attn_w, inputs_team, out_own = order.step(attn_w, inputs_team, out_own)
-
-    out_own, cotangent = order.step(out_own, cotangent)
+    attn_w, inputs_team = order.step(attn_w, inputs_team)
+
+    normed_first, queries, own_piece = project(inputs_team, attn_w, cosine, sine_table)
+    own_piece, out_own, attn_w = order.step(own_piece, out_own, attn_w)
+    arrived = [grid.shift(own_piece, step, False) for step in range(1, steps_back + 1)]
     out_z = grid.spread(out_own)
-    cotangent_chips = [cotangent, grid.turn(cotangent, 2), grid.turn(cotangent, 4)]
-    normed_first, queries, own_piece = project(inputs_team, attn_w, cosine, sine_table)
-    own_piece, out_z, attn_w = order.step(own_piece, out_z, attn_w)
-    arrived = [grid.shift(own_piece, step, False) for step in range(1, steps_back + 1)]
-    cotangent_chips = order.step(cotangent_chips)
-    cotangent_chips = cotangent_chips + [grid.turn(cotangent_chips[0], 6)]
-    out_rows = place_rows(grid, [block[None] for block in out_z], 0, width)
-    out_rows = out_rows.reshape(Q_WIDTH, width)
     gain_first = attn_w[:, LINED : LINED + 1].astype(f32)
     gain_second = attn_w[:, LINED + 1 : LINED + 2].astype(f32)
     mixer_own = jnp.concatenate([team_rows[..., attn_wide:], down_thirds], axis=-1)
-    arrived, gain_first, gain_second, mixer_own, out_rows = order.step(
-        arrived, gain_first, gain_second, mixer_own, out_rows
+    arrived, gain_first, gain_second, mixer_own, out_z, cotangent = order.step(
+        arrived, gain_first, gain_second, mixer_own, out_z, cotangent
     )
 
     mixer_hops = [grid.both_ways(mixer_own, mixer_own)]
@@ -1118,6 +1112,9 @@
         if len(mixer_hops) < teams - 1:
             mixer_hops.append(grid.both_ways(*mixer_hops[-1]))
 
+    cotangent_chips = grid.chips(cotangent)
+    out_rows = place_rows(grid, [block[None] for block in out_z], 0, width)
+    out_rows = out_rows.reshape(Q_WIDTH, width)
     pieces = [own_piece] + arrived
     attended, normalizer = attend(low, starts, queries, pieces, 0, OWN_KV)
     keep, give = project_out(attended, out_rows)

time: 629 us -> 648 us (1.030)
  waiting for transfers between devices: 190 us -> 207 us
    ppermute x1, waiting for transfers between devices: 2.36 us -> 35.1 us  [to_members(): return lax.ppermute(value, 'dev', pairs)]
    ppermute x64, waiting for transfers between devices: 102 us -> 82.2 us  [turn(): lax.ppermute(value, 'dev', [(d, d ^ bits) for d in range(self.count)])]
    unnamed x157 -> x159, local copies, waits for them, and re-layouts: 10.9 us -> 13.1 us
  transfers between devices with their start and end apart: 95 -> 95, of which waited for: 33 -> 28; matrix products, arithmetic and copies ran while one was open for 5% -> 5% of each run, Pallas kernels for 41% -> 39%
where the time goes in v5:
time: 648 us; the launch traced here: 638 us
  Pallas kernels  270 us (42%)
  waiting for transfers between devices  207 us (32%)
  starting transfers between devices  111 us (17%)
  local copies, waits for them, and re-layouts  35 us (5%)
  other arithmetic  12.1 us (2%)
    ppermute x29, waiting for transfers between devices, shift(): return lax.ppermute(value, 'dev', pairs)  82.8 us
    ppermute x64, waiting for transfers between devices, turn(): lax.ppermute(value, 'dev', [(d, d ^ bits) for d in range(self.count)])  82.2 us
    ppermute x29, starting transfers between devices, shift(): return lax.ppermute(value, 'dev', pairs)  56.4 us
    ppermute x64, starting transfers between devices, turn(): lax.ppermute(value, 'dev', [(d, d ^ bits) for d in range(self.count)])  50.9 us
    pallas_call x4, Pallas kernels, mixer(): call(kernel, (2,), [fixed(normed[0]), fixed(normed[1]), block, block, fix...  42.7 us
    ppermute x1, waiting for transfers between devices, to_members(): return lax.ppermute(value, 'dev', pairs)  35.1 us
    pallas_call x1, Pallas kernels, token_product(): call(kernel, (TEAM,), [fixed(block) for block in list(lefts) + list(right...  30.3 us
    pallas_call x1, Pallas kernels, attend_back(): pl.pallas_call(gradient_kernel, grid=(count,), in_specs=[low_spec, whole,...  25.9 us
  transfers between devices with their start and end apart: 95, of which 28 were waited for; matrix products, arithmetic and copies ran while one was open for 5% of the time, Pallas kernels for 39%

profile of v5, /device:TPU:10, one launch (start us, length us, event | category | flops | bytes accessed | tf_op | source)
XLA Modules:
  0.0 638.3 jit_solution(7325055750255567783)
XLA Ops:
  21.0 3.6 fusion
  24.6 12.8 %collective-permute-done.4 = bf16[2,48,1536]{2,1,0:T(8,128)(2,1)S(1)} collective-permute-done((bf16[2,48,1536]{2,1,0:T(8,128)(2,1)}, bf16[2,48,1536]{2,1,0:T(8,128)(2,1)S(1)}, u32[]{:S(2)}, u32[]{:S(2)}) %collective-permute-start.4) | collective-permute-done | bytes 294944 | tf_op jit(solution)/shard_map/ppermute | solution.py:281
  37.4 3.7 collective-permute-done.5
  51.9 35.1 %collective-permute-done.14 = bf16[48,1536]{1,0:T(8,128)(2,1)S(1)} collective-permute-done((bf16[48,1536]{1,0:T(8,128)(2,1)S(1)}, bf16[48,1536]{1,0:T(8,128)(2,1)S(1)}, u32[]{:S(2)}, u32[]{:S(2)}) %collective-permute-start.14) | collective-permute-done | bytes 147488 | tf_op jit(solution)/shard_map/ppermute | solution.py:308
  89.4 3.8 shard_map.212
  93.3 11.8 %shard_map.213 = (bf16[1536,2048]{1,0:T(8,128)(2,1)}, bf16[2,96,2048]{2,1,0:T(8,128)(2,1)}, bf16[2,1,96,2048]{3,2,1,0:T(8,128)(2,1)}) custom-call(bf16[1536,512]{1,0:T(8,128)(2,1)} %bitcast.194, f32[96,2048]{1,0:T(8,128)} %get-tuple-element.317.cosine_ref, f32[96,2048]{1,0:T(8,128)} %get-tuple-element.318.sine_ref, bf16[1536,256]{1,0:T(8,128)(2,1)} %bitcast.201, ...), custom_call_target="tpu_custom_call" | custom-call | flops 1000 | bytes 1000 | tf_op jit(solution)/shard_map/pallas_call | solution.py:514
  105.1 4.4 collective-permute-start.19
  114.0 23.1 %collective-permute-done.20 = bf16[48,1536]{1,0:T(8,128)(2,1)S(1)} collective-permute-done((bf16[48,1536]{1,0:T(8,128)(2,1)S(1)}, bf16[48,1536]{1,0:T(8,128)(2,1)S(1)}, u32[]{:S(2)}, u32[]{:S(2)}) %collective-permute-start.20) | collective-permute-done | bytes 147488 | tf_op jit(solution)/shard_map/ppermute | solution.py:289
  141.5 4.0 collective-permute-start.24
  149.1 19.4 %shard_map.214 = (f32[2,96,2048]{2,1,0:T(8,128)}, f32[2,1,2048]{2,1,0:T(1,128)}) custom-call(s32[9]{0:T(128)} %pad_add_fusion.1.low_ref, s32[1,2048]{1,0:T(1,128)} %bitcast.245, bf16[2,96,2048]{2,1,0:T(8,128)(2,1)} %get-tuple-element.338.query_ref, bf16[2,1,96,2048]{3,2,1,0:T(8,128)(2,1)} %get-tuple-element.330.refs_0_, bf16[2,1,96,2048]{3,2,1,0:T(8,128)(2,1)} %copy-done.7), custom_call_target="tpu_custom_call" | custom-call | flops 1000 | bytes 1000 | tf_op jit(solution)/shard_map/pallas_call | solution.py:209
  168.5 3.3 shard_map.215
  171.8 9.4 %shard_map.216 = (f32[1536,1024]{1,0:T(8,128)}, bf16[1536,1024]{1,0:T(8,128)(2,1)}) custom-call(f32[2,96,2048]{2,1,0:T(8,128)} %get-tuple-element.340.attended_ref.out_ref, bf16[192,1536]{1,0:T(8,128)(2,1)} %bitcast.204), custom_call_target="tpu_custom_call" | custom-call | flops 1000 | bytes 1000 | tf_op jit(solution)/shard_map/pallas_call | solution.py:552
  183.2 4.1 collective-permute-done.28.arrived_ref
  187.4 3.8 collective-permute-start.32
  191.2 3.1 collective-permute-start.33
  194.3 6.8 %shard_map.217 = (f32[1536,256]{1,0:T(8,128)}, bf16[1536,256]{1,0:T(8,128)(2,1)}, bf16[1536,256]{1,0:T(8,128)(2,1)}, bf16[1536,256]{1,0:T(8,128)(2,1)}) custom-call(f32[1536,1024]{1,0:T(8,128)} %get-tuple-element.355.keep_ref, bf16[1536,1024]{1,0:T(8,128)(2,1)} %collective-permute-done.28.arrived_ref), custom_call_target="tpu_custom_call" | custom-call | flops 1000 | bytes 1000 | tf_op jit(solution)/shard_map/pallas_call | solution.py:875
  202.8 14.8 %collective-permute-done.32.refs_3_ = bf16[8,48,1536]{2,1,0:T(8,128)(2,1)} collective-permute-done((bf16[8,48,1536]{2,1,0:T(8,128)(2,1)S(1)}, bf16[8,48,1536]{2,1,0:T(8,128)(2,1)}, u32[]{:S(2)}, u32[]{:S(2)}) %collective-permute-start.32) | collective-permute-done | bytes 1179680 | tf_op jit(solution)/shard_map/ppermute | solution.py:289
  217.6 4.6 collective-permute-done.33.refs_4_
  222.3 3.6 collective-permute-start.35
  229.7 18.1 %collective-permute-done.34.refs_3_ = bf16[1536,256]{1,0:T(8,128)(2,1)S(1)} collective-permute-done((bf16[1536,256]{1,0:T(8,128)(2,1)}, bf16[1536,256]{1,0:T(8,128)(2,1)S(1)}, u32[]{:S(2)}, u32[]{:S(2)}) %collective-permute-start.34) | collective-permute-done | bytes 786464 | tf_op jit(solution)/shard_map/ppermute | solution.py:281
  248.7 4.7 shard_map.218
  257.0 6.7 %shard_map.219 = (bf16[4,8,48,1024]{3,2,1,0:T(8,128)(2,1)}, bf16[4,128,1536]{2,1,0:T(8,128)(2,1)}) custom-call(s32[2]{0:T(128)} %pad_add_fusion.2.places_ref, bf16[8,48,1536]{2,1,0:T(8,128)(2,1)} %copy-done.5, bf16[8,48,1536]{2,1,0:T(8,128)(2,1)} %copy-done.22, bf16[8,48,1536]{2,1,0:T(8,128)(2,1)} %collective-permute-done.24.refs_2_, ...), custom_call_target="tpu_custom_call" | custom-call | flops 1000 | bytes 1000 | tf_op jit(solution)/shard_map/pallas_call | solution.py:461
  264.6 10.6 %shard_map.220 = (bf16[512,512]{1,0:T(8,128)(2,1)}, bf16[512,1024]{1,0:T(8,128)(2,1)}, f32[1536,256]{1,0:T(8,128)}, bf16[1536,256]{1,0:T(8,128)(2,1)}) custom-call(bf16[1536,256]{1,0:T(8,128)(2,1)} %get-tuple-element.400.first_ref.refs_0_, bf16[1536,256]{1,0:T(8,128)(2,1)} %copy-done.12, bf16[4,256,1536]{2,1,0:T(8,128)(2,1)} %copy-done, ...), custom_call_target="tpu_custom_call" | custom-call | flops 1000 | bytes 1000 | tf_op jit(solution)/shard_map/pallas_call | solution.py:602
  279.9 10.9 %shard_map.221 = (bf16[512,512]{1,0:T(8,128)(2,1)}, bf16[512,1024]{1,0:T(8,128)(2,1)}, f32[1536,256]{1,0:T(8,128)}, bf16[1536,256]{1,0:T(8,128)(2,1)}) custom-call(bf16[1536,256]{1,0:T(8,128)(2,1)} %copy-done.13, bf16[1536,256]{1,0:T(8,128)(2,1)} %copy-done.15, bf16[4,256,1536]{2,1,0:T(8,128)(2,1)} %copy-done, bf16[4,256,1536]{2,1,0:T(8,128)(2,1)} %copy-done.1, ...), custom_call_target="tpu_custom_call" | custom-call | flops 1000 | bytes 1000 | tf_op jit(solution)/shard_map/pallas_call | solution.py:602
  290.9 6.5 %collective-permute-done.42.first_ref.refs_3_ = bf16[1536,256]{1,0:T(8,128)(2,1)S(1)} collective-permute-done((bf16[1536,256]{1,0:T(8,128)(2,1)S(1)}, bf16[1536,256]{1,0:T(8,128)(2,1)S(1)}, u32[]{:S(2)}, u32[]{:S(2)}) %collective-permute-start.42) | collective-permute-done | bytes 786464 | tf_op jit(solution)/shard_map/ppermute | solution.py:281
  297.9 10.6 %shard_map.222 = (bf16[512,512]{1,0:T(8,128)(2,1)}, bf16[512,1024]{1,0:T(8,128)(2,1)}, f32[1536,256]{1,0:T(8,128)}, bf16[1536,256]{1,0:T(8,128)(2,1)}) custom-call(bf16[1536,256]{1,0:T(8,128)(2,1)} %copy-done.14, bf16[1536,256]{1,0:T(8,128)(2,1)} %copy-done.16, bf16[4,256,1536]{2,1,0:T(8,128)(2,1)} %copy-done, bf16[4,256,1536]{2,1,0:T(8,128)(2,1)} %copy-done.1, ...), custom_call_target="tpu_custom_call" | custom-call | flops 1000 | bytes 1000 | tf_op jit(solution)/shard_map/pallas_call | solution.py:602
  309.6 10.5 %shard_map.224 = (bf16[512,512]{1,0:T(8,128)(2,1)}, bf16[512,1024]{1,0:T(8,128)(2,1)}, f32[1536,256]{1,0:T(8,128)}, bf16[1536,256]{1,0:T(8,128)(2,1)}) custom-call(bf16[1536,256]{1,0:T(8,128)(2,1)} %copy-done.17, bf16[1536,256]{1,0:T(8,128)(2,1)} %copy-done.18, bf16[4,256,1536]{2,1,0:T(8,128)(2,1)} %copy-done, bf16[4,256,1536]{2,1,0:T(8,128)(2,1)} %copy-done.1, ...), custom_call_target="tpu_custom_call" | custom-call | flops 1000 | bytes 1000 | tf_op jit(solution)/shard_map/pallas_call | solution.py:602
  333.4 30.3 %shard_map.227.own_ref = bf16[4,384,1024]{2,1,0:T(8,128)(2,1)} custom-call(s32[2]{0:T(128)} %pad_add_fusion.2.places_ref, bf16[1536,256]{1,0:T(8,128)(2,1)} %get-tuple-element.400.first_ref.refs_0_, bf16[1536,256]{1,0:T(8,128)(2,1)} %copy-done.13, bf16[1536,256]{1,0:T(8,128)(2,1)} %copy-done.14, bf16[1536,256]{1,0:T(8,128)(2,1)} %copy-done.17, ...), custom_call_target="tpu_custom_call" | custom-call | flops 1000 | bytes 1000 | tf_op jit(solution)/shard_map/pallas_call | solution.py:695
  368.6 13.8 %shard_map.228.own_ref = bf16[4,128,1536]{2,1,0:T(8,128)(2,1)} custom-call(s32[2]{0:T(128)} %pad_add_fusion.2.places_ref, bf16[512,512]{1,0:T(8,128)(2,1)} %get-tuple-element.461.refs_0_, bf16[512,512]{1,0:T(8,128)(2,1)} %get-tuple-element.462.refs_1_, bf16[512,512]{1,0:T(8,128)(2,1)} %get-tuple-element.463.refs_2_, ...), custom_call_target="tpu_custom_call" | custom-call | flops 1000 | bytes 1000 | tf_op jit(solution)/shard_map/pallas_call | solution.py:730
  383.8 6.2 shard_map.229
  393.5 10.0 %shard_map.230 = (f32[1024,1536]{1,0:T(8,128)}, bf16[1024,1536]{1,0:T(8,128)(2,1)}) custom-call(bf16[512,1536]{1,0:T(8,128)(2,1)} %bitcast.193, bf16[512,512]{1,0:T(8,128)(2,1)} %get-tuple-element.461.refs_0_, bf16[512,512]{1,0:T(8,128)(2,1)} %get-tuple-element.462.refs_1_, bf16[512,512]{1,0:T(8,128)(2,1)} %get-tuple-element.463.refs_2_, ...), custom_call_target="tpu_custom_call" | custom-call | flops 1000 | bytes 1000 | tf_op jit(solution)/shard_map/pallas_call | solution.py:647
  403.6 12.6 %collective-permute-done.55.refs_1_ = bf16[384,1024]{1,0:T(8,128)(2,1)S(1)} collective-permute-done((bf16[384,1024]{1,0:T(8,128)(2,1)S(1)}, bf16[384,1024]{1,0:T(8,128)(2,1)S(1)}, u32[]{:S(2)}, u32[]{:S(2)}) %collective-permute-start.55) | collective-permute-done | bytes 786464 | tf_op jit(solution)/shard_map/ppermute | solution.py:289
  416.2 9.3 %collective-permute-done.52.refs_2_ = bf16[1536,256]{1,0:T(8,128)(2,1)S(1)} collective-permute-done((bf16[1536,256]{1,0:T(8,128)(2,1)}, bf16[1536,256]{1,0:T(8,128)(2,1)S(1)}, u32[]{:S(2)}, u32[]{:S(2)}) %collective-permute-start.52) | collective-permute-done | bytes 786464 | tf_op jit(solution)/shard_map/ppermute | solution.py:281
  432.2 11.3 %shard_map.231 = (bf16[2,96,2048]{2,1,0:T(8,128)(2,1)}, bf16[4,48,1536]{2,1,0:T(8,128)(2,1)}) custom-call(s32[2]{0:T(128)} %pad_add_fusion.2.places_ref, bf16[192,1536]{1,0:T(8,128)(2,1)} %bitcast.205, f32[2,96,2048]{2,1,0:T(8,128)} %get-tuple-element.340.attended_ref.out_ref, bf16[1536,256]{1,0:T(8,128)(2,1)} %get-tuple-element.473.refs_0_, ...), custom_call_target="tpu_custom_call" | custom-call | flops 1000 | bytes 1000 | tf_op jit(solution)/shard_map/pallas_call | solution.py:777
  447.7 25.9 %shard_map.232 = (f32[2,96,2048]{2,1,0:T(8,128)}, f32[2,1,96,2048]{3,2,1,0:T(8,128)}, bf16[1,2,1,96,2048]{4,3,2,1,0:T(8,128)(2,1)}) custom-call(s32[9]{0:T(128)} %pad_add_fusion.1.low_ref, s32[1,2048]{1,0:T(1,128)} %bitcast.246, bf16[2,96,2048]{2,1,0:T(8,128)(2,1)} %get-tuple-element.338.query_ref, bf16[2,96,2048]{2,1,0:T(8,128)(2,1)} %get-tuple-element.485.grad_ref, ...), custom_call_target="tpu_custom_call" | custom-call | flops 1000 | bytes 1000 | tf_op jit(solution)/shard_map/pallas_call | solution.py:235
  478.3 6.7 %shard_map.233 = (f32[256,1536]{1,0:T(8,128)}, bf16[256,1536]{1,0:T(8,128)(2,1)}, bf16[256,1536]{1,0:T(8,128)(2,1)}, bf16[256,1536]{1,0:T(8,128)(2,1)}) custom-call(f32[1024,1536]{1,0:T(8,128)} %get-tuple-element.493.keep_ref, bf16[1024,1536]{1,0:T(8,128)(2,1)} %copy-done.9), custom_call_target="tpu_custom_call" | custom-call | flops 1000 | bytes 1000 | tf_op jit(solution)/shard_map/pallas_call | solution.py:875
  488.5 3.1 shard_map.234
  491.6 17.4 %collective-permute-done.63.refs_1_ = bf16[2,1,96,2048]{3,2,1,0:T(8,128)(2,1)S(1)} collective-permute-done((bf16[2,1,96,2048]{3,2,1,0:T(8,128)(2,1)}, bf16[2,1,96,2048]{3,2,1,0:T(8,128)(2,1)S(1)}, u32[]{:S(2)}, u32[]{:S(2)}) %collective-permute-start.63) | collective-permute-done | bytes 786464 | tf_op jit(solution)/shard_map/ppermute | solution.py:289
  511.2 23.7 %shard_map.235 = (f32[1536,1024]{1,0:T(8,128)}, bf16[1536,1024]{1,0:T(8,128)(2,1)}, bf16[4,384,384]{2,1,0:T(8,128)(2,1)}) custom-call(s32[2]{0:T(128)} %pad_add_fusion.2.places_ref, bf16[1536,2048]{1,0:T(8,128)(2,1)} %get-tuple-element.504.normed_ref, f32[2,96,2048]{2,1,0:T(8,128)} %get-tuple-element.505.query_ref, ...), custom_call_target="tpu_custom_call" | custom-call | flops 1000 | bytes 1000 | tf_op jit(solution)/shard_map/pallas_call | solution.py:837
  543.4 4.0 shard_map.237
  547.4 3.2 collective-permute-start.75
  550.5 6.8 %shard_map.236 = (f32[1536,256]{1,0:T(8,128)}, bf16[1536,256]{1,0:T(8,128)(2,1)}, bf16[1536,256]{1,0:T(8,128)(2,1)}, bf16[1536,256]{1,0:T(8,128)(2,1)}) custom-call(f32[1536,1024]{1,0:T(8,128)} %get-tuple-element.517.keep_ref, bf16[1536,1024]{1,0:T(8,128)(2,1)} %collective-permute-done.70.arrived_ref), custom_call_target="tpu_custom_call" | custom-call | flops 1000 | bytes 1000 | tf_op jit(solution)/shard_map/pallas_call | solution.py:875
  563.2 6.3 collective-permute-done.75.refs_1_
  572.2 3.4 collective-permute-start.83
  579.9 13.0 %collective-permute-done.77.refs_2_ = bf16[1536,256]{1,0:T(8,128)(2,1)} collective-permute-done((bf16[1536,256]{1,0:T(8,128)(2,1)}, bf16[1536,256]{1,0:T(8,128)(2,1)}, u32[]{:S(2)}, u32[]{:S(2)}) %collective-permute-start.77) | collective-permute-done | bytes 786464 | tf_op jit(solution)/shard_map/ppermute | solution.py:281
  592.9 5.5 shard_map.239
  618.6 7.1 %collective-permute-done.91 = bf16[48,1536]{1,0:T(8,128)(2,1)S(1)} collective-permute-done((bf16[48,1536]{1,0:T(8,128)(2,1)}, bf16[48,1536]{1,0:T(8,128)(2,1)S(1)}, u32[]{:S(2)}, u32[]{:S(2)}) %collective-permute-start.91) | collective-permute-done | bytes 147488 | tf_op jit(solution)/shard_map/ppermute | solution.py:315
  626.1 3.4 collective-permute-start.94
  (409 shorter events, 158.6 us)
Async XLA Ops:
  10.5 32.1 %collective-permute-start.7 = (bf16[1536,256]{1,0:T(8,128)(2,1)S(1)}, bf16[1536,256]{1,0:T(8,128)(2,1)}, u32[]{:S(2)}, u32[]{:S(2)}) collective-permute-start(bf16[1536,256]{1,0:T(8,128)(2,1)S(1)} %bitcast.197), channel_id=1, source_target_pairs={{0,2},{1,3},{2,0},{3,1},{4,6},{5,7},{6,4},{7,5},{8,10},{9,11},{10,... | collective-permute-start | bytes 2359304 | tf_op jit(solution)/shard_map/ppermute | solution.py:281
  11.1 31.5 %collective-permute-start.8 = (bf16[1536,256]{1,0:T(8,128)(2,1)S(1)}, bf16[1536,256]{1,0:T(8,128)(2,1)}, u32[]{:S(2)}, u32[]{:S(2)}) collective-permute-start(bf16[1536,256]{1,0:T(8,128)(2,1)S(1)} %bitcast.198), channel_id=1, source_target_pairs={{0,4},{1,5},{2,6},{3,7},{4,0},{5,1},{6,2},{7,3},{8,12},{9,13},{10,... | collective-permute-start | bytes 2359304 | tf_op jit(solution)/shard_map/ppermute | solution.py:281
  14.7 22.7 %collective-permute-start.4 = (bf16[2,48,1536]{2,1,0:T(8,128)(2,1)}, bf16[2,48,1536]{2,1,0:T(8,128)(2,1)S(1)}, u32[]{:S(2)}, u32[]{:S(2)}) collective-permute-start(bf16[2,48,1536]{2,1,0:T(8,128)(2,1)} %get-tuple-element.596), channel_id=1, source_target_pairs={{0,2},{1,3},{2,0},{3,1},{4,6},{5,7},{6,4},{7,5},{8,10},{9,11},{10,... | collective-permute-start | bytes 884744 | tf_op jit(solution)/shard_map/ppermute | solution.py:281
  16.2 24.8 %collective-permute-start.5 = (bf16[2,48,1536]{2,1,0:T(8,128)(2,1)}, bf16[2,48,1536]{2,1,0:T(8,128)(2,1)S(1)}, u32[]{:S(2)}, u32[]{:S(2)}) collective-permute-start(bf16[2,48,1536]{2,1,0:T(8,128)(2,1)} %get-tuple-element.595), channel_id=1, source_target_pairs={{0,4},{1,5},{2,6},{3,7},{4,0},{5,1},{6,2},{7,3},{8,12},{9,13},{10,... | collective-permute-start | bytes 884744 | tf_op jit(solution)/shard_map/ppermute | solution.py:281
  18.0 24.6 %collective-permute-start.6 = (bf16[2,48,1536]{2,1,0:T(8,128)(2,1)S(1)}, bf16[2,48,1536]{2,1,0:T(8,128)(2,1)S(1)}, u32[]{:S(2)}, u32[]{:S(2)}) collective-permute-start(bf16[2,48,1536]{2,1,0:T(8,128)(2,1)S(1)} %get-tuple-element.594), channel_id=1, source_target_pairs={{0,6},{1,7},{2,4},{3,5},{4,2},{5,3},{6,0},{7,1},{8,14},{9,15},{10,... | collective-permute-start | bytes 884744 | tf_op jit(solution)/shard_map/ppermute | solution.py:281
  42.9 44.1 %collective-permute-start.13 = (bf16[1536,256]{1,0:T(8,128)(2,1)S(1)}, bf16[1536,256]{1,0:T(8,128)(2,1)}, u32[]{:S(2)}, u32[]{:S(2)}) collective-permute-start(bf16[1536,256]{1,0:T(8,128)(2,1)S(1)} %bitcast.199), channel_id=1, source_target_pairs={{0,6},{1,7},{2,4},{3,5},{4,2},{5,3},{6,0},{7,1},{8,14},{9,15},{10,... | collective-permute-start | bytes 2359304 | tf_op jit(solution)/shard_map/ppermute | solution.py:281
  45.1 42.4 %collective-permute-start.10 = (bf16[8,48,512]{2,1,0:T(8,128)(2,1)S(1)}, bf16[8,48,512]{2,1,0:T(8,128)(2,1)S(1)}, u32[]{:S(2)}, u32[]{:S(2)}) collective-permute-start(bf16[8,48,512]{2,1,0:T(8,128)(2,1)S(1)} %fusion.2.refs_0_), channel_id=1, source_target_pairs={{0,8},{1,9},{2,10},{3,11},{4,12},{5,13},{6,14},{7,15},{8,16},{9,17... | collective-permute-start | bytes 1179656 | tf_op jit(solution)/shard_map/ppermute | solution.py:289
  46.7 40.9 %collective-permute-start.11 = (bf16[8,48,512]{2,1,0:T(8,128)(2,1)S(1)}, bf16[8,48,512]{2,1,0:T(8,128)(2,1)S(1)}, u32[]{:S(2)}, u32[]{:S(2)}) collective-permute-start(bf16[8,48,512]{2,1,0:T(8,128)(2,1)S(1)} %fusion.2.refs_0_), channel_id=1, source_target_pairs={{0,16},{1,17},{2,18},{3,19},{4,20},{5,21},{6,22},{7,23},{8,24},{9,... | collective-permute-start | bytes 1179656 | tf_op jit(solution)/shard_map/ppermute | solution.py:289
  48.0 39.7 %collective-permute-start.12 = (bf16[8,48,512]{2,1,0:T(8,128)(2,1)S(1)}, bf16[8,48,512]{2,1,0:T(8,128)(2,1)S(1)}, u32[]{:S(2)}, u32[]{:S(2)}) collective-permute-start(bf16[8,48,512]{2,1,0:T(8,128)(2,1)S(1)} %fusion.2.refs_0_), channel_id=1, source_target_pairs={{0,24},{1,25},{2,26},{3,27},{4,28},{5,29},{6,30},{7,31},{8,0},{9,1... | collective-permute-start | bytes 1179656 | tf_op jit(solution)/shard_map/ppermute | solution.py:289
  49.8 37.2 %collective-permute-start.14 = (bf16[48,1536]{1,0:T(8,128)(2,1)S(1)}, bf16[48,1536]{1,0:T(8,128)(2,1)S(1)}, u32[]{:S(2)}, u32[]{:S(2)}) collective-permute-start(bf16[48,1536]{1,0:T(8,128)(2,1)S(1)} %copy-done.74), channel_id=1, source_target_pairs={{0,0},{1,8},{2,16},{3,24},{4,1},{5,9},{6,17},{7,25},{8,2},{9,10},{... | collective-permute-start | bytes 442376 | tf_op jit(solution)/shard_map/ppermute | solution.py:308
  105.1 34.4 %collective-permute-start.19 = (bf16[2,1,96,2048]{3,2,1,0:T(8,128)(2,1)}, bf16[2,1,96,2048]{3,2,1,0:T(8,128)(2,1)S(1)}, u32[]{:S(2)}, u32[]{:S(2)}) collective-permute-start(bf16[2,1,96,2048]{3,2,1,0:T(8,128)(2,1)} %get-tuple-element.330.refs_0_), channel_id=1, source_target_pairs={{0,8},{1,9},{2,10},{3,11},{4,12},{5,13},{6,14},{7,15},{8,16},{9,17... | collective-permute-start | bytes 2359304 | tf_op jit(solution)/shard_map/ppermute | solution.py:289
  110.6 26.5 %collective-permute-start.20 = (bf16[48,1536]{1,0:T(8,128)(2,1)S(1)}, bf16[48,1536]{1,0:T(8,128)(2,1)S(1)}, u32[]{:S(2)}, u32[]{:S(2)}) collective-permute-start(bf16[48,1536]{1,0:T(8,128)(2,1)S(1)} %copy-done.68), channel_id=1, source_target_pairs={{0,8},{1,9},{2,10},{3,11},{4,12},{5,13},{6,14},{7,15},{8,16},{9,17... | collective-permute-start | bytes 442376 | tf_op jit(solution)/shard_map/ppermute | solution.py:289
  111.2 28.3 %collective-permute-start.21 = (bf16[48,1536]{1,0:T(8,128)(2,1)S(1)}, bf16[48,1536]{1,0:T(8,128)(2,1)S(1)}, u32[]{:S(2)}, u32[]{:S(2)}) collective-permute-start(bf16[48,1536]{1,0:T(8,128)(2,1)S(1)} %copy-done.68), channel_id=1, source_target_pairs={{0,16},{1,17},{2,18},{3,19},{4,20},{5,21},{6,22},{7,23},{8,24},{9,... | collective-permute-start | bytes 442376 | tf_op jit(solution)/shard_map/ppermute | solution.py:289
  112.5 27.1 %collective-permute-start.22 = (bf16[48,1536]{1,0:T(8,128)(2,1)S(1)}, bf16[48,1536]{1,0:T(8,128)(2,1)S(1)}, u32[]{:S(2)}, u32[]{:S(2)}) collective-permute-start(bf16[48,1536]{1,0:T(8,128)(2,1)S(1)} %copy-done.68), channel_id=1, source_target_pairs={{0,24},{1,25},{2,26},{3,27},{4,28},{5,29},{6,30},{7,31},{8,0},{9,1... | collective-permute-start | bytes 442376 | tf_op jit(solution)/shard_map/ppermute | solution.py:289
  139.6 41.6 %collective-permute-start.23 = (bf16[8,48,1536]{2,1,0:T(8,128)(2,1)S(1)}, bf16[8,48,1536]{2,1,0:T(8,128)(2,1)S(1)}, u32[]{:S(2)}, u32[]{:S(2)}) collective-permute-start(bf16[8,48,1536]{2,1,0:T(8,128)(2,1)S(1)} %pad_maximum_fusion.3.refs_0_), channel_id=1, source_target_pairs={{0,8},{1,9},{2,10},{3,11},{4,12},{5,13},{6,14},{7,15},{8,16},{9,17... | collective-permute-start | bytes 3538952 | tf_op jit(solution)/shard_map/ppermute | solution.py:289
  141.5 39.6 %collective-permute-start.24 = (bf16[8,48,1536]{2,1,0:T(8,128)(2,1)S(1)}, bf16[8,48,1536]{2,1,0:T(8,128)(2,1)}, u32[]{:S(2)}, u32[]{:S(2)}) collective-permute-start(bf16[8,48,1536]{2,1,0:T(8,128)(2,1)S(1)} %pad_maximum_fusion.3.refs_0_), channel_id=1, source_target_pairs={{8,0},{9,1},{10,2},{11,3},{12,4},{13,5},{14,6},{15,7},{16,8},{17,9... | collective-permute-start | bytes 3538952 | tf_op jit(solution)/shard_map/ppermute | solution.py:289
  145.5 35.6 %collective-permute-start.25 = (bf16[256,1536]{1,0:T(8,128)(2,1)S(1)}, bf16[256,1536]{1,0:T(8,128)(2,1)S(1)}, u32[]{:S(2)}, u32[]{:S(2)}) collective-permute-start(bf16[256,1536]{1,0:T(8,128)(2,1)S(1)} %copy-done.10), channel_id=1, source_target_pairs={{0,2},{1,3},{2,0},{3,1},{4,6},{5,7},{6,4},{7,5},{8,10},{9,11},{10,... | collective-permute-start | bytes 2359304 | tf_op jit(solution)/shard_map/ppermute | solution.py:281
  145.6 35.5 %collective-permute-start.26 = (bf16[256,1536]{1,0:T(8,128)(2,1)S(1)}, bf16[256,1536]{1,0:T(8,128)(2,1)}, u32[]{:S(2)}, u32[]{:S(2)}) collective-permute-start(bf16[256,1536]{1,0:T(8,128)(2,1)S(1)} %copy-done.10), channel_id=1, source_target_pairs={{0,4},{1,5},{2,6},{3,7},{4,0},{5,1},{6,2},{7,3},{8,12},{9,13},{10,... | collective-permute-start | bytes 2359304 | tf_op jit(solution)/shard_map/ppermute | solution.py:281
  147.3 33.8 %collective-permute-start.27 = (bf16[256,1536]{1,0:T(8,128)(2,1)S(1)}, bf16[256,1536]{1,0:T(8,128)(2,1)}, u32[]{:S(2)}, u32[]{:S(2)}) collective-permute-start(bf16[256,1536]{1,0:T(8,128)(2,1)S(1)} %copy-done.10), channel_id=1, source_target_pairs={{0,6},{1,7},{2,4},{3,5},{4,2},{5,3},{6,0},{7,1},{8,14},{9,15},{10,... | collective-permute-start | bytes 2359304 | tf_op jit(solution)/shard_map/ppermute | solution.py:281
  187.4 30.2 %collective-permute-start.32 = (bf16[8,48,1536]{2,1,0:T(8,128)(2,1)S(1)}, bf16[8,48,1536]{2,1,0:T(8,128)(2,1)}, u32[]{:S(2)}, u32[]{:S(2)}) collective-permute-start(bf16[8,48,1536]{2,1,0:T(8,128)(2,1)S(1)} %collective-permute-done.23.refs_1_), channel_id=1, source_target_pairs={{0,8},{1,9},{2,10},{3,11},{4,12},{5,13},{6,14},{7,15},{8,16},{9,17... | collective-permute-start | bytes 3538952 | tf_op jit(solution)/shard_map/ppermute | solution.py:289
  191.2 31.1 %collective-permute-start.33 = (bf16[8,48,1536]{2,1,0:T(8,128)(2,1)}, bf16[8,48,1536]{2,1,0:T(8,128)(2,1)}, u32[]{:S(2)}, u32[]{:S(2)}) collective-permute-start(bf16[8,48,1536]{2,1,0:T(8,128)(2,1)} %collective-permute-done.24.refs_2_), channel_id=1, source_target_pairs={{8,0},{9,1},{10,2},{11,3},{12,4},{13,5},{14,6},{15,7},{16,8},{17,9... | collective-permute-start | bytes 3538952 | tf_op jit(solution)/shard_map/ppermute | solution.py:289
  201.0 21.2 %collective-permute-start.30 = (bf16[1536,256]{1,0:T(8,128)(2,1)}, bf16[1536,256]{1,0:T(8,128)(2,1)S(1)}, u32[]{:S(2)}, u32[]{:S(2)}) collective-permute-start(bf16[1536,256]{1,0:T(8,128)(2,1)} %get-tuple-element.362), channel_id=1, source_target_pairs={{0,2},{1,3},{2,0},{3,1},{4,6},{5,7},{6,4},{7,5},{8,10},{9,11},{10,... | collective-permute-start | bytes 2359304 | tf_op jit(solution)/shard_map/ppermute | solution.py:281
  222.3 31.2 %collective-permute-start.35 = (bf16[8,48,1536]{2,1,0:T(8,128)(2,1)}, bf16[8,48,1536]{2,1,0:T(8,128)(2,1)S(1)}, u32[]{:S(2)}, u32[]{:S(2)}) collective-permute-start(bf16[8,48,1536]{2,1,0:T(8,128)(2,1)} %collective-permute-done.32.refs_3_), channel_id=1, source_target_pairs={{0,8},{1,9},{2,10},{3,11},{4,12},{5,13},{6,14},{7,15},{8,16},{9,17... | collective-permute-start | bytes 3538952 | tf_op jit(solution)/shard_map/ppermute | solution.py:289
  225.9 29.1 %collective-permute-start.36 = (bf16[8,48,1536]{2,1,0:T(8,128)(2,1)}, bf16[8,48,1536]{2,1,0:T(8,128)(2,1)S(1)}, u32[]{:S(2)}, u32[]{:S(2)}) collective-permute-start(bf16[8,48,1536]{2,1,0:T(8,128)(2,1)} %collective-permute-done.33.refs_4_), channel_id=1, source_target_pairs={{8,0},{9,1},{10,2},{11,3},{12,4},{13,5},{14,6},{15,7},{16,8},{17,9... | collective-permute-start | bytes 3538952 | tf_op jit(solution)/shard_map/ppermute | solution.py:289
  326.5 55.8 %collective-permute-start.48 = (bf16[1536,256]{1,0:T(8,128)(2,1)S(1)}, bf16[1536,256]{1,0:T(8,128)(2,1)S(1)}, u32[]{:S(2)}, u32[]{:S(2)}) collective-permute-start(bf16[1536,256]{1,0:T(8,128)(2,1)S(1)} %copy-done.39), channel_id=1, source_target_pairs={{0,2},{1,3},{2,0},{3,1},{4,6},{5,7},{6,4},{7,5},{8,10},{9,11},{10,... | collective-permute-start | bytes 2359304 | tf_op jit(solution)/shard_map/ppermute | solution.py:281
  327.0 55.4 %collective-permute-start.49 = (bf16[1536,256]{1,0:T(8,128)(2,1)}, bf16[1536,256]{1,0:T(8,128)(2,1)S(1)}, u32[]{:S(2)}, u32[]{:S(2)}) collective-permute-start(bf16[1536,256]{1,0:T(8,128)(2,1)} %shard_map.225), channel_id=1, source_target_pairs={{0,4},{1,5},{2,6},{3,7},{4,0},{5,1},{6,2},{7,3},{8,12},{9,13},{10,... | collective-permute-start | bytes 2359304 | tf_op jit(solution)/shard_map/ppermute | solution.py:281
  331.8 50.6 %collective-permute-start.50 = (bf16[1536,256]{1,0:T(8,128)(2,1)}, bf16[1536,256]{1,0:T(8,128)(2,1)S(1)}, u32[]{:S(2)}, u32[]{:S(2)}) collective-permute-start(bf16[1536,256]{1,0:T(8,128)(2,1)} %shard_map.226), channel_id=1, source_target_pairs={{0,6},{1,7},{2,4},{3,5},{4,2},{5,3},{6,0},{7,1},{8,14},{9,15},{10,... | collective-permute-start | bytes 2359304 | tf_op jit(solution)/shard_map/ppermute | solution.py:281
  365.5 38.1 %collective-permute-start.54 = (bf16[384,1024]{1,0:T(8,128)(2,1)S(1)}, bf16[384,1024]{1,0:T(8,128)(2,1)S(1)}, u32[]{:S(2)}, u32[]{:S(2)}) collective-permute-start(bf16[384,1024]{1,0:T(8,128)(2,1)S(1)} %get-tuple-element.581), channel_id=1, source_target_pairs={{0,8},{1,9},{2,10},{3,11},{4,12},{5,13},{6,14},{7,15},{8,16},{9,17... | collective-permute-start | bytes 2359304 | tf_op jit(solution)/shard_map/ppermute | solution.py:289
  366.3 49.9 %collective-permute-start.55 = (bf16[384,1024]{1,0:T(8,128)(2,1)S(1)}, bf16[384,1024]{1,0:T(8,128)(2,1)S(1)}, u32[]{:S(2)}, u32[]{:S(2)}) collective-permute-start(bf16[384,1024]{1,0:T(8,128)(2,1)S(1)} %get-tuple-element.580), channel_id=1, source_target_pairs={{0,16},{1,17},{2,18},{3,19},{4,20},{5,21},{6,22},{7,23},{8,24},{9,... | collective-permute-start | bytes 2359304 | tf_op jit(solution)/shard_map/ppermute | solution.py:289
  390.1 26.1 %collective-permute-start.51 = (bf16[1536,256]{1,0:T(8,128)(2,1)}, bf16[1536,256]{1,0:T(8,128)(2,1)S(1)}, u32[]{:S(2)}, u32[]{:S(2)}) collective-permute-start(bf16[1536,256]{1,0:T(8,128)(2,1)} %get-tuple-element.473.refs_0_), channel_id=1, source_target_pairs={{0,2},{1,3},{2,0},{3,1},{4,6},{5,7},{6,4},{7,5},{8,10},{9,11},{10,... | collective-permute-start | bytes 2359304 | tf_op jit(solution)/shard_map/ppermute | solution.py:281
  390.5 34.9 %collective-permute-start.52 = (bf16[1536,256]{1,0:T(8,128)(2,1)}, bf16[1536,256]{1,0:T(8,128)(2,1)S(1)}, u32[]{:S(2)}, u32[]{:S(2)}) collective-permute-start(bf16[1536,256]{1,0:T(8,128)(2,1)} %get-tuple-element.473.refs_0_), channel_id=1, source_target_pairs={{0,4},{1,5},{2,6},{3,7},{4,0},{5,1},{6,2},{7,3},{8,12},{9,13},{10,... | collective-permute-start | bytes 2359304 | tf_op jit(solution)/shard_map/ppermute | solution.py:281
  392.0 33.4 %collective-permute-start.53 = (bf16[1536,256]{1,0:T(8,128)(2,1)}, bf16[1536,256]{1,0:T(8,128)(2,1)S(1)}, u32[]{:S(2)}, u32[]{:S(2)}) collective-permute-start(bf16[1536,256]{1,0:T(8,128)(2,1)} %get-tuple-element.473.refs_0_), channel_id=1, source_target_pairs={{0,6},{1,7},{2,4},{3,5},{4,2},{5,3},{6,0},{7,1},{8,14},{9,15},{10,... | collective-permute-start | bytes 2359304 | tf_op jit(solution)/shard_map/ppermute | solution.py:281
  443.5 30.1 %collective-permute-start.62 = (bf16[1024,1536]{1,0:T(8,128)(2,1)}, bf16[1024,1536]{1,0:T(8,128)(2,1)S(1)}, u32[]{:S(2)}, u32[]{:S(2)}) collective-permute-start(bf16[1024,1536]{1,0:T(8,128)(2,1)} %get-tuple-element.491), channel_id=1, source_target_pairs={{0,1},{1,0},{2,3},{3,2},{4,5},{5,4},{6,7},{7,6},{8,9},{9,8},{10,11... | collective-permute-start | bytes 9437192 | tf_op jit(solution)/shard_map/ppermute | solution.py:281
  443.7 29.9 %collective-permute-start.60 = (bf16[384,1024]{1,0:T(8,128)(2,1)S(1)}, bf16[384,1024]{1,0:T(8,128)(2,1)S(1)}, u32[]{:S(2)}, u32[]{:S(2)}) collective-permute-start(bf16[384,1024]{1,0:T(8,128)(2,1)S(1)} %get-tuple-element.579), channel_id=1, source_target_pairs={{0,24},{1,25},{2,26},{3,27},{4,28},{5,29},{6,30},{7,31},{8,0},{9,1... | collective-permute-start | bytes 2359304 | tf_op jit(solution)/shard_map/ppermute | solution.py:289
  445.1 28.5 %collective-permute-start.61 = (bf16[128,1536]{1,0:T(8,128)(2,1)S(1)}, bf16[128,1536]{1,0:T(8,128)(2,1)S(1)}, u32[]{:S(2)}, u32[]{:S(2)}) collective-permute-start(bf16[128,1536]{1,0:T(8,128)(2,1)S(1)} %get-tuple-element.584), channel_id=1, source_target_pairs={{0,24},{1,25},{2,26},{3,27},{4,28},{5,29},{6,30},{7,31},{8,0},{9,1... | collective-permute-start | bytes 1179656 | tf_op jit(solution)/shard_map/ppermute | solution.py:289
  474.3 34.7 %collective-permute-start.63 = (bf16[2,1,96,2048]{3,2,1,0:T(8,128)(2,1)}, bf16[2,1,96,2048]{3,2,1,0:T(8,128)(2,1)S(1)}, u32[]{:S(2)}, u32[]{:S(2)}) collective-permute-start(bf16[2,1,96,2048]{3,2,1,0:T(8,128)(2,1)} %bitcast.261), channel_id=1, source_target_pairs={{8,0},{9,1},{10,2},{11,3},{12,4},{13,5},{14,6},{15,7},{16,8},{17,9... | collective-permute-start | bytes 2359304 | tf_op jit(solution)/shard_map/ppermute | solution.py:289
  476.3 34.1 %collective-permute-start.67 = (bf16[128,1536]{1,0:T(8,128)(2,1)}, bf16[128,1536]{1,0:T(8,128)(2,1)S(1)}, u32[]{:S(2)}, u32[]{:S(2)}) collective-permute-start(bf16[128,1536]{1,0:T(8,128)(2,1)} %get-tuple-element.583), channel_id=1, source_target_pairs={{0,8},{1,9},{2,10},{3,11},{4,12},{5,13},{6,14},{7,15},{8,16},{9,17... | collective-permute-start | bytes 1179656 | tf_op jit(solution)/shard_map/ppermute | solution.py:289
  485.0 50.0 %collective-permute-start.64 = (bf16[256,1536]{1,0:T(8,128)(2,1)}, bf16[256,1536]{1,0:T(8,128)(2,1)S(1)}, u32[]{:S(2)}, u32[]{:S(2)}) collective-permute-start(bf16[256,1536]{1,0:T(8,128)(2,1)} %get-tuple-element.510), channel_id=1, source_target_pairs={{0,2},{1,3},{2,0},{3,1},{4,6},{5,7},{6,4},{7,5},{8,10},{9,11},{10,... | collective-permute-start | bytes 2359304 | tf_op jit(solution)/shard_map/ppermute | solution.py:281
  485.7 49.3 %collective-permute-start.65 = (bf16[256,1536]{1,0:T(8,128)(2,1)}, bf16[256,1536]{1,0:T(8,128)(2,1)S(1)}, u32[]{:S(2)}, u32[]{:S(2)}) collective-permute-start(bf16[256,1536]{1,0:T(8,128)(2,1)} %get-tuple-element.511), channel_id=1, source_target_pairs={{0,4},{1,5},{2,6},{3,7},{4,0},{5,1},{6,2},{7,3},{8,12},{9,13},{10,... | collective-permute-start | bytes 2359304 | tf_op jit(solution)/shard_map/ppermute | solution.py:281
  487.0 48.0 %collective-permute-start.66 = (bf16[256,1536]{1,0:T(8,128)(2,1)}, bf16[256,1536]{1,0:T(8,128)(2,1)}, u32[]{:S(2)}, u32[]{:S(2)}) collective-permute-start(bf16[256,1536]{1,0:T(8,128)(2,1)} %get-tuple-element.512), channel_id=1, source_target_pairs={{0,6},{1,7},{2,4},{3,5},{4,2},{5,3},{6,0},{7,1},{8,14},{9,15},{10,... | collective-permute-start | bytes 2359304 | tf_op jit(solution)/shard_map/ppermute | solution.py:281
  509.1 25.9 %collective-permute-start.68 = (bf16[128,1536]{1,0:T(8,128)(2,1)S(1)}, bf16[128,1536]{1,0:T(8,128)(2,1)S(1)}, u32[]{:S(2)}, u32[]{:S(2)}) collective-permute-start(bf16[128,1536]{1,0:T(8,128)(2,1)S(1)} %copy-done.54), channel_id=1, source_target_pairs={{0,16},{1,17},{2,18},{3,19},{4,20},{5,21},{6,22},{7,23},{8,24},{9,... | collective-permute-start | bytes 1179656 | tf_op jit(solution)/shard_map/ppermute | solution.py:289
  510.4 24.6 %collective-permute-start.69 = (bf16[4,48,1024]{2,1,0:T(8,128)(2,1)S(1)}, bf16[4,48,1024]{2,1,0:T(8,128)(2,1)}, u32[]{:S(2)}, u32[]{:S(2)}) collective-permute-start(bf16[4,48,1024]{2,1,0:T(8,128)(2,1)S(1)} %dynamic-slice_bitcast_fusion.2), channel_id=1, source_target_pairs={{0,1},{1,0},{2,3},{3,2},{4,5},{5,4},{6,7},{7,6},{8,9},{9,8},{10,11... | collective-permute-start | bytes 1179656 | tf_op jit(solution)/shard_map/ppermute | solution.py:281
  547.4 22.1 %collective-permute-start.75 = (bf16[384,384]{1,0:T(8,128)(2,1)S(1)}, bf16[384,384]{1,0:T(8,128)(2,1)S(1)}, u32[]{:S(2)}, u32[]{:S(2)}) collective-permute-start(bf16[384,384]{1,0:T(8,128)(2,1)S(1)} %get-tuple-element.588), channel_id=1, source_target_pairs={{0,16},{1,17},{2,18},{3,19},{4,20},{5,21},{6,22},{7,23},{8,24},{9,... | collective-permute-start | bytes 884744 | tf_op jit(solution)/shard_map/ppermute | solution.py:289
  558.1 34.8 %collective-permute-start.77 = (bf16[1536,256]{1,0:T(8,128)(2,1)}, bf16[1536,256]{1,0:T(8,128)(2,1)}, u32[]{:S(2)}, u32[]{:S(2)}) collective-permute-start(bf16[1536,256]{1,0:T(8,128)(2,1)} %get-tuple-element.537), channel_id=1, source_target_pairs={{0,4},{1,5},{2,6},{3,7},{4,0},{5,1},{6,2},{7,3},{8,12},{9,13},{10,... | collective-permute-start | bytes 2359304 | tf_op jit(solution)/shard_map/ppermute | solution.py:281
  559.4 33.5 %collective-permute-start.78 = (bf16[1536,256]{1,0:T(8,128)(2,1)}, bf16[1536,256]{1,0:T(8,128)(2,1)}, u32[]{:S(2)}, u32[]{:S(2)}) collective-permute-start(bf16[1536,256]{1,0:T(8,128)(2,1)} %get-tuple-element.538), channel_id=1, source_target_pairs={{0,6},{1,7},{2,4},{3,5},{4,2},{5,3},{6,0},{7,1},{8,14},{9,15},{10,... | collective-permute-start | bytes 2359304 | tf_op jit(solution)/shard_map/ppermute | solution.py:281
  569.5 36.2 %collective-permute-start.82 = (bf16[48,1536]{1,0:T(8,128)(2,1)}, bf16[48,1536]{1,0:T(8,128)(2,1)}, u32[]{:S(2)}, u32[]{:S(2)}) collective-permute-start(bf16[48,1536]{1,0:T(8,128)(2,1)} %get-tuple-element.610), channel_id=1, source_target_pairs={{0,8},{1,9},{2,10},{3,11},{4,12},{5,13},{6,14},{7,15},{8,16},{9,17... | collective-permute-start | bytes 442376 | tf_op jit(solution)/shard_map/ppermute | solution.py:289
  572.2 33.6 %collective-permute-start.83 = (bf16[48,1536]{1,0:T(8,128)(2,1)S(1)}, bf16[48,1536]{1,0:T(8,128)(2,1)S(1)}, u32[]{:S(2)}, u32[]{:S(2)}) collective-permute-start(bf16[48,1536]{1,0:T(8,128)(2,1)S(1)} %copy-done.66), channel_id=1, source_target_pairs={{0,16},{1,17},{2,18},{3,19},{4,20},{5,21},{6,22},{7,23},{8,24},{9,... | collective-permute-start | bytes 442376 | tf_op jit(solution)/shard_map/ppermute | solution.py:289
  578.2 27.5 %collective-permute-start.84 = (bf16[48,1536]{1,0:T(8,128)(2,1)S(1)}, bf16[48,1536]{1,0:T(8,128)(2,1)S(1)}, u32[]{:S(2)}, u32[]{:S(2)}) collective-permute-start(bf16[48,1536]{1,0:T(8,128)(2,1)S(1)} %copy-done.65), channel_id=1, source_target_pairs={{0,24},{1,25},{2,26},{3,27},{4,28},{5,29},{6,30},{7,31},{8,0},{9,1... | collective-permute-start | bytes 442376 | tf_op jit(solution)/shard_map/ppermute | solution.py:289
  (123 other events, 1389.8 us)

commit v6 on v4

--- a/solution.py
+++ b/solution.py
@@ -1095,22 +1095,21 @@
     attn_w = place_rows(grid, attn_z, 0, attn_wide).reshape(width, attn_wide)
     attn_w, inputs_team, out_own = order.step(attn_w, inputs_team, out_own)
 
-    out_own, cotangent = order.step(out_own, cotangent)
+    out_own = order.step(out_own)
     out_z = grid.spread(out_own)
+    normed_first, queries, own_piece = project(inputs_team, attn_w, cosine, sine_table)
+    own_piece, out_z, attn_w, cotangent = order.step(own_piece, out_z, attn_w, cotangent)
+    arrived = [grid.shift(own_piece, step, False) for step in range(1, steps_back + 1)]
     cotangent_chips = [cotangent, grid.turn(cotangent, 2), grid.turn(cotangent, 4)]
-    normed_first, queries, own_piece = project(inputs_team, attn_w, cosine, sine_table)
-    own_piece, out_z, attn_w = order.step(own_piece, out_z, attn_w)
-    arrived = [grid.shift(own_piece, step, False) for step in range(1, steps_back + 1)]
-    cotangent_chips = order.step(cotangent_chips)
-    cotangent_chips = cotangent_chips + [grid.turn(cotangent_chips[0], 6)]
     out_rows = place_rows(grid, [block[None] for block in out_z], 0, width)
     out_rows = out_rows.reshape(Q_WIDTH, width)
     gain_first = attn_w[:, LINED : LINED + 1].astype(f32)
     gain_second = attn_w[:, LINED + 1 : LINED + 2].astype(f32)
     mixer_own = jnp.concatenate([team_rows[..., attn_wide:], down_thirds], axis=-1)
-    arrived, gain_first, gain_second, mixer_own, out_rows = order.step(
-        arrived, gain_first, gain_second, mixer_own, out_rows
-    )
+    arrived, gain_first, gain_second, mixer_own, out_rows, cotangent_chips = order.step(
+        arrived, gain_first, gain_second, mixer_own, out_rows, cotangent_chips
+    )
+    cotangent_chips = cotangent_chips + [grid.turn(cotangent_chips[0], 6)]
 
     mixer_hops = [grid.both_ways(mixer_own, mixer_own)]
 

time: 629 us -> 631 us (level)
  transfers between devices with their start and end apart: 95 -> 95, of which waited for: 33 -> 35; matrix products, arithmetic and copies ran while one was open for 5% -> 5% of each run, Pallas kernels for 41% -> 42%
where the time goes in v6:
time: 631 us; the launch traced here: 622 us
  Pallas kernels  270 us (43%)
  waiting for transfers between devices  190 us (30%)
  starting transfers between devices  114 us (18%)
  local copies, waits for them, and re-layouts  32.8 us (5%)
  other arithmetic  12.2 us (2%)
    ppermute x64, waiting for transfers between devices, turn(): lax.ppermute(value, 'dev', [(d, d ^ bits) for d in range(self.count)])  96.3 us
    ppermute x29, waiting for transfers between devices, shift(): return lax.ppermute(value, 'dev', pairs)  84.2 us
    ppermute x29, starting transfers between devices, shift(): return lax.ppermute(value, 'dev', pairs)  58.1 us
    ppermute x64, starting transfers between devices, turn(): lax.ppermute(value, 'dev', [(d, d ^ bits) for d in range(self.count)])  52.6 us
    pallas_call x4, Pallas kernels, mixer(): call(kernel, (2,), [fixed(normed[0]), fixed(normed[1]), block, block, fix...  42.8 us
    pallas_call x1, Pallas kernels, token_product(): call(kernel, (TEAM,), [fixed(block) for block in list(lefts) + list(right...  30.3 us
    pallas_call x1, Pallas kernels, attend_back(): pl.pallas_call(gradient_kernel, grid=(count,), in_specs=[low_spec, whole,...  25.9 us
    pallas_call x1, Pallas kernels, project_back(): call(kernel, (TEAM,), [lanes_at(width, own), heads, lanes_at(HEAD_DIM, ow...  23.7 us
  transfers between devices with their start and end apart: 95, of which 35 were waited for; matrix products, arithmetic and copies ran while one was open for 5% of the time, Pallas kernels for 42%

profile of v6, /device:TPU:10, one launch (start us, length us, event | category | flops | bytes accessed | tf_op | source)
XLA Modules:
  0.0 622.2 jit_solution(8762830652708402122)
XLA Ops:
  21.1 3.6 fusion
  24.6 12.7 %collective-permute-done.4 = bf16[2,48,1536]{2,1,0:T(8,128)(2,1)S(1)} collective-permute-done((bf16[2,48,1536]{2,1,0:T(8,128)(2,1)}, bf16[2,48,1536]{2,1,0:T(8,128)(2,1)S(1)}, u32[]{:S(2)}, u32[]{:S(2)}) %collective-permute-start.4) | collective-permute-done | bytes 294944 | tf_op jit(solution)/shard_map/ppermute | solution.py:281
  37.4 3.7 collective-permute-done.5
  49.8 14.1 %collective-permute-done.13.refs_3_ = bf16[1536,256]{1,0:T(8,128)(2,1)} collective-permute-done((bf16[1536,256]{1,0:T(8,128)(2,1)S(1)}, bf16[1536,256]{1,0:T(8,128)(2,1)}, u32[]{:S(2)}, u32[]{:S(2)}) %collective-permute-start.13) | collective-permute-done | bytes 786464 | tf_op jit(solution)/shard_map/ppermute | solution.py:281
  63.9 9.1 %collective-permute-done.10.refs_1_ = bf16[8,48,512]{2,1,0:T(8,128)(2,1)S(1)} collective-permute-done((bf16[8,48,512]{2,1,0:T(8,128)(2,1)S(1)}, bf16[8,48,512]{2,1,0:T(8,128)(2,1)S(1)}, u32[]{:S(2)}, u32[]{:S(2)}) %collective-permute-start.10) | collective-permute-done | bytes 393248 | tf_op jit(solution)/shard_map/ppermute | solution.py:289
  73.0 7.6 %collective-permute-done.11.refs_2_ = bf16[8,48,512]{2,1,0:T(8,128)(2,1)S(1)} collective-permute-done((bf16[8,48,512]{2,1,0:T(8,128)(2,1)S(1)}, bf16[8,48,512]{2,1,0:T(8,128)(2,1)S(1)}, u32[]{:S(2)}, u32[]{:S(2)}) %collective-permute-start.11) | collective-permute-done | bytes 393248 | tf_op jit(solution)/shard_map/ppermute | solution.py:289
  85.8 3.8 shard_map.212
  98.4 11.8 %shard_map.213 = (bf16[1536,2048]{1,0:T(8,128)(2,1)}, bf16[2,96,2048]{2,1,0:T(8,128)(2,1)}, bf16[2,1,96,2048]{3,2,1,0:T(8,128)(2,1)}) custom-call(bf16[1536,512]{1,0:T(8,128)(2,1)} %bitcast.194, f32[96,2048]{1,0:T(8,128)} %get-tuple-element.324.cosine_ref, f32[96,2048]{1,0:T(8,128)} %get-tuple-element.325.sine_ref, bf16[1536,256]{1,0:T(8,128)(2,1)} %bitcast.201, ...), custom_call_target="tpu_custom_call" | custom-call | flops 1000 | bytes 1000 | tf_op jit(solution)/shard_map/pallas_call | solution.py:514
  114.1 3.4 shard_map.214
  118.8 13.2 %collective-permute-done.22.refs_1_ = bf16[2,1,96,2048]{3,2,1,0:T(8,128)(2,1)S(1)} collective-permute-done((bf16[2,1,96,2048]{3,2,1,0:T(8,128)(2,1)}, bf16[2,1,96,2048]{3,2,1,0:T(8,128)(2,1)S(1)}, u32[]{:S(2)}, u32[]{:S(2)}) %collective-permute-start.22) | collective-permute-done | bytes 786464 | tf_op jit(solution)/shard_map/ppermute | solution.py:289
  134.3 3.8 collective-permute-start.26
  139.6 19.4 %shard_map.215 = (f32[2,96,2048]{2,1,0:T(8,128)}, f32[2,1,2048]{2,1,0:T(1,128)}) custom-call(s32[9]{0:T(128)} %pad_add_fusion.1.low_ref, s32[1,2048]{1,0:T(1,128)} %bitcast.245, bf16[2,96,2048]{2,1,0:T(8,128)(2,1)} %get-tuple-element.349.query_ref, bf16[2,1,96,2048]{3,2,1,0:T(8,128)(2,1)} %get-tuple-element.337.refs_0_, bf16[2,1,96,2048]{3,2,1,0:T(8,128)(2,1)} %copy-done.7), custom_call_target="tpu_custom_call" | custom-call | flops 1000 | bytes 1000 | tf_op jit(solution)/shard_map/pallas_call | solution.py:209
  158.9 9.4 %shard_map.216 = (f32[1536,1024]{1,0:T(8,128)}, bf16[1536,1024]{1,0:T(8,128)(2,1)}) custom-call(f32[2,96,2048]{2,1,0:T(8,128)} %get-tuple-element.351.attended_ref.out_ref, bf16[192,1536]{1,0:T(8,128)(2,1)} %bitcast.204), custom_call_target="tpu_custom_call" | custom-call | flops 1000 | bytes 1000 | tf_op jit(solution)/shard_map/pallas_call | solution.py:552
  170.3 4.1 collective-permute-done.28.arrived_ref
  176.5 4.9 collective-permute-start.33
  181.4 6.8 %shard_map.217 = (f32[1536,256]{1,0:T(8,128)}, bf16[1536,256]{1,0:T(8,128)(2,1)}, bf16[1536,256]{1,0:T(8,128)(2,1)}, bf16[1536,256]{1,0:T(8,128)(2,1)}) custom-call(f32[1536,1024]{1,0:T(8,128)} %get-tuple-element.365.keep_ref, bf16[1536,1024]{1,0:T(8,128)(2,1)} %collective-permute-done.28.arrived_ref), custom_call_target="tpu_custom_call" | custom-call | flops 1000 | bytes 1000 | tf_op jit(solution)/shard_map/pallas_call | solution.py:875
  190.4 14.4 %collective-permute-done.32.refs_3_ = bf16[8,48,1536]{2,1,0:T(8,128)(2,1)} collective-permute-done((bf16[8,48,1536]{2,1,0:T(8,128)(2,1)S(1)}, bf16[8,48,1536]{2,1,0:T(8,128)(2,1)}, u32[]{:S(2)}, u32[]{:S(2)}) %collective-permute-start.32) | collective-permute-done | bytes 1179680 | tf_op jit(solution)/shard_map/ppermute | solution.py:289
  209.7 4.0 collective-permute-start.36
  216.6 16.1 %collective-permute-done.34.refs_3_ = bf16[1536,256]{1,0:T(8,128)(2,1)S(1)} collective-permute-done((bf16[1536,256]{1,0:T(8,128)(2,1)}, bf16[1536,256]{1,0:T(8,128)(2,1)S(1)}, u32[]{:S(2)}, u32[]{:S(2)}) %collective-permute-start.34) | collective-permute-done | bytes 786464 | tf_op jit(solution)/shard_map/ppermute | solution.py:281
  233.6 4.7 shard_map.218
  241.7 6.7 %shard_map.219 = (bf16[4,8,48,1024]{3,2,1,0:T(8,128)(2,1)}, bf16[4,128,1536]{2,1,0:T(8,128)(2,1)}) custom-call(s32[2]{0:T(128)} %pad_add_fusion.2.places_ref, bf16[8,48,1536]{2,1,0:T(8,128)(2,1)} %copy-done.5, bf16[8,48,1536]{2,1,0:T(8,128)(2,1)} %copy-done.23, bf16[8,48,1536]{2,1,0:T(8,128)(2,1)} %collective-permute-done.26.refs_2_, ...), custom_call_target="tpu_custom_call" | custom-call | flops 1000 | bytes 1000 | tf_op jit(solution)/shard_map/pallas_call | solution.py:461
  249.3 10.6 %shard_map.220 = (bf16[512,512]{1,0:T(8,128)(2,1)}, bf16[512,1024]{1,0:T(8,128)(2,1)}, f32[1536,256]{1,0:T(8,128)}, bf16[1536,256]{1,0:T(8,128)(2,1)}) custom-call(bf16[1536,256]{1,0:T(8,128)(2,1)} %get-tuple-element.410.first_ref.refs_0_, bf16[1536,256]{1,0:T(8,128)(2,1)} %copy-done.13, bf16[4,256,1536]{2,1,0:T(8,128)(2,1)} %copy-done, ...), custom_call_target="tpu_custom_call" | custom-call | flops 1000 | bytes 1000 | tf_op jit(solution)/shard_map/pallas_call | solution.py:602
  263.5 10.9 %shard_map.221 = (bf16[512,512]{1,0:T(8,128)(2,1)}, bf16[512,1024]{1,0:T(8,128)(2,1)}, f32[1536,256]{1,0:T(8,128)}, bf16[1536,256]{1,0:T(8,128)(2,1)}) custom-call(bf16[1536,256]{1,0:T(8,128)(2,1)} %copy-done.14, bf16[1536,256]{1,0:T(8,128)(2,1)} %copy-done.16, bf16[4,256,1536]{2,1,0:T(8,128)(2,1)} %copy-done, bf16[4,256,1536]{2,1,0:T(8,128)(2,1)} %copy-done.1, ...), custom_call_target="tpu_custom_call" | custom-call | flops 1000 | bytes 1000 | tf_op jit(solution)/shard_map/pallas_call | solution.py:602
  274.4 6.6 %collective-permute-done.42.first_ref.refs_3_ = bf16[1536,256]{1,0:T(8,128)(2,1)S(1)} collective-permute-done((bf16[1536,256]{1,0:T(8,128)(2,1)S(1)}, bf16[1536,256]{1,0:T(8,128)(2,1)S(1)}, u32[]{:S(2)}, u32[]{:S(2)}) %collective-permute-start.42) | collective-permute-done | bytes 786464 | tf_op jit(solution)/shard_map/ppermute | solution.py:281
  281.6 10.6 %shard_map.222 = (bf16[512,512]{1,0:T(8,128)(2,1)}, bf16[512,1024]{1,0:T(8,128)(2,1)}, f32[1536,256]{1,0:T(8,128)}, bf16[1536,256]{1,0:T(8,128)(2,1)}) custom-call(bf16[1536,256]{1,0:T(8,128)(2,1)} %copy-done.15, bf16[1536,256]{1,0:T(8,128)(2,1)} %copy-done.17, bf16[4,256,1536]{2,1,0:T(8,128)(2,1)} %copy-done, bf16[4,256,1536]{2,1,0:T(8,128)(2,1)} %copy-done.1, ...), custom_call_target="tpu_custom_call" | custom-call | flops 1000 | bytes 1000 | tf_op jit(solution)/shard_map/pallas_call | solution.py:602
  293.2 10.6 %shard_map.224 = (bf16[512,512]{1,0:T(8,128)(2,1)}, bf16[512,1024]{1,0:T(8,128)(2,1)}, f32[1536,256]{1,0:T(8,128)}, bf16[1536,256]{1,0:T(8,128)(2,1)}) custom-call(bf16[1536,256]{1,0:T(8,128)(2,1)} %copy-done.18, bf16[1536,256]{1,0:T(8,128)(2,1)} %copy-done.19, bf16[4,256,1536]{2,1,0:T(8,128)(2,1)} %copy-done, bf16[4,256,1536]{2,1,0:T(8,128)(2,1)} %copy-done.1, ...), custom_call_target="tpu_custom_call" | custom-call | flops 1000 | bytes 1000 | tf_op jit(solution)/shard_map/pallas_call | solution.py:602
  317.1 30.3 %shard_map.227.own_ref = bf16[4,384,1024]{2,1,0:T(8,128)(2,1)} custom-call(s32[2]{0:T(128)} %pad_add_fusion.2.places_ref, bf16[1536,256]{1,0:T(8,128)(2,1)} %get-tuple-element.410.first_ref.refs_0_, bf16[1536,256]{1,0:T(8,128)(2,1)} %copy-done.14, bf16[1536,256]{1,0:T(8,128)(2,1)} %copy-done.15, bf16[1536,256]{1,0:T(8,128)(2,1)} %copy-done.18, ...), custom_call_target="tpu_custom_call" | custom-call | flops 1000 | bytes 1000 | tf_op jit(solution)/shard_map/pallas_call | solution.py:695
  349.4 4.0 collective-permute-start.55
  353.4 13.8 %shard_map.228.own_ref = bf16[4,128,1536]{2,1,0:T(8,128)(2,1)} custom-call(s32[2]{0:T(128)} %pad_add_fusion.2.places_ref, bf16[512,512]{1,0:T(8,128)(2,1)} %get-tuple-element.471.refs_0_, bf16[512,512]{1,0:T(8,128)(2,1)} %get-tuple-element.472.refs_1_, bf16[512,512]{1,0:T(8,128)(2,1)} %get-tuple-element.473.refs_2_, ...), custom_call_target="tpu_custom_call" | custom-call | flops 1000 | bytes 1000 | tf_op jit(solution)/shard_map/pallas_call | solution.py:730
  368.7 6.2 %shard_map.229 = (f32[1536,256]{1,0:T(8,128)}, bf16[1536,256]{1,0:T(8,128)(2,1)}, f32[1536,1]{1,0:T(8,128)}) custom-call(f32[1536,256]{1,0:T(8,128)} %get-tuple-element.462.refs_0_, bf16[1536,256]{1,0:T(8,128)(2,1)} %copy-done.48, bf16[1536,256]{1,0:T(8,128)(2,1)} %copy-done.49, bf16[1536,256]{1,0:T(8,128)(2,1)} %copy-done.50, bf16[1536,256]{1,0:T(8,128)(2,1)} %copy-done.52, ...), custom_call_target="tpu_custom_call" | custom-call | flops 1000 | bytes 1000 | tf_op jit(solution)/shard_map/pallas_call | solution.py:894
  378.4 10.0 %shard_map.230 = (f32[1024,1536]{1,0:T(8,128)}, bf16[1024,1536]{1,0:T(8,128)(2,1)}) custom-call(bf16[512,1536]{1,0:T(8,128)(2,1)} %bitcast.193, bf16[512,512]{1,0:T(8,128)(2,1)} %get-tuple-element.471.refs_0_, bf16[512,512]{1,0:T(8,128)(2,1)} %get-tuple-element.472.refs_1_, bf16[512,512]{1,0:T(8,128)(2,1)} %get-tuple-element.473.refs_2_, ...), custom_call_target="tpu_custom_call" | custom-call | flops 1000 | bytes 1000 | tf_op jit(solution)/shard_map/pallas_call | solution.py:647
  388.5 11.0 %collective-permute-done.55.refs_1_ = bf16[384,1024]{1,0:T(8,128)(2,1)S(1)} collective-permute-done((bf16[384,1024]{1,0:T(8,128)(2,1)S(1)}, bf16[384,1024]{1,0:T(8,128)(2,1)S(1)}, u32[]{:S(2)}, u32[]{:S(2)}) %collective-permute-start.55) | collective-permute-done | bytes 786464 | tf_op jit(solution)/shard_map/ppermute | solution.py:289
  399.5 10.2 %collective-permute-done.52.refs_2_ = bf16[1536,256]{1,0:T(8,128)(2,1)S(1)} collective-permute-done((bf16[1536,256]{1,0:T(8,128)(2,1)}, bf16[1536,256]{1,0:T(8,128)(2,1)S(1)}, u32[]{:S(2)}, u32[]{:S(2)}) %collective-permute-start.52) | collective-permute-done | bytes 786464 | tf_op jit(solution)/shard_map/ppermute | solution.py:281
  417.6 11.3 %shard_map.231 = (bf16[2,96,2048]{2,1,0:T(8,128)(2,1)}, bf16[4,48,1536]{2,1,0:T(8,128)(2,1)}) custom-call(s32[2]{0:T(128)} %pad_add_fusion.2.places_ref, bf16[192,1536]{1,0:T(8,128)(2,1)} %bitcast.205, f32[2,96,2048]{2,1,0:T(8,128)} %get-tuple-element.351.attended_ref.out_ref, bf16[1536,256]{1,0:T(8,128)(2,1)} %get-tuple-element.483.refs_0_, ...), custom_call_target="tpu_custom_call" | custom-call | flops 1000 | bytes 1000 | tf_op jit(solution)/shard_map/pallas_call | solution.py:777
  431.8 25.9 %shard_map.232 = (f32[2,96,2048]{2,1,0:T(8,128)}, f32[2,1,96,2048]{3,2,1,0:T(8,128)}, bf16[1,2,1,96,2048]{4,3,2,1,0:T(8,128)(2,1)}) custom-call(s32[9]{0:T(128)} %pad_add_fusion.1.low_ref, s32[1,2048]{1,0:T(1,128)} %bitcast.246, bf16[2,96,2048]{2,1,0:T(8,128)(2,1)} %get-tuple-element.349.query_ref, bf16[2,96,2048]{2,1,0:T(8,128)(2,1)} %get-tuple-element.495.grad_ref, ...), custom_call_target="tpu_custom_call" | custom-call | flops 1000 | bytes 1000 | tf_op jit(solution)/shard_map/pallas_call | solution.py:235
  461.8 6.7 %shard_map.233 = (f32[256,1536]{1,0:T(8,128)}, bf16[256,1536]{1,0:T(8,128)(2,1)}, bf16[256,1536]{1,0:T(8,128)(2,1)}, bf16[256,1536]{1,0:T(8,128)(2,1)}) custom-call(f32[1024,1536]{1,0:T(8,128)} %get-tuple-element.503.keep_ref, bf16[1024,1536]{1,0:T(8,128)(2,1)} %copy-done.9), custom_call_target="tpu_custom_call" | custom-call | flops 1000 | bytes 1000 | tf_op jit(solution)/shard_map/pallas_call | solution.py:875
  472.0 3.1 shard_map.234
  475.1 17.4 %collective-permute-done.63.refs_1_ = bf16[2,1,96,2048]{3,2,1,0:T(8,128)(2,1)S(1)} collective-permute-done((bf16[2,1,96,2048]{3,2,1,0:T(8,128)(2,1)}, bf16[2,1,96,2048]{3,2,1,0:T(8,128)(2,1)S(1)}, u32[]{:S(2)}, u32[]{:S(2)}) %collective-permute-start.63) | collective-permute-done | bytes 786464 | tf_op jit(solution)/shard_map/ppermute | solution.py:289
  494.6 23.7 %shard_map.235 = (f32[1536,1024]{1,0:T(8,128)}, bf16[1536,1024]{1,0:T(8,128)(2,1)}, bf16[4,384,384]{2,1,0:T(8,128)(2,1)}) custom-call(s32[2]{0:T(128)} %pad_add_fusion.2.places_ref, bf16[1536,2048]{1,0:T(8,128)(2,1)} %get-tuple-element.514.normed_ref, f32[2,96,2048]{2,1,0:T(8,128)} %get-tuple-element.515.query_ref, ...), custom_call_target="tpu_custom_call" | custom-call | flops 1000 | bytes 1000 | tf_op jit(solution)/shard_map/pallas_call | solution.py:837
  526.4 4.0 shard_map.237
  530.4 3.2 collective-permute-start.75
  533.6 6.8 %shard_map.236 = (f32[1536,256]{1,0:T(8,128)}, bf16[1536,256]{1,0:T(8,128)(2,1)}, bf16[1536,256]{1,0:T(8,128)(2,1)}, bf16[1536,256]{1,0:T(8,128)(2,1)}) custom-call(f32[1536,1024]{1,0:T(8,128)} %get-tuple-element.527.keep_ref, bf16[1536,1024]{1,0:T(8,128)(2,1)} %collective-permute-done.70.arrived_ref), custom_call_target="tpu_custom_call" | custom-call | flops 1000 | bytes 1000 | tf_op jit(solution)/shard_map/pallas_call | solution.py:875
  546.2 6.7 %collective-permute-done.75.refs_1_ = bf16[384,384]{1,0:T(8,128)(2,1)S(1)} collective-permute-done((bf16[384,384]{1,0:T(8,128)(2,1)S(1)}, bf16[384,384]{1,0:T(8,128)(2,1)S(1)}, u32[]{:S(2)}, u32[]{:S(2)}) %collective-permute-start.75) | collective-permute-done | bytes 294944 | tf_op jit(solution)/shard_map/ppermute | solution.py:289
  555.6 3.4 collective-permute-start.83
  563.0 13.7 %collective-permute-done.77.refs_2_ = bf16[1536,256]{1,0:T(8,128)(2,1)} collective-permute-done((bf16[1536,256]{1,0:T(8,128)(2,1)}, bf16[1536,256]{1,0:T(8,128)(2,1)}, u32[]{:S(2)}, u32[]{:S(2)}) %collective-permute-start.77) | collective-permute-done | bytes 786464 | tf_op jit(solution)/shard_map/ppermute | solution.py:281
  576.7 5.5 shard_map.239
  602.5 6.9 %collective-permute-done.91 = bf16[48,1536]{1,0:T(8,128)(2,1)S(1)} collective-permute-done((bf16[48,1536]{1,0:T(8,128)(2,1)}, bf16[48,1536]{1,0:T(8,128)(2,1)S(1)}, u32[]{:S(2)}, u32[]{:S(2)}) %collective-permute-start.91) | collective-permute-done | bytes 147488 | tf_op jit(solution)/shard_map/ppermute | solution.py:315
  609.9 3.4 collective-permute-start.94
  (407 shorter events, 165.2 us)
Async XLA Ops:
  10.5 32.1 %collective-permute-start.7 = (bf16[1536,256]{1,0:T(8,128)(2,1)S(1)}, bf16[1536,256]{1,0:T(8,128)(2,1)}, u32[]{:S(2)}, u32[]{:S(2)}) collective-permute-start(bf16[1536,256]{1,0:T(8,128)(2,1)S(1)} %bitcast.197), channel_id=1, source_target_pairs={{0,2},{1,3},{2,0},{3,1},{4,6},{5,7},{6,4},{7,5},{8,10},{9,11},{10,... | collective-permute-start | bytes 2359304 | tf_op jit(solution)/shard_map/ppermute | solution.py:281
  11.1 31.5 %collective-permute-start.8 = (bf16[1536,256]{1,0:T(8,128)(2,1)S(1)}, bf16[1536,256]{1,0:T(8,128)(2,1)}, u32[]{:S(2)}, u32[]{:S(2)}) collective-permute-start(bf16[1536,256]{1,0:T(8,128)(2,1)S(1)} %bitcast.198), channel_id=1, source_target_pairs={{0,4},{1,5},{2,6},{3,7},{4,0},{5,1},{6,2},{7,3},{8,12},{9,13},{10,... | collective-permute-start | bytes 2359304 | tf_op jit(solution)/shard_map/ppermute | solution.py:281
  14.7 22.7 %collective-permute-start.4 = (bf16[2,48,1536]{2,1,0:T(8,128)(2,1)}, bf16[2,48,1536]{2,1,0:T(8,128)(2,1)S(1)}, u32[]{:S(2)}, u32[]{:S(2)}) collective-permute-start(bf16[2,48,1536]{2,1,0:T(8,128)(2,1)} %get-tuple-element.606), channel_id=1, source_target_pairs={{0,2},{1,3},{2,0},{3,1},{4,6},{5,7},{6,4},{7,5},{8,10},{9,11},{10,... | collective-permute-start | bytes 884744 | tf_op jit(solution)/shard_map/ppermute | solution.py:281
  16.2 24.8 %collective-permute-start.5 = (bf16[2,48,1536]{2,1,0:T(8,128)(2,1)}, bf16[2,48,1536]{2,1,0:T(8,128)(2,1)S(1)}, u32[]{:S(2)}, u32[]{:S(2)}) collective-permute-start(bf16[2,48,1536]{2,1,0:T(8,128)(2,1)} %get-tuple-element.605), channel_id=1, source_target_pairs={{0,4},{1,5},{2,6},{3,7},{4,0},{5,1},{6,2},{7,3},{8,12},{9,13},{10,... | collective-permute-start | bytes 884744 | tf_op jit(solution)/shard_map/ppermute | solution.py:281
  18.0 24.6 %collective-permute-start.6 = (bf16[2,48,1536]{2,1,0:T(8,128)(2,1)S(1)}, bf16[2,48,1536]{2,1,0:T(8,128)(2,1)S(1)}, u32[]{:S(2)}, u32[]{:S(2)}) collective-permute-start(bf16[2,48,1536]{2,1,0:T(8,128)(2,1)S(1)} %get-tuple-element.604), channel_id=1, source_target_pairs={{0,6},{1,7},{2,4},{3,5},{4,2},{5,3},{6,0},{7,1},{8,14},{9,15},{10,... | collective-permute-start | bytes 884744 | tf_op jit(solution)/shard_map/ppermute | solution.py:281
  42.9 21.0 %collective-permute-start.13 = (bf16[1536,256]{1,0:T(8,128)(2,1)S(1)}, bf16[1536,256]{1,0:T(8,128)(2,1)}, u32[]{:S(2)}, u32[]{:S(2)}) collective-permute-start(bf16[1536,256]{1,0:T(8,128)(2,1)S(1)} %bitcast.199), channel_id=1, source_target_pairs={{0,6},{1,7},{2,4},{3,5},{4,2},{5,3},{6,0},{7,1},{8,14},{9,15},{10,... | collective-permute-start | bytes 2359304 | tf_op jit(solution)/shard_map/ppermute | solution.py:281
  45.1 28.0 %collective-permute-start.10 = (bf16[8,48,512]{2,1,0:T(8,128)(2,1)S(1)}, bf16[8,48,512]{2,1,0:T(8,128)(2,1)S(1)}, u32[]{:S(2)}, u32[]{:S(2)}) collective-permute-start(bf16[8,48,512]{2,1,0:T(8,128)(2,1)S(1)} %fusion.2.refs_0_), channel_id=1, source_target_pairs={{0,8},{1,9},{2,10},{3,11},{4,12},{5,13},{6,14},{7,15},{8,16},{9,17... | collective-permute-start | bytes 1179656 | tf_op jit(solution)/shard_map/ppermute | solution.py:289
  46.7 34.0 %collective-permute-start.11 = (bf16[8,48,512]{2,1,0:T(8,128)(2,1)S(1)}, bf16[8,48,512]{2,1,0:T(8,128)(2,1)S(1)}, u32[]{:S(2)}, u32[]{:S(2)}) collective-permute-start(bf16[8,48,512]{2,1,0:T(8,128)(2,1)S(1)} %fusion.2.refs_0_), channel_id=1, source_target_pairs={{0,16},{1,17},{2,18},{3,19},{4,20},{5,21},{6,22},{7,23},{8,24},{9,... | collective-permute-start | bytes 1179656 | tf_op jit(solution)/shard_map/ppermute | solution.py:289
  47.9 34.5 %collective-permute-start.12 = (bf16[8,48,512]{2,1,0:T(8,128)(2,1)S(1)}, bf16[8,48,512]{2,1,0:T(8,128)(2,1)S(1)}, u32[]{:S(2)}, u32[]{:S(2)}) collective-permute-start(bf16[8,48,512]{2,1,0:T(8,128)(2,1)S(1)} %fusion.2.refs_0_), channel_id=1, source_target_pairs={{0,24},{1,25},{2,26},{3,27},{4,28},{5,29},{6,30},{7,31},{8,0},{9,1... | collective-permute-start | bytes 1179656 | tf_op jit(solution)/shard_map/ppermute | solution.py:289
  49.8 42.4 %collective-permute-start.14 = (bf16[1536,256]{1,0:T(8,128)(2,1)S(1)}, bf16[1536,256]{1,0:T(8,128)(2,1)}, u32[]{:S(2)}, u32[]{:S(2)}) collective-permute-start(bf16[1536,256]{1,0:T(8,128)(2,1)S(1)} %bitcast.200), channel_id=1, source_target_pairs={{0,1},{1,0},{2,3},{3,2},{4,5},{5,4},{6,7},{7,6},{8,9},{9,8},{10,11... | collective-permute-start | bytes 2359304 | tf_op jit(solution)/shard_map/ppermute | solution.py:281
  63.9 28.2 %collective-permute-start.15 = (bf16[1536,256]{1,0:T(8,128)(2,1)}, bf16[1536,256]{1,0:T(8,128)(2,1)}, u32[]{:S(2)}, u32[]{:S(2)}) collective-permute-start(bf16[1536,256]{1,0:T(8,128)(2,1)} %collective-permute-done.7.refs_1_), channel_id=1, source_target_pairs={{0,1},{1,0},{2,3},{3,2},{4,5},{5,4},{6,7},{7,6},{8,9},{9,8},{10,11... | collective-permute-start | bytes 2359304 | tf_op jit(solution)/shard_map/ppermute | solution.py:281
  110.5 21.6 %collective-permute-start.22 = (bf16[2,1,96,2048]{3,2,1,0:T(8,128)(2,1)}, bf16[2,1,96,2048]{3,2,1,0:T(8,128)(2,1)S(1)}, u32[]{:S(2)}, u32[]{:S(2)}) collective-permute-start(bf16[2,1,96,2048]{3,2,1,0:T(8,128)(2,1)} %get-tuple-element.337.refs_0_), channel_id=1, source_target_pairs={{0,8},{1,9},{2,10},{3,11},{4,12},{5,13},{6,14},{7,15},{8,16},{9,17... | collective-permute-start | bytes 2359304 | tf_op jit(solution)/shard_map/ppermute | solution.py:289
  132.2 36.1 %collective-permute-start.25 = (bf16[8,48,1536]{2,1,0:T(8,128)(2,1)S(1)}, bf16[8,48,1536]{2,1,0:T(8,128)(2,1)S(1)}, u32[]{:S(2)}, u32[]{:S(2)}) collective-permute-start(bf16[8,48,1536]{2,1,0:T(8,128)(2,1)S(1)} %pad_maximum_fusion.3.refs_0_), channel_id=1, source_target_pairs={{0,8},{1,9},{2,10},{3,11},{4,12},{5,13},{6,14},{7,15},{8,16},{9,17... | collective-permute-start | bytes 3538952 | tf_op jit(solution)/shard_map/ppermute | solution.py:289
  134.3 34.0 %collective-permute-start.26 = (bf16[8,48,1536]{2,1,0:T(8,128)(2,1)S(1)}, bf16[8,48,1536]{2,1,0:T(8,128)(2,1)}, u32[]{:S(2)}, u32[]{:S(2)}) collective-permute-start(bf16[8,48,1536]{2,1,0:T(8,128)(2,1)S(1)} %pad_maximum_fusion.3.refs_0_), channel_id=1, source_target_pairs={{8,0},{9,1},{10,2},{11,3},{12,4},{13,5},{14,6},{15,7},{16,8},{17,9... | collective-permute-start | bytes 3538952 | tf_op jit(solution)/shard_map/ppermute | solution.py:289
  138.1 30.2 %collective-permute-start.27 = (bf16[256,1536]{1,0:T(8,128)(2,1)S(1)}, bf16[256,1536]{1,0:T(8,128)(2,1)S(1)}, u32[]{:S(2)}, u32[]{:S(2)}) collective-permute-start(bf16[256,1536]{1,0:T(8,128)(2,1)S(1)} %copy-done.10), channel_id=1, source_target_pairs={{0,6},{1,7},{2,4},{3,5},{4,2},{5,3},{6,0},{7,1},{8,14},{9,15},{10,... | collective-permute-start | bytes 2359304 | tf_op jit(solution)/shard_map/ppermute | solution.py:281
  174.5 30.2 %collective-permute-start.32 = (bf16[8,48,1536]{2,1,0:T(8,128)(2,1)S(1)}, bf16[8,48,1536]{2,1,0:T(8,128)(2,1)}, u32[]{:S(2)}, u32[]{:S(2)}) collective-permute-start(bf16[8,48,1536]{2,1,0:T(8,128)(2,1)S(1)} %collective-permute-done.25.refs_1_), channel_id=1, source_target_pairs={{0,8},{1,9},{2,10},{3,11},{4,12},{5,13},{6,14},{7,15},{8,16},{9,17... | collective-permute-start | bytes 3538952 | tf_op jit(solution)/shard_map/ppermute | solution.py:289
  176.5 30.7 %collective-permute-start.33 = (bf16[8,48,1536]{2,1,0:T(8,128)(2,1)}, bf16[8,48,1536]{2,1,0:T(8,128)(2,1)}, u32[]{:S(2)}, u32[]{:S(2)}) collective-permute-start(bf16[8,48,1536]{2,1,0:T(8,128)(2,1)} %collective-permute-done.26.refs_2_), channel_id=1, source_target_pairs={{8,0},{9,1},{10,2},{11,3},{12,4},{13,5},{14,6},{15,7},{16,8},{17,9... | collective-permute-start | bytes 3538952 | tf_op jit(solution)/shard_map/ppermute | solution.py:289
  207.8 30.6 %collective-permute-start.35 = (bf16[8,48,1536]{2,1,0:T(8,128)(2,1)}, bf16[8,48,1536]{2,1,0:T(8,128)(2,1)S(1)}, u32[]{:S(2)}, u32[]{:S(2)}) collective-permute-start(bf16[8,48,1536]{2,1,0:T(8,128)(2,1)} %collective-permute-done.32.refs_3_), channel_id=1, source_target_pairs={{0,8},{1,9},{2,10},{3,11},{4,12},{5,13},{6,14},{7,15},{8,16},{9,17... | collective-permute-start | bytes 3538952 | tf_op jit(solution)/shard_map/ppermute | solution.py:289
  209.7 28.9 %collective-permute-start.36 = (bf16[8,48,1536]{2,1,0:T(8,128)(2,1)}, bf16[8,48,1536]{2,1,0:T(8,128)(2,1)S(1)}, u32[]{:S(2)}, u32[]{:S(2)}) collective-permute-start(bf16[8,48,1536]{2,1,0:T(8,128)(2,1)} %collective-permute-done.33.refs_4_), channel_id=1, source_target_pairs={{8,0},{9,1},{10,2},{11,3},{12,4},{13,5},{14,6},{15,7},{16,8},{17,9... | collective-permute-start | bytes 3538952 | tf_op jit(solution)/shard_map/ppermute | solution.py:289
  238.6 21.3 %collective-permute-start.38 = (bf16[1536,256]{1,0:T(8,128)(2,1)}, bf16[1536,256]{1,0:T(8,128)(2,1)S(1)}, u32[]{:S(2)}, u32[]{:S(2)}) collective-permute-start(bf16[1536,256]{1,0:T(8,128)(2,1)} %get-tuple-element.410.first_ref.refs_0_), channel_id=1, source_target_pairs={{0,2},{1,3},{2,0},{3,1},{4,6},{5,7},{6,4},{7,5},{8,10},{9,11},{10,... | collective-permute-start | bytes 2359304 | tf_op jit(solution)/shard_map/ppermute | solution.py:281
  260.6 20.4 %collective-permute-start.42 = (bf16[1536,256]{1,0:T(8,128)(2,1)S(1)}, bf16[1536,256]{1,0:T(8,128)(2,1)S(1)}, u32[]{:S(2)}, u32[]{:S(2)}) collective-permute-start(bf16[1536,256]{1,0:T(8,128)(2,1)S(1)} %copy-done.12), channel_id=1, source_target_pairs={{0,6},{1,7},{2,4},{3,5},{4,2},{5,3},{6,0},{7,1},{8,14},{9,15},{10,... | collective-permute-start | bytes 2359304 | tf_op jit(solution)/shard_map/ppermute | solution.py:281
  310.3 57.0 %collective-permute-start.48 = (bf16[1536,256]{1,0:T(8,128)(2,1)S(1)}, bf16[1536,256]{1,0:T(8,128)(2,1)S(1)}, u32[]{:S(2)}, u32[]{:S(2)}) collective-permute-start(bf16[1536,256]{1,0:T(8,128)(2,1)S(1)} %copy-done.41), channel_id=1, source_target_pairs={{0,2},{1,3},{2,0},{3,1},{4,6},{5,7},{6,4},{7,5},{8,10},{9,11},{10,... | collective-permute-start | bytes 2359304 | tf_op jit(solution)/shard_map/ppermute | solution.py:281
  311.0 56.3 %collective-permute-start.49 = (bf16[1536,256]{1,0:T(8,128)(2,1)}, bf16[1536,256]{1,0:T(8,128)(2,1)S(1)}, u32[]{:S(2)}, u32[]{:S(2)}) collective-permute-start(bf16[1536,256]{1,0:T(8,128)(2,1)} %shard_map.225), channel_id=1, source_target_pairs={{0,4},{1,5},{2,6},{3,7},{4,0},{5,1},{6,2},{7,3},{8,12},{9,13},{10,... | collective-permute-start | bytes 2359304 | tf_op jit(solution)/shard_map/ppermute | solution.py:281
  315.8 51.5 %collective-permute-start.50 = (bf16[1536,256]{1,0:T(8,128)(2,1)}, bf16[1536,256]{1,0:T(8,128)(2,1)S(1)}, u32[]{:S(2)}, u32[]{:S(2)}) collective-permute-start(bf16[1536,256]{1,0:T(8,128)(2,1)} %shard_map.226), channel_id=1, source_target_pairs={{0,6},{1,7},{2,4},{3,5},{4,2},{5,3},{6,0},{7,1},{8,14},{9,15},{10,... | collective-permute-start | bytes 2359304 | tf_op jit(solution)/shard_map/ppermute | solution.py:281
  349.2 39.2 %collective-permute-start.54 = (bf16[384,1024]{1,0:T(8,128)(2,1)S(1)}, bf16[384,1024]{1,0:T(8,128)(2,1)S(1)}, u32[]{:S(2)}, u32[]{:S(2)}) collective-permute-start(bf16[384,1024]{1,0:T(8,128)(2,1)S(1)} %get-tuple-element.591), channel_id=1, source_target_pairs={{0,8},{1,9},{2,10},{3,11},{4,12},{5,13},{6,14},{7,15},{8,16},{9,17... | collective-permute-start | bytes 2359304 | tf_op jit(solution)/shard_map/ppermute | solution.py:289
  349.4 50.0 %collective-permute-start.55 = (bf16[384,1024]{1,0:T(8,128)(2,1)S(1)}, bf16[384,1024]{1,0:T(8,128)(2,1)S(1)}, u32[]{:S(2)}, u32[]{:S(2)}) collective-permute-start(bf16[384,1024]{1,0:T(8,128)(2,1)S(1)} %get-tuple-element.590), channel_id=1, source_target_pairs={{0,16},{1,17},{2,18},{3,19},{4,20},{5,21},{6,22},{7,23},{8,24},{9,... | collective-permute-start | bytes 2359304 | tf_op jit(solution)/shard_map/ppermute | solution.py:289
  374.9 24.5 %collective-permute-start.51 = (bf16[1536,256]{1,0:T(8,128)(2,1)}, bf16[1536,256]{1,0:T(8,128)(2,1)S(1)}, u32[]{:S(2)}, u32[]{:S(2)}) collective-permute-start(bf16[1536,256]{1,0:T(8,128)(2,1)} %get-tuple-element.483.refs_0_), channel_id=1, source_target_pairs={{0,2},{1,3},{2,0},{3,1},{4,6},{5,7},{6,4},{7,5},{8,10},{9,11},{10,... | collective-permute-start | bytes 2359304 | tf_op jit(solution)/shard_map/ppermute | solution.py:281
  375.6 34.0 %collective-permute-start.52 = (bf16[1536,256]{1,0:T(8,128)(2,1)}, bf16[1536,256]{1,0:T(8,128)(2,1)S(1)}, u32[]{:S(2)}, u32[]{:S(2)}) collective-permute-start(bf16[1536,256]{1,0:T(8,128)(2,1)} %get-tuple-element.483.refs_0_), channel_id=1, source_target_pairs={{0,4},{1,5},{2,6},{3,7},{4,0},{5,1},{6,2},{7,3},{8,12},{9,13},{10,... | collective-permute-start | bytes 2359304 | tf_op jit(solution)/shard_map/ppermute | solution.py:281
  377.1 33.9 %collective-permute-start.53 = (bf16[1536,256]{1,0:T(8,128)(2,1)}, bf16[1536,256]{1,0:T(8,128)(2,1)S(1)}, u32[]{:S(2)}, u32[]{:S(2)}) collective-permute-start(bf16[1536,256]{1,0:T(8,128)(2,1)} %get-tuple-element.483.refs_0_), channel_id=1, source_target_pairs={{0,6},{1,7},{2,4},{3,5},{4,2},{5,3},{6,0},{7,1},{8,14},{9,15},{10,... | collective-permute-start | bytes 2359304 | tf_op jit(solution)/shard_map/ppermute | solution.py:281
  428.9 28.8 %collective-permute-start.62 = (bf16[1024,1536]{1,0:T(8,128)(2,1)}, bf16[1024,1536]{1,0:T(8,128)(2,1)S(1)}, u32[]{:S(2)}, u32[]{:S(2)}) collective-permute-start(bf16[1024,1536]{1,0:T(8,128)(2,1)} %get-tuple-element.501), channel_id=1, source_target_pairs={{0,1},{1,0},{2,3},{3,2},{4,5},{5,4},{6,7},{7,6},{8,9},{9,8},{10,11... | collective-permute-start | bytes 9437192 | tf_op jit(solution)/shard_map/ppermute | solution.py:281
  429.1 28.6 %collective-permute-start.60 = (bf16[384,1024]{1,0:T(8,128)(2,1)S(1)}, bf16[384,1024]{1,0:T(8,128)(2,1)S(1)}, u32[]{:S(2)}, u32[]{:S(2)}) collective-permute-start(bf16[384,1024]{1,0:T(8,128)(2,1)S(1)} %get-tuple-element.589), channel_id=1, source_target_pairs={{0,24},{1,25},{2,26},{3,27},{4,28},{5,29},{6,30},{7,31},{8,0},{9,1... | collective-permute-start | bytes 2359304 | tf_op jit(solution)/shard_map/ppermute | solution.py:289
  430.1 27.7 %collective-permute-start.61 = (bf16[128,1536]{1,0:T(8,128)(2,1)S(1)}, bf16[128,1536]{1,0:T(8,128)(2,1)S(1)}, u32[]{:S(2)}, u32[]{:S(2)}) collective-permute-start(bf16[128,1536]{1,0:T(8,128)(2,1)S(1)} %get-tuple-element.594), channel_id=1, source_target_pairs={{0,24},{1,25},{2,26},{3,27},{4,28},{5,29},{6,30},{7,31},{8,0},{9,1... | collective-permute-start | bytes 1179656 | tf_op jit(solution)/shard_map/ppermute | solution.py:289
  457.8 34.8 %collective-permute-start.63 = (bf16[2,1,96,2048]{3,2,1,0:T(8,128)(2,1)}, bf16[2,1,96,2048]{3,2,1,0:T(8,128)(2,1)S(1)}, u32[]{:S(2)}, u32[]{:S(2)}) collective-permute-start(bf16[2,1,96,2048]{3,2,1,0:T(8,128)(2,1)} %bitcast.261), channel_id=1, source_target_pairs={{8,0},{9,1},{10,2},{11,3},{12,4},{13,5},{14,6},{15,7},{16,8},{17,9... | collective-permute-start | bytes 2359304 | tf_op jit(solution)/shard_map/ppermute | solution.py:289
  459.7 34.2 %collective-permute-start.67 = (bf16[128,1536]{1,0:T(8,128)(2,1)}, bf16[128,1536]{1,0:T(8,128)(2,1)S(1)}, u32[]{:S(2)}, u32[]{:S(2)}) collective-permute-start(bf16[128,1536]{1,0:T(8,128)(2,1)} %get-tuple-element.593), channel_id=1, source_target_pairs={{0,8},{1,9},{2,10},{3,11},{4,12},{5,13},{6,14},{7,15},{8,16},{9,17... | collective-permute-start | bytes 1179656 | tf_op jit(solution)/shard_map/ppermute | solution.py:289
  468.5 50.0 %collective-permute-start.64 = (bf16[256,1536]{1,0:T(8,128)(2,1)}, bf16[256,1536]{1,0:T(8,128)(2,1)S(1)}, u32[]{:S(2)}, u32[]{:S(2)}) collective-permute-start(bf16[256,1536]{1,0:T(8,128)(2,1)} %get-tuple-element.520), channel_id=1, source_target_pairs={{0,2},{1,3},{2,0},{3,1},{4,6},{5,7},{6,4},{7,5},{8,10},{9,11},{10,... | collective-permute-start | bytes 2359304 | tf_op jit(solution)/shard_map/ppermute | solution.py:281
  469.5 49.0 %collective-permute-start.65 = (bf16[256,1536]{1,0:T(8,128)(2,1)}, bf16[256,1536]{1,0:T(8,128)(2,1)S(1)}, u32[]{:S(2)}, u32[]{:S(2)}) collective-permute-start(bf16[256,1536]{1,0:T(8,128)(2,1)} %get-tuple-element.521), channel_id=1, source_target_pairs={{0,4},{1,5},{2,6},{3,7},{4,0},{5,1},{6,2},{7,3},{8,12},{9,13},{10,... | collective-permute-start | bytes 2359304 | tf_op jit(solution)/shard_map/ppermute | solution.py:281
  470.9 47.5 %collective-permute-start.66 = (bf16[256,1536]{1,0:T(8,128)(2,1)}, bf16[256,1536]{1,0:T(8,128)(2,1)}, u32[]{:S(2)}, u32[]{:S(2)}) collective-permute-start(bf16[256,1536]{1,0:T(8,128)(2,1)} %get-tuple-element.522), channel_id=1, source_target_pairs={{0,6},{1,7},{2,4},{3,5},{4,2},{5,3},{6,0},{7,1},{8,14},{9,15},{10,... | collective-permute-start | bytes 2359304 | tf_op jit(solution)/shard_map/ppermute | solution.py:281
  492.5 25.9 %collective-permute-start.68 = (bf16[128,1536]{1,0:T(8,128)(2,1)S(1)}, bf16[128,1536]{1,0:T(8,128)(2,1)S(1)}, u32[]{:S(2)}, u32[]{:S(2)}) collective-permute-start(bf16[128,1536]{1,0:T(8,128)(2,1)S(1)} %copy-done.56), channel_id=1, source_target_pairs={{0,16},{1,17},{2,18},{3,19},{4,20},{5,21},{6,22},{7,23},{8,24},{9,... | collective-permute-start | bytes 1179656 | tf_op jit(solution)/shard_map/ppermute | solution.py:289
  493.9 24.6 %collective-permute-start.69 = (bf16[4,48,1024]{2,1,0:T(8,128)(2,1)S(1)}, bf16[4,48,1024]{2,1,0:T(8,128)(2,1)}, u32[]{:S(2)}, u32[]{:S(2)}) collective-permute-start(bf16[4,48,1024]{2,1,0:T(8,128)(2,1)S(1)} %dynamic-slice_bitcast_fusion.2), channel_id=1, source_target_pairs={{0,1},{1,0},{2,3},{3,2},{4,5},{5,4},{6,7},{7,6},{8,9},{9,8},{10,11... | collective-permute-start | bytes 1179656 | tf_op jit(solution)/shard_map/ppermute | solution.py:281
  520.3 20.1 %collective-permute-start.71 = (bf16[2,48,1024]{2,1,0:T(8,128)(2,1)S(1)}, bf16[2,48,1024]{2,1,0:T(8,128)(2,1)S(1)}, u32[]{:S(2)}, u32[]{:S(2)}) collective-permute-start(bf16[2,48,1024]{2,1,0:T(8,128)(2,1)S(1)} %get-tuple-element.616), channel_id=1, source_target_pairs={{0,2},{1,3},{2,0},{3,1},{4,6},{5,7},{6,4},{7,5},{8,10},{9,11},{10,... | collective-permute-start | bytes 589832 | tf_op jit(solution)/shard_map/ppermute | solution.py:281
  523.9 20.8 %collective-permute-start.74 = (bf16[384,384]{1,0:T(8,128)(2,1)S(1)}, bf16[384,384]{1,0:T(8,128)(2,1)S(1)}, u32[]{:S(2)}, u32[]{:S(2)}) collective-permute-start(bf16[384,384]{1,0:T(8,128)(2,1)S(1)} %get-tuple-element.599), channel_id=1, source_target_pairs={{0,8},{1,9},{2,10},{3,11},{4,12},{5,13},{6,14},{7,15},{8,16},{9,17... | collective-permute-start | bytes 884744 | tf_op jit(solution)/shard_map/ppermute | solution.py:289
  530.4 22.5 %collective-permute-start.75 = (bf16[384,384]{1,0:T(8,128)(2,1)S(1)}, bf16[384,384]{1,0:T(8,128)(2,1)S(1)}, u32[]{:S(2)}, u32[]{:S(2)}) collective-permute-start(bf16[384,384]{1,0:T(8,128)(2,1)S(1)} %get-tuple-element.598), channel_id=1, source_target_pairs={{0,16},{1,17},{2,18},{3,19},{4,20},{5,21},{6,22},{7,23},{8,24},{9,... | collective-permute-start | bytes 884744 | tf_op jit(solution)/shard_map/ppermute | solution.py:289
  540.4 20.9 %collective-permute-start.76 = (bf16[1536,256]{1,0:T(8,128)(2,1)}, bf16[1536,256]{1,0:T(8,128)(2,1)}, u32[]{:S(2)}, u32[]{:S(2)}) collective-permute-start(bf16[1536,256]{1,0:T(8,128)(2,1)} %get-tuple-element.546), channel_id=1, source_target_pairs={{0,2},{1,3},{2,0},{3,1},{4,6},{5,7},{6,4},{7,5},{8,10},{9,11},{10,... | collective-permute-start | bytes 2359304 | tf_op jit(solution)/shard_map/ppermute | solution.py:281
  541.5 35.2 %collective-permute-start.77 = (bf16[1536,256]{1,0:T(8,128)(2,1)}, bf16[1536,256]{1,0:T(8,128)(2,1)}, u32[]{:S(2)}, u32[]{:S(2)}) collective-permute-start(bf16[1536,256]{1,0:T(8,128)(2,1)} %get-tuple-element.547), channel_id=1, source_target_pairs={{0,4},{1,5},{2,6},{3,7},{4,0},{5,1},{6,2},{7,3},{8,12},{9,13},{10,... | collective-permute-start | bytes 2359304 | tf_op jit(solution)/shard_map/ppermute | solution.py:281
  542.9 33.8 %collective-permute-start.78 = (bf16[1536,256]{1,0:T(8,128)(2,1)}, bf16[1536,256]{1,0:T(8,128)(2,1)}, u32[]{:S(2)}, u32[]{:S(2)}) collective-permute-start(bf16[1536,256]{1,0:T(8,128)(2,1)} %get-tuple-element.548), channel_id=1, source_target_pairs={{0,6},{1,7},{2,4},{3,5},{4,2},{5,3},{6,0},{7,1},{8,14},{9,15},{10,... | collective-permute-start | bytes 2359304 | tf_op jit(solution)/shard_map/ppermute | solution.py:281
  552.9 36.6 %collective-permute-start.82 = (bf16[48,1536]{1,0:T(8,128)(2,1)}, bf16[48,1536]{1,0:T(8,128)(2,1)}, u32[]{:S(2)}, u32[]{:S(2)}) collective-permute-start(bf16[48,1536]{1,0:T(8,128)(2,1)} %get-tuple-element.620), channel_id=1, source_target_pairs={{0,8},{1,9},{2,10},{3,11},{4,12},{5,13},{6,14},{7,15},{8,16},{9,17... | collective-permute-start | bytes 442376 | tf_op jit(solution)/shard_map/ppermute | solution.py:289
  555.6 33.9 %collective-permute-start.83 = (bf16[48,1536]{1,0:T(8,128)(2,1)S(1)}, bf16[48,1536]{1,0:T(8,128)(2,1)S(1)}, u32[]{:S(2)}, u32[]{:S(2)}) collective-permute-start(bf16[48,1536]{1,0:T(8,128)(2,1)S(1)} %copy-done.68), channel_id=1, source_target_pairs={{0,16},{1,17},{2,18},{3,19},{4,20},{5,21},{6,22},{7,23},{8,24},{9,... | collective-permute-start | bytes 442376 | tf_op jit(solution)/shard_map/ppermute | solution.py:289
  561.3 28.2 %collective-permute-start.84 = (bf16[48,1536]{1,0:T(8,128)(2,1)S(1)}, bf16[48,1536]{1,0:T(8,128)(2,1)S(1)}, u32[]{:S(2)}, u32[]{:S(2)}) collective-permute-start(bf16[48,1536]{1,0:T(8,128)(2,1)S(1)} %copy-done.67), channel_id=1, source_target_pairs={{0,24},{1,25},{2,26},{3,27},{4,28},{5,29},{6,30},{7,31},{8,0},{9,1... | collective-permute-start | bytes 442376 | tf_op jit(solution)/shard_map/ppermute | solution.py:289
  (122 other events, 1298.7 us)
